TPU v7x, 32 devices: a whole 2x2x4 slice. The times are simulated.
32 devices in a mesh: pipe: 2 (over x), dp: 16 (over z, y, core).
Axes of the slice: x: 2, y: 2, z: 4, core: 2. Of those that a mesh axis runs over, the one named last changes fastest.
Arguments:
- inputs: bfloat16 [32, 384, 1280], P('dp'), may hold values from -6 to 6
- out_grad: bfloat16 [32, 384, 1280], P('dp'), may hold values from -6 to 6
- query_counts: int32 [32], P('dp'), may hold values from 50 to 2000
- gains: bfloat16 [2, 2, 1280], P('pipe', None, 'dp'), may hold values from 0.5 to 1.5
- shifts: bfloat16 [2, 6, 1280], P('pipe', None, 'dp'), may hold values from -1.75 to 1.75
- w_qkv: bfloat16 [2, 1280, 3840], P('pipe', 'dp'), may hold values from -0.15625 to 0.15625
- w_out: bfloat16 [2, 1280, 1280], P('pipe', 'dp'), may hold values from -2 to 2
- w_up: bfloat16 [2, 1280, 5120], P('pipe', 'dp'), may hold values from -0.15625 to 0.15625
- b_up: bfloat16 [2, 5120], P('pipe', 'dp'), may hold values from -1.75 to 1.75
- w_down: bfloat16 [2, 5120, 1280], P('pipe', 'dp'), may hold values from -0.078125 to 0.078125
Outputs:
- section_outputs: bfloat16 [2, 32, 384, 1280], P('pipe', 'dp')
- input_grads: bfloat16 [2, 32, 384, 1280], P('pipe', 'dp')
- gains_grad: float32 [2, 2, 1280], P('pipe', None, 'dp')
- shifts_grad: float32 [2, 6, 1280], P('pipe', None, 'dp')
- w_qkv_grad: float32 [2, 1280, 3840], P('pipe', 'dp')
- w_out_grad: float32 [2, 1280, 1280], P('pipe', 'dp')
- w_up_grad: float32 [2, 1280, 5120], P('pipe', 'dp')
- b_up_grad: float32 [2, 5120], P('pipe', 'dp')
- w_down_grad: float32 [2, 5120, 1280], P('pipe', 'dp')
Inputs may be any that keep to these rules, and one draw needn't show every extreme that they name: `query_counts`: per-cell query counts.
All inputs are finite; a program needn't handle non-finite values.
Results may differ from a plain program's by a relative error of at most 0.014.
Values may be sent and summed in bfloat16 or wider, within the bound.
A program may use at most 320 MiB of HBM per device.

v0:
```python
import math

import jax
import jax.numpy as jnp
from jax import lax
from jax.sharding import PartitionSpec as P

HEAD_DIM = 64


def passed_along(value, axis, steps):
    count = lax.axis_size(axis)
    leading, last = (max(0, -steps), min(count, count - steps))
    return lax.ppermute(value, axis, [(source, source + steps) for source in range(leading, last)])


def layer_norm(rows_in):
    center = rows_in - jnp.mean(rows_in, axis=-1, keepdims=True)
    inverse = lax.rsqrt(jnp.mean(center * center, axis=-1, keepdims=True) + 1e-05)
    return (center * inverse, inverse)


def norm_back(grad_rows, normed, inverse):
    return inverse * (
        grad_rows
        - jnp.mean(grad_rows, axis=-1, keepdims=True)
        - normed * jnp.mean(grad_rows * normed, axis=-1, keepdims=True)
    )


def gelu_parts(hidden_pre):
    cumulative = 0.5 * (1.0 + lax.erf(hidden_pre * (1.0 / math.sqrt(2.0))))
    slope = cumulative + hidden_pre * jnp.exp(-0.5 * hidden_pre * hidden_pre) * (
        1.0 / math.sqrt(2.0 * math.pi)
    )
    return (hidden_pre * cumulative, slope)


def split_heads(packed, model_width):
    length = packed.shape[0]
    head_count = model_width // HEAD_DIM
    queries = packed[:, :model_width].reshape(length, head_count, HEAD_DIM)
    key_rows = packed[:, model_width : 2 * model_width].reshape(length, head_count, HEAD_DIM)
    values = packed[:, 2 * model_width :].reshape(length, head_count, HEAD_DIM)
    return (queries, key_rows, values)


def attend(packed, model_width):
    queries, key_rows, values = split_heads(packed, model_width)
    scores = jnp.einsum("qhd,khd->hqk", queries, key_rows, preferred_element_type=jnp.float32) * (
        1.0 / math.sqrt(HEAD_DIM)
    )
    row_max = jnp.max(scores, axis=-1, keepdims=True)
    shifted = jnp.exp(scores - row_max)
    row_total = jnp.sum(shifted, axis=-1, keepdims=True)
    attn_probs = (shifted / row_total).astype(jnp.bfloat16)
    mixed_out = jnp.einsum("hqk,khd->qhd", attn_probs, values, preferred_element_type=jnp.float32)
    log_total = (row_max + jnp.log(row_total))[:, :, 0]
    return (mixed_out.reshape(packed.shape[0], model_width).astype(jnp.bfloat16), log_total)


def attend_back(packed, log_total, grad_mixed, model_width):
    queries, key_rows, values = split_heads(packed, model_width)
    length = packed.shape[0]
    score_scale = 1.0 / math.sqrt(HEAD_DIM)
    scores = (
        jnp.einsum("qhd,khd->hqk", queries, key_rows, preferred_element_type=jnp.float32)
        * score_scale
    )
    attn_probs = jnp.exp(scores - log_total[:, :, None])
    grad_heads = grad_mixed.reshape(length, -1, HEAD_DIM)
    grad_probs = jnp.einsum("qhd,khd->hqk", grad_heads, values, preferred_element_type=jnp.float32)
    weighted = jnp.sum(grad_probs * attn_probs, axis=-1, keepdims=True)
    grad_scores = (attn_probs * (grad_probs - weighted)).astype(jnp.bfloat16)
    grad_query = (
        jnp.einsum("hqk,khd->qhd", grad_scores, key_rows, preferred_element_type=jnp.float32)
        * score_scale
    )
    grad_key = (
        jnp.einsum("hqk,qhd->khd", grad_scores, queries, preferred_element_type=jnp.float32)
        * score_scale
    )
    grad_value = jnp.einsum(
        "hqk,qhd->khd",
        attn_probs.astype(jnp.bfloat16),
        grad_heads,
        preferred_element_type=jnp.float32,
    )
    joined = jnp.concatenate(
        [
            grad_query.reshape(length, model_width),
            grad_key.reshape(length, model_width),
            grad_value.reshape(length, model_width),
        ],
        axis=1,
    )
    return joined.astype(jnp.bfloat16)


def forward_layer(entry_rows, params):
    gain_rows, shift_rows, w_qkv, w_out, w_up, b_up, w_down = params
    model_width = entry_rows.shape[-1]
    gain_values = gain_rows.astype(jnp.float32)
    shift_values = shift_rows.astype(jnp.float32)
    rows_in = entry_rows.astype(jnp.float32)
    normed, inverse = layer_norm(rows_in)
    lowered = (normed * gain_values[0] + shift_values[0]).astype(jnp.bfloat16)
    projected = jnp.dot(lowered, w_qkv, preferred_element_type=jnp.float32)
    extra = jnp.concatenate([shift_values[1], jnp.zeros_like(shift_values[1]), shift_values[2]])
    packed = (projected + extra).astype(jnp.bfloat16)
    mixed_out, log_total = attend(packed, model_width)
    middle = (
        rows_in + jnp.dot(mixed_out, w_out, preferred_element_type=jnp.float32) + shift_values[3]
    )
    normed_two, inverse_two = layer_norm(middle)
    second = (normed_two * gain_values[1] + shift_values[4]).astype(jnp.bfloat16)
    hidden_pre = jnp.dot(second, w_up, preferred_element_type=jnp.float32) + b_up.astype(
        jnp.float32
    )
    activated, slope = gelu_parts(hidden_pre)
    output = middle + (
        jnp.dot(activated.astype(jnp.bfloat16), w_down, preferred_element_type=jnp.float32)
        + shift_values[5]
    )
    return (output, (entry_rows, packed, log_total, mixed_out, middle, hidden_pre))


def backward_layer(saved_items, grad_out, params):
    entry_rows, packed, log_total, mixed_out, middle, hidden_pre = saved_items
    gain_rows, shift_rows, w_qkv, w_out, w_up, b_up, w_down = params
    model_width = entry_rows.shape[-1]
    gain_values = gain_rows.astype(jnp.float32)
    shift_values = shift_rows.astype(jnp.float32)
    normed, inverse = layer_norm(entry_rows.astype(jnp.float32))
    lowered = (normed * gain_values[0] + shift_values[0]).astype(jnp.bfloat16)
    normed_two, inverse_two = layer_norm(middle)
    second = (normed_two * gain_values[1] + shift_values[4]).astype(jnp.bfloat16)
    activated, slope = gelu_parts(hidden_pre)
    activated = activated.astype(jnp.bfloat16)
    grad_ff = grad_out.astype(jnp.bfloat16)
    grad_act = jnp.dot(grad_ff, w_down.T, preferred_element_type=jnp.float32)
    grad_inner = (grad_act * slope).astype(jnp.bfloat16)
    grad_second = jnp.dot(grad_inner, w_up.T, preferred_element_type=jnp.float32)
    grad_middle = grad_out + norm_back(grad_second * gain_values[1], normed_two, inverse_two)
    grad_branch = grad_middle.astype(jnp.bfloat16)
    grad_mixed = jnp.dot(grad_branch, w_out.T, preferred_element_type=jnp.float32).astype(
        jnp.bfloat16
    )
    grad_packed = attend_back(packed, log_total, grad_mixed, model_width)
    grad_lowered = jnp.dot(grad_packed, w_qkv.T, preferred_element_type=jnp.float32)
    grad_rows = grad_middle + norm_back(grad_lowered * gain_values[0], normed, inverse)
    packed_sums = jnp.sum(grad_packed, axis=0, dtype=jnp.float32)
    grad_gains = jnp.stack(
        [jnp.sum(grad_lowered * normed, axis=0), jnp.sum(grad_second * normed_two, axis=0)]
    )
    grad_shifts = jnp.stack(
        [
            jnp.sum(grad_lowered, axis=0),
            packed_sums[:model_width],
            packed_sums[2 * model_width :],
            jnp.sum(grad_branch, axis=0, dtype=jnp.float32),
            jnp.sum(grad_second, axis=0),
            jnp.sum(grad_ff, axis=0, dtype=jnp.float32),
        ]
    )
    grad_bias = jnp.sum(grad_inner, axis=0, dtype=jnp.float32)
    product_pairs = (
        lowered,
        grad_packed,
        mixed_out,
        grad_branch,
        second,
        grad_inner,
        activated,
        grad_ff,
    )
    return (grad_rows, (grad_gains, grad_shifts, grad_bias), product_pairs)


def outer_sum(left_rows, right_rows):
    return lax.dot_general(
        left_rows, right_rows, (((0,), (0,)), ((), ())), preferred_element_type=jnp.float32
    )


def attention_products(product_pairs):
    return (
        outer_sum(product_pairs[0], product_pairs[1]),
        outer_sum(product_pairs[2], product_pairs[3]),
    )


def ffn_products(product_pairs):
    return (
        outer_sum(product_pairs[4], product_pairs[5]),
        outer_sum(product_pairs[6], product_pairs[7]),
    )


def on_device(inputs, out_grad, query_counts, gains, shifts, w_qkv, w_out, w_up, b_up, w_down):
    section_index = lax.axis_index("pipe")
    sections = lax.axis_size("pipe")
    cell_count, length, model_width = inputs.shape
    params = (
        lax.all_gather(gains[0], "dp", axis=1, tiled=True),
        lax.all_gather(shifts[0], "dp", axis=1, tiled=True),
        lax.all_gather(w_qkv[0], "dp", axis=0, tiled=True),
        lax.all_gather(w_out[0], "dp", axis=0, tiled=True),
        lax.all_gather(w_up[0], "dp", axis=0, tiled=True),
        lax.all_gather(b_up[0], "dp", axis=0, tiled=True),
        lax.all_gather(w_down[0], "dp", axis=0, tiled=True),
    )
    ff_width = params[4].shape[1]
    head_count = model_width // HEAD_DIM
    tick_count = cell_count + sections - 1
    low_type = jnp.bfloat16
    scales = jnp.sqrt(query_counts.astype(jnp.float32) / 500.0)
    kept_init = (
        jnp.zeros((cell_count, length, model_width), low_type),
        jnp.zeros((cell_count, length, 3 * model_width), low_type),
        jnp.zeros((cell_count, head_count, length), jnp.float32),
        jnp.zeros((cell_count, length, model_width), low_type),
        jnp.zeros((cell_count, length, model_width), jnp.float32),
        jnp.zeros((cell_count, length, ff_width), jnp.float32),
    )
    section_init = jnp.zeros((cell_count, length, model_width), low_type)
    empty_rows = jnp.zeros((length, model_width), low_type)

    def forward_tick(step_index, carried):
        kept_buffers, section_out, arrived = carried
        position = step_index - section_index
        slot_index = jnp.clip(position, 0, cell_count - 1)
        own_rows = lax.dynamic_index_in_dim(inputs, slot_index, 0, keepdims=False)
        entry_rows = jnp.where(section_index == 0, own_rows, arrived)

        def forward_run(operand):
            buffers, outputs = operand
            output, saved_items = forward_layer(entry_rows, params)
            sent_rows = output.astype(low_type)
            buffers = tuple(
                (
                    lax.dynamic_update_index_in_dim(buffer, element, slot_index, 0)
                    for buffer, element in zip(buffers, saved_items)
                )
            )
            outputs = lax.dynamic_update_index_in_dim(outputs, sent_rows, slot_index, 0)
            return (buffers, outputs, sent_rows)

        def forward_skip(operand):
            buffers, outputs = operand
            return (buffers, outputs, jnp.zeros_like(entry_rows))

        valid = (position >= 0) & (position < cell_count)
        kept_buffers, section_out, sent_rows = lax.cond(
            valid, forward_run, forward_skip, (kept_buffers, section_out)
        )
        arrived = passed_along(sent_rows, "pipe", 1)
        return (kept_buffers, section_out, arrived)

    kept_buffers, section_out, unused_rows = lax.fori_loop(
        0, tick_count, forward_tick, (kept_init, section_init, empty_rows)
    )
    small_init = (
        jnp.zeros((2, model_width), jnp.float32),
        jnp.zeros((6, model_width), jnp.float32),
        jnp.zeros((ff_width,), jnp.float32),
    )
    stored_init = (
        jnp.zeros((model_width, 3 * model_width), jnp.float32),
        jnp.zeros((model_width, model_width), jnp.float32),
        jnp.zeros((model_width, ff_width), jnp.float32),
        jnp.zeros((ff_width, model_width), jnp.float32),
    )
    grads_init = jnp.zeros((cell_count, length, model_width), low_type)

    def backward_tick(step_index, carried):
        small_sums, stored, grads_rows, arrived = carried
        position = step_index - (sections - 1 - section_index)
        slot_index = jnp.clip(position, 0, cell_count - 1)
        own_grad = lax.dynamic_index_in_dim(out_grad, slot_index, 0, keepdims=False).astype(
            jnp.float32
        ) * lax.dynamic_index_in_dim(scales, slot_index, 0, keepdims=False)
        incoming = jnp.where(section_index == sections - 1, own_grad, arrived.astype(jnp.float32))

        def backward_run(operand):
            sums_now, stored_now, grads_now = operand
            saved_items = tuple(
                (
                    lax.dynamic_index_in_dim(buffer, slot_index, 0, keepdims=False)
                    for buffer in kept_buffers
                )
            )
            grad_rows, small_terms, product_pairs = backward_layer(saved_items, incoming, params)
            sent_rows = grad_rows.astype(low_type)
            sums_now = tuple((left + right for left, right in zip(sums_now, small_terms)))
            stored_now = tuple(
                (
                    left + right
                    for left, right in zip(
                        stored_now, attention_products(product_pairs) + ffn_products(product_pairs)
                    )
                )
            )
            grads_now = lax.dynamic_update_index_in_dim(grads_now, sent_rows, slot_index, 0)
            return (sums_now, stored_now, grads_now, sent_rows)

        def backward_skip(operand):
            sums_now, stored_now, grads_now = operand
            return (sums_now, stored_now, grads_now, jnp.zeros_like(arrived))

        valid = (position >= 0) & (position < cell_count)
        small_sums, stored, grads_rows, sent_rows = lax.cond(
            valid, backward_run, backward_skip, (small_sums, stored, grads_rows)
        )
        arrived = passed_along(sent_rows, "pipe", -1)
        return (small_sums, stored, grads_rows, arrived)

    small_sums, stored, grads_rows, unused_back = lax.fori_loop(
        0, tick_count, backward_tick, (small_init, stored_init, grads_init, empty_rows)
    )
    grad_gains, grad_shifts, grad_bias = small_sums
    ffn_grads = (stored[2], stored[3])
    attn_grads = (stored[0], stored[1])
    shares = (
        lax.psum_scatter(grad_gains, "dp", scatter_dimension=1, tiled=True),
        lax.psum_scatter(grad_shifts, "dp", scatter_dimension=1, tiled=True),
        lax.psum_scatter(attn_grads[0], "dp", scatter_dimension=0, tiled=True),
        lax.psum_scatter(attn_grads[1], "dp", scatter_dimension=0, tiled=True),
        lax.psum_scatter(ffn_grads[0], "dp", scatter_dimension=0, tiled=True),
        lax.psum_scatter(grad_bias, "dp", scatter_dimension=0, tiled=True),
        lax.psum_scatter(ffn_grads[1], "dp", scatter_dimension=0, tiled=True),
    )
    return (section_out[None], grads_rows[None]) + tuple((share[None] for share in shares))


def solution(mesh):
    in_specs = (
        P("dp", None, None),
        P("dp", None, None),
        P("dp"),
        P("pipe", None, "dp"),
        P("pipe", None, "dp"),
        P("pipe", "dp", None),
        P("pipe", "dp", None),
        P("pipe", "dp", None),
        P("pipe", "dp"),
        P("pipe", "dp", None),
    )
    out_specs = (
        P("pipe", "dp", None, None),
        P("pipe", "dp", None, None),
        P("pipe", None, "dp"),
        P("pipe", None, "dp"),
        P("pipe", "dp", None),
        P("pipe", "dp", None),
        P("pipe", "dp", None),
        P("pipe", "dp"),
        P("pipe", "dp", None),
    )
    return jax.shard_map(
        on_device, mesh=mesh, in_specs=in_specs, out_specs=out_specs, check_vma=False
    )
```

profile of v0, /device:TPU:0, one launch (start us, length us, event | category | flops | bytes accessed | tf_op | source)
XLA Modules:
  0.0 2118.5 jit_solution(9546580191460273901)
XLA Ops:
  11.6 26.5 %all-gather.1 = bf16[1,6,1280]{1,0,2:T(2,128)(2,1)S(1)} all-gather(bf16[1,6,80]{1,0,2:T(2,128)(2,1)S(1)} %copy.70), channel_id=3, replica_groups=mesh['pipe'=2,'dp'=16] {'dp'}, dimensions={2}, use_global_device_ids=true | all-gather | bytes 16320 | tf_op jit(solution)/shard_map/all_gather | solution.py:206
  38.5 21.8 %all-gather = bf16[1,2,1280]{1,0,2:T(2,128)(2,1)S(1)} all-gather(bf16[1,2,80]{1,0,2:T(2,128)(2,1)S(1)} %copy.68), channel_id=2, replica_groups=mesh['pipe'=2,'dp'=16] {'dp'}, dimensions={2}, use_global_device_ids=true | all-gather | bytes 5440 | tf_op jit(solution)/shard_map/all_gather | solution.py:205
  62.3 61.0 %all-reduce = bf16[5120]{0:T(1024)(128)(2,1)S(1)} all-reduce(bf16[5120]{0:T(1024)(128)(2,1)S(1)} %dynamic-update-slice), channel_id=7, replica_groups=mesh['pipe'=2,'dp'=16] {'dp'}, use_global_device_ids=true, to_apply=%add | all-reduce | flops 5120 | bytes 20480 | tf_op jit(solution)/shard_map/all_gather | solution.py:210
  123.9 26.1 %all-gather.12.cloned.1.call-done = bf16[1,1280,3840]{2,1,0:T(8,128)(2,1)} async-done(((bf16[1,80,3840]{2,1,0:T(8,128)(2,1)}), bf16[1,1280,3840]{2,1,0:T(8,128)(2,1)}) %all-gather.12.cloned.1.call-update) | async-done | bytes 9830416 | tf_op jit(solution)/shard_map/all_gather | solution.py:207
  150.0 104.7 %all-gather.16.cloned.1.call-done = bf16[1,1280,5120]{2,1,0:T(8,128)(2,1)} async-done(((bf16[1,80,5120]{2,1,0:T(8,128)(2,1)}), bf16[1,1280,5120]{2,1,0:T(8,128)(2,1)}) %all-gather.16.cloned.1.call-update) | async-done | bytes 13107216 | tf_op jit(solution)/shard_map/all_gather | solution.py:209
  254.8 104.3 %all-gather.18.cloned.1.call-done = bf16[1,5120,1280]{2,1,0:T(8,128)(2,1)} async-done(((bf16[1,320,1280]{2,1,0:T(8,128)(2,1)}), bf16[1,5120,1280]{2,1,0:T(8,128)(2,1)}) %all-gather.18.cloned.1.call-update) | async-done | bytes 13107216 | tf_op jit(solution)/shard_map/all_gather | solution.py:211
  376.6 242.2 %while.59 = (s32[]{:T(128)}, bf16[2,384,1280]{2,1,0:T(8,128)(2,1)}, bf16[2,384,3840]{2,1,0:T(8,128)(2,1)}, f32[2,20,384]{2,1,0:T(8,128)}, bf16[2,384,1280]{1,2,0...) while((s32[]{:T(128)}, bf16[2,384,1280]{2,1,0:T(8,128)(2,1)}, ...), condition=%wide.region_9.10_spmd, body=%wide.region_0.9_spmd.sunk | while | flops 15911993344 | bytes 228973440 | solution.py:260
  377.1 56.1 %conditional.4 = (bf16[2,384,1280]{2,1,0:T(8,128)(2,1)}, bf16[2,384,3840]{2,1,0:T(8,128)(2,1)}, f32[2,20,384]{2,1,0:T(8,128)}, bf16[2,384,1280]{1,2,0:T(8,128)(2...) conditional(s32[]{:T(128)} %convert_element_type.331, ...), branch_computations={%region_1.1_spmd, %region_2.8_spmd} | conditional | flops 15911993344 | bytes 225040800 | solution.py:254
  408.7 13.7 bitcast_dynamic-update-slice_fusion
  434.5 21.9 %collective-permute-done = bf16[384,1280]{1,0:T(8,128)(2,1)S(1)} collective-permute-done((bf16[384,1280]{1,0:T(8,128)(2,1)}, bf16[384,1280]{1,0:T(8,128)(2,1)S(1)}, u32[]{:S(2)}, u32[]{:S(2)}) %collective-permute-start) | collective-permute-done | bytes 983072 | tf_op jit(solution)/shard_map/while/body/eval_jaxpr/ppermute | solution.py:14
  456.5 56.0 %conditional.4 = (bf16[2,384,1280]{2,1,0:T(8,128)(2,1)}, bf16[2,384,3840]{2,1,0:T(8,128)(2,1)}, f32[2,20,384]{2,1,0:T(8,128)}, bf16[2,384,1280]{1,2,0:T(8,128)(2...) conditional(s32[]{:T(128)} %convert_element_type.331, ...), branch_computations={%region_1.1_spmd, %region_2.8_spmd} | conditional | flops 15911993344 | bytes 225040800 | solution.py:254
  516.8 21.2 collective-permute-done
  539.0 59.4 %collective-permute-start = (bf16[384,1280]{1,0:T(8,128)(2,1)}, bf16[384,1280]{1,0:T(8,128)(2,1)S(1)}, u32[]{:S(2)}, u32[]{:S(2)}) collective-permute-start(bf16[384,1280]{1,0:T(8,128)(2,1)} %get-tuple-element.2024), channel_id=1, source_target_pairs={{0,16},{1,17},{2,18},{3,19},{4,20},{5,21},{6,22},{7,23},{8,24},{9,... | collective-permute-start | bytes 2949128 | tf_op jit(solution)/shard_map/while/body/eval_jaxpr/ppermute | solution.py:14
  598.4 20.3 collective-permute-done
  666.6 521.3 %while.60 = (s32[]{:T(128)}, f32[2,1280]{1,0:T(2,128)}, f32[6,1280]{1,0:T(8,128)S(1)}, f32[5120]{0:T(1024)S(1)}, f32[1280,3840]{1,0:T(8,128)}, /*index=5*/f32[12...) while((s32[]{:T(128)}, f32[2,1280]{1,0:T(2,128)}, ...), condition=%wide.region_30.31_spmd, body=%wide.region_10.30_spmd.sunk | while | flops 32242241536 | bytes 490807584 | solution.py:318
  677.5 163.0 %collective-permute-done.1 = bf16[384,1280]{1,0:T(8,128)(2,1)S(1)} collective-permute-done((bf16[384,1280]{1,0:T(8,128)(2,1)}, bf16[384,1280]{1,0:T(8,128)(2,1)S(1)}, u32[]{:S(2)}, u32[]{:S(2)}) %collective-permute-start.1) | collective-permute-done | bytes 983072 | tf_op jit(solution)/shard_map/while/body/eval_jaxpr/ppermute | solution.py:14
  840.4 149.9 %conditional.5 = (f32[2,1280]{1,0:T(2,128)}, f32[6,1280]{1,0:T(8,128)S(1)}, f32[5120]{0:T(1024)S(1)}, f32[1280,3840]{1,0:T(8,128)}, f32[1280,1280]{1,0:T(8,128)}...) conditional(s32[]{:T(128)} %convert_element_type.332, ...), branch_computations={%region_11.11_spmd, %region_12.29_spmd} | conditional | flops 32242241536 | bytes 486874848 | solution.py:312
  898.0 23.7 %convolution_add_fusion.1 = f32[5120,1280]{1,0:T(8,128)} fusion(f32[5120,1280]{1,0:T(8,128)} %get-tuple-element.1329, bf16[384,1280]{1,0:T(8,128)(2,1)S(1)} %copy-done.9, f32[2,384,5120]{2,1,0:T(8,128)} %get-tuple-element.1316, s32[]{:T(128)S(6)} %min.19), kind=kOutput, calls=%fused_computation.58 | convolution fusion | flops 5049548800 | bytes 61276164 | tf_op jit(solution)/shard_map/while/body/eval_jaxpr/cond/branch_1_fun/dot_general | solution.py:181
  951.5 19.9 convolution_add_fusion.3
  971.4 18.7 convolution_add_fusion.2
  991.7 21.7 %collective-permute-done.1 = bf16[384,1280]{1,0:T(8,128)(2,1)S(1)} collective-permute-done((bf16[384,1280]{1,0:T(8,128)(2,1)}, bf16[384,1280]{1,0:T(8,128)(2,1)S(1)}, u32[]{:S(2)}, u32[]{:S(2)}) %collective-permute-start.1) | collective-permute-done | bytes 983072 | tf_op jit(solution)/shard_map/while/body/eval_jaxpr/ppermute | solution.py:14
  1013.9 150.2 %conditional.5 = (f32[2,1280]{1,0:T(2,128)}, f32[6,1280]{1,0:T(8,128)S(1)}, f32[5120]{0:T(1024)S(1)}, f32[1280,3840]{1,0:T(8,128)}, f32[1280,1280]{1,0:T(8,128)}...) conditional(s32[]{:T(128)} %convert_element_type.332, ...), branch_computations={%region_11.11_spmd, %region_12.29_spmd} | conditional | flops 32242241536 | bytes 486874848 | solution.py:312
  1071.1 23.7 %convolution_add_fusion.1 = f32[5120,1280]{1,0:T(8,128)} fusion(f32[5120,1280]{1,0:T(8,128)} %get-tuple-element.1329, bf16[384,1280]{1,0:T(8,128)(2,1)S(1)} %copy-done.9, f32[2,384,5120]{2,1,0:T(8,128)} %get-tuple-element.1316, s32[]{:T(128)S(6)} %min.19), kind=kOutput, calls=%fused_computation.58 | convolution fusion | flops 5049548800 | bytes 61276164 | tf_op jit(solution)/shard_map/while/body/eval_jaxpr/cond/branch_1_fun/dot_general | solution.py:181
  1124.7 20.0 convolution_add_fusion.3
  1144.7 18.9 convolution_add_fusion.2
  1165.4 20.8 collective-permute-done.1
  1194.4 57.7 %all-reduce.1 = f32[5120]{0:T(1024)S(1)} all-reduce(f32[5120]{0:T(1024)S(1)} %get-tuple-element.1404), channel_id=14, replica_groups=mesh['pipe'=2,'dp'=16] {'dp'}, use_global_device_ids=true, to_apply=%region_36.37.clone | all-reduce | flops 5120 | bytes 40960
  1254.2 48.4 %reduce-scatter.21.cloned.1.call-done = f32[80,6]{1,0:T(8,128)} async-done(((f32[1280,6]{1,0:T(8,128)}), f32[80,6]{1,0:T(8,128)}) %reduce-scatter.21.cloned.1.call-update) | async-done | bytes 1936
  1304.0 89.1 %reduce-scatter.13.cloned.1.call-done = f32[80,1280]{1,0:T(8,128)} async-done(((f32[1280,1280]{1,0:T(8,128)}), f32[80,1280]{1,0:T(8,128)}) %reduce-scatter.13.cloned.1.call-update) | async-done | bytes 409616 | tf_op jit(solution)/shard_map/reduce_scatter | solution.py:328
  1393.2 204.9 %reduce-scatter.11.cloned.1.call-done = f32[80,3840]{1,0:T(8,128)} async-done(((f32[1280,3840]{1,0:T(8,128)}), f32[80,3840]{1,0:T(8,128)}) %reduce-scatter.11.cloned.1.call-update) | async-done | bytes 1228816 | tf_op jit(solution)/shard_map/reduce_scatter | solution.py:327
  1598.1 256.8 %reduce-scatter.15.cloned.1.call-done = f32[80,5120]{1,0:T(8,128)} async-done(((f32[1280,5120]{1,0:T(8,128)}), f32[80,5120]{1,0:T(8,128)}) %reduce-scatter.15.cloned.1.call-update) | async-done | bytes 1638416 | tf_op jit(solution)/shard_map/reduce_scatter | solution.py:329
  1854.9 256.6 %reduce-scatter.17.cloned.1.call-done = f32[320,1280]{1,0:T(8,128)} async-done(((f32[5120,1280]{1,0:T(8,128)}), f32[320,1280]{1,0:T(8,128)}) %reduce-scatter.17.cloned.1.call-update) | async-done | bytes 1638416 | tf_op jit(solution)/shard_map/reduce_scatter | solution.py:331
  (339 shorter events, 374.9 us)
Async XLA Ops:
  7.2 53.5 %copy-start.23 = (u32[32]{0:T(128)S(1)}, u32[32]{0:T(128)}, u32[]{:S(2)}) copy-start(u32[32]{0:T(128)} %constant.266) | copy-start | bytes 388
  7.2 54.8 %copy-start.24 = (bf16[1,320]{1,0:T(2,128)(2,1)S(1)}, bf16[1,320]{1,0:T(2,128)(2,1)}, u32[]{:S(2)}) copy-start(bf16[1,320]{1,0:T(2,128)(2,1)} %param.26) | copy-start | bytes 1924
  7.2 116.2 %copy-start.27 = (s32[2]{0:T(128)S(1)}, s32[2]{0:T(128)}, u32[]{:S(2)}) copy-start(s32[2]{0:T(128)} %param.20) | copy-start | bytes 28
  7.2 116.7 %all-gather.14.cloned.1.call-start = ((), (), s32[]{:S(2)}) async-start(), calls=%async_computation.11 | async-start | bytes 3481600 | tf_op jit(solution)/shard_map/all_gather | solution.py:208
  7.9 142.1 %all-gather.12.cloned.1.call-start = ((), (), s32[]{:S(2)}) async-start(), calls=%async_computation.10 | async-start | bytes 10444800 | tf_op jit(solution)/shard_map/all_gather | solution.py:207
  8.7 246.1 %all-gather.16.cloned.1.call-start = ((), (), s32[]{:S(2)}) async-start(), calls=%async_computation.12 | async-start | bytes 13926400 | tf_op jit(solution)/shard_map/all_gather | solution.py:209
  9.4 349.7 %all-gather.18.cloned.1.call-start = ((), (), s32[]{:S(2)}) async-start(), calls=%async_computation.13 | async-start | bytes 13926400 | tf_op jit(solution)/shard_map/all_gather | solution.py:211
  10.0 1242.8 %reduce-scatter.19.cloned.1.call-start = ((), (), s32[]{:S(2)}) async-start(), calls=%async_computation.14 | async-start | bytes 696320
  406.6 15.8 slice-start
  408.7 13.7 slice-start.1
  408.7 13.8 slice-start.2
  408.7 13.8 slice-start.3
  433.2 23.3 %collective-permute-start = (bf16[384,1280]{1,0:T(8,128)(2,1)}, bf16[384,1280]{1,0:T(8,128)(2,1)S(1)}, u32[]{:S(2)}, u32[]{:S(2)}) collective-permute-start(bf16[384,1280]{1,0:T(8,128)(2,1)} %get-tuple-element.2024), channel_id=1, source_target_pairs={{0,16},{1,17},{2,18},{3,19},{4,20},{5,21},{6,22},{7,23},{8,24},{9,... | collective-permute-start | bytes 2949128 | tf_op jit(solution)/shard_map/while/body/eval_jaxpr/ppermute | solution.py:14
  486.0 15.8 slice-start
  512.5 25.5 %collective-permute-start = (bf16[384,1280]{1,0:T(8,128)(2,1)}, bf16[384,1280]{1,0:T(8,128)(2,1)S(1)}, u32[]{:S(2)}, u32[]{:S(2)}) collective-permute-start(bf16[384,1280]{1,0:T(8,128)(2,1)} %get-tuple-element.2024), channel_id=1, source_target_pairs={{0,16},{1,17},{2,18},{3,19},{4,20},{5,21},{6,22},{7,23},{8,24},{9,... | collective-permute-start | bytes 2949128 | tf_op jit(solution)/shard_map/while/body/eval_jaxpr/ppermute | solution.py:14
  539.0 79.6 %collective-permute-start = (bf16[384,1280]{1,0:T(8,128)(2,1)}, bf16[384,1280]{1,0:T(8,128)(2,1)S(1)}, u32[]{:S(2)}, u32[]{:S(2)}) collective-permute-start(bf16[384,1280]{1,0:T(8,128)(2,1)} %get-tuple-element.2024), channel_id=1, source_target_pairs={{0,16},{1,17},{2,18},{3,19},{4,20},{5,21},{6,22},{7,23},{8,24},{9,... | collective-permute-start | bytes 2949128 | tf_op jit(solution)/shard_map/while/body/eval_jaxpr/ppermute | solution.py:14
  676.2 164.3 %collective-permute-start.1 = (bf16[384,1280]{1,0:T(8,128)(2,1)}, bf16[384,1280]{1,0:T(8,128)(2,1)S(1)}, u32[]{:S(2)}, u32[]{:S(2)}) collective-permute-start(bf16[384,1280]{1,0:T(8,128)(2,1)} %get-tuple-element.2059), channel_id=1, source_target_pairs={{16,0},{17,1},{18,2},{19,3},{20,4},{21,5},{22,6},{23,7},{24,8},{25... | collective-permute-start | bytes 2949128 | tf_op jit(solution)/shard_map/while/body/eval_jaxpr/ppermute | solution.py:14
  888.9 34.4 %copy-start.3 = (bf16[384,1280]{0,1:T(8,128)(2,1)}, bf16[384,1280]{0,1:T(8,128)(2,1)S(1)}, u32[]{:S(2)}) copy-start(bf16[384,1280]{0,1:T(8,128)(2,1)S(1)} %copy.64) | copy-start | bytes 2949124 | tf_op jit(solution)/shard_map/while/body/eval_jaxpr/cond
  898.0 23.7 %copy-start.4 = (bf16[384,1280]{0,1:T(8,128)(2,1)S(1)}, bf16[384,1280]{0,1:T(8,128)(2,1)}, u32[]{:S(2)}) copy-start(bf16[384,1280]{0,1:T(8,128)(2,1)} %get-tuple-element.1739) | copy-start | bytes 2949124 | tf_op jit(solution)/shard_map/while/body/eval_jaxpr/cond
  898.0 23.7 %copy-start.6 = (bf16[384,1280]{0,1:T(8,128)(2,1)S(1)}, bf16[384,1280]{0,1:T(8,128)(2,1)}, u32[]{:S(2)}) copy-start(bf16[384,1280]{0,1:T(8,128)(2,1)} %get-tuple-element.1738) | copy-start | bytes 2949124 | tf_op jit(solution)/shard_map/while/body/eval_jaxpr/cond
  936.1 14.6 copy-start.1
  990.4 23.0 %collective-permute-start.1 = (bf16[384,1280]{1,0:T(8,128)(2,1)}, bf16[384,1280]{1,0:T(8,128)(2,1)S(1)}, u32[]{:S(2)}, u32[]{:S(2)}) collective-permute-start(bf16[384,1280]{1,0:T(8,128)(2,1)} %get-tuple-element.2059), channel_id=1, source_target_pairs={{16,0},{17,1},{18,2},{19,3},{20,4},{21,5},{22,6},{23,7},{24,8},{25... | collective-permute-start | bytes 2949128 | tf_op jit(solution)/shard_map/while/body/eval_jaxpr/ppermute | solution.py:14
  1062.1 34.4 %copy-start.3 = (bf16[384,1280]{0,1:T(8,128)(2,1)}, bf16[384,1280]{0,1:T(8,128)(2,1)S(1)}, u32[]{:S(2)}) copy-start(bf16[384,1280]{0,1:T(8,128)(2,1)S(1)} %copy.64) | copy-start | bytes 2949124 | tf_op jit(solution)/shard_map/while/body/eval_jaxpr/cond
  1071.1 23.7 %copy-start.4 = (bf16[384,1280]{0,1:T(8,128)(2,1)S(1)}, bf16[384,1280]{0,1:T(8,128)(2,1)}, u32[]{:S(2)}) copy-start(bf16[384,1280]{0,1:T(8,128)(2,1)} %get-tuple-element.1739) | copy-start | bytes 2949124 | tf_op jit(solution)/shard_map/while/body/eval_jaxpr/cond
  1071.1 23.7 %copy-start.6 = (bf16[384,1280]{0,1:T(8,128)(2,1)S(1)}, bf16[384,1280]{0,1:T(8,128)(2,1)}, u32[]{:S(2)}) copy-start(bf16[384,1280]{0,1:T(8,128)(2,1)} %get-tuple-element.1738) | copy-start | bytes 2949124 | tf_op jit(solution)/shard_map/while/body/eval_jaxpr/cond
  1109.4 14.6 copy-start.1
  1164.1 22.1 %collective-permute-start.1 = (bf16[384,1280]{1,0:T(8,128)(2,1)}, bf16[384,1280]{1,0:T(8,128)(2,1)S(1)}, u32[]{:S(2)}, u32[]{:S(2)}) collective-permute-start(bf16[384,1280]{1,0:T(8,128)(2,1)} %get-tuple-element.2059), channel_id=1, source_target_pairs={{16,0},{17,1},{18,2},{19,3},{20,4},{21,5},{22,6},{23,7},{24,8},{25... | collective-permute-start | bytes 2949128 | tf_op jit(solution)/shard_map/while/body/eval_jaxpr/ppermute | solution.py:14
  1189.7 112.9 %reduce-scatter.21.cloned.1.call-start = ((), (), s32[]{:S(2)}) async-start(), calls=%async_computation.15 | async-start | bytes 696320
  1190.9 202.2 %reduce-scatter.13.cloned.1.call-start = ((), (), s32[]{:S(2)}) async-start(), calls=%async_computation.7 | async-start | bytes 6963200 | tf_op jit(solution)/shard_map/reduce_scatter | solution.py:328
  1191.7 406.4 %reduce-scatter.11.cloned.1.call-start = ((), (), s32[]{:S(2)}) async-start(), calls=%async_computation.6 | async-start | bytes 20889600 | tf_op jit(solution)/shard_map/reduce_scatter | solution.py:327
  1192.4 662.4 %reduce-scatter.15.cloned.1.call-start = ((), (), s32[]{:S(2)}) async-start(), calls=%async_computation.8 | async-start | bytes 27852800 | tf_op jit(solution)/shard_map/reduce_scatter | solution.py:329
  1193.2 918.3 %reduce-scatter.17.cloned.1.call-start = ((), (), s32[]{:S(2)}) async-start(), calls=%async_computation.9 | async-start | bytes 27852800 | tf_op jit(solution)/shard_map/reduce_scatter | solution.py:331
  (45 other events, 261.9 us)
Sparse Core Ops, SparseCore 0:
  10.3 53.3 all-gather.13
  66.0 83.9 all-gather.11
  152.3 102.4 all-gather.15
  256.9 102.1 all-gather.17
  1189.8 53.5 reduce-scatter.18
  1247.3 55.2 reduce-scatter.20
  1307.1 85.9 reduce-scatter.12
  1398.5 199.5 reduce-scatter.10
  1603.4 251.4 reduce-scatter.14
  1860.1 251.3 reduce-scatter.16
where the time goes:
time: 2120 us
  waiting for transfers between devices  1370 us (65%)
  matrix products  322 us (15%)
  blocking collectives  167 us (8%)
  local copies, waits for them, and re-layouts  115 us (5%)
  starting transfers between devices  69.3 us (3%)
  other arithmetic  51 us (2%)
    ppermute x6, waiting for transfers between devices, passed_along(): lax.ppermute(value, axis, [(source, source + steps) for source in range(l...  269 us
    reduce_scatter x1, waiting for transfers between devices, on_device(): lax.psum_scatter(ffn_grads[0], 'dp', scatter_dimension=0, tiled=True)  257 us
    reduce_scatter x1, waiting for transfers between devices, on_device(): lax.psum_scatter(ffn_grads[1], 'dp', scatter_dimension=0, tiled=True)  257 us
    reduce_scatter x1, waiting for transfers between devices, on_device(): lax.psum_scatter(attn_grads[0], 'dp', scatter_dimension=0, tiled=True)  205 us
    dot_general x8, matrix products, outer_sum(): lax.dot_general(left_rows, right_rows, (((0,), (0,)), ((), ())), preferre...  140 us
    all_gather x1, waiting for transfers between devices, on_device(): lax.all_gather(w_up[0], 'dp', axis=0, tiled=True)  105 us
    all_gather x1, waiting for transfers between devices, on_device(): lax.all_gather(w_down[0], 'dp', axis=0, tiled=True)  104 us
    reduce_scatter x1, waiting for transfers between devices, on_device(): lax.psum_scatter(attn_grads[1], 'dp', scatter_dimension=0, tiled=True)  89.1 us
  transfers between devices with their start and end apart: 16, of which 14 were waited for; matrix products, arithmetic and copies ran while one was open for 0% of the time, Pallas kernels for 0%

commit v1 on v0

v1 whole, which is shorter than its diff:
```python
import functools
import math

import jax
import jax.numpy as jnp
from jax import lax
from jax.experimental import pallas as pl
from jax.experimental.pallas import tpu as pltpu
from jax.sharding import PartitionSpec as P

HEAD_DIM = 64
MESH = pl.DeviceIdType.MESH
LOW = jnp.bfloat16
F32 = jnp.float32


def ring_chip(position, chips):
    position = lax.rem(position + 2 * chips, chips)
    half = chips // 2
    return jnp.where(position < half, 2 * position, 2 * (chips - 1 - position) + 1)


def ring_place(chips):
    me = lax.axis_index("dp")
    core = lax.rem(me, 2)
    chip = me // 2
    position = jnp.where(lax.rem(chip, 2) == 0, chip // 2, chips - 1 - chip // 2)
    right = ring_chip(position + 1, chips) * 2 + core
    left = ring_chip(position - 1, chips) * 2 + core
    return (me, core, position, right, left, me + 1 - 2 * core)


def greet(devices):
    barrier = pltpu.get_barrier_semaphore()
    for device in devices:
        pl.semaphore_signal(barrier, inc=1, device_id={"dp": device}, device_id_type=MESH)
    pl.semaphore_wait(barrier, len(devices))


def gather_kernel(chips, splits, *refs):
    count = len(splits)
    shards, outs = (refs[:count], refs[count : 2 * count])
    ring_send, ring_recv, pair_send, pair_recv, own_sem = refs[2 * count :]
    half = chips // 2
    me, core, position, right, left, sibling = ring_place(chips)
    greet((left, right, sibling))

    def owner(step, way):
        return ring_chip(position - step if way == 0 else position + step, chips) * 2 + core

    def travels(item, way, step):
        return step < half or (step == half and splits[item] == way)

    def ring_copy(item, way, step):
        block = owner(step - 1, way)
        return pltpu.make_async_remote_copy(
            src_ref=shards[item] if step == 1 else outs[item].at[block],
            dst_ref=outs[item].at[block],
            send_sem=ring_send.at[item, way, step - 1],
            recv_sem=ring_recv.at[item, way, step - 1],
            device_id={"dp": right if way == 0 else left},
            device_id_type=MESH,
        )

    def pair_copy(item, offset, block, source):
        return pltpu.make_async_remote_copy(
            src_ref=source,
            dst_ref=outs[item].at[block],
            send_sem=pair_send.at[item, offset],
            recv_sem=pair_recv.at[item, offset],
            device_id={"dp": sibling},
            device_id_type=MESH,
        )

    sent, paired, kept = ([], [], [])
    for item in range(count):
        for way in (0, 1):
            if travels(item, way, 1):
                sent.append(ring_copy(item, way, 1))
                sent[-1].start()
    for item in range(count):
        paired.append(pair_copy(item, 0, me, shards[item]))
        paired[-1].start()
        kept.append(pltpu.make_async_copy(shards[item], outs[item].at[me], own_sem.at[item]))
        kept[-1].start()
    for step in range(1, half + 1):
        for item in range(count):
            for way in (0, 1):
                if not travels(item, way, step):
                    continue
                ring_copy(item, way, step).wait_recv()
                if travels(item, way, step + 1):
                    sent.append(ring_copy(item, way, step + 1))
                    sent[-1].start()
                block = owner(step, way)
                offset = step if way == 0 else chips - step
                paired.append(pair_copy(item, offset, block, outs[item].at[block]))
                paired[-1].start()
    for copy in sent:
        copy.wait_send()
    for copy in paired:
        copy.wait()
    for copy in kept:
        copy.wait()


def gather(shards, splits, count):
    chips = count // 2
    items = len(shards)
    return pl.pallas_call(
        functools.partial(gather_kernel, chips, splits),
        out_shape=[jax.ShapeDtypeStruct((count,) + shard.shape, shard.dtype) for shard in shards],
        in_specs=[pl.BlockSpec(memory_space=pl.ANY)] * items,
        out_specs=[pl.BlockSpec(memory_space=pl.ANY)] * items,
        scratch_shapes=[
            pltpu.SemaphoreType.DMA((items, 2, chips // 2)),
            pltpu.SemaphoreType.DMA((items, 2, chips // 2)),
            pltpu.SemaphoreType.DMA((items, chips)),
            pltpu.SemaphoreType.DMA((items, chips)),
            pltpu.SemaphoreType.DMA((items,)),
        ],
        compiler_params=pltpu.CompilerParams(collective_id=0, has_side_effects=True),
    )(*shards)


def scatter_kernel(chips, splits, *refs):
    count = len(splits)
    parts, outs = (refs[:count], refs[count : 2 * count])
    landed, paired, mine = (refs[2 * count : 3 * count], refs[3 * count : 4 * count], refs[4 * count : 5 * count])
    ring_send, ring_recv, pair_send, pair_recv, mine_sem = refs[5 * count :]
    half = chips // 2
    me, core, position, right, left, sibling = ring_place(chips)
    greet((left, right, sibling))

    def first(item, way):
        return 1 if splits[item] == way else 2

    def slot(item, way, step):
        return step - 1 if splits[item] == way else half + step - 2

    def offset_of(step, way):
        return half - step + 1 if way == 0 else chips - (half - step + 1)

    def pair_copy(item, offset):
        block = ring_chip(position + offset, chips) * 2 + 1 - core
        return pltpu.make_async_remote_copy(
            src_ref=parts[item].at[block],
            dst_ref=paired[item].at[offset],
            send_sem=pair_send.at[item, offset],
            recv_sem=pair_recv.at[item, offset],
            device_id={"dp": sibling},
            device_id_type=MESH,
        )

    def ring_copy(item, way, step):
        if step == first(item, way):
            source = paired[item].at[offset_of(step, way)]
        else:
            source = landed[item].at[slot(item, way, step - 1)]
        here = slot(item, way, step)
        return pltpu.make_async_remote_copy(
            src_ref=source,
            dst_ref=landed[item].at[here],
            send_sem=ring_send.at[item, here],
            recv_sem=ring_recv.at[item, here],
            device_id={"dp": right if way == 0 else left},
            device_id_type=MESH,
        )

    def load(item, offset, buffer):
        block = ring_chip(position + offset, chips) * 2 + core
        return pltpu.make_async_copy(parts[item].at[block], mine[item].at[buffer], mine_sem.at[item, buffer])

    plan, uses = ([], [0] * count)
    for step in range(1, half + 2):
        for item in range(count):
            for way in (0, 1):
                if step <= half and step >= first(item, way):
                    plan.append((step, item, way, offset_of(step, way), uses[item] % 2))
                    uses[item] += 1
            if step > half:
                plan.append((step, item, None, 0, uses[item] % 2))
                uses[item] += 1
    for step, item, way, offset, buffer in plan:
        pair_copy(item, offset).start()
    load(plan[0][1], plan[0][3], plan[0][4]).start()
    sent = []
    for number, (step, item, way, offset, buffer) in enumerate(plan):
        if number + 1 < len(plan):
            load(plan[number + 1][1], plan[number + 1][3], plan[number + 1][4]).start()
        load(item, offset, buffer).wait()
        pair_copy(item, offset).wait_recv()
        rows = parts[item].shape[1]
        kind = parts[item].dtype
        chunk = 16 if rows % 16 == 0 else rows
        from_pair, from_mine, from_ring = (paired[item], mine[item], landed[item])
        if way is None:
            ring_copy(item, 0, half).wait_recv()
            ring_copy(item, 1, half).wait_recv()
            slot_a, slot_b = (slot(item, 0, half), slot(item, 1, half))

            @pl.loop(0, rows // chunk)
            def _(index):
                here = pl.ds(pl.multiple_of(index * chunk, chunk), chunk)
                outs[item][here, :] = (
                    from_ring[slot_a, here, :].astype(F32) + from_ring[slot_b, here, :].astype(F32)
                ) + (from_mine[buffer, here, :].astype(F32) + from_pair[offset, here, :].astype(F32))

            continue
        if step == first(item, way):

            @pl.loop(0, rows // chunk)
            def _(index):
                here = pl.ds(pl.multiple_of(index * chunk, chunk), chunk)
                from_pair[offset, here, :] = (
                    from_mine[buffer, here, :].astype(F32) + from_pair[offset, here, :].astype(F32)
                ).astype(kind)

        else:
            ring_copy(item, way, step - 1).wait_recv()
            arrived = slot(item, way, step - 1)

            @pl.loop(0, rows // chunk)
            def _(index):
                here = pl.ds(pl.multiple_of(index * chunk, chunk), chunk)
                from_ring[arrived, here, :] = (
                    from_ring[arrived, here, :].astype(F32)
                    + (from_mine[buffer, here, :].astype(F32) + from_pair[offset, here, :].astype(F32))
                ).astype(kind)

        sent.append(ring_copy(item, way, step))
        sent[-1].start()
    for copy in sent:
        copy.wait_send()
    for step, item, way, offset, buffer in plan:
        pair_copy(item, offset).wait_send()


def scatter(parts, splits, count):
    chips = count // 2
    items = len(parts)
    shapes = [part.shape[1:] for part in parts]
    kinds = [part.dtype for part in parts]
    return pl.pallas_call(
        functools.partial(scatter_kernel, chips, splits),
        out_shape=[jax.ShapeDtypeStruct(shape, F32) for shape in shapes],
        in_specs=[pl.BlockSpec(memory_space=pl.ANY)] * items,
        out_specs=[pl.BlockSpec(memory_space=pltpu.VMEM)] * items,
        scratch_shapes=[pltpu.VMEM((chips - 1,) + shape, kind) for shape, kind in zip(shapes, kinds)]
        + [pltpu.VMEM((chips,) + shape, kind) for shape, kind in zip(shapes, kinds)]
        + [pltpu.VMEM((2,) + shape, kind) for shape, kind in zip(shapes, kinds)]
        + [
            pltpu.SemaphoreType.DMA((items, chips - 1)),
            pltpu.SemaphoreType.DMA((items, chips - 1)),
            pltpu.SemaphoreType.DMA((items, chips)),
            pltpu.SemaphoreType.DMA((items, chips)),
            pltpu.SemaphoreType.DMA((items, 2)),
        ],
        compiler_params=pltpu.CompilerParams(
            collective_id=1, has_side_effects=True, vmem_limit_bytes=62 * 2**20
        ),
    )(*parts)


def block_shape(rows, columns):
    return (rows, columns) if rows % 16 == 0 else (rows * columns // 128, 128)


def small_pack(gains, shifts, bias, count):
    width = gains.shape[1] // count
    ups = bias.shape[0] // gains.shape[1]
    rows = [
        gains.reshape(2, count, width).swapaxes(0, 1),
        shifts.reshape(6, count, width).swapaxes(0, 1),
        bias.reshape(count, ups, width),
    ]
    blank = jnp.zeros((count, 8 - ups, width), gains.dtype)
    return jnp.concatenate(rows + [blank], axis=1)


def small_split(blocks, ups):
    count, _, width = blocks.shape
    gains = blocks[:, 0:2].swapaxes(0, 1).reshape(2, count * width)
    shifts = blocks[:, 2:8].swapaxes(0, 1).reshape(6, count * width)
    bias = blocks[:, 8 : 8 + ups].reshape(count * ups * width)
    return (gains, shifts, bias)


def layer_norm(rows_in):
    center = rows_in - jnp.mean(rows_in, axis=-1, keepdims=True)
    inverse = lax.rsqrt(jnp.mean(center * center, axis=-1, keepdims=True) + 1e-05)
    return (center * inverse, inverse)


def norm_back(grad_rows, normed, inverse):
    return inverse * (
        grad_rows
        - jnp.mean(grad_rows, axis=-1, keepdims=True)
        - normed * jnp.mean(grad_rows * normed, axis=-1, keepdims=True)
    )


def gelu_parts(hidden_pre):
    cumulative = 0.5 * (1.0 + lax.erf(hidden_pre * (1.0 / math.sqrt(2.0))))
    slope = cumulative + hidden_pre * jnp.exp(-0.5 * hidden_pre * hidden_pre) * (
        1.0 / math.sqrt(2.0 * math.pi)
    )
    return (hidden_pre * cumulative, slope)


def split_heads(packed, model_width):
    length = packed.shape[0]
    head_count = model_width // HEAD_DIM
    queries = packed[:, :model_width].reshape(length, head_count, HEAD_DIM)
    key_rows = packed[:, model_width : 2 * model_width].reshape(length, head_count, HEAD_DIM)
    values = packed[:, 2 * model_width :].reshape(length, head_count, HEAD_DIM)
    return (queries, key_rows, values)


def attend(packed, model_width):
    queries, key_rows, values = split_heads(packed, model_width)
    scores = jnp.einsum("qhd,khd->hqk", queries, key_rows, preferred_element_type=jnp.float32) * (
        1.0 / math.sqrt(HEAD_DIM)
    )
    row_max = jnp.max(scores, axis=-1, keepdims=True)
    shifted = jnp.exp(scores - row_max)
    row_total = jnp.sum(shifted, axis=-1, keepdims=True)
    attn_probs = (shifted / row_total).astype(jnp.bfloat16)
    mixed_out = jnp.einsum("hqk,khd->qhd", attn_probs, values, preferred_element_type=jnp.float32)
    log_total = (row_max + jnp.log(row_total))[:, :, 0]
    return (mixed_out.reshape(packed.shape[0], model_width).astype(jnp.bfloat16), log_total)


def attend_back(packed, log_total, grad_mixed, model_width):
    queries, key_rows, values = split_heads(packed, model_width)
    length = packed.shape[0]
    score_scale = 1.0 / math.sqrt(HEAD_DIM)
    scores = (
        jnp.einsum("qhd,khd->hqk", queries, key_rows, preferred_element_type=jnp.float32)
        * score_scale
    )
    attn_probs = jnp.exp(scores - log_total[:, :, None])
    grad_heads = grad_mixed.reshape(length, -1, HEAD_DIM)
    grad_probs = jnp.einsum("qhd,khd->hqk", grad_heads, values, preferred_element_type=jnp.float32)
    weighted = jnp.sum(grad_probs * attn_probs, axis=-1, keepdims=True)
    grad_scores = (attn_probs * (grad_probs - weighted)).astype(jnp.bfloat16)
    grad_query = (
        jnp.einsum("hqk,khd->qhd", grad_scores, key_rows, preferred_element_type=jnp.float32)
        * score_scale
    )
    grad_key = (
        jnp.einsum("hqk,qhd->khd", grad_scores, queries, preferred_element_type=jnp.float32)
        * score_scale
    )
    grad_value = jnp.einsum(
        "hqk,qhd->khd",
        attn_probs.astype(jnp.bfloat16),
        grad_heads,
        preferred_element_type=jnp.float32,
    )
    joined = jnp.concatenate(
        [
            grad_query.reshape(length, model_width),
            grad_key.reshape(length, model_width),
            grad_value.reshape(length, model_width),
        ],
        axis=1,
    )
    return joined.astype(jnp.bfloat16)


def forward_layer(entry_rows, params):
    gain_values, shift_values, bias, w_qkv, w_out, w_up, w_down = params
    model_width = entry_rows.shape[-1]
    rows_in = entry_rows.astype(F32)
    normed, inverse = layer_norm(rows_in)
    lowered = (normed * gain_values[0] + shift_values[0]).astype(LOW)
    projected = jnp.dot(lowered, w_qkv, preferred_element_type=F32)
    extra = jnp.concatenate([shift_values[1], jnp.zeros_like(shift_values[1]), shift_values[2]])
    packed = (projected + extra).astype(LOW)
    mixed_out, log_total = attend(packed, model_width)
    middle = rows_in + jnp.dot(mixed_out, w_out, preferred_element_type=F32) + shift_values[3]
    normed_two, inverse_two = layer_norm(middle)
    second = (normed_two * gain_values[1] + shift_values[4]).astype(LOW)
    hidden_pre = jnp.dot(second, w_up, preferred_element_type=F32) + bias
    activated, slope = gelu_parts(hidden_pre)
    activated = activated.astype(LOW)
    output = middle + (jnp.dot(activated, w_down, preferred_element_type=F32) + shift_values[5])
    return (output.astype(LOW), (entry_rows, lowered, packed, log_total, mixed_out, middle, second, activated, slope.astype(LOW)))


def backward_layer(saved_items, grad_out, params):
    entry_rows, lowered, packed, log_total, mixed_out, middle, second, activated, slope = saved_items
    gain_values, shift_values, bias, w_qkv, w_out, w_up, w_down = params
    model_width = entry_rows.shape[-1]
    normed, inverse = layer_norm(entry_rows.astype(F32))
    normed_two, inverse_two = layer_norm(middle)
    grad_ff = grad_out.astype(LOW)
    grad_act = jnp.dot(grad_ff, w_down.T, preferred_element_type=F32)
    grad_inner = (grad_act * slope.astype(F32)).astype(LOW)
    grad_second = jnp.dot(grad_inner, w_up.T, preferred_element_type=F32)
    grad_middle = grad_out + norm_back(grad_second * gain_values[1], normed_two, inverse_two)
    grad_branch = grad_middle.astype(LOW)
    grad_mixed = jnp.dot(grad_branch, w_out.T, preferred_element_type=F32).astype(LOW)
    grad_packed = attend_back(packed, log_total, grad_mixed, model_width)
    grad_lowered = jnp.dot(grad_packed, w_qkv.T, preferred_element_type=F32)
    grad_rows = grad_middle + norm_back(grad_lowered * gain_values[0], normed, inverse)
    packed_sums = jnp.sum(grad_packed, axis=0, dtype=F32)
    grad_gains = jnp.stack(
        [jnp.sum(grad_lowered * normed, axis=0), jnp.sum(grad_second * normed_two, axis=0)]
    )
    grad_shifts = jnp.stack(
        [
            jnp.sum(grad_lowered, axis=0),
            packed_sums[:model_width],
            packed_sums[2 * model_width :],
            jnp.sum(grad_branch, axis=0, dtype=F32),
            jnp.sum(grad_second, axis=0),
            jnp.sum(grad_ff, axis=0, dtype=F32),
        ]
    )
    grad_bias = jnp.sum(grad_inner, axis=0, dtype=F32)
    pairs = (lowered, grad_packed, mixed_out, grad_branch, second, grad_inner, activated, grad_ff)
    return (grad_rows.astype(LOW), (grad_gains, grad_shifts, grad_bias), pairs)


def outer_sum(left_rows, right_rows):
    return lax.dot_general(
        left_rows, right_rows, (((0,), (0,)), ((), ())), preferred_element_type=F32
    )


def either(flag, run, keep):
    return lax.cond(flag, lambda kept: run(), lambda kept: kept, keep)


def blank_like(run):
    return jax.tree.map(lambda leaf: jnp.zeros(leaf.shape, leaf.dtype), jax.eval_shape(run))


def on_device(inputs, out_grad, query_counts, gains, shifts, w_qkv, w_out, w_up, b_up, w_down):
    stage = lax.axis_index("pipe")
    count = lax.axis_size("dp")
    cell_count, length, model_width = inputs.shape
    own = model_width // count
    ups = b_up.shape[1] // own
    ff_width = ups * model_width
    low_half = w_down.shape[1] // 2
    shards = [
        small_pack(gains[0], shifts[0], b_up[0], 1)[0],
        w_qkv[0].reshape(block_shape(own, 3 * model_width)),
        w_out[0].reshape(block_shape(own, model_width)),
        w_up[0].reshape(block_shape(own, ff_width)),
        w_down[0, :low_half].reshape(block_shape(low_half, model_width)),
        w_down[0, low_half:].reshape(block_shape(low_half, model_width)),
    ]
    splits = (0, 0, 0, 1, 0, 1)
    small, all_qkv, all_out, all_up, down_a, down_b = gather(shards, splits, count)
    gain_rows, shift_rows, bias = small_split(small.astype(F32), ups)
    down_parts = [part.reshape(count, 1, low_half, model_width) for part in (down_a, down_b)]
    params = (
        gain_rows,
        shift_rows,
        bias,
        all_qkv.reshape(model_width, 3 * model_width),
        all_out.reshape(model_width, model_width),
        all_up.reshape(model_width, ff_width),
        jnp.concatenate(down_parts, axis=1).reshape(ff_width, model_width),
    )
    scales = jnp.sqrt(query_counts.astype(F32) / 500.0)
    last = lax.axis_size("pipe") - 1

    def along(value, steps):
        stages = lax.axis_size("pipe")
        pairs = [(source, source + steps) for source in range(stages) if 0 <= source + steps < stages]
        return lax.ppermute(value, "pipe", pairs)

    stages = lax.axis_size("pipe")
    forward = [None] * cell_count
    arrived = [inputs[cell] for cell in range(cell_count)]
    for turn in range(stages):
        here = []
        for cell in range(cell_count):
            def run(cell=cell):
                return forward_layer(arrived[cell], params)
            if turn == 0:
                forward[cell] = either(stage == 0, run, blank_like(run))
            else:
                forward[cell] = either(stage == turn, run, forward[cell])
            if turn + 1 < stages:
                here.append(along(forward[cell][0], 1))
        arrived = here
    backward = [None] * cell_count
    incoming = [out_grad[cell].astype(F32) * scales[cell] for cell in range(cell_count)]
    for turn in range(stages):
        here = []
        for cell in range(cell_count):
            def run(cell=cell):
                return backward_layer(forward[cell][1], incoming[cell].astype(F32), params)
            if turn == 0:
                backward[cell] = either(stage == last, run, blank_like(run))
            else:
                backward[cell] = either(stage == last - turn, run, backward[cell])
            if turn + 1 < stages:
                here.append(along(backward[cell][0], -1))
        incoming = here
    section_out = jnp.stack([forward[cell][0] for cell in range(cell_count)])
    input_grads = jnp.stack([backward[cell][0] for cell in range(cell_count)])
    sums = functools.reduce(
        lambda left, right: jax.tree.map(jnp.add, left, right),
        [backward[cell][1] for cell in range(cell_count)],
    )
    sides = [
        jnp.concatenate([backward[cell][2][side] for cell in range(cell_count)]) for side in range(8)
    ]
    grads = [outer_sum(sides[at], sides[at + 1]).astype(LOW) for at in (0, 2, 4, 6)]
    down_grads = grads[3].reshape(count, 2, low_half, model_width)
    parts = [
        small_pack(*sums, count),
        grads[0].reshape((count,) + block_shape(own, 3 * model_width)),
        grads[1].reshape((count,) + block_shape(own, model_width)),
        grads[2].reshape((count,) + block_shape(own, ff_width)),
        down_grads[:, 0].reshape((count,) + block_shape(low_half, model_width)),
        down_grads[:, 1].reshape((count,) + block_shape(low_half, model_width)),
    ]
    shares = scatter(parts, splits, count)
    grad_gains, grad_shifts, grad_bias = small_split(shares[0][None], ups)
    return (
        section_out[None],
        input_grads[None],
        grad_gains[None],
        grad_shifts[None],
        shares[1].reshape(1, own, 3 * model_width),
        shares[2].reshape(1, own, model_width),
        shares[3].reshape(1, own, ff_width),
        grad_bias[None],
        jnp.concatenate([part.reshape(low_half, model_width) for part in shares[4:]])[None],
    )


def solution(mesh):
    in_specs = (
        P("dp", None, None),
        P("dp", None, None),
        P("dp"),
        P("pipe", None, "dp"),
        P("pipe", None, "dp"),
        P("pipe", "dp", None),
        P("pipe", "dp", None),
        P("pipe", "dp", None),
        P("pipe", "dp"),
        P("pipe", "dp", None),
    )
    out_specs = (
        P("pipe", "dp", None, None),
        P("pipe", "dp", None, None),
        P("pipe", None, "dp"),
        P("pipe", None, "dp"),
        P("pipe", "dp", None),
        P("pipe", "dp", None),
        P("pipe", "dp", None),
        P("pipe", "dp"),
        P("pipe", "dp", None),
    )
    return jax.shard_map(
        on_device, mesh=mesh, in_specs=in_specs, out_specs=out_specs, check_vma=False
    )
```

time: 2120 us -> 1000 us (0.47)
  waiting for transfers between devices: 1370 us -> 127 us
  Pallas kernels: 0 us -> 390 us
  blocking collectives: 167 us -> 0 us
  matrix products: 322 us -> 233 us
  starting transfers between devices: 69.3 us -> 6.24 us
  loops' own time: 13.2 us -> 41.3 us
  other arithmetic: 51 us -> 77.7 us
    reduce_scatter x4 -> x0, waiting for transfers between devices: 807 us -> none  [the longest x1 257 us: on_device(): lax.psum_scatter(ffn_grads[0], 'dp', scatter_dimension=0, tiled=True)]
    pallas_call x0 -> x2, Pallas kernels: none -> 390 us  [the longest x1 196 us: scatter(): pl.pallas_call(functools.partial(scatter_kernel, chips, splits), out_shap...]
    all_gather x4 -> x0, waiting for transfers between devices: 235 us -> none  [the longest x1 105 us: on_device(): lax.all_gather(w_up[0], 'dp', axis=0, tiled=True)]
    ppermute x6 -> x4, waiting for transfers between devices: 269 us -> 127 us  [along(): return lax.ppermute(value, 'pipe', pairs)]
    all_gather x3 -> x0, blocking collectives: 109 us -> none  [the longest x1 61 us: on_device(): lax.all_gather(b_up[0], 'dp', axis=0, tiled=True)]
    dot_general x8 -> x4, matrix products: 140 us -> 52.5 us  [outer_sum(): lax.dot_general(left_rows, right_rows, (((0,), (0,)), ((), ())), preferre...]
    ppermute x6 -> x4, starting transfers between devices: 68.9 us -> 6.24 us  [along(): return lax.ppermute(value, 'pipe', pairs)]
    unnamed x1 -> x0, blocking collectives: 57.7 us -> none
  transfers between devices with their start and end apart: 16 -> 4, of which waited for: 14 -> 2; matrix products, arithmetic and copies ran while one was open for 0% -> 18% of each run, Pallas kernels for 0% -> 0%
where the time goes in v1:
time: 1000 us; the launch traced here: 991 us
  Pallas kernels  390 us (39%)
  matrix products  233 us (23%)
  waiting for transfers between devices  127 us (13%)
  local copies, waits for them, and re-layouts  115 us (12%)
  other arithmetic  77.7 us (8%)
  loops' own time  41.3 us (4%)
    pallas_call x1, Pallas kernels, scatter(): pl.pallas_call(functools.partial(scatter_kernel, chips, splits), out_shap...  196 us
    pallas_call x1, Pallas kernels, gather(): pl.pallas_call(functools.partial(gather_kernel, chips, splits), out_shape...  194 us
    ppermute x4, waiting for transfers between devices, along(): return lax.ppermute(value, 'pipe', pairs)  127 us
    dot_general x4, matrix products, outer_sum(): lax.dot_general(left_rows, right_rows, (((0,), (0,)), ((), ())), preferre...  52.5 us
    another operation x8, loops' own time, either(): return lax.cond(flag, lambda kept: run(), lambda kept: kept, keep)  41.3 us
    another operation x30, local copies, waits for them, and re-layouts  39.3 us
    dot_general x2, matrix products, forward_layer(): hidden_pre = jnp.dot(second, w_up, preferred_element_type=F32) + bias  25.4 us
    dot_general x2, matrix products, backward_layer(): grad_second = jnp.dot(grad_inner, w_up.T, preferred_element_type=F32)  24.1 us
  transfers between devices with their start and end apart: 4, of which 2 were waited for; matrix products, arithmetic and copies ran while one was open for 18% of the time, Pallas kernels for 0%

profile of v1, /device:TPU:0, one launch (start us, length us, event | category | flops | bytes accessed | tf_op | source)
XLA Modules:
  0.0 991.3 jit_solution(3328067665724663931)
XLA Ops:
  4.9 194.0 %shard_map.169 = (bf16[16,16,80]{2,1,0:T(8,128)(2,1)}, bf16[16,80,3840]{2,1,0:T(8,128)(2,1)}, bf16[16,80,1280]{2,1,0:T(8,128)(2,1)}, bf16[16,80,5120]{2,1,0:T(8,...) custom-call(bf16[16,80]{1,0:T(8,128)(2,1)} %maximum_bitcast_fusion.3.refs_0_, ...), custom_call_target="tpu_custom_call" | custom-call | tf_op jit(solution)/shard_map/pallas_call | solution.py:110
  200.8 7.0 pad_maximum_fusion.12
  213.6 58.8 %conditional.10 = (bf16[384,1280]{1,0:T(8,128)(2,1)}, bf16[384,1280]{1,0:T(8,128)(2,1)S(1)}, bf16[384,1280]{1,0:T(8,128)(2,1)}, bf16[384,3840]{1,0:T(8,128)(2,1)...) conditional(s32[]{:T(128)} %convert_element_type.329, () %tuple.92, ...), branch_computations={%region_16.0_spmd, %region_17.0_spmd} | conditional | flops 15921315840 | bytes 188587312 | solution.py:434
  217.1 9.7 add_convert_fusion.4
  251.1 12.6 %fusion.42 = (bf16[384,5120]{1,0:T(8,128)(2,1)}, bf16[384,5120]{1,0:T(8,128)(2,1)}) fusion(f32[5120]{0:T(1024)S(1)} %add.412, bf16[384,1280]{1,0:T(8,128)(2,1)} %add_convert_fusion.5, bf16[1280,5120]{1,0:T(8,128)(2,1)} %get-tuple-element.385), kind=kOutput, calls=%fused_computation.103 | convolution fusion | flops 5056757760 | bytes 21975040 | tf_op jit(solution)/shard_map/cond/branch_1_fun/dot_general | solution.py:385
  263.8 8.3 fusion.46
  274.7 59.7 %conditional.8 = (bf16[384,1280]{1,0:T(8,128)(2,1)}, bf16[384,1280]{1,0:T(8,128)(2,1)S(1)}, bf16[384,1280]{1,0:T(8,128)(2,1)S(1)}, bf16[384,3840]{1,0:T(8,128)(2...) conditional(s32[]{:T(128)} %convert_element_type.329, () %tuple.88, ...), branch_computations={%region_0.0_spmd, %region_1.0_spmd} | conditional | flops 15921315840 | bytes 200383888 | solution.py:434
  277.3 9.5 add_convert_fusion
  313.0 12.8 %fusion.5 = (bf16[384,5120]{1,0:T(8,128)(2,1)}, bf16[384,5120]{1,0:T(8,128)(2,1)}) fusion(f32[5120]{0:T(1024)S(1)} %add.364, bf16[384,1280]{1,0:T(8,128)(2,1)S(1)} %add_convert_fusion.1, bf16[1280,5120]{1,0:T(8,128)(2,1)} %get-tuple-element.369), kind=kOutput, calls=%fused_computation.9 | convolution fusion | flops 5056757760 | bytes 21975040 | tf_op jit(solution)/shard_map/cond/branch_1_fun/dot_general | solution.py:385
  325.9 8.3 fusion.9
  340.4 11.7 %conditional.11 = (bf16[384,1280]{1,0:T(8,128)(2,1)S(1)}, bf16[384,1280]{1,0:T(8,128)(2,1)}, bf16[384,3840]{1,0:T(8,128)(2,1)}, f32[20,384]{1,0:T(8,128)S(1)}, b...) conditional(s32[]{:T(128)} %convert_element_type.328, ...), branch_computations={%region_24.0_spmd, %region_25.0_spmd} | conditional | flops 15921316864 | bytes 181705968 | solution.py:434
  352.1 20.9 %conditional.14 = (bf16[384,1280]{1,0:T(8,128)(2,1)}, f32[2,1280]{1,0:T(2,128)S(1)}, f32[6,1280]{1,0:T(8,128)S(1)}, f32[5120]{0:T(1024)S(1)}, bf16[384,1280]{1,0...) conditional(s32[]{:T(128)} %convert_element_type.328, ...), branch_computations={%region_70.0_spmd, %region_71.0_spmd} | conditional | flops 17073909760 | bytes 252489952 | solution.py:434
  374.3 11.3 %conditional.9 = (bf16[384,1280]{1,0:T(8,128)(2,1)S(1)}, bf16[384,1280]{1,0:T(8,128)(2,1)}, bf16[384,3840]{1,0:T(8,128)(2,1)}, f32[20,384]{1,0:T(8,128)S(1)}, bf...) conditional(s32[]{:T(128)} %convert_element_type.328, ...), branch_computations={%region_8.0_spmd, %region_9.0_spmd} | conditional | flops 15921316864 | bytes 189570384 | solution.py:434
  385.6 21.1 %conditional.12 = (bf16[384,1280]{1,0:T(8,128)(2,1)}, f32[2,1280]{1,0:T(2,128)S(1)}, f32[6,1280]{1,0:T(8,128)S(1)}, f32[5120]{0:T(1024)S(1)}, bf16[384,1280]{1,0...) conditional(s32[]{:T(128)} %convert_element_type.328, () %tuple.96, ...), branch_computations={%region_32.0_spmd, %region_33.0_spmd} | conditional | flops 17073909760 | bytes 252489952 | solution.py:434
  408.6 70.5 %collective-permute-done.3 = bf16[384,1280]{1,0:T(8,128)(2,1)} collective-permute-done((bf16[384,1280]{1,0:T(8,128)(2,1)}, bf16[384,1280]{1,0:T(8,128)(2,1)}, u32[]{:S(2)}, u32[]{:S(2)}) %collective-permute-start.3) | collective-permute-done | bytes 983072 | tf_op jit(solution)/shard_map/ppermute | solution.py:476
  479.1 92.7 %conditional.15 = (f32[2,1280]{1,0:T(2,128)S(1)}, f32[6,1280]{1,0:T(8,128)S(1)}, f32[5120]{0:T(1024)S(1)}, bf16[384,1280]{1,0:T(8,128)(2,1)}, bf16[384,3840]{0,1...) conditional(s32[]{:T(128)} %convert_element_type.329, ...), branch_computations={%region_89.0_spmd, %region_90.0_spmd} | conditional | flops 17072433152 | bytes 250523904 | solution.py:434
  504.1 10.5 %convert_reduce_fusion.19 = (f32[5120]{0:T(1024)S(1)}, bf16[384,5120]{1,0:T(8,128)(2,1)}) fusion(bf16[384,5120]{1,0:T(8,128)(2,1)} %get-tuple-element.446, bf16[384,1280]{1,0:T(8,128)(2,1)} %get-tuple-element.1239, bf16[5120,1280]{1,0:T(8,128)(2,1)} %get-tuple-element.445), kind=kOutput, calls=%fused_computation.344 | convolution fusion | flops 5042990080 | bytes 21975040 | tf_op jit(solution)/shard_map/cond/branch_1_fun/dot_general | solution.py:399
  514.6 12.1 %multiply_reduce_fusion.28 = (f32[384]{0:T(512)S(1)}, f32[1280]{0:T(1024)S(1)}, f32[384]{0:T(512)S(1)}, f32[1280]{0:T(1024)S(1)}, f32[384,1280]{1,0:T(8,128)S(1)}) fusion(f32[384,1280]{1,0:T(8,128)} %get-tuple-element.444, f32[1280]{0:T(1024)S(1)} %get-tuple-element.982, f32[384]{0:T(512)S(1)} %add_rsqrt_fusion.15, f32[384]{0:T(512)S(1)} %broadcast_multiply_fusion.31, ...), kind=kOutput, calls=%fused_computation.373 | convolution fusion | flops 5037584384 | bytes 20993024 | tf_op jit(solution)/shard_map/cond/branch_1_fun/dot_general | solution.py:401
  548.4 6.4 multiply_convert_fusion.16
  560.3 9.2 fusion.149
  571.8 56.8 %collective-permute-done.2 = bf16[384,1280]{1,0:T(8,128)(2,1)} collective-permute-done((bf16[384,1280]{1,0:T(8,128)(2,1)}, bf16[384,1280]{1,0:T(8,128)(2,1)}, u32[]{:S(2)}, u32[]{:S(2)}) %collective-permute-start.2) | collective-permute-done | bytes 983072 | tf_op jit(solution)/shard_map/ppermute | solution.py:476
  628.6 89.5 %conditional.13 = (f32[2,1280]{1,0:T(2,128)S(1)}, f32[6,1280]{1,0:T(8,128)S(1)}, f32[5120]{0:T(1024)S(1)}, bf16[384,1280]{1,0:T(8,128)(2,1)}, bf16[384,3840]{0,1...) conditional(s32[]{:T(128)} %convert_element_type.329, ...), branch_computations={%region_51.0_spmd, %region_52.0_spmd} | conditional | flops 17072433152 | bytes 254456096 | solution.py:434
  651.1 10.5 %convert_reduce_fusion.9 = (f32[5120]{0:T(1024)S(1)}, bf16[384,5120]{1,0:T(8,128)(2,1)}) fusion(bf16[384,5120]{1,0:T(8,128)(2,1)} %get-tuple-element.416, bf16[384,1280]{1,0:T(8,128)(2,1)} %get-tuple-element.1287, bf16[5120,1280]{1,0:T(8,128)(2,1)} %get-tuple-element.415), kind=kOutput, calls=%fused_computation.242 | convolution fusion | flops 5042990080 | bytes 21975040 | tf_op jit(solution)/shard_map/cond/branch_1_fun/dot_general | solution.py:399
  661.6 12.1 %multiply_reduce_fusion.16 = (f32[384]{0:T(512)S(1)}, f32[1280]{0:T(1024)S(1)}, f32[384]{0:T(512)S(1)}, f32[1280]{0:T(1024)S(1)}, f32[384,1280]{1,0:T(8,128)S(1)}) fusion(f32[384,1280]{1,0:T(8,128)} %get-tuple-element.414, f32[1280]{0:T(1024)S(1)} %get-tuple-element.962, f32[384]{0:T(512)S(1)} %add_rsqrt_fusion.11, f32[384]{0:T(512)S(1)} %broadcast_multiply_fusion.19, ...), kind=kOutput, calls=%fused_computation.271 | convolution fusion | flops 5037584384 | bytes 20993024 | tf_op jit(solution)/shard_map/cond/branch_1_fun/dot_general | solution.py:401
  695.1 6.4 multiply_convert_fusion.8
  706.9 9.2 fusion.106
  718.5 16.1 %convolution_convert_fusion.4 = bf16[5120,1280]{1,0:T(8,128)(2,1)} fusion(bf16[384,5120]{1,0:T(8,128)(2,1)} %get-tuple-element.656, bf16[384,5120]{1,0:T(8,128)(2,1)} %get-tuple-element.655, bf16[384,1280]{1,0:T(8,128)(2,1)} %get-tuple-element.658, bf16[384,1280]{1,0:T(8,128)(2,1)} %get-tuple-element.657), kind=kOutput, calls=%fused_computation.392 | convolution fusion | flops 10092544000 | bytes 22937600 | tf_op jit(solution)/shard_map/dot_general | solution.py:428
  734.6 9.5 slice_bitcast_fusion.2
  744.7 6.6 convolution_convert_fusion.7
  751.4 13.6 %convolution_convert_fusion.6 = bf16[1280,3840]{1,0:T(8,128)(2,1)} fusion(bf16[384,3840]{0,1:T(8,128)(2,1)} %get-tuple-element.646, bf16[384,3840]{0,1:T(8,128)(2,1)} %get-tuple-element.645, bf16[384,1280]{1,0:T(8,128)(2,1)} %get-tuple-element.644, bf16[384,1280]{1,0:T(8,128)(2,1)} %get-tuple-element.643), kind=kOutput, calls=%fused_computation.394 | convolution fusion | flops 7570391040 | bytes 17694720 | tf_op jit(solution)/shard_map/dot_general | solution.py:428
  765.0 16.3 %convolution_convert_fusion.5 = bf16[1280,5120]{1,0:T(8,128)(2,1)} fusion(bf16[384,5120]{1,0:T(8,128)(2,1)} %get-tuple-element.654, bf16[384,5120]{1,0:T(8,128)(2,1)} %get-tuple-element.653, bf16[384,1280]{1,0:T(8,128)(2,1)} %get-tuple-element.652, bf16[384,1280]{1,0:T(8,128)(2,1)} %get-tuple-element.651), kind=kOutput, calls=%fused_computation.393 | convolution fusion | flops 10092544000 | bytes 22937600 | tf_op jit(solution)/shard_map/dot_general | solution.py:428
  781.2 195.6 %shard_map.170 = (f32[16,80]{1,0:T(8,128)}, f32[80,3840]{1,0:T(8,128)}, f32[80,1280]{1,0:T(8,128)}, f32[80,5120]{1,0:T(8,128)}, f32[160,1280]{1,0:T(8,128)}, /*index=5*/f32[160,1280]{1,0:T(8,128)}) custom-call(f32[16,16,80]{2,1,0:T(8,128)} %maximum_maximum_fusion.refs_0_, bf16[16,80,3840]{2,1,0:T(8,128)(2,1)} %bitcast.284, bf16[16,80,1280]{2,1,0:T(8,128)(2,1)} %bitcast.335, ...), custom_call_target="tpu_custom_call" | custom-call | tf_op jit(solution)/shard_map/pallas_call | solution.py:244
  (266 shorter events, 225.3 us)
Async XLA Ops:
  215.3 26.9 %copy-start = (bf16[384,1280]{1,0:T(8,128)(2,1)}, bf16[384,1280]{1,0:T(8,128)(2,1)S(1)}, u32[]{:S(2)}) copy-start(bf16[384,1280]{1,0:T(8,128)(2,1)S(1)} %get-tuple-element.1124) | copy-start | bytes 2949124 | tf_op jit(solution)/shard_map/cond
  248.1 15.6 %slice-start = ((s8[13107200]{0:T(1024)(128)(4,1)}), s8[4194304]{0:T(1024)(128)(4,1)S(1)}, s32[]{:S(2)}) async-start(s8[13107200]{0:T(1024)(128)(4,1)} %bitcast.274), calls=%async_computation | async-start | bytes 8388608 | tf_op jit(solution)/shard_map/cond
  251.1 12.6 %slice-start.1 = ((s8[13107200]{0:T(1024)(128)(4,1)}), s8[4194304]{0:T(1024)(128)(4,1)S(1)}, s32[]{:S(2)}) async-start(s8[13107200]{0:T(1024)(128)(4,1)} %bitcast.274), calls=%async_computation.1 | async-start | bytes 8388608 | tf_op jit(solution)/shard_map/cond
  251.1 12.6 %slice-start.2 = ((s8[13107200]{0:T(1024)(128)(4,1)}), s8[4194304]{0:T(1024)(128)(4,1)S(1)}, s32[]{:S(2)}) async-start(s8[13107200]{0:T(1024)(128)(4,1)} %bitcast.274), calls=%async_computation.2 | async-start | bytes 8388608 | tf_op jit(solution)/shard_map/cond
  251.1 12.6 %slice-start.3 = ((s8[13107200]{0:T(1024)(128)(4,1)}), s8[524288]{0:T(1024)(128)(4,1)S(1)}, s32[]{:S(2)}) async-start(s8[13107200]{0:T(1024)(128)(4,1)} %bitcast.274), calls=%async_computation.3 | async-start | bytes 1048576 | tf_op jit(solution)/shard_map/cond
  263.8 8.3 copy-start.1
  272.4 68.0 %collective-permute-start.1 = (bf16[384,1280]{1,0:T(8,128)(2,1)}, bf16[384,1280]{1,0:T(8,128)(2,1)}, u32[]{:S(2)}, u32[]{:S(2)}) collective-permute-start(bf16[384,1280]{1,0:T(8,128)(2,1)} %get-tuple-element.1308), channel_id=1, source_target_pairs={{0,16},{1,17},{2,18},{3,19},{4,20},{5,21},{6,22},{7,23},{8,24},{9,... | collective-permute-start | bytes 2949128 | tf_op jit(solution)/shard_map/ppermute | solution.py:476
  274.7 62.0 %copy-start.41 = (s32[2]{0:T(128)S(1)}, s32[2]{0:T(128)}, u32[]{:S(2)}) copy-start(s32[2]{0:T(128)} %param.28) | copy-start | bytes 28
  276.4 28.6 %copy-start.2 = (bf16[384,1280]{1,0:T(8,128)(2,1)}, bf16[384,1280]{1,0:T(8,128)(2,1)S(1)}, u32[]{:S(2)}) copy-start(bf16[384,1280]{1,0:T(8,128)(2,1)S(1)} %get-tuple-element.1164) | copy-start | bytes 2949124 | tf_op jit(solution)/shard_map/cond
  277.3 9.5 copy-start.11
  301.3 3.7 copy-start.34
  310.9 15.0 %slice-start.4 = ((s8[13107200]{0:T(1024)(128)(4,1)}), s8[4194304]{0:T(1024)(128)(4,1)S(1)}, s32[]{:S(2)}) async-start(s8[13107200]{0:T(1024)(128)(4,1)} %bitcast.276), calls=%async_computation.4 | async-start | bytes 8388608 | tf_op jit(solution)/shard_map/cond
  313.0 12.8 %copy-start.7 = (bf16[384,1280]{1,0:T(8,128)(2,1)}, bf16[384,1280]{1,0:T(8,128)(2,1)S(1)}, u32[]{:S(2)}) copy-start(bf16[384,1280]{1,0:T(8,128)(2,1)S(1)} %add_convert_fusion.1) | copy-start | bytes 2949124 | tf_op jit(solution)/shard_map/cond
  313.0 12.8 %slice-start.5 = ((s8[13107200]{0:T(1024)(128)(4,1)}), s8[4194304]{0:T(1024)(128)(4,1)S(1)}, s32[]{:S(2)}) async-start(s8[13107200]{0:T(1024)(128)(4,1)} %bitcast.276), calls=%async_computation.5 | async-start | bytes 8388608 | tf_op jit(solution)/shard_map/cond
  313.0 12.8 %slice-start.6 = ((s8[13107200]{0:T(1024)(128)(4,1)}), s8[4194304]{0:T(1024)(128)(4,1)S(1)}, s32[]{:S(2)}) async-start(s8[13107200]{0:T(1024)(128)(4,1)} %bitcast.276), calls=%async_computation.6 | async-start | bytes 8388608 | tf_op jit(solution)/shard_map/cond
  313.0 12.8 %slice-start.7 = ((s8[13107200]{0:T(1024)(128)(4,1)}), s8[524288]{0:T(1024)(128)(4,1)S(1)}, s32[]{:S(2)}) async-start(s8[13107200]{0:T(1024)(128)(4,1)} %bitcast.276), calls=%async_computation.7 | async-start | bytes 1048576 | tf_op jit(solution)/shard_map/cond
  325.9 8.3 copy-start.3
  325.9 8.3 copy-start.12
  335.4 39.0 %collective-permute-start = (bf16[384,1280]{1,0:T(8,128)(2,1)}, bf16[384,1280]{1,0:T(8,128)(2,1)S(1)}, u32[]{:S(2)}, u32[]{:S(2)}) collective-permute-start(bf16[384,1280]{1,0:T(8,128)(2,1)} %get-tuple-element.1298), channel_id=1, source_target_pairs={{0,16},{1,17},{2,18},{3,19},{4,20},{5,21},{6,22},{7,23},{8,24},{9,... | collective-permute-start | bytes 2949128 | tf_op jit(solution)/shard_map/ppermute | solution.py:476
  373.0 106.1 %collective-permute-start.3 = (bf16[384,1280]{1,0:T(8,128)(2,1)}, bf16[384,1280]{1,0:T(8,128)(2,1)}, u32[]{:S(2)}, u32[]{:S(2)}) collective-permute-start(bf16[384,1280]{1,0:T(8,128)(2,1)} %get-tuple-element.1332), channel_id=1, source_target_pairs={{16,0},{17,1},{18,2},{19,3},{20,4},{21,5},{22,6},{23,7},{24,8},{25... | collective-permute-start | bytes 2949128 | tf_op jit(solution)/shard_map/ppermute | solution.py:476
  406.7 221.9 %collective-permute-start.2 = (bf16[384,1280]{1,0:T(8,128)(2,1)}, bf16[384,1280]{1,0:T(8,128)(2,1)}, u32[]{:S(2)}, u32[]{:S(2)}) collective-permute-start(bf16[384,1280]{1,0:T(8,128)(2,1)} %get-tuple-element.1320), channel_id=1, source_target_pairs={{16,0},{17,1},{18,2},{19,3},{20,4},{21,5},{22,6},{23,7},{24,8},{25... | collective-permute-start | bytes 2949128 | tf_op jit(solution)/shard_map/ppermute | solution.py:476
  526.7 4.6 copy-start.39
  548.4 6.4 copy-start.17
  560.3 9.2 copy-start.21
  632.9 3.8 copy-start.10
  634.8 5.3 copy-start.15
  673.7 4.6 copy-start.40
  695.1 6.4 copy-start.18
  706.9 9.2 copy-start.22
  734.6 9.5 copy-start.32
  983.4 4.5 copy-start.26
  983.4 5.5 copy-start.31
  (8 other events, 17.2 us)

commit v2 on v1

v2 whole, which is shorter than its diff:
```python
import functools
import math

import jax
import jax.numpy as jnp
from jax import lax
from jax.experimental import pallas as pl
from jax.experimental.pallas import tpu as pltpu
from jax.sharding import PartitionSpec as P

HEAD_DIM = 64
MESH = pl.DeviceIdType.MESH
LOW = jnp.bfloat16
F32 = jnp.float32


def ring_chip(position, chips):
    position = lax.rem(position + 2 * chips, chips)
    half = chips // 2
    return jnp.where(position < half, 2 * position, 2 * (chips - 1 - position) + 1)


def ring_place(chips):
    me = lax.axis_index("dp")
    core = lax.rem(me, 2)
    chip = me // 2
    position = jnp.where(lax.rem(chip, 2) == 0, chip // 2, chips - 1 - chip // 2)
    right = ring_chip(position + 1, chips) * 2 + core
    left = ring_chip(position - 1, chips) * 2 + core
    return (me, core, position, right, left, me + 1 - 2 * core)


def greet(devices):
    barrier = pltpu.get_barrier_semaphore()
    for device in devices:
        pl.semaphore_signal(barrier, inc=1, device_id={"dp": device}, device_id_type=MESH)
    pl.semaphore_wait(barrier, len(devices))


def gather_kernel(chips, arrays, items, *refs):
    count = len(items)
    ring_send, ring_recv, pair_send, pair_recv, own_sem = refs[2 * arrays :]
    shards = [refs[array].at[pl.ds(start, rows)] for array, start, rows, _ in items]
    splits = [way for _, _, _, way in items]
    half = chips // 2
    me, core, position, right, left, sibling = ring_place(chips)
    greet((left, right, sibling))

    def out(item, block):
        array, start, rows, _ = items[item]
        return refs[arrays + array].at[block, pl.ds(start, rows)]

    def owner(step, way):
        return ring_chip(position - step if way == 0 else position + step, chips) * 2 + core

    def travels(item, way, step):
        return step < half or (step == half and splits[item] == way)

    def ring_copy(item, way, step):
        block = owner(step - 1, way)
        return pltpu.make_async_remote_copy(
            src_ref=shards[item] if step == 1 else out(item, block),
            dst_ref=out(item, block),
            send_sem=ring_send.at[item, way, step - 1],
            recv_sem=ring_recv.at[item, way, step - 1],
            device_id={"dp": right if way == 0 else left},
            device_id_type=MESH,
        )

    def pair_copy(item, offset, block, source):
        return pltpu.make_async_remote_copy(
            src_ref=source,
            dst_ref=out(item, block),
            send_sem=pair_send.at[item, offset],
            recv_sem=pair_recv.at[item, offset],
            device_id={"dp": sibling},
            device_id_type=MESH,
        )

    sent, paired, kept = ([], [], [])
    for item in range(count):
        for way in (0, 1):
            if travels(item, way, 1):
                sent.append(ring_copy(item, way, 1))
                sent[-1].start()
    for item in range(count):
        paired.append(pair_copy(item, 0, me, shards[item]))
        paired[-1].start()
        kept.append(pltpu.make_async_copy(shards[item], out(item, me), own_sem.at[item]))
        kept[-1].start()
    for step in range(1, half + 1):
        for item in range(count):
            for way in (0, 1):
                if not travels(item, way, step):
                    continue
                ring_copy(item, way, step).wait_recv()
                if travels(item, way, step + 1):
                    sent.append(ring_copy(item, way, step + 1))
                    sent[-1].start()
                block = owner(step, way)
                offset = step if way == 0 else chips - step
                paired.append(pair_copy(item, offset, block, out(item, block)))
                paired[-1].start()
    for copy in sent:
        copy.wait_send()
    for copy in paired:
        copy.wait()
    for copy in kept:
        copy.wait()


def gather(shards, items, count):
    chips = count // 2
    arrays, pieces = (len(shards), len(items))
    return pl.pallas_call(
        functools.partial(gather_kernel, chips, arrays, items),
        out_shape=[jax.ShapeDtypeStruct((count,) + shard.shape, shard.dtype) for shard in shards],
        in_specs=[pl.BlockSpec(memory_space=pl.ANY)] * arrays,
        out_specs=[pl.BlockSpec(memory_space=pl.ANY)] * arrays,
        scratch_shapes=[
            pltpu.SemaphoreType.DMA((pieces, 2, chips // 2)),
            pltpu.SemaphoreType.DMA((pieces, 2, chips // 2)),
            pltpu.SemaphoreType.DMA((pieces, chips)),
            pltpu.SemaphoreType.DMA((pieces, chips)),
            pltpu.SemaphoreType.DMA((pieces,)),
        ],
        compiler_params=pltpu.CompilerParams(collective_id=0, has_side_effects=True),
    )(*shards)


def scatter_kernel(chips, arrays, items, *refs):
    count = len(items)
    parts, outs, refs = (refs[:arrays], refs[arrays : 2 * arrays], refs[2 * arrays :])
    landed, paired, mine = (refs[:count], refs[count : 2 * count], refs[2 * count : 3 * count])
    ring_send, ring_recv, pair_send, pair_recv, mine_sem = refs[3 * count :]
    splits = [way for _, _, _, way in items]
    half = chips // 2
    me, core, position, right, left, sibling = ring_place(chips)
    greet((left, right, sibling))

    def part(item, block):
        array, start, rows, _ = items[item]
        return parts[array].at[block, pl.ds(start, rows)]

    def first(item, way):
        return 1 if splits[item] == way else 2

    def slot(item, way, step):
        return step - 1 if splits[item] == way else half + step - 2

    def offset_of(step, way):
        return half - step + 1 if way == 0 else chips - (half - step + 1)

    def pair_copy(item, offset):
        block = ring_chip(position + offset, chips) * 2 + 1 - core
        return pltpu.make_async_remote_copy(
            src_ref=part(item, block),
            dst_ref=paired[item].at[offset],
            send_sem=pair_send.at[item, offset],
            recv_sem=pair_recv.at[item, offset],
            device_id={"dp": sibling},
            device_id_type=MESH,
        )

    def ring_copy(item, way, step):
        if step == first(item, way):
            source = paired[item].at[offset_of(step, way)]
        else:
            source = landed[item].at[slot(item, way, step - 1)]
        here = slot(item, way, step)
        return pltpu.make_async_remote_copy(
            src_ref=source,
            dst_ref=landed[item].at[here],
            send_sem=ring_send.at[item, here],
            recv_sem=ring_recv.at[item, here],
            device_id={"dp": right if way == 0 else left},
            device_id_type=MESH,
        )

    def load(item, offset, buffer):
        block = ring_chip(position + offset, chips) * 2 + core
        return pltpu.make_async_copy(part(item, block), mine[item].at[buffer], mine_sem.at[item, buffer])

    plan, uses = ([], [0] * count)
    for step in range(1, half + 2):
        for item in range(count):
            for way in (0, 1):
                if step <= half and step >= first(item, way):
                    plan.append((step, item, way, offset_of(step, way), uses[item] % 2))
                    uses[item] += 1
            if step > half:
                plan.append((step, item, None, 0, uses[item] % 2))
                uses[item] += 1
    for step, item, way, offset, buffer in plan:
        pair_copy(item, offset).start()
    load(plan[0][1], plan[0][3], plan[0][4]).start()
    sent = []
    for number, (step, item, way, offset, buffer) in enumerate(plan):
        if number + 1 < len(plan):
            load(plan[number + 1][1], plan[number + 1][3], plan[number + 1][4]).start()
        load(item, offset, buffer).wait()
        pair_copy(item, offset).wait_recv()
        array, start, rows, _ = items[item]
        kind = parts[array].dtype
        chunk = 16 if rows % 16 == 0 else rows
        from_pair, from_mine, from_ring = (paired[item], mine[item], landed[item])
        if way is None:
            ring_copy(item, 0, half).wait_recv()
            ring_copy(item, 1, half).wait_recv()
            slot_a, slot_b = (slot(item, 0, half), slot(item, 1, half))

            @pl.loop(0, rows // chunk)
            def _(index):
                here = pl.ds(pl.multiple_of(index * chunk, chunk), chunk)
                outs[array][pl.ds(pl.multiple_of(start + index * chunk, chunk), chunk), :] = (
                    from_ring[slot_a, here, :].astype(F32) + from_ring[slot_b, here, :].astype(F32)
                ) + (from_mine[buffer, here, :].astype(F32) + from_pair[offset, here, :].astype(F32))

            continue
        if step == first(item, way):

            @pl.loop(0, rows // chunk)
            def _(index):
                here = pl.ds(pl.multiple_of(index * chunk, chunk), chunk)
                from_pair[offset, here, :] = (
                    from_mine[buffer, here, :].astype(F32) + from_pair[offset, here, :].astype(F32)
                ).astype(kind)

        else:
            ring_copy(item, way, step - 1).wait_recv()
            arrived = slot(item, way, step - 1)

            @pl.loop(0, rows // chunk)
            def _(index):
                here = pl.ds(pl.multiple_of(index * chunk, chunk), chunk)
                from_ring[arrived, here, :] = (
                    from_ring[arrived, here, :].astype(F32)
                    + (from_mine[buffer, here, :].astype(F32) + from_pair[offset, here, :].astype(F32))
                ).astype(kind)

        sent.append(ring_copy(item, way, step))
        sent[-1].start()
    for copy in sent:
        copy.wait_send()
    for step, item, way, offset, buffer in plan:
        pair_copy(item, offset).wait_send()


def scatter(parts, items, count):
    chips = count // 2
    arrays, pieces = (len(parts), len(items))
    shapes = [(rows,) + parts[array].shape[2:] for array, _, rows, _ in items]
    kinds = [parts[array].dtype for array, _, _, _ in items]
    return pl.pallas_call(
        functools.partial(scatter_kernel, chips, arrays, items),
        out_shape=[jax.ShapeDtypeStruct(part.shape[1:], F32) for part in parts],
        in_specs=[pl.BlockSpec(memory_space=pl.ANY)] * arrays,
        out_specs=[pl.BlockSpec(memory_space=pltpu.VMEM)] * arrays,
        scratch_shapes=[pltpu.VMEM((chips - 1,) + shape, kind) for shape, kind in zip(shapes, kinds)]
        + [pltpu.VMEM((chips,) + shape, kind) for shape, kind in zip(shapes, kinds)]
        + [pltpu.VMEM((2,) + shape, kind) for shape, kind in zip(shapes, kinds)]
        + [
            pltpu.SemaphoreType.DMA((pieces, chips - 1)),
            pltpu.SemaphoreType.DMA((pieces, chips - 1)),
            pltpu.SemaphoreType.DMA((pieces, chips)),
            pltpu.SemaphoreType.DMA((pieces, chips)),
            pltpu.SemaphoreType.DMA((pieces, 2)),
        ],
        compiler_params=pltpu.CompilerParams(
            collective_id=1, has_side_effects=True, vmem_limit_bytes=62 * 2**20
        ),
    )(*parts)


def block_shape(rows, columns):
    return (rows, columns) if rows % 16 == 0 else (rows * columns // 128, 128)


def small_pack(gains, shifts, bias, count):
    width = gains.shape[1] // count
    ups = bias.shape[0] // gains.shape[1]
    rows = [
        gains.reshape(2, count, width).swapaxes(0, 1),
        shifts.reshape(6, count, width).swapaxes(0, 1),
        bias.reshape(count, ups, width),
    ]
    blank = jnp.zeros((count, 8 - ups, width), gains.dtype)
    return jnp.concatenate(rows + [blank], axis=1)


def small_split(blocks, ups):
    count, _, width = blocks.shape
    gains = blocks[:, 0:2].swapaxes(0, 1).reshape(2, count * width)
    shifts = blocks[:, 2:8].swapaxes(0, 1).reshape(6, count * width)
    bias = blocks[:, 8 : 8 + ups].reshape(count * ups * width)
    return (gains, shifts, bias)


def row_norm(rows_in):
    center = rows_in - jnp.mean(rows_in, axis=-1, keepdims=True)
    inverse = lax.rsqrt(jnp.mean(center * center, axis=-1, keepdims=True) + 1e-05)
    return (center * inverse, inverse)


def norm_back(grad_rows, normed, inverse):
    return inverse * (
        grad_rows
        - jnp.mean(grad_rows, axis=-1, keepdims=True)
        - normed * jnp.mean(grad_rows * normed, axis=-1, keepdims=True)
    )


def gelu_parts(hidden):
    size = jnp.abs(hidden)
    turn = 1.0 / (1.0 + (0.3275911 / math.sqrt(2.0)) * size)
    bell = jnp.exp(-0.5 * hidden * hidden)
    series = turn * (
        0.5 * 0.254829592
        + turn
        * (
            0.5 * -0.284496736
            + turn * (0.5 * 1.421413741 + turn * (0.5 * -1.453152027 + turn * (0.5 * 1.061405429)))
        )
    )
    tail = series * bell
    cumulative = jnp.where(hidden < 0.0, tail, 1.0 - tail)
    slope = cumulative + hidden * bell * (1.0 / math.sqrt(2.0 * math.pi))
    return (hidden * cumulative, slope)


def dot(left, right):
    return lax.dot_general(left, right, (((1,), (0,)), ((), ())), preferred_element_type=F32)


def dot_right(left, right):
    return lax.dot_general(left, right, (((1,), (1,)), ((), ())), preferred_element_type=F32)


def dot_left(left, right):
    return lax.dot_general(left, right, (((0,), (0,)), ((), ())), preferred_element_type=F32)


class Stream:
    def __init__(self, blocks, buffers, sems):
        self.blocks, self.buffers, self.sems = (blocks, buffers, sems)
        self.depth = buffers.shape[0]
        self.started = 0
        for _ in range(min(self.depth, len(blocks))):
            self.start()

    def copy(self, number):
        slot = number % self.depth
        return pltpu.make_async_copy(self.blocks[number], self.buffers.at[slot], self.sems.at[slot])

    def start(self):
        self.copy(self.started).start()
        self.started += 1

    def take(self, number):
        self.copy(number).wait()
        return self.buffers.at[number % self.depth]

    def release(self):
        if self.started < len(self.blocks):
            self.start()


def weight_blocks(w_qkv, w_out, w_up, w_down):
    width = w_out.shape[0]
    def cut(ref, axis, number):
        window = pl.ds(number * width, width)
        return ref.at[:, window] if axis else ref.at[window, :]
    heads = [cut(w_qkv, 1, number) for number in range(3)]
    ups = [cut(w_up, 1, number) for number in range(w_up.shape[1] // width)]
    downs = [cut(w_down, 0, number) for number in range(w_down.shape[0] // width)]
    return (heads, w_out, ups, downs)


def attend(packed, mixed, width):
    length = packed.shape[0]
    side = lax.broadcasted_iota(jnp.int32, (length, 128), 1) < HEAD_DIM

    @pl.loop(0, width // 128)
    def _(pair):
        start = pl.multiple_of(pair * 128, 128)
        queries = packed[:, pl.ds(start, 128)] * jnp.asarray(1.0 / math.sqrt(HEAD_DIM), LOW)
        keys = packed[:, pl.ds(start + width, 128)]
        values = packed[:, pl.ds(start + 2 * width, 128)]
        blank = jnp.zeros_like(queries)
        parts = []
        for head in (0, 1):
            mine = jnp.where(side, queries, blank) if head == 0 else jnp.where(side, blank, queries)
            scores = dot_right(mine, keys)
            shifted = jnp.exp(scores - jnp.max(scores, axis=-1, keepdims=True))
            total = jnp.sum(shifted, axis=-1, keepdims=True)
            parts.append(dot(shifted.astype(LOW), values) * (1.0 / total))
        mixed[:, pl.ds(start, 128)] = jnp.where(side, parts[0], parts[1]).astype(LOW)


def attend_back(packed, grad_mixed, grad_packed, width):
    length = packed.shape[0]
    side = lax.broadcasted_iota(jnp.int32, (length, 128), 1) < HEAD_DIM
    scale = 1.0 / math.sqrt(HEAD_DIM)

    @pl.loop(0, width // 128)
    def _(pair):
        start = pl.multiple_of(pair * 128, 128)
        queries = packed[:, pl.ds(start, 128)]
        keys = packed[:, pl.ds(start + width, 128)]
        values = packed[:, pl.ds(start + 2 * width, 128)]
        grads = grad_mixed[:, pl.ds(start, 128)]
        blank = jnp.zeros_like(queries)
        scaled = keys * jnp.asarray(scale, LOW)
        parts = []
        for head in (0, 1):
            def mine(array):
                return jnp.where(side, array, blank) if head == 0 else jnp.where(side, blank, array)
            scores = dot_right(mine(scaled), queries)
            shifted = jnp.exp(scores - jnp.max(scores, axis=0, keepdims=True))
            probs = shifted * (1.0 / jnp.sum(shifted, axis=0, keepdims=True))
            grad_probs = dot_right(mine(values), grads)
            product = grad_probs * probs
            weighted = jnp.sum(product, axis=0, keepdims=True)
            grad_scores = (product - probs * weighted).astype(LOW)
            parts.append((dot_left(grad_scores, scaled), dot(grad_scores, queries) * scale, dot(probs.astype(LOW), grads)))
        for number in range(3):
            grad_packed[:, pl.ds(start + number * width, 128)] = jnp.where(
                side, parts[0][number], parts[1][number]
            ).astype(LOW)


def forward_kernel(cell, held, active, entry, gains, shifts, bias, w_qkv, w_out, w_up, w_down, *refs):
    sent_h = refs[held]
    out_h, lowered_h, packed_h, mixed_h, middle_h, second_h, active_h, slope_h = [
        ref.at[cell] for ref in refs[held + 1 : held + 9]
    ]
    (buffers, buffer_sems, save_sems, out_v, lowered_v, packed_v, mixed_v, middle_v) = refs[held + 9 : held + 17]
    (second_v, active_v, slope_v, hidden_v, total_v) = refs[held + 17 :]
    width = entry.shape[1]
    ups = w_up.shape[1] // width

    @pl.when(active[0] != 0)
    def _():
        heads, outer, up, down = weight_blocks(w_qkv, w_out, w_up, w_down)
        order = heads + [outer]
        place_up, place_down = ({}, {})
        for number in range(ups + 1):
            if number < ups:
                place_up[number] = len(order)
                order.append(up[number])
            if number > 0:
                place_down[number - 1] = len(order)
                order.append(down[number - 1])
        stream = Stream(order, buffers, buffer_sems)
        saves = []

        def save(source, target):
            saves.append(pltpu.make_async_copy(source, target, save_sems.at[len(saves)]))
            saves[-1].start()

        rows_in = entry[...].astype(F32)
        normed, _ = row_norm(rows_in)
        lowered_v[...] = (normed * gains[0:1, :] + shifts[0:1, :]).astype(LOW)
        save(lowered_v, lowered_h)
        for number in range(3):
            block = stream.take(number)
            window = pl.ds(number * width, width)
            part = dot(lowered_v[...], block[...])
            if number != 1:
                part = part + shifts[1 + number // 2 : 2 + number // 2, :]
            packed_v[:, window] = part.astype(LOW)
            stream.release()
        save(packed_v, packed_h)
        attend(packed_v, mixed_v, width)
        save(mixed_v, mixed_h)
        block = stream.take(3)
        middle = entry[...].astype(F32) + dot(mixed_v[...], block[...]) + shifts[3:4, :]
        middle_v[...] = middle
        stream.release()
        save(middle_v, middle_h)
        normed, _ = row_norm(middle_v[...])
        second_v[...] = (normed * gains[1:2, :] + shifts[4:5, :]).astype(LOW)
        save(second_v, second_h)
        for number in range(ups + 1):
            if number < ups:
                up_block = stream.take(place_up[number])
            if number > 0:
                down_block = stream.take(place_down[number - 1])
            if number < ups:
                hidden_v[number % 2] = dot(second_v[...], up_block[...]) + bias[0:1, pl.ds(number * width, width)]
            if number > 0:
                window = pl.ds((number - 1) * width, width)
                activated, slope = gelu_parts(hidden_v[(number - 1) % 2])
                active_v[:, window] = activated.astype(LOW)
                slope_v[:, window] = slope.astype(LOW)
                part = dot(active_v[:, window], down_block[...])
                if number == 1:
                    total_v[...] = part
                elif number < ups:
                    total_v[...] += part
                else:
                    out_v[...] = (middle_v[...] + (total_v[...] + part + shifts[5:6, :])).astype(LOW)
                save(active_v.at[:, window], active_h.at[:, window])
                save(slope_v.at[:, window], slope_h.at[:, window])
            if number < ups:
                stream.release()
            if number > 0:
                stream.release()
        save(out_v, sent_h)
        save(out_v, out_h)
        for copy in saves:
            copy.wait()


def forward_tick(active, entry, small, weights, kept, cell, cell_count):
    length, width = entry.shape
    deep = weights[2].shape[1]
    ups = deep // width
    shapes = [
        ((length, width), LOW),
        ((length, width), LOW),
        ((length, 3 * width), LOW),
        ((length, width), LOW),
        ((length, width), F32),
        ((length, width), LOW),
        ((length, deep), LOW),
        ((length, deep), LOW),
    ]
    outs = [jax.ShapeDtypeStruct(*shapes[0])] + [
        jax.ShapeDtypeStruct((cell_count,) + shape, kind) for shape, kind in shapes
    ]
    vmem, hbm = (pl.BlockSpec(memory_space=pltpu.VMEM), pl.BlockSpec(memory_space=pl.ANY))
    flops = 2 * length * width * (4 * width + 2 * deep) + 16 * length * length * width
    kept = () if kept is None else tuple(kept)
    held = len(kept)
    sent, *kept = pl.pallas_call(
        functools.partial(forward_kernel, cell, held),
        out_shape=outs,
        in_specs=[pl.BlockSpec(memory_space=pltpu.SMEM)] + [vmem] * 4 + [hbm] * (4 + held),
        out_specs=[hbm] * 9,
        input_output_aliases={9 + number: 1 + number for number in range(held)},
        scratch_shapes=[
            pltpu.VMEM((4, width, width), LOW),
            pltpu.SemaphoreType.DMA((4,)),
            pltpu.SemaphoreType.DMA((7 + 2 * ups,)),
        ]
        + [pltpu.VMEM(*shape) for shape in shapes]
        + [pltpu.VMEM((2, length, width), F32), pltpu.VMEM((length, width), F32)],
        compiler_params=pltpu.CompilerParams(vmem_limit_bytes=60 * 2**20),
        cost_estimate=pl.CostEstimate(
            flops=flops, bytes_accessed=2 * width * (4 * width + 2 * deep), transcendentals=0
        ),
    )(active, entry, *small, *weights, *kept)
    return (sent, kept)


def backward_kernel(cell, held, active, scale, grad, entry, gains, shifts, *refs):
    packed, middle, slope = [ref.at[cell] for ref in refs[:3]]
    w_qkv, w_out, w_up, w_down = refs[3:7]
    refs = refs[7 + held :]
    sent_h = refs[0]
    rows_h, packed_h, branch_h, inner_h, low_h, sums_h = [ref.at[cell] for ref in refs[1:7]]
    (buffers, buffer_sems, load_sems, save_sems, rows_v, grad_packed_v, branch_v, inner_v, low_v, sums_v) = refs[7:17]
    (packed_v, middle_v, slope_v, mixed_v, grad_act_v, total_v, grad_middle_v) = refs[17:]
    length, width = entry.shape
    ups = w_up.shape[1] // width

    @pl.when(active[0] != 0)
    def _():
        heads, outer, up, down = weight_blocks(w_qkv, w_out, w_up, w_down)
        loads = [
            pltpu.make_async_copy(slope, slope_v, load_sems.at[0]),
            pltpu.make_async_copy(middle, middle_v, load_sems.at[1]),
            pltpu.make_async_copy(packed, packed_v, load_sems.at[2]),
        ]
        loads[0].start()
        order, place_up, place_down = ([], {}, {})
        for number in range(ups + 1):
            if number < ups:
                place_down[number] = len(order)
                order.append(down[number])
            if number > 0:
                place_up[number - 1] = len(order)
                order.append(up[number - 1])
        place_out = len(order)
        order = order + [outer] + heads
        stream = Stream(order, buffers, buffer_sems)
        loads[1].start()
        loads[2].start()
        saves = []

        def save(source, target):
            saves.append(pltpu.make_async_copy(source, target, save_sems.at[len(saves)]))
            saves[-1].start()

        def column_sum(array):
            return jnp.sum(array.astype(F32), axis=0, keepdims=True)

        low_v[...] = (grad[...].astype(F32) * scale[0]).astype(LOW)
        save(low_v, low_h)
        sums_v[7:8, :] = column_sum(low_v[...])
        loads[0].wait()
        for number in range(ups + 1):
            if number < ups:
                down_block = stream.take(place_down[number])
            if number > 0:
                up_block = stream.take(place_up[number - 1])
            if number < ups:
                grad_act_v[number % 2] = dot_right(low_v[...], down_block[...])
            if number > 0:
                window = pl.ds((number - 1) * width, width)
                inner = (grad_act_v[(number - 1) % 2] * slope_v[:, window].astype(F32)).astype(LOW)
                inner_v[:, window] = inner
                sums_v[7 + number : 8 + number, :] = column_sum(inner)
                part = dot_right(inner, up_block[...])
                if number == 1:
                    total_v[...] = part
                else:
                    total_v[...] += part
                save(inner_v.at[:, window], inner_h.at[:, window])
            if number < ups:
                stream.release()
            if number > 0:
                stream.release()
        loads[1].wait()
        normed, inverse = row_norm(middle_v[...])
        grad_second = total_v[...]
        sums_v[1:2, :] = column_sum(grad_second * normed)
        sums_v[6:7, :] = column_sum(grad_second)
        grad_middle = grad[...].astype(F32) * scale[0] + norm_back(grad_second * gains[1:2, :], normed, inverse)
        grad_middle_v[...] = grad_middle
        branch_v[...] = grad_middle.astype(LOW)
        sums_v[5:6, :] = column_sum(branch_v[...])
        save(branch_v, branch_h)
        block = stream.take(place_out)
        mixed_v[...] = dot_right(branch_v[...], block[...]).astype(LOW)
        stream.release()
        loads[2].wait()
        attend_back(packed_v, mixed_v, grad_packed_v, width)
        save(grad_packed_v, packed_h)
        sums_v[3:4, :] = column_sum(grad_packed_v[:, pl.ds(0, width)])
        sums_v[4:5, :] = column_sum(grad_packed_v[:, pl.ds(2 * width, width)])
        for number in range(3):
            block = stream.take(place_out + 1 + number)
            part = dot_right(grad_packed_v[:, pl.ds(number * width, width)], block[...])
            if number == 0:
                total_v[...] = part
            else:
                total_v[...] += part
            stream.release()
        normed, inverse = row_norm(entry[...].astype(F32))
        grad_lowered = total_v[...]
        sums_v[0:1, :] = column_sum(grad_lowered * normed)
        sums_v[2:3, :] = column_sum(grad_lowered)
        rows_v[...] = (grad_middle_v[...] + norm_back(grad_lowered * gains[0:1, :], normed, inverse)).astype(LOW)
        save(sums_v, sums_h)
        save(rows_v, sent_h)
        save(rows_v, rows_h)
        for copy in saves:
            copy.wait()


def backward_tick(active, incoming, entry, small, saved, weights, kept, cell, cell_count):
    length, width = entry.shape
    deep = weights[2].shape[1]
    ups = deep // width
    shapes = [
        ((length, width), LOW),
        ((length, 3 * width), LOW),
        ((length, width), LOW),
        ((length, deep), LOW),
        ((length, width), LOW),
        ((16, width), F32),
    ]
    outs = [jax.ShapeDtypeStruct(*shapes[0])] + [
        jax.ShapeDtypeStruct((cell_count,) + shape, kind) for shape, kind in shapes
    ]
    vmem, hbm = (pl.BlockSpec(memory_space=pltpu.VMEM), pl.BlockSpec(memory_space=pl.ANY))
    smem = pl.BlockSpec(memory_space=pltpu.SMEM)
    flops = 2 * length * width * (4 * width + 2 * deep) + 40 * length * length * width
    kept = () if kept is None else tuple(kept)
    held = len(kept)
    grad, scale = incoming
    sent, *kept = pl.pallas_call(
        functools.partial(backward_kernel, cell, held),
        out_shape=outs,
        in_specs=[smem] * 2 + [vmem] * 4 + [hbm] * (7 + held),
        out_specs=[hbm] * 7,
        input_output_aliases={13 + number: 1 + number for number in range(held)},
        scratch_shapes=[
            pltpu.VMEM((4, width, width), LOW),
            pltpu.SemaphoreType.DMA((4,)),
            pltpu.SemaphoreType.DMA((3,)),
            pltpu.SemaphoreType.DMA((6 + ups,)),
        ]
        + [pltpu.VMEM(*shape) for shape in shapes]
        + [
            pltpu.VMEM((length, 3 * width), LOW),
            pltpu.VMEM((length, width), F32),
            pltpu.VMEM((length, deep), LOW),
            pltpu.VMEM((length, width), LOW),
            pltpu.VMEM((2, length, width), F32),
            pltpu.VMEM((length, width), F32),
            pltpu.VMEM((length, width), F32),
        ],
        compiler_params=pltpu.CompilerParams(vmem_limit_bytes=60 * 2**20),
        cost_estimate=pl.CostEstimate(
            flops=flops, bytes_accessed=2 * width * (4 * width + 2 * deep), transcendentals=0
        ),
    )(active, scale, grad, entry, *small[:2], *saved, *weights, *kept)
    return (sent, kept)


def on_device(inputs, out_grad, query_counts, gains, shifts, w_qkv, w_out, w_up, b_up, w_down):
    stage = lax.axis_index("pipe")
    stages = lax.axis_size("pipe")
    count = lax.axis_size("dp")
    cell_count, length, width = inputs.shape
    own = width // count
    ups = b_up.shape[1] // own
    deep = ups * width
    deep_own = w_down.shape[1]
    shapes = [
        block_shape(own, 3 * width),
        block_shape(own, width),
        block_shape(own, deep),
        block_shape(deep_own, width),
    ]
    cut = (shapes[3][0] // 2 + 15) // 16 * 16
    items = (
        (0, 0, 16, 0),
        (1, 0, shapes[0][0], 0),
        (2, 0, shapes[1][0], 0),
        (3, 0, shapes[2][0], 1),
        (4, 0, cut, 0),
        (4, cut, shapes[3][0] - cut, 1),
    )
    shards = [small_pack(gains[0], shifts[0], b_up[0], 1)[0]] + [
        array[0].reshape(shape) for array, shape in zip((w_qkv, w_out, w_up, w_down), shapes)
    ]
    packs = gather(shards, items, count)
    gain_rows, shift_rows, bias = small_split(packs[0].astype(F32), ups)
    small = (gain_rows, shift_rows, bias[None])
    weights = (
        packs[1].reshape(width, 3 * width),
        packs[2].reshape(width, width),
        packs[3].reshape(width, deep),
        packs[4].reshape(deep, width),
    )
    scales = jnp.sqrt(query_counts.astype(F32) / 500.0)

    def along(value, steps):
        pairs = [(source, source + steps) for source in range(stages) if 0 <= source + steps < stages]
        return lax.ppermute(value, "pipe", pairs)

    entries, kept = ([[inputs[cell] for cell in range(cell_count)]], None)
    for turn in range(stages):
        active = (stage == turn).astype(jnp.int32)[None]
        arrived = []
        for cell in range(cell_count):
            sent, kept = forward_tick(active, entries[turn][cell], small, weights, kept, cell, cell_count)
            if turn + 1 < stages:
                arrived.append(along(sent, 1))
        entries.append(arrived)
    section_out, lowered, packed, mixed, middle, second, activated, slope = kept
    incoming = [(out_grad[cell], scales[cell][None]) for cell in range(cell_count)]
    back = None
    for turn in range(stages - 1, -1, -1):
        active = (stage == turn).astype(jnp.int32)[None]
        arrived = []
        for cell in range(cell_count):
            sent, back = backward_tick(
                active, incoming[cell], entries[turn][cell], small, (packed, middle, slope), weights, back, cell, cell_count
            )
            if turn > 0:
                arrived.append((along(sent, -1), jnp.ones((1,), F32)))
        incoming = arrived
    input_grads, grad_packed, grad_branch, grad_inner, grad_ff, sums = back
    sums = jnp.sum(sums, axis=0)

    def product(left, right):
        return dot_left(left.reshape(cell_count * length, -1), right.reshape(cell_count * length, -1)).astype(LOW)

    parts = [
        small_pack(sums[0:2], sums[2:8], sums[8 : 8 + ups].reshape(deep), count),
        product(lowered, grad_packed).reshape((count,) + shapes[0]),
        product(mixed, grad_branch).reshape((count,) + shapes[1]),
        product(second, grad_inner).reshape((count,) + shapes[2]),
        product(activated, grad_ff).reshape((count,) + shapes[3]),
    ]
    shares = scatter(parts, items, count)
    grad_gains, grad_shifts, grad_bias = small_split(shares[0][None], ups)
    return (
        section_out[None],
        input_grads[None],
        grad_gains[None],
        grad_shifts[None],
        shares[1].reshape(1, own, 3 * width),
        shares[2].reshape(1, own, width),
        shares[3].reshape(1, own, deep),
        grad_bias[None],
        shares[4].reshape(1, deep_own, width),
    )


def solution(mesh):
    in_specs = (
        P("dp", None, None),
        P("dp", None, None),
        P("dp"),
        P("pipe", None, "dp"),
        P("pipe", None, "dp"),
        P("pipe", "dp", None),
        P("pipe", "dp", None),
        P("pipe", "dp", None),
        P("pipe", "dp"),
        P("pipe", "dp", None),
    )
    out_specs = (
        P("pipe", "dp", None, None),
        P("pipe", "dp", None, None),
        P("pipe", None, "dp"),
        P("pipe", None, "dp"),
        P("pipe", "dp", None),
        P("pipe", "dp", None),
        P("pipe", "dp", None),
        P("pipe", "dp"),
        P("pipe", "dp", None),
    )
    return jax.shard_map(
        on_device, mesh=mesh, in_specs=in_specs, out_specs=out_specs, check_vma=False
    )
```

time: 1000 us -> 762 us (0.76)
  Pallas kernels: 390 us -> 597 us
  matrix products: 233 us -> 44 us
  local copies, waits for them, and re-layouts: 115 us -> 19.8 us
  other arithmetic: 77.7 us -> 4.72 us
  waiting for transfers between devices: 127 us -> 83.3 us
  loops' own time: 41.3 us -> 0 us
    pallas_call x2 -> x10, Pallas kernels: 390 us -> 597 us  [the longest x1 196 us: scatter(): pl.pallas_call(functools.partial(scatter_kernel, chips, arrays, items), o...]
    dot_general x34 -> x4, matrix products: 233 us -> 44 us  [dot_left(): lax.dot_general(left, right, (((0,), (0,)), ((), ())), preferred_element_...]
    ppermute x4, waiting for transfers between devices: 127 us -> 83.3 us  [along(): return lax.ppermute(value, 'pipe', pairs)]
    another operation x8 -> x0, loops' own time: 41.3 us -> none  [either(): return lax.cond(flag, lambda kept: run(), lambda kept: kept, keep)]
    another operation x48 -> x1, local copies, waits for them, and re-layouts: 39.5 us -> 0.72 us  [on_device(): small = (gain_rows, shift_rows, bias[None])]
    reduce_sum x18 -> x1, other arithmetic: 32.8 us -> 0.94 us  [on_device(): sums = jnp.sum(sums, axis=0)]
    slice x16 -> x4, local copies, waits for them, and re-layouts: 24.7 us -> 0.69 us  [the longest x1 0.67 us: on_device(): scales[cell][None]]
    convert_element_type x8 -> x1, other arithmetic: 24.3 us -> 0.85 us  [on_device(): gain_rows, shift_rows, bias = small_split(packs[0].astype(F32), ups)]
  transfers between devices with their start and end apart: 4 -> 4, of which waited for: 2 -> 3; matrix products, arithmetic and copies ran while one was open for 18% -> 0% of each run, Pallas kernels for 0% -> 13%
where the time goes in v2:
time: 762 us; the launch traced here: 756 us
  Pallas kernels  597 us (78%)
  waiting for transfers between devices  83.3 us (11%)
  matrix products  44 us (6%)
  local copies, waits for them, and re-layouts  19.8 us (3%)
    pallas_call x1, Pallas kernels, scatter(): pl.pallas_call(functools.partial(scatter_kernel, chips, arrays, items), o...  196 us
    pallas_call x1, Pallas kernels, gather(): pl.pallas_call(functools.partial(gather_kernel, chips, arrays, items), ou...  194 us
    pallas_call x4, Pallas kernels, backward_tick(): pl.pallas_call(functools.partial(backward_kernel, cell, held), out_shape=...  115 us
    pallas_call x4, Pallas kernels, forward_tick(): pl.pallas_call(functools.partial(forward_kernel, cell, held), out_shape=o...  91.7 us
    ppermute x4, waiting for transfers between devices, along(): return lax.ppermute(value, 'pipe', pairs)  83.3 us
    dot_general x4, matrix products, dot_left(): lax.dot_general(left, right, (((0,), (0,)), ((), ())), preferred_element_...  44 us
  transfers between devices with their start and end apart: 4, of which 3 were waited for; matrix products, arithmetic and copies ran while one was open for 0% of the time, Pallas kernels for 13%

profile of v2, /device:TPU:0, one launch (start us, length us, event | category | flops | bytes accessed | tf_op | source)
XLA Modules:
  0.0 755.9 jit_solution(9731306503565448773)
XLA Ops:
  1.7 1.4 maximum_bitcast_fusion.refs_0_
  3.0 194.0 %shard_map.169 = (bf16[16,16,80]{2,1,0:T(8,128)(2,1)}, bf16[16,80,3840]{2,1,0:T(8,128)(2,1)}, bf16[16,80,1280]{2,1,0:T(8,128)(2,1)}, bf16[16,80,5120]{2,1,0:T(8,128)(2,1)}, bf16[16,320,1280]{2,1,0:T(8,128)(2,1)}) custom-call(bf16[16,80]{1,0:T(8,128)(2,1)} %maximum_bitcast_fusion.refs_0_, bf16[80,3840]{1,0:T(8,128)(2,1)} %bitcast.101, ...), custom_call_target="tpu_custom_call" | custom-call | tf_op jit(solution)/shard_map/pallas_call | solution.py:115
  200.8 1.4 slice_bitcast_fusion.2
  202.2 37.8 %shard_map.170 = (bf16[384,1280]{1,0:T(8,128)(2,1)}, bf16[2,384,1280]{2,1,0:T(8,128)(2,1)}, bf16[2,384,1280]{2,1,0:T(8,128)(2,1)}, bf16[2,384,3840]{2,1,0:T(8,12...) custom-call(s32[1]{0:T(128)} %bitcast.1.active, ...), custom_call_target="tpu_custom_call" | custom-call | flops 18119393280 | bytes 39321600 | tf_op jit(solution)/shard_map/pallas_call | solution.py:536
  240.0 1.4 collective-permute-start.1
  241.4 37.3 %shard_map.171 = (bf16[384,1280]{1,0:T(8,128)(2,1)}, bf16[2,384,1280]{2,1,0:T(8,128)(2,1)}, bf16[2,384,1280]{2,1,0:T(8,128)(2,1)}, bf16[2,384,3840]{2,1,0:T(8,12...) custom-call(s32[1]{0:T(128)} %bitcast.1.active, ...), custom_call_target="tpu_custom_call", output_to_operand_aliasing={{1}: (9, {}), {2}: (10, {}), {3}: (11, {}), {4}: (12, {}), ... | custom-call | flops 18119393280 | bytes 39321600 | tf_op jit(solution)/shard_map/pallas_call | solution.py:536
  278.8 2.3 collective-permute-start
  282.4 1.4 slice_bitcast_fusion
  283.7 0.9 copy-done.7
  284.7 6.6 shard_map.172
  291.3 10.9 %collective-permute-done.entry = bf16[384,1280]{1,0:T(8,128)(2,1)} collective-permute-done((bf16[384,1280]{1,0:T(8,128)(2,1)}, bf16[384,1280]{1,0:T(8,128)(2,1)}, u32[]{:S(2)}, u32[]{:S(2)}) %collective-permute-start) | collective-permute-done | bytes 983072 | tf_op jit(solution)/shard_map/ppermute | solution.py:754
  302.2 9.9 %shard_map.173 = (bf16[384,1280]{1,0:T(8,128)(2,1)}, bf16[2,384,1280]{2,1,0:T(8,128)(2,1)}, bf16[2,384,1280]{2,1,0:T(8,128)(2,1)}, bf16[2,384,3840]{2,1,0:T(8,12...) custom-call(s32[1]{0:T(128)} %bitcast.active, ...), custom_call_target="tpu_custom_call", output_to_operand_aliasing={{1}: (9, {}), {2}: (10, {}), {3}: (11, {}), {4}: (12, {}), ... | custom-call | flops 18119393280 | bytes 39321600 | tf_op jit(solution)/shard_map/pallas_call | solution.py:536
  312.1 12.9 %shard_map.174 = (bf16[384,1280]{1,0:T(8,128)(2,1)}, bf16[2,384,1280]{2,1,0:T(8,128)(2,1)}, bf16[2,384,3840]{2,1,0:T(8,128)(2,1)}, bf16[2,384,1280]{2,1,0:T(8,12...) custom-call(s32[1]{0:T(128)} %bitcast.active, ...), custom_call_target="tpu_custom_call" | custom-call | flops 22649241600 | bytes 39321600 | tf_op jit(solution)/shard_map/pallas_call | solution.py:684
  325.0 1.3 collective-permute-start.3
  326.3 11.9 %shard_map.175 = (bf16[384,1280]{1,0:T(8,128)(2,1)}, bf16[2,384,1280]{2,1,0:T(8,128)(2,1)}, bf16[2,384,3840]{2,1,0:T(8,128)(2,1)}, bf16[2,384,1280]{2,1,0:T(8,12...) custom-call(s32[1]{0:T(128)} %bitcast.active, ...), custom_call_target="tpu_custom_call", output_to_operand_aliasing={{1}: (13, {}), {2}: (14, {}), {3}: (15, {}), {4}: (16, {}),... | custom-call | flops 22649241600 | bytes 39321600 | tf_op jit(solution)/shard_map/pallas_call | solution.py:684
  338.2 1.3 collective-permute-start.2
  339.5 71.3 %collective-permute-done.3.grad = bf16[384,1280]{1,0:T(8,128)(2,1)S(1)} collective-permute-done((bf16[384,1280]{1,0:T(8,128)(2,1)}, bf16[384,1280]{1,0:T(8,128)(2,1)S(1)}, u32[]{:S(2)}, u32[]{:S(2)}) %collective-permute-start.3) | collective-permute-done | bytes 983072 | tf_op jit(solution)/shard_map/ppermute | solution.py:754
  410.8 1.0 copy-done.11
  411.8 45.1 %shard_map.176 = (bf16[384,1280]{1,0:T(8,128)(2,1)}, bf16[2,384,1280]{2,1,0:T(8,128)(2,1)}, bf16[2,384,3840]{2,1,0:T(8,128)(2,1)}, bf16[2,384,1280]{2,1,0:T(8,12...) custom-call(s32[1]{0:T(128)} %bitcast.1.active, ...), custom_call_target="tpu_custom_call", output_to_operand_aliasing={{1}: (13, {}), {2}: (14, {}), {3}: (15, {}), {4}: (16, {}),... | custom-call | flops 22649241600 | bytes 39321600 | tf_op jit(solution)/shard_map/pallas_call | solution.py:684
  456.8 1.2 collective-permute-done.2.grad
  458.0 0.9 copy-done.10
  458.9 45.4 %shard_map.177 = (bf16[384,1280]{1,0:T(8,128)(2,1)}, bf16[2,384,1280]{2,1,0:T(8,128)(2,1)}, bf16[2,384,3840]{2,1,0:T(8,128)(2,1)}, bf16[2,384,1280]{2,1,0:T(8,12...) custom-call(s32[1]{0:T(128)} %bitcast.1.active, ...), custom_call_target="tpu_custom_call", output_to_operand_aliasing={{1}: (13, {}), {2}: (14, {}), {3}: (15, {}), {4}: (16, {}),... | custom-call | flops 22649241600 | bytes 39321600 | tf_op jit(solution)/shard_map/pallas_call | solution.py:684
  504.4 0.9 reduce_sum.9
  505.7 16.3 %bitcast_convert_fusion = bf16[5120,1280]{1,0:T(8,128)(2,1)} fusion(bf16[2,384,5120]{2,1,0:T(8,128)(2,1)} %get-tuple-element.142, bf16[2,384,1280]{2,1,0:T(8,128)(2,1)} %get-tuple-element.143), kind=kOutput, calls=%fused_computation | convolution fusion | flops 10072883200 | bytes 22937600 | tf_op jit(solution)/shard_map/dot_general | solution.py:340
  522.0 13.2 %bitcast_convert_fusion.1 = bf16[1280,5120]{1,0:T(8,128)(2,1)} fusion(bf16[2,384,1280]{2,1,0:T(8,128)(2,1)S(1)} %copy-done.2, bf16[2,384,5120]{2,1,0:T(8,128)(2,1)S(1)} %copy-done.13), kind=kOutput, calls=%fused_computation.1 | convolution fusion | flops 10072883200 | bytes 22937600 | tf_op jit(solution)/shard_map/dot_general | solution.py:340
  535.2 4.2 fusion
  539.4 10.3 %bitcast_convert_fusion.2 = bf16[1280,3840]{1,0:T(8,128)(2,1)} fusion(bf16[2,384,1280]{2,1,0:T(8,128)(2,1)S(1)} %copy-done, bf16[2,384,3840]{2,1,0:T(8,128)(2,1)S(1)} %copy-done.14), kind=kOutput, calls=%fused_computation.2 | convolution fusion | flops 7554662400 | bytes 17694720 | tf_op jit(solution)/shard_map/dot_general | solution.py:340
  550.5 195.7 %shard_map.178 = (f32[16,80]{1,0:T(8,128)}, f32[80,3840]{1,0:T(8,128)}, f32[80,1280]{1,0:T(8,128)}, f32[80,5120]{1,0:T(8,128)}, f32[320,1280]{1,0:T(8,128)}) custom-call(f32[16,16,80]{2,1,0:T(8,128)} %maximum_maximum_fusion.refs_0_, bf16[16,80,3840]{2,1,0:T(8,128)(2,1)} %bitcast.94, bf16[16,80,1280]{2,1,0:T(8,128)(2,1)} %bitcast.95, ...), custom_call_target="tpu_custom_call" | custom-call | tf_op jit(solution)/shard_map/pallas_call | solution.py:254
  747.7 1.2 slice.66
  750.2 2.4 copy.131
  753.4 1.2 copy.133
  754.5 1.2 copy.134
  (61 shorter events, 10.6 us)
Async XLA Ops:
  0.6 200.2 %copy-start.3 = (bf16[2,384,1280]{2,1,0:T(8,128)(2,1)S(1)}, bf16[2,384,1280]{2,1,0:T(8,128)(2,1)}, u32[]{:S(2)}) copy-start(bf16[2,384,1280]{2,1,0:T(8,128)(2,1)} %param.10) | copy-start | bytes 5898244
  240.0 43.7 %collective-permute-start.1 = (bf16[384,1280]{1,0:T(8,128)(2,1)}, bf16[384,1280]{1,0:T(8,128)(2,1)S(1)}, u32[]{:S(2)}, u32[]{:S(2)}) collective-permute-start(bf16[384,1280]{1,0:T(8,128)(2,1)} %get-tuple-element.93), channel_id=1, source_target_pairs={{0,16},{1,17},{2,18},{3,19},{4,20},{5,21},{6,22},{7,23},{8,24},{9,... | collective-permute-start | bytes 2949128 | tf_op jit(solution)/shard_map/ppermute | solution.py:754
  241.4 40.3 %copy-start.12 = (s32[2]{0:T(128)S(1)}, s32[2]{0:T(128)}, u32[]{:S(2)}) copy-start(s32[2]{0:T(128)} %param.12) | copy-start | bytes 28
  241.4 41.0 %copy-start.4 = (bf16[2,384,1280]{2,1,0:T(8,128)(2,1)S(1)}, bf16[2,384,1280]{2,1,0:T(8,128)(2,1)}, u32[]{:S(2)}) copy-start(bf16[2,384,1280]{2,1,0:T(8,128)(2,1)} %param.11) | copy-start | bytes 5898244
  278.8 23.4 %collective-permute-start = (bf16[384,1280]{1,0:T(8,128)(2,1)}, bf16[384,1280]{1,0:T(8,128)(2,1)}, u32[]{:S(2)}, u32[]{:S(2)}) collective-permute-start(bf16[384,1280]{1,0:T(8,128)(2,1)} %get-tuple-element.92), channel_id=1, source_target_pairs={{0,16},{1,17},{2,18},{3,19},{4,20},{5,21},{6,22},{7,23},{8,24},{9,... | collective-permute-start | bytes 2949128 | tf_op jit(solution)/shard_map/ppermute | solution.py:754
  283.7 0.9 copy-start.7
  325.0 85.8 %collective-permute-start.3 = (bf16[384,1280]{1,0:T(8,128)(2,1)}, bf16[384,1280]{1,0:T(8,128)(2,1)S(1)}, u32[]{:S(2)}, u32[]{:S(2)}) collective-permute-start(bf16[384,1280]{1,0:T(8,128)(2,1)} %get-tuple-element.121), channel_id=1, source_target_pairs={{16,0},{17,1},{18,2},{19,3},{20,4},{21,5},{22,6},{23,7},{24,8},{25... | collective-permute-start | bytes 2949128 | tf_op jit(solution)/shard_map/ppermute | solution.py:754
  338.2 119.8 %collective-permute-start.2 = (bf16[384,1280]{1,0:T(8,128)(2,1)}, bf16[384,1280]{1,0:T(8,128)(2,1)S(1)}, u32[]{:S(2)}, u32[]{:S(2)}) collective-permute-start(bf16[384,1280]{1,0:T(8,128)(2,1)} %get-tuple-element.120), channel_id=1, source_target_pairs={{16,0},{17,1},{18,2},{19,3},{20,4},{21,5},{22,6},{23,7},{24,8},{25... | collective-permute-start | bytes 2949128 | tf_op jit(solution)/shard_map/ppermute | solution.py:754
  410.8 1.0 copy-start.11
  458.0 0.9 copy-start.10
  505.7 16.3 %copy-start.2 = (bf16[2,384,1280]{2,1,0:T(8,128)(2,1)S(1)}, bf16[2,384,1280]{2,1,0:T(8,128)(2,1)}, u32[]{:S(2)}) copy-start(bf16[2,384,1280]{2,1,0:T(8,128)(2,1)} %get-tuple-element.140) | copy-start | bytes 5898244
  505.7 16.3 %copy-start.13 = (bf16[2,384,5120]{2,1,0:T(8,128)(2,1)S(1)}, bf16[2,384,5120]{2,1,0:T(8,128)(2,1)}, u32[]{:S(2)}) copy-start(bf16[2,384,5120]{2,1,0:T(8,128)(2,1)} %get-tuple-element.141) | copy-start | bytes 23592964
  522.0 13.2 %copy-start.1 = (bf16[2,384,1280]{2,1,0:T(8,128)(2,1)S(1)}, bf16[2,384,1280]{2,1,0:T(8,128)(2,1)}, u32[]{:S(2)}) copy-start(bf16[2,384,1280]{2,1,0:T(8,128)(2,1)} %get-tuple-element.138) | copy-start | bytes 5898244
  522.0 13.2 %copy-start.15 = (bf16[2,384,1280]{2,1,0:T(8,128)(2,1)S(1)}, bf16[2,384,1280]{2,1,0:T(8,128)(2,1)}, u32[]{:S(2)}) copy-start(bf16[2,384,1280]{2,1,0:T(8,128)(2,1)} %get-tuple-element.139) | copy-start | bytes 5898244
  535.2 4.2 copy-start
  535.2 4.2 copy-start.14
  539.4 10.3 %copy-start.9 = (f32[16]{0:T(128)S(1)}, f32[16]{0:T(128)}, u32[]{:S(2)}) copy-start(f32[16]{0:T(128)} %pad.3.clone) | copy-start | bytes 196
  746.2 6.4 copy-start.8
  746.2 7.1 copy-start.6
  752.6 1.9 copy-start.5

commit v3 on v2

--- a/solution.py
+++ b/solution.py
@@ -711,6 +711,363 @@
     return (sent, kept)
 
 
+def grads_kernel(chips, width, items, *refs):
+    count = len(items)
+    small_part, sides = (refs[0], refs[1:9])
+    outs, parts = (refs[9:14], [small_part] + list(refs[14:18]))
+    refs = refs[18:]
+    landed, paired, mine = (refs[:count], refs[count : 2 * count], refs[2 * count : 3 * count])
+    (big, cuts, stage, stage_down, final) = refs[3 * count : 3 * count + 5]
+    (ring_send, ring_recv, pair_send, pair_recv, mine_sem, big_sem, cut_sem, stage_sem, final_sem) = refs[3 * count + 5 :]
+    lowered, grad_packed, mixed, grad_branch, second, grad_inner, activated, grad_ff = sides
+    splits = [way for _, _, _, way in items]
+    half = chips // 2
+    devices = 2 * chips
+    own = width // devices
+    deep_own = activated.shape[1] // devices
+    cut = cuts.shape[2]
+    me, core, position, right, left, sibling = ring_place(chips)
+
+    def load_big(source, slot):
+        return pltpu.make_async_copy(source, big.at[slot], big_sem.at[slot])
+
+    def load_cut(source, index, slot):
+        window = pl.ds(pl.multiple_of(index * cut, cut), cut)
+        return pltpu.make_async_copy(source.at[:, window], cuts.at[slot], cut_sem.at[slot])
+
+    load_big(grad_ff, 0).start()
+    greet((left, right, sibling))
+
+    def part(item, block):
+        array, start, rows, _ = items[item]
+        return parts[array].at[block, pl.ds(start, rows)]
+
+    def first(item, way):
+        return 1 if splits[item] == way else 2
+
+    def slot_of(item, way, step):
+        return step - 1 if splits[item] == way else half + step - 2
+
+    def offset_of(step, way):
+        return half - step + 1 if way == 0 else chips - (half - step + 1)
+
+    def pair_copy(item, offset):
+        block = ring_chip(position + offset, chips) * 2 + 1 - core
+        return pltpu.make_async_remote_copy(
+            src_ref=part(item, block),
+            dst_ref=paired[item].at[offset],
+            send_sem=pair_send.at[item, offset],
+            recv_sem=pair_recv.at[item, offset],
+            device_id={"dp": sibling},
+            device_id_type=MESH,
+        )
+
+    def ring_copy(item, way, step):
+        if step == first(item, way):
+            source = paired[item].at[offset_of(step, way)]
+        else:
+            source = landed[item].at[slot_of(item, way, step - 1)]
+        here = slot_of(item, way, step)
+        return pltpu.make_async_remote_copy(
+            src_ref=source,
+            dst_ref=landed[item].at[here],
+            send_sem=ring_send.at[item, here],
+            recv_sem=ring_recv.at[item, here],
+            device_id={"dp": right if way == 0 else left},
+            device_id_type=MESH,
+        )
+
+    def load(item, offset, buffer):
+        block = ring_chip(position + offset, chips) * 2 + core
+        return pltpu.make_async_copy(part(item, block), mine[item].at[buffer], mine_sem.at[item, buffer])
+
+    def starts(wanted):
+        return [
+            (step, item, way, offset_of(step, way))
+            for step in (1, 2)
+            for item in wanted
+            for way in (0, 1)
+            if step == first(item, way)
+        ]
+
+    downs = [item for item in range(count) if items[item][0] == 4]
+    ups = [item for item in range(count) if items[item][0] == 3]
+    others = [item for item in range(count) if items[item][0] < 3]
+    every = downs + ups + others
+    rest = [
+        (step, item, way, offset_of(step, way))
+        for step in range(2, half + 1)
+        for item in every
+        for way in (0, 1)
+        if step > first(item, way)
+    ] + [(half + 1, item, None, 0) for item in every]
+    uses = [0] * count
+
+    def numbered(plan):
+        result = []
+        for entry in plan:
+            result.append(entry + (uses[entry[1]] % 2,))
+            uses[entry[1]] += 1
+        return result
+
+    finals = [0]
+
+    def fetch(entry):
+        load(entry[1], entry[3], entry[4]).start()
+
+    def work(entry):
+        step, item, way, offset, buffer = entry
+        array, start, rows, _ = items[item]
+        load(item, offset, buffer).wait()
+        pair_copy(item, offset).wait_recv()
+        kind = parts[array].dtype
+        columns = parts[array].shape[2]
+        chunk = 16
+        from_pair, from_mine, from_ring = (paired[item], mine[item], landed[item])
+        if way is None:
+            ring_copy(item, 0, half).wait_recv()
+            ring_copy(item, 1, half).wait_recv()
+            slot_a, slot_b = (slot_of(item, 0, half), slot_of(item, 1, half))
+            if array == 0:
+                outs[0][...] = (from_ring[slot_a] + from_ring[slot_b]) + (from_mine[buffer] + from_pair[offset])
+                return
+            high, wide = (min(rows, final.shape[1]), min(columns, final.shape[2]))
+            for top in range(0, rows, high):
+                for across in range(0, columns, wide):
+                    number = finals[0]
+                    finals[0] += 1
+                    turn = number % final.shape[0]
+                    if number >= final.shape[0]:
+                        final_copies[number - final.shape[0]].wait()
+                    span = pl.ds(across, wide)
+
+                    @pl.loop(0, high // chunk)
+                    def _(index):
+                        here = pl.ds(pl.multiple_of(top + index * chunk, chunk), chunk)
+                        final[turn, pl.ds(pl.multiple_of(index * chunk, chunk), chunk), pl.ds(0, wide)] = (
+                            from_ring[slot_a, here, span].astype(F32) + from_ring[slot_b, here, span].astype(F32)
+                        ) + (from_mine[buffer, here, span].astype(F32) + from_pair[offset, here, span].astype(F32))
+
+                    final_copies.append(
+                        pltpu.make_async_copy(
+                            final.at[turn, pl.ds(0, high), pl.ds(0, wide)],
+                            outs[array].at[pl.ds(start + top, high), span],
+                            final_sem.at[turn],
+                        )
+                    )
+                    final_copies[-1].start()
+            return
+        if step == first(item, way):
+
+            @pl.loop(0, rows // chunk)
+            def _(index):
+                here = pl.ds(pl.multiple_of(index * chunk, chunk), chunk)
+                from_pair[offset, here, :] = (
+                    from_mine[buffer, here, :].astype(F32) + from_pair[offset, here, :].astype(F32)
+                ).astype(kind)
+
+        else:
+            ring_copy(item, way, step - 1).wait_recv()
+            arrived = slot_of(item, way, step - 1)
+
+            @pl.loop(0, rows // chunk)
+            def _(index):
+                here = pl.ds(pl.multiple_of(index * chunk, chunk), chunk)
+                from_ring[arrived, here, :] = (
+                    from_ring[arrived, here, :].astype(F32)
+                    + (from_mine[buffer, here, :].astype(F32) + from_pair[offset, here, :].astype(F32))
+                ).astype(kind)
+
+        sent.append(ring_copy(item, way, step))
+        sent[-1].start()
+
+    def run(plan):
+        plan = numbered(plan)
+        if plan:
+            fetch(plan[0])
+        for number, entry in enumerate(plan):
+            if number + 1 < len(plan):
+                fetch(plan[number + 1])
+            work(entry)
+
+    sent, final_copies = ([], [])
+    def farthest_first(index):
+        step = index // 2
+        return ring_chip(position + jnp.where(lax.rem(index, 2) == 0, half - step, half + step + 1), chips)
+
+    def keep_down(index):
+        return pltpu.make_async_copy(
+            stage_down.at[lax.rem(index, 2)],
+            parts[4].at[pl.ds(farthest_first(index) * 2, 2)],
+            stage_sem.at[lax.rem(index, 2)],
+        )
+
+    def cut_down(index):
+        return load_cut(activated, farthest_first(index), lax.rem(index, 2))
+
+    def down_products(low, high):
+        @pl.loop(low, high)
+        def _(index):
+            slot = lax.rem(index, 2)
+
+            @pl.when(index + 1 < chips)
+            def _():
+                cut_down(index + 1).start()
+
+            cut_down(index).wait()
+
+            @pl.when(index >= low + 2)
+            def _():
+                keep_down(index - 2).wait()
+
+            product = dot_left(cuts[slot], big[0]).astype(LOW)
+            for side in (0, 1):
+                stage_down[slot, side] = product[side * deep_own : (side + 1) * deep_own]
+            keep_down(index).start()
+
+        for index in range(max(low, high - 2), high):
+            keep_down(index).wait()
+
+    def block(source, index, slot):
+        window = pl.ds(pl.multiple_of(index * width, width), width)
+        return pltpu.make_async_copy(source.at[:, window], big.at[slot], big_sem.at[slot])
+
+    def keep(array, index):
+        window = pl.ds(pl.multiple_of(index // 2 * width, width), width)
+        return pltpu.make_async_copy(
+            stage.at[lax.rem(index, 2)],
+            parts[array].at[pl.ds(lax.rem(index, 2) * chips, chips), :, window],
+            stage_sem.at[2 + lax.rem(index, 2)],
+        )
+
+    def open_products(left_side, right_side, slot):
+        for index in (0, 1):
+            load_cut(left_side, index, index).start()
+        block(right_side, 0, slot).start()
+
+    def products(array, left_side, right_side, shift, low, high):
+        number = 2 * (right_side.shape[1] // width)
+        if low == 0:
+            for index in (0, 1):
+                load_cut(left_side, index, index).wait()
+
+        @pl.loop(low, high)
+        def _(index):
+            slot = lax.rem(index, 2)
+            here = lax.rem(index // 2 + shift, 2)
+
+            @pl.when(slot == 0)
+            def _():
+                block(right_side, index // 2, here).wait()
+
+                @pl.when(index + 2 < number)
+                def _():
+                    block(right_side, index // 2 + 1, 1 - here).start()
+
+            @pl.when(index >= low + 2)
+            def _():
+                keep(array, index - 2).wait()
+
+            product = dot_left(cuts[slot], big[here]).astype(LOW)
+            for device in range(chips):
+                stage[slot, device] = product[device * own : (device + 1) * own]
+            keep(array, index).start()
+
+        for index in range(max(low, high - 2), high):
+            keep(array, index).wait()
+
+    def exchange(wanted, offsets):
+        for offset in offsets:
+            for item in wanted:
+                pair_copy(item, offset).start()
+
+    far = [half, half - 1, half + 1]
+    near = [offset for offset in range(chips) if offset not in far]
+    order = far + near
+
+    def advance(wanted, steps):
+        return [entry for entry in rest if entry[1] in wanted and entry[0] in steps]
+
+    deep_blocks = grad_inner.shape[1] // width
+    head_blocks = grad_packed.shape[1] // width
+    cut_down(0).start()
+    load_big(grad_ff, 0).wait()
+    down_products(0, 3)
+    exchange(downs, far)
+    down_products(3, 5)
+    run(starts(downs))
+    down_products(5, chips)
+    exchange(downs, near)
+    open_products(second, grad_inner, 1)
+    products(3, second, grad_inner, 1, 0, deep_blocks)
+    run(advance(downs, (2,)))
+    products(3, second, grad_inner, 1, deep_blocks, 2 * deep_blocks)
+    exchange(ups, order)
+    open_products(mixed, grad_branch, 1)
+    run(advance(downs, (3,)))
+    products(2, mixed, grad_branch, 1, 0, 2)
+    open_products(lowered, grad_packed, 0)
+    run(starts(ups))
+    products(1, lowered, grad_packed, 0, 0, head_blocks)
+    run(advance(ups, (2,)))
+    products(1, lowered, grad_packed, 0, head_blocks, 2 * head_blocks)
+    exchange(others, order)
+    run(advance(ups, (3,)))
+    run(starts(others))
+    done = advance(downs, (2, 3)) + advance(ups, (2, 3))
+    run([entry for entry in rest if entry not in done])
+    for copy in sent:
+        copy.wait_send()
+    for item in every:
+        for offset in range(chips):
+            pair_copy(item, offset).wait_send()
+    for copy in final_copies[-final.shape[0] :]:
+        copy.wait()
+
+
+def weight_grads(small_part, sides, items, shapes, count):
+    chips = count // 2
+    rows_in, width = sides[0].shape
+    pieces = len(items)
+    wholes = [small_part.shape[1:]] + list(shapes)
+    held = [(rows,) + wholes[array][1:] for array, _, rows, _ in items]
+    kinds = [F32 if array == 0 else LOW for array, _, _, _ in items]
+    hbm = pl.BlockSpec(memory_space=pl.ANY)
+    cut = width // 2
+    flops = 2 * rows_in * sum(shape[0] * shape[1] for shape in shapes) * count
+    outs = pl.pallas_call(
+        functools.partial(grads_kernel, chips, width, items),
+        out_shape=[jax.ShapeDtypeStruct(shape, F32) for shape in wholes]
+        + [jax.ShapeDtypeStruct((count,) + tuple(shape), LOW) for shape in shapes],
+        in_specs=[hbm] * 9,
+        out_specs=[pl.BlockSpec(memory_space=pltpu.VMEM)] + [hbm] * 8,
+        scratch_shapes=[pltpu.VMEM((chips - 1,) + shape, kind) for shape, kind in zip(held, kinds)]
+        + [pltpu.VMEM((chips,) + shape, kind) for shape, kind in zip(held, kinds)]
+        + [pltpu.VMEM((2,) + shape, kind) for shape, kind in zip(held, kinds)]
+        + [
+            pltpu.VMEM((2, rows_in, width), LOW),
+            pltpu.VMEM((2, rows_in, cut), LOW),
+            pltpu.VMEM((2, chips, width // count, width), LOW),
+            pltpu.VMEM((2, 2, shapes[3][0], width), LOW),
+            pltpu.VMEM((4, shapes[0][0], width), F32),
+            pltpu.SemaphoreType.DMA((pieces, chips - 1)),
+            pltpu.SemaphoreType.DMA((pieces, chips - 1)),
+            pltpu.SemaphoreType.DMA((pieces, chips)),
+            pltpu.SemaphoreType.DMA((pieces, chips)),
+            pltpu.SemaphoreType.DMA((pieces, 2)),
+            pltpu.SemaphoreType.DMA((2,)),
+            pltpu.SemaphoreType.DMA((2,)),
+            pltpu.SemaphoreType.DMA((4,)),
+            pltpu.SemaphoreType.DMA((4,)),
+        ],
+        compiler_params=pltpu.CompilerParams(
+            collective_id=2, has_side_effects=True, vmem_limit_bytes=62 * 2**20
+        ),
+        cost_estimate=pl.CostEstimate(flops=flops, bytes_accessed=8 * width * width * 12, transcendentals=0),
+    )(small_part, *sides)
+    return outs[:5]
+
+
 def on_device(inputs, out_grad, query_counts, gains, shifts, w_qkv, w_out, w_up, b_up, w_down):
     stage = lax.axis_index("pipe")
     stages = lax.axis_size("pipe")
@@ -778,17 +1135,17 @@
     input_grads, grad_packed, grad_branch, grad_inner, grad_ff, sums = back
     sums = jnp.sum(sums, axis=0)
 
-    def product(left, right):
-        return dot_left(left.reshape(cell_count * length, -1), right.reshape(cell_count * length, -1)).astype(LOW)
-
-    parts = [
-        small_pack(sums[0:2], sums[2:8], sums[8 : 8 + ups].reshape(deep), count),
-        product(lowered, grad_packed).reshape((count,) + shapes[0]),
-        product(mixed, grad_branch).reshape((count,) + shapes[1]),
-        product(second, grad_inner).reshape((count,) + shapes[2]),
-        product(activated, grad_ff).reshape((count,) + shapes[3]),
+    small_part = small_pack(sums[0:2], sums[2:8], sums[8 : 8 + ups].reshape(deep), count)
+    sides = [
+        array.reshape(cell_count * length, -1)
+        for array in (lowered, grad_packed, mixed, grad_branch, second, grad_inner, activated, grad_ff)
     ]
-    shares = scatter(parts, items, count)
+    if own % 16 == 0 and width % 256 == 0 and 4 * deep_own == width:
+        shares = weight_grads(small_part, sides, items, shapes, count)
+    else:
+        products = [dot_left(sides[at], sides[at + 1]).astype(LOW) for at in (0, 2, 4, 6)]
+        parts = [small_part] + [whole.reshape((count,) + shape) for whole, shape in zip(products, shapes)]
+        shares = scatter(parts, items, count)
     grad_gains, grad_shifts, grad_bias = small_split(shares[0][None], ups)
     return (
         section_out[None],

time: 762 us -> 734 us (0.963)
  matrix products: 44 us -> 0 us
  Pallas kernels: 597 us -> 614 us
    dot_general x4 -> x0, matrix products: 44 us -> none  [dot_left(): lax.dot_general(left, right, (((0,), (0,)), ((), ())), preferred_element_...]
    pallas_call x1, Pallas kernels: 196 us -> 212 us  [weight_grads(): pl.pallas_call(functools.partial(grads_kernel, chips, width, items), out_...]
  transfers between devices with their start and end apart: 4 -> 4, of which waited for: 3 -> 3; matrix products, arithmetic and copies ran while one was open for 0% -> 0% of each run, Pallas kernels for 13% -> 14%
where the time goes in v3:
time: 734 us; the launch traced here: 728 us
  Pallas kernels  614 us (84%)
  waiting for transfers between devices  83.3 us (11%)
  local copies, waits for them, and re-layouts  19.1 us (3%)
    pallas_call x1, Pallas kernels, weight_grads(): pl.pallas_call(functools.partial(grads_kernel, chips, width, items), out_...  212 us
    pallas_call x1, Pallas kernels, gather(): pl.pallas_call(functools.partial(gather_kernel, chips, arrays, items), ou...  194 us
    pallas_call x4, Pallas kernels, backward_tick(): pl.pallas_call(functools.partial(backward_kernel, cell, held), out_shape=...  115 us
    pallas_call x4, Pallas kernels, forward_tick(): pl.pallas_call(functools.partial(forward_kernel, cell, held), out_shape=o...  92.2 us
    ppermute x4, waiting for transfers between devices, along(): return lax.ppermute(value, 'pipe', pairs)  83.3 us
  transfers between devices with their start and end apart: 4, of which 3 were waited for; matrix products, arithmetic and copies ran while one was open for 0% of the time, Pallas kernels for 14%

profile of v3, /device:TPU:0, one launch (start us, length us, event | category | flops | bytes accessed | tf_op | source)
XLA Modules:
  0.0 727.9 jit_solution(2467905597607345200)
XLA Ops:
  0.7 0.8 reduce
  1.7 1.4 maximum_bitcast_fusion.refs_0_
  3.0 194.0 %shard_map.169 = (bf16[16,16,80]{2,1,0:T(8,128)(2,1)}, bf16[16,80,3840]{2,1,0:T(8,128)(2,1)}, bf16[16,80,1280]{2,1,0:T(8,128)(2,1)}, bf16[16,80,5120]{2,1,0:T(8,128)(2,1)}, bf16[16,320,1280]{2,1,0:T(8,128)(2,1)}) custom-call(bf16[16,80]{1,0:T(8,128)(2,1)} %maximum_bitcast_fusion.refs_0_, bf16[80,3840]{1,0:T(8,128)(2,1)} %bitcast.87, ...), custom_call_target="tpu_custom_call" | custom-call | tf_op jit(solution)/shard_map/pallas_call | solution.py:115
  197.0 0.9 convert_element_type.4
  197.9 0.8 slice.62
  200.8 1.4 slice_bitcast_fusion.2
  202.2 37.7 %shard_map.170 = (bf16[384,1280]{1,0:T(8,128)(2,1)}, bf16[2,384,1280]{2,1,0:T(8,128)(2,1)}, bf16[2,384,1280]{2,1,0:T(8,128)(2,1)}, bf16[2,384,3840]{2,1,0:T(8,12...) custom-call(s32[1]{0:T(128)} %bitcast.1.active, ...), custom_call_target="tpu_custom_call" | custom-call | flops 18119393280 | bytes 39321600 | tf_op jit(solution)/shard_map/pallas_call | solution.py:536
  239.9 1.4 collective-permute-start.1
  241.3 37.4 %shard_map.171 = (bf16[384,1280]{1,0:T(8,128)(2,1)}, bf16[2,384,1280]{2,1,0:T(8,128)(2,1)}, bf16[2,384,1280]{2,1,0:T(8,128)(2,1)}, bf16[2,384,3840]{2,1,0:T(8,12...) custom-call(s32[1]{0:T(128)} %bitcast.1.active, ...), custom_call_target="tpu_custom_call", output_to_operand_aliasing={{1}: (9, {}), {2}: (10, {}), {3}: (11, {}), {4}: (12, {}), ... | custom-call | flops 18119393280 | bytes 39321600 | tf_op jit(solution)/shard_map/pallas_call | solution.py:536
  278.7 2.3 collective-permute-start
  281.6 1.4 slice_bitcast_fusion
  283.0 0.9 copy-done.4
  283.9 7.3 shard_map.172
  291.2 10.9 %collective-permute-done.entry = bf16[384,1280]{1,0:T(8,128)(2,1)} collective-permute-done((bf16[384,1280]{1,0:T(8,128)(2,1)}, bf16[384,1280]{1,0:T(8,128)(2,1)}, u32[]{:S(2)}, u32[]{:S(2)}) %collective-permute-start) | collective-permute-done | bytes 983072 | tf_op jit(solution)/shard_map/ppermute | solution.py:1111
  302.1 9.9 %shard_map.173 = (bf16[384,1280]{1,0:T(8,128)(2,1)}, bf16[2,384,1280]{2,1,0:T(8,128)(2,1)}, bf16[2,384,1280]{2,1,0:T(8,128)(2,1)}, bf16[2,384,3840]{2,1,0:T(8,12...) custom-call(s32[1]{0:T(128)} %bitcast.active, ...), custom_call_target="tpu_custom_call", output_to_operand_aliasing={{1}: (9, {}), {2}: (10, {}), {3}: (11, {}), {4}: (12, {}), ... | custom-call | flops 18119393280 | bytes 39321600 | tf_op jit(solution)/shard_map/pallas_call | solution.py:536
  312.0 12.9 %shard_map.174 = (bf16[384,1280]{1,0:T(8,128)(2,1)}, bf16[2,384,1280]{2,1,0:T(8,128)(2,1)}, bf16[2,384,3840]{2,1,0:T(8,128)(2,1)}, bf16[2,384,1280]{2,1,0:T(8,12...) custom-call(s32[1]{0:T(128)} %bitcast.active, ...), custom_call_target="tpu_custom_call" | custom-call | flops 22649241600 | bytes 39321600 | tf_op jit(solution)/shard_map/pallas_call | solution.py:684
  324.9 1.3 collective-permute-start.3
  326.2 11.9 %shard_map.175 = (bf16[384,1280]{1,0:T(8,128)(2,1)}, bf16[2,384,1280]{2,1,0:T(8,128)(2,1)}, bf16[2,384,3840]{2,1,0:T(8,128)(2,1)}, bf16[2,384,1280]{2,1,0:T(8,12...) custom-call(s32[1]{0:T(128)} %bitcast.active, ...), custom_call_target="tpu_custom_call", output_to_operand_aliasing={{1}: (13, {}), {2}: (14, {}), {3}: (15, {}), {4}: (16, {}),... | custom-call | flops 22649241600 | bytes 39321600 | tf_op jit(solution)/shard_map/pallas_call | solution.py:684
  338.1 1.3 collective-permute-start.2
  339.4 71.3 %collective-permute-done.3.grad = bf16[384,1280]{1,0:T(8,128)(2,1)S(1)} collective-permute-done((bf16[384,1280]{1,0:T(8,128)(2,1)}, bf16[384,1280]{1,0:T(8,128)(2,1)S(1)}, u32[]{:S(2)}, u32[]{:S(2)}) %collective-permute-start.3) | collective-permute-done | bytes 983072 | tf_op jit(solution)/shard_map/ppermute | solution.py:1111
  410.7 1.0 copy-done.7
  411.7 45.1 %shard_map.176 = (bf16[384,1280]{1,0:T(8,128)(2,1)}, bf16[2,384,1280]{2,1,0:T(8,128)(2,1)}, bf16[2,384,3840]{2,1,0:T(8,128)(2,1)}, bf16[2,384,1280]{2,1,0:T(8,12...) custom-call(s32[1]{0:T(128)} %bitcast.1.active, ...), custom_call_target="tpu_custom_call", output_to_operand_aliasing={{1}: (13, {}), {2}: (14, {}), {3}: (15, {}), {4}: (16, {}),... | custom-call | flops 22649241600 | bytes 39321600 | tf_op jit(solution)/shard_map/pallas_call | solution.py:684
  456.8 1.1 collective-permute-done.2.grad
  457.9 0.9 copy-done.6
  458.8 45.4 %shard_map.177 = (bf16[384,1280]{1,0:T(8,128)(2,1)}, bf16[2,384,1280]{2,1,0:T(8,128)(2,1)}, bf16[2,384,3840]{2,1,0:T(8,128)(2,1)}, bf16[2,384,1280]{2,1,0:T(8,12...) custom-call(s32[1]{0:T(128)} %bitcast.1.active, ...), custom_call_target="tpu_custom_call", output_to_operand_aliasing={{1}: (13, {}), {2}: (14, {}), {3}: (15, {}), {4}: (16, {}),... | custom-call | flops 22649241600 | bytes 39321600 | tf_op jit(solution)/shard_map/pallas_call | solution.py:684
  504.2 0.9 reduce_sum.9
  506.2 212.1 %shard_map.178 = (f32[16,80]{1,0:T(8,128)}, f32[80,3840]{1,0:T(8,128)}, f32[80,1280]{1,0:T(8,128)}, f32[80,5120]{1,0:T(8,128)}, f32[320,1280]{1,0:T(8,128)}, /*i...) custom-call(f32[16,16,80]{2,1,0:T(8,128)} %maximum_maximum_fusion.re, ...), custom_call_target="tpu_custom_call" | custom-call | flops 30198988800 | bytes 157286400 | tf_op jit(solution)/shard_map/pallas_call | solution.py:1038
  718.3 0.8 slice.67
  719.8 1.2 slice.66
  722.3 2.4 copy.119
  725.5 1.2 copy.121
  726.6 1.2 copy.122
  (43 shorter events, 6.7 us)
Async XLA Ops:
  0.6 200.2 %copy-start = (bf16[2,384,1280]{2,1,0:T(8,128)(2,1)S(1)}, bf16[2,384,1280]{2,1,0:T(8,128)(2,1)}, u32[]{:S(2)}) copy-start(bf16[2,384,1280]{2,1,0:T(8,128)(2,1)} %param.10) | copy-start | bytes 5898244
  239.9 43.1 %collective-permute-start.1 = (bf16[384,1280]{1,0:T(8,128)(2,1)}, bf16[384,1280]{1,0:T(8,128)(2,1)S(1)}, u32[]{:S(2)}, u32[]{:S(2)}) collective-permute-start(bf16[384,1280]{1,0:T(8,128)(2,1)} %get-tuple-element.93), channel_id=1, source_target_pairs={{0,16},{1,17},{2,18},{3,19},{4,20},{5,21},{6,22},{7,23},{8,24},{9,... | collective-permute-start | bytes 2949128 | tf_op jit(solution)/shard_map/ppermute | solution.py:1111
  241.3 39.7 %copy-start.8 = (s32[2]{0:T(128)S(1)}, s32[2]{0:T(128)}, u32[]{:S(2)}) copy-start(s32[2]{0:T(128)} %param.12) | copy-start | bytes 28
  241.3 40.4 %copy-start.1 = (bf16[2,384,1280]{2,1,0:T(8,128)(2,1)S(1)}, bf16[2,384,1280]{2,1,0:T(8,128)(2,1)}, u32[]{:S(2)}) copy-start(bf16[2,384,1280]{2,1,0:T(8,128)(2,1)} %param.11) | copy-start | bytes 5898244
  278.7 23.4 %collective-permute-start = (bf16[384,1280]{1,0:T(8,128)(2,1)}, bf16[384,1280]{1,0:T(8,128)(2,1)}, u32[]{:S(2)}, u32[]{:S(2)}) collective-permute-start(bf16[384,1280]{1,0:T(8,128)(2,1)} %get-tuple-element.92), channel_id=1, source_target_pairs={{0,16},{1,17},{2,18},{3,19},{4,20},{5,21},{6,22},{7,23},{8,24},{9,... | collective-permute-start | bytes 2949128 | tf_op jit(solution)/shard_map/ppermute | solution.py:1111
  283.0 0.9 copy-start.4
  324.9 85.8 %collective-permute-start.3 = (bf16[384,1280]{1,0:T(8,128)(2,1)}, bf16[384,1280]{1,0:T(8,128)(2,1)S(1)}, u32[]{:S(2)}, u32[]{:S(2)}) collective-permute-start(bf16[384,1280]{1,0:T(8,128)(2,1)} %get-tuple-element.121), channel_id=1, source_target_pairs={{16,0},{17,1},{18,2},{19,3},{20,4},{21,5},{22,6},{23,7},{24,8},{25... | collective-permute-start | bytes 2949128 | tf_op jit(solution)/shard_map/ppermute | solution.py:1111
  338.1 119.7 %collective-permute-start.2 = (bf16[384,1280]{1,0:T(8,128)(2,1)}, bf16[384,1280]{1,0:T(8,128)(2,1)S(1)}, u32[]{:S(2)}, u32[]{:S(2)}) collective-permute-start(bf16[384,1280]{1,0:T(8,128)(2,1)} %get-tuple-element.120), channel_id=1, source_target_pairs={{16,0},{17,1},{18,2},{19,3},{20,4},{21,5},{22,6},{23,7},{24,8},{25... | collective-permute-start | bytes 2949128 | tf_op jit(solution)/shard_map/ppermute | solution.py:1111
  410.7 1.0 copy-start.7
  457.9 0.9 copy-start.6
  718.3 6.4 copy-start.5
  718.3 7.1 copy-start.3
  724.7 1.9 copy-start.2

commit v4 on v3

--- a/solution.py
+++ b/solution.py
@@ -311,20 +311,8 @@
 
 
 def gelu_parts(hidden):
-    size = jnp.abs(hidden)
-    turn = 1.0 / (1.0 + (0.3275911 / math.sqrt(2.0)) * size)
-    bell = jnp.exp(-0.5 * hidden * hidden)
-    series = turn * (
-        0.5 * 0.254829592
-        + turn
-        * (
-            0.5 * -0.284496736
-            + turn * (0.5 * 1.421413741 + turn * (0.5 * -1.453152027 + turn * (0.5 * 1.061405429)))
-        )
-    )
-    tail = series * bell
-    cumulative = jnp.where(hidden < 0.0, tail, 1.0 - tail)
-    slope = cumulative + hidden * bell * (1.0 / math.sqrt(2.0 * math.pi))
+    cumulative = 0.5 * (1.0 + lax.erf(hidden * (1.0 / math.sqrt(2.0))))
+    slope = cumulative + hidden * jnp.exp(-0.5 * hidden * hidden) * (1.0 / math.sqrt(2.0 * math.pi))
     return (hidden * cumulative, slope)
 
 
@@ -376,66 +364,82 @@
     return (heads, w_out, ups, downs)
 
 
+def head_masks(length):
+    return lax.broadcasted_iota(jnp.int32, (length, 128), 1) < HEAD_DIM
+
+
+def two_heads(array, side):
+    blank = jnp.zeros_like(array)
+    return jnp.concatenate([jnp.where(side, array, blank), jnp.where(side, blank, array)], axis=0)
+
+
 def attend(packed, mixed, width):
     length = packed.shape[0]
-    side = lax.broadcasted_iota(jnp.int32, (length, 128), 1) < HEAD_DIM
-
-    @pl.loop(0, width // 128)
-    def _(pair):
+    side = head_masks(length)
+
+    def pair_of(pair):
         start = pl.multiple_of(pair * 128, 128)
         queries = packed[:, pl.ds(start, 128)] * jnp.asarray(1.0 / math.sqrt(HEAD_DIM), LOW)
-        keys = packed[:, pl.ds(start + width, 128)]
-        values = packed[:, pl.ds(start + 2 * width, 128)]
-        blank = jnp.zeros_like(queries)
-        parts = []
+        keys = two_heads(packed[:, pl.ds(start + width, 128)], side)
+        values = two_heads(packed[:, pl.ds(start + 2 * width, 128)], side)
+        scores = dot_right(queries, keys)
+        probs, totals = ([], [])
         for head in (0, 1):
-            mine = jnp.where(side, queries, blank) if head == 0 else jnp.where(side, blank, queries)
-            scores = dot_right(mine, keys)
-            shifted = jnp.exp(scores - jnp.max(scores, axis=-1, keepdims=True))
-            total = jnp.sum(shifted, axis=-1, keepdims=True)
-            parts.append(dot(shifted.astype(LOW), values) * (1.0 / total))
-        mixed[:, pl.ds(start, 128)] = jnp.where(side, parts[0], parts[1]).astype(LOW)
+            mine = scores[:, head * length : (head + 1) * length]
+            shifted = jnp.exp(mine - jnp.max(mine, axis=-1, keepdims=True))
+            totals.append(1.0 / jnp.sum(shifted, axis=-1, keepdims=True))
+            probs.append(shifted.astype(LOW))
+        result = dot(jnp.concatenate(probs, axis=1), values)
+        mixed[:, pl.ds(start, 128)] = (result * jnp.where(side, totals[0], totals[1])).astype(LOW)
+
+    @pl.loop(0, width // 256)
+    def _(index):
+        pair_of(index * 2)
+        pair_of(index * 2 + 1)
 
 
 def attend_back(packed, grad_mixed, grad_packed, width):
     length = packed.shape[0]
-    side = lax.broadcasted_iota(jnp.int32, (length, 128), 1) < HEAD_DIM
+    side = head_masks(length)
     scale = 1.0 / math.sqrt(HEAD_DIM)
 
-    @pl.loop(0, width // 128)
-    def _(pair):
+    def pair_of(pair):
         start = pl.multiple_of(pair * 128, 128)
         queries = packed[:, pl.ds(start, 128)]
-        keys = packed[:, pl.ds(start + width, 128)]
-        values = packed[:, pl.ds(start + 2 * width, 128)]
+        keys = packed[:, pl.ds(start + width, 128)] * jnp.asarray(scale, LOW)
         grads = grad_mixed[:, pl.ds(start, 128)]
-        blank = jnp.zeros_like(queries)
-        scaled = keys * jnp.asarray(scale, LOW)
-        parts = []
+        keys_two = two_heads(keys, side)
+        queries_two = two_heads(queries, side)
+        grads_two = two_heads(grads, side)
+        scores = dot_right(keys, queries_two)
+        grad_probs = dot_right(packed[:, pl.ds(start + 2 * width, 128)], grads_two)
+        probs, grad_scores = ([], [])
         for head in (0, 1):
-            def mine(array):
-                return jnp.where(side, array, blank) if head == 0 else jnp.where(side, blank, array)
-            scores = dot_right(mine(scaled), queries)
-            shifted = jnp.exp(scores - jnp.max(scores, axis=0, keepdims=True))
-            probs = shifted * (1.0 / jnp.sum(shifted, axis=0, keepdims=True))
-            grad_probs = dot_right(mine(values), grads)
-            product = grad_probs * probs
+            mine = slice(head * length, (head + 1) * length)
+            shifted = jnp.exp(scores[:, mine] - jnp.max(scores[:, mine], axis=0, keepdims=True))
+            prob = shifted * (1.0 / jnp.sum(shifted, axis=0, keepdims=True))
+            product = grad_probs[:, mine] * prob
             weighted = jnp.sum(product, axis=0, keepdims=True)
-            grad_scores = (product - probs * weighted).astype(LOW)
-            parts.append((dot_left(grad_scores, scaled), dot(grad_scores, queries) * scale, dot(probs.astype(LOW), grads)))
-        for number in range(3):
-            grad_packed[:, pl.ds(start + number * width, 128)] = jnp.where(
-                side, parts[0][number], parts[1][number]
-            ).astype(LOW)
-
-
-def forward_kernel(cell, held, active, entry, gains, shifts, bias, w_qkv, w_out, w_up, w_down, *refs):
+            probs.append(prob.astype(LOW))
+            grad_scores.append((product - prob * weighted).astype(LOW))
+        beside = jnp.concatenate(grad_scores, axis=1)
+        grad_packed[:, pl.ds(start, 128)] = dot_left(jnp.concatenate(grad_scores, axis=0), keys_two).astype(LOW)
+        grad_packed[:, pl.ds(start + width, 128)] = (dot(beside, queries_two) * scale).astype(LOW)
+        grad_packed[:, pl.ds(start + 2 * width, 128)] = dot(jnp.concatenate(probs, axis=1), grads_two).astype(LOW)
+
+    @pl.loop(0, width // 256)
+    def _(index):
+        pair_of(index * 2)
+        pair_of(index * 2 + 1)
+
+
+def forward_kernel(cell, held, active, entry_h, gains, shifts, bias, w_qkv, w_out, w_up, w_down, *refs):
     sent_h = refs[held]
     out_h, lowered_h, packed_h, mixed_h, middle_h, second_h, active_h, slope_h = [
         ref.at[cell] for ref in refs[held + 1 : held + 9]
     ]
     (buffers, buffer_sems, save_sems, out_v, lowered_v, packed_v, mixed_v, middle_v) = refs[held + 9 : held + 17]
-    (second_v, active_v, slope_v, hidden_v, total_v) = refs[held + 17 :]
+    (second_v, active_v, slope_v, hidden_v, total_v, entry, entry_sem) = refs[held + 17 :]
     width = entry.shape[1]
     ups = w_up.shape[1] // width
 
@@ -451,13 +455,16 @@
             if number > 0:
                 place_down[number - 1] = len(order)
                 order.append(down[number - 1])
-        stream = Stream(order, buffers, buffer_sems)
+        fetched = pltpu.make_async_copy(entry_h, entry, entry_sem)
+        fetched.start()
         saves = []
 
         def save(source, target):
             saves.append(pltpu.make_async_copy(source, target, save_sems.at[len(saves)]))
             saves[-1].start()
 
+        fetched.wait()
+        stream = Stream(order, buffers, buffer_sems)
         rows_in = entry[...].astype(F32)
         normed, _ = row_norm(rows_in)
         lowered_v[...] = (normed * gains[0:1, :] + shifts[0:1, :]).astype(LOW)
@@ -536,7 +543,7 @@
     sent, *kept = pl.pallas_call(
         functools.partial(forward_kernel, cell, held),
         out_shape=outs,
-        in_specs=[pl.BlockSpec(memory_space=pltpu.SMEM)] + [vmem] * 4 + [hbm] * (4 + held),
+        in_specs=[pl.BlockSpec(memory_space=pltpu.SMEM), hbm] + [vmem] * 3 + [hbm] * (4 + held),
         out_specs=[hbm] * 9,
         input_output_aliases={9 + number: 1 + number for number in range(held)},
         scratch_shapes=[
@@ -545,7 +552,12 @@
             pltpu.SemaphoreType.DMA((7 + 2 * ups,)),
         ]
         + [pltpu.VMEM(*shape) for shape in shapes]
-        + [pltpu.VMEM((2, length, width), F32), pltpu.VMEM((length, width), F32)],
+        + [
+            pltpu.VMEM((2, length, width), F32),
+            pltpu.VMEM((length, width), F32),
+            pltpu.VMEM((length, width), LOW),
+            pltpu.SemaphoreType.DMA,
+        ],
         compiler_params=pltpu.CompilerParams(vmem_limit_bytes=60 * 2**20),
         cost_estimate=pl.CostEstimate(
             flops=flops, bytes_accessed=2 * width * (4 * width + 2 * deep), transcendentals=0
@@ -554,14 +566,14 @@
     return (sent, kept)
 
 
-def backward_kernel(cell, held, active, scale, grad, entry, gains, shifts, *refs):
+def backward_kernel(cell, held, active, scale, grad_h, entry_h, gains, shifts, *refs):
     packed, middle, slope = [ref.at[cell] for ref in refs[:3]]
     w_qkv, w_out, w_up, w_down = refs[3:7]
     refs = refs[7 + held :]
     sent_h = refs[0]
     rows_h, packed_h, branch_h, inner_h, low_h, sums_h = [ref.at[cell] for ref in refs[1:7]]
     (buffers, buffer_sems, load_sems, save_sems, rows_v, grad_packed_v, branch_v, inner_v, low_v, sums_v) = refs[7:17]
-    (packed_v, middle_v, slope_v, mixed_v, grad_act_v, total_v, grad_middle_v) = refs[17:]
+    (packed_v, middle_v, slope_v, mixed_v, grad_act_v, total_v, grad_middle_v, grad, entry) = refs[17:]
     length, width = entry.shape
     ups = w_up.shape[1] // width
 
@@ -572,8 +584,10 @@
             pltpu.make_async_copy(slope, slope_v, load_sems.at[0]),
             pltpu.make_async_copy(middle, middle_v, load_sems.at[1]),
             pltpu.make_async_copy(packed, packed_v, load_sems.at[2]),
+            pltpu.make_async_copy(grad_h, grad, load_sems.at[3]),
+            pltpu.make_async_copy(entry_h, entry, load_sems.at[4]),
         ]
-        loads[0].start()
+        loads[3].start()
         order, place_up, place_down = ([], {}, {})
         for number in range(ups + 1):
             if number < ups:
@@ -584,9 +598,6 @@
                 order.append(up[number - 1])
         place_out = len(order)
         order = order + [outer] + heads
-        stream = Stream(order, buffers, buffer_sems)
-        loads[1].start()
-        loads[2].start()
         saves = []
 
         def save(source, target):
@@ -596,11 +607,19 @@
         def column_sum(array):
             return jnp.sum(array.astype(F32), axis=0, keepdims=True)
 
+        loads[3].wait()
+        stream = Stream(order, buffers, buffer_sems)
+        loads[0].start()
         low_v[...] = (grad[...].astype(F32) * scale[0]).astype(LOW)
         save(low_v, low_h)
         sums_v[7:8, :] = column_sum(low_v[...])
-        loads[0].wait()
         for number in range(ups + 1):
+            if number == 1:
+                loads[0].wait()
+                loads[1].start()
+            if number == 2:
+                loads[2].start()
+                loads[4].start()
             if number < ups:
                 down_block = stream.take(place_down[number])
             if number > 0:
@@ -648,6 +667,7 @@
             else:
                 total_v[...] += part
             stream.release()
+        loads[4].wait()
         normed, inverse = row_norm(entry[...].astype(F32))
         grad_lowered = total_v[...]
         sums_v[0:1, :] = column_sum(grad_lowered * normed)
@@ -684,13 +704,13 @@
     sent, *kept = pl.pallas_call(
         functools.partial(backward_kernel, cell, held),
         out_shape=outs,
-        in_specs=[smem] * 2 + [vmem] * 4 + [hbm] * (7 + held),
+        in_specs=[smem] * 2 + [hbm] * 2 + [vmem] * 2 + [hbm] * (7 + held),
         out_specs=[hbm] * 7,
         input_output_aliases={13 + number: 1 + number for number in range(held)},
         scratch_shapes=[
             pltpu.VMEM((4, width, width), LOW),
             pltpu.SemaphoreType.DMA((4,)),
-            pltpu.SemaphoreType.DMA((3,)),
+            pltpu.SemaphoreType.DMA((5,)),
             pltpu.SemaphoreType.DMA((6 + ups,)),
         ]
         + [pltpu.VMEM(*shape) for shape in shapes]
@@ -702,6 +722,8 @@
             pltpu.VMEM((2, length, width), F32),
             pltpu.VMEM((length, width), F32),
             pltpu.VMEM((length, width), F32),
+            pltpu.VMEM((length, width), LOW),
+            pltpu.VMEM((length, width), LOW),
         ],
         compiler_params=pltpu.CompilerParams(vmem_limit_bytes=60 * 2**20),
         cost_estimate=pl.CostEstimate(

time: 734 us -> 711 us (0.969)
  Pallas kernels: 614 us -> 598 us
  waiting for transfers between devices: 83.3 us -> 74.9 us
    pallas_call x4, Pallas kernels: 92.2 us -> 79.9 us  [forward_tick(): pl.pallas_call(functools.partial(forward_kernel, cell, held), out_shape=o...]
    ppermute x4, waiting for transfers between devices: 83.3 us -> 74.9 us  [along(): return lax.ppermute(value, 'pipe', pairs)]
  transfers between devices with their start and end apart: 4 -> 4, of which waited for: 3 -> 3; matrix products, arithmetic and copies ran while one was open for 0% -> 0% of each run, Pallas kernels for 14% -> 13%
where the time goes in v4:
time: 711 us; the launch traced here: 704 us
  Pallas kernels  598 us (84%)
  waiting for transfers between devices  74.9 us (11%)
  local copies, waits for them, and re-layouts  19.1 us (3%)
    pallas_call x1, Pallas kernels, weight_grads(): pl.pallas_call(functools.partial(grads_kernel, chips, width, items), out_...  212 us
    pallas_call x1, Pallas kernels, gather(): pl.pallas_call(functools.partial(gather_kernel, chips, arrays, items), ou...  194 us
    pallas_call x4, Pallas kernels, backward_tick(): pl.pallas_call(functools.partial(backward_kernel, cell, held), out_shape=...  112 us
    pallas_call x4, Pallas kernels, forward_tick(): pl.pallas_call(functools.partial(forward_kernel, cell, held), out_shape=o...  79.9 us
    ppermute x4, waiting for transfers between devices, along(): return lax.ppermute(value, 'pipe', pairs)  74.9 us
  transfers between devices with their start and end apart: 4, of which 3 were waited for; matrix products, arithmetic and copies ran while one was open for 0% of the time, Pallas kernels for 13%

profile of v4, /device:TPU:0, one launch (start us, length us, event | category | flops | bytes accessed | tf_op | source)
XLA Modules:
  0.0 703.9 jit_solution(14521943702090740136)
XLA Ops:
  0.7 0.8 reduce
  1.7 1.4 maximum_bitcast_fusion.refs_0_
  3.0 194.0 %shard_map.169 = (bf16[16,16,80]{2,1,0:T(8,128)(2,1)}, bf16[16,80,3840]{2,1,0:T(8,128)(2,1)}, bf16[16,80,1280]{2,1,0:T(8,128)(2,1)}, bf16[16,80,5120]{2,1,0:T(8,128)(2,1)}, bf16[16,320,1280]{2,1,0:T(8,128)(2,1)}) custom-call(bf16[16,80]{1,0:T(8,128)(2,1)} %maximum_bitcast_fusion.refs_0_, bf16[80,3840]{1,0:T(8,128)(2,1)} %bitcast.87, ...), custom_call_target="tpu_custom_call" | custom-call | tf_op jit(solution)/shard_map/pallas_call | solution.py:115
  197.0 0.9 convert_element_type.4
  197.9 0.8 slice.62
  200.8 1.4 slice_bitcast_fusion.2
  202.2 31.6 %shard_map.170 = (bf16[384,1280]{1,0:T(8,128)(2,1)}, bf16[2,384,1280]{2,1,0:T(8,128)(2,1)}, bf16[2,384,1280]{2,1,0:T(8,128)(2,1)}, bf16[2,384,3840]{2,1,0:T(8,12...) custom-call(s32[1]{0:T(128)} %bitcast.1.active, ...), custom_call_target="tpu_custom_call" | custom-call | flops 18119393280 | bytes 39321600 | tf_op jit(solution)/shard_map/pallas_call | solution.py:543
  233.8 1.4 collective-permute-start.1
  235.2 31.9 %shard_map.171 = (bf16[384,1280]{1,0:T(8,128)(2,1)}, bf16[2,384,1280]{2,1,0:T(8,128)(2,1)}, bf16[2,384,1280]{2,1,0:T(8,128)(2,1)}, bf16[2,384,3840]{2,1,0:T(8,12...) custom-call(s32[1]{0:T(128)} %bitcast.1.active, ...), custom_call_target="tpu_custom_call", output_to_operand_aliasing={{1}: (9, {}), {2}: (10, {}), {3}: (11, {}), {4}: (12, {}), ... | custom-call | flops 18119393280 | bytes 39321600 | tf_op jit(solution)/shard_map/pallas_call | solution.py:543
  267.1 2.3 collective-permute-start
  270.1 1.4 slice_bitcast_fusion
  271.4 0.9 copy-done.4
  272.4 6.9 shard_map.172
  279.3 11.2 %collective-permute-done.entry_h = bf16[384,1280]{1,0:T(8,128)(2,1)} collective-permute-done((bf16[384,1280]{1,0:T(8,128)(2,1)}, bf16[384,1280]{1,0:T(8,128)(2,1)}, u32[]{:S(2)}, u32[]{:S(2)}) %collective-permute-start) | collective-permute-done | bytes 983072 | tf_op jit(solution)/shard_map/ppermute | solution.py:1133
  290.5 9.5 %shard_map.173 = (bf16[384,1280]{1,0:T(8,128)(2,1)}, bf16[2,384,1280]{2,1,0:T(8,128)(2,1)}, bf16[2,384,1280]{2,1,0:T(8,128)(2,1)}, bf16[2,384,3840]{2,1,0:T(8,12...) custom-call(s32[1]{0:T(128)} %bitcast.active, ...), custom_call_target="tpu_custom_call", output_to_operand_aliasing={{1}: (9, {}), {2}: (10, {}), {3}: (11, {}), {4}: (12, {}), ... | custom-call | flops 18119393280 | bytes 39321600 | tf_op jit(solution)/shard_map/pallas_call | solution.py:543
  300.0 13.8 %shard_map.174 = (bf16[384,1280]{1,0:T(8,128)(2,1)}, bf16[2,384,1280]{2,1,0:T(8,128)(2,1)}, bf16[2,384,3840]{2,1,0:T(8,128)(2,1)}, bf16[2,384,1280]{2,1,0:T(8,12...) custom-call(s32[1]{0:T(128)} %bitcast.active, ...), custom_call_target="tpu_custom_call" | custom-call | flops 22649241600 | bytes 39321600 | tf_op jit(solution)/shard_map/pallas_call | solution.py:704
  313.8 1.3 collective-permute-start.3
  315.1 12.3 %shard_map.175 = (bf16[384,1280]{1,0:T(8,128)(2,1)}, bf16[2,384,1280]{2,1,0:T(8,128)(2,1)}, bf16[2,384,3840]{2,1,0:T(8,128)(2,1)}, bf16[2,384,1280]{2,1,0:T(8,12...) custom-call(s32[1]{0:T(128)} %bitcast.active, ...), custom_call_target="tpu_custom_call", output_to_operand_aliasing={{1}: (13, {}), {2}: (14, {}), {3}: (15, {}), {4}: (16, {}),... | custom-call | flops 22649241600 | bytes 39321600 | tf_op jit(solution)/shard_map/pallas_call | solution.py:704
  327.4 1.3 collective-permute-start.2
  328.7 62.8 %collective-permute-done.3.grad_h = bf16[384,1280]{1,0:T(8,128)(2,1)S(1)} collective-permute-done((bf16[384,1280]{1,0:T(8,128)(2,1)}, bf16[384,1280]{1,0:T(8,128)(2,1)S(1)}, u32[]{:S(2)}, u32[]{:S(2)}) %collective-permute-start.3) | collective-permute-done | bytes 983072 | tf_op jit(solution)/shard_map/ppermute | solution.py:1133
  391.6 1.0 copy-done.7
  392.5 42.9 %shard_map.176 = (bf16[384,1280]{1,0:T(8,128)(2,1)}, bf16[2,384,1280]{2,1,0:T(8,128)(2,1)}, bf16[2,384,3840]{2,1,0:T(8,128)(2,1)}, bf16[2,384,1280]{2,1,0:T(8,12...) custom-call(s32[1]{0:T(128)} %bitcast.1.active, ...), custom_call_target="tpu_custom_call", output_to_operand_aliasing={{1}: (13, {}), {2}: (14, {}), {3}: (15, {}), {4}: (16, {}),... | custom-call | flops 22649241600 | bytes 39321600 | tf_op jit(solution)/shard_map/pallas_call | solution.py:704
  435.4 0.8 collective-permute-done.2.grad_h
  436.2 0.9 copy-done.6
  437.2 42.8 %shard_map.177 = (bf16[384,1280]{1,0:T(8,128)(2,1)}, bf16[2,384,1280]{2,1,0:T(8,128)(2,1)}, bf16[2,384,3840]{2,1,0:T(8,128)(2,1)}, bf16[2,384,1280]{2,1,0:T(8,12...) custom-call(s32[1]{0:T(128)} %bitcast.1.active, ...), custom_call_target="tpu_custom_call", output_to_operand_aliasing={{1}: (13, {}), {2}: (14, {}), {3}: (15, {}), {4}: (16, {}),... | custom-call | flops 22649241600 | bytes 39321600 | tf_op jit(solution)/shard_map/pallas_call | solution.py:704
  480.0 0.9 reduce_sum.9
  482.0 212.0 %shard_map.178 = (f32[16,80]{1,0:T(8,128)}, f32[80,3840]{1,0:T(8,128)}, f32[80,1280]{1,0:T(8,128)}, f32[80,5120]{1,0:T(8,128)}, f32[320,1280]{1,0:T(8,128)}, /*i...) custom-call(f32[16,16,80]{2,1,0:T(8,128)} %maximum_maximum_fusion.re, ...), custom_call_target="tpu_custom_call" | custom-call | flops 30198988800 | bytes 157286400 | tf_op jit(solution)/shard_map/pallas_call | solution.py:1060
  694.0 0.8 slice.67
  695.5 1.2 slice.66
  698.0 2.4 copy.119
  701.1 1.2 copy.121
  702.3 1.2 copy.122
  (43 shorter events, 6.7 us)
Async XLA Ops:
  0.6 200.2 %copy-start = (bf16[2,384,1280]{2,1,0:T(8,128)(2,1)S(1)}, bf16[2,384,1280]{2,1,0:T(8,128)(2,1)}, u32[]{:S(2)}) copy-start(bf16[2,384,1280]{2,1,0:T(8,128)(2,1)} %param.10) | copy-start | bytes 5898244
  233.8 37.6 %collective-permute-start.1 = (bf16[384,1280]{1,0:T(8,128)(2,1)}, bf16[384,1280]{1,0:T(8,128)(2,1)S(1)}, u32[]{:S(2)}, u32[]{:S(2)}) collective-permute-start(bf16[384,1280]{1,0:T(8,128)(2,1)} %get-tuple-element.93), channel_id=1, source_target_pairs={{0,16},{1,17},{2,18},{3,19},{4,20},{5,21},{6,22},{7,23},{8,24},{9,... | collective-permute-start | bytes 2949128 | tf_op jit(solution)/shard_map/ppermute | solution.py:1133
  235.2 34.3 %copy-start.8 = (s32[2]{0:T(128)S(1)}, s32[2]{0:T(128)}, u32[]{:S(2)}) copy-start(s32[2]{0:T(128)} %param.12) | copy-start | bytes 28
  235.2 34.9 %copy-start.1 = (bf16[2,384,1280]{2,1,0:T(8,128)(2,1)S(1)}, bf16[2,384,1280]{2,1,0:T(8,128)(2,1)}, u32[]{:S(2)}) copy-start(bf16[2,384,1280]{2,1,0:T(8,128)(2,1)} %param.11) | copy-start | bytes 5898244
  267.1 23.4 %collective-permute-start = (bf16[384,1280]{1,0:T(8,128)(2,1)}, bf16[384,1280]{1,0:T(8,128)(2,1)}, u32[]{:S(2)}, u32[]{:S(2)}) collective-permute-start(bf16[384,1280]{1,0:T(8,128)(2,1)} %get-tuple-element.92), channel_id=1, source_target_pairs={{0,16},{1,17},{2,18},{3,19},{4,20},{5,21},{6,22},{7,23},{8,24},{9,... | collective-permute-start | bytes 2949128 | tf_op jit(solution)/shard_map/ppermute | solution.py:1133
  271.4 0.9 copy-start.4
  313.8 77.7 %collective-permute-start.3 = (bf16[384,1280]{1,0:T(8,128)(2,1)}, bf16[384,1280]{1,0:T(8,128)(2,1)S(1)}, u32[]{:S(2)}, u32[]{:S(2)}) collective-permute-start(bf16[384,1280]{1,0:T(8,128)(2,1)} %get-tuple-element.121), channel_id=1, source_target_pairs={{16,0},{17,1},{18,2},{19,3},{20,4},{21,5},{22,6},{23,7},{24,8},{25... | collective-permute-start | bytes 2949128 | tf_op jit(solution)/shard_map/ppermute | solution.py:1133
  327.4 108.8 %collective-permute-start.2 = (bf16[384,1280]{1,0:T(8,128)(2,1)}, bf16[384,1280]{1,0:T(8,128)(2,1)S(1)}, u32[]{:S(2)}, u32[]{:S(2)}) collective-permute-start(bf16[384,1280]{1,0:T(8,128)(2,1)} %get-tuple-element.120), channel_id=1, source_target_pairs={{16,0},{17,1},{18,2},{19,3},{20,4},{21,5},{22,6},{23,7},{24,8},{25... | collective-permute-start | bytes 2949128 | tf_op jit(solution)/shard_map/ppermute | solution.py:1133
  391.5 1.0 copy-start.7
  436.2 0.9 copy-start.6
  694.0 6.4 copy-start.5
  694.0 7.1 %copy-start.3 = (f32[80,5120]{1,0:T(8,128)S(1)}, f32[80,5120]{1,0:T(8,128)}, u32[]{:S(2)}) copy-start(f32[80,5120]{1,0:T(8,128)} %get-tuple-element.147) | copy-start | bytes 4915204
  700.4 1.9 copy-start.2

commit v5 on v4

--- a/solution.py
+++ b/solution.py
@@ -373,12 +373,12 @@
     return jnp.concatenate([jnp.where(side, array, blank), jnp.where(side, blank, array)], axis=0)
 
 
-def attend(packed, mixed, width):
+def attend(packed, mixed, width, low=0, high=None):
     length = packed.shape[0]
     side = head_masks(length)
 
     def pair_of(pair):
-        start = pl.multiple_of(pair * 128, 128)
+        start = pair * 128 if isinstance(pair, int) else pl.multiple_of(pair * 128, 128)
         queries = packed[:, pl.ds(start, 128)] * jnp.asarray(1.0 / math.sqrt(HEAD_DIM), LOW)
         keys = two_heads(packed[:, pl.ds(start + width, 128)], side)
         values = two_heads(packed[:, pl.ds(start + 2 * width, 128)], side)
@@ -391,6 +391,11 @@
             probs.append(shifted.astype(LOW))
         result = dot(jnp.concatenate(probs, axis=1), values)
         mixed[:, pl.ds(start, 128)] = (result * jnp.where(side, totals[0], totals[1])).astype(LOW)
+
+    if high is not None:
+        for pair in range(low, high):
+            pair_of(pair)
+        return
 
     @pl.loop(0, width // 256)
     def _(index):
@@ -433,7 +438,7 @@
         pair_of(index * 2 + 1)
 
 
-def forward_kernel(cell, held, active, entry_h, gains, shifts, bias, w_qkv, w_out, w_up, w_down, *refs):
+def forward_kernel(cell, held, active, entry_h, rows, w_qkv, w_out, w_up, w_down, *refs):
     sent_h = refs[held]
     out_h, lowered_h, packed_h, mixed_h, middle_h, second_h, active_h, slope_h = [
         ref.at[cell] for ref in refs[held + 1 : held + 9]
@@ -441,6 +446,7 @@
     (buffers, buffer_sems, save_sems, out_v, lowered_v, packed_v, mixed_v, middle_v) = refs[held + 9 : held + 17]
     (second_v, active_v, slope_v, hidden_v, total_v, entry, entry_sem) = refs[held + 17 :]
     width = entry.shape[1]
+    gains, shifts, bias = (rows.at[0:2], rows.at[2:8], rows.at[8:16])
     ups = w_up.shape[1] // width
 
     @pl.when(active[0] != 0)
@@ -494,7 +500,7 @@
             if number > 0:
                 down_block = stream.take(place_down[number - 1])
             if number < ups:
-                hidden_v[number % 2] = dot(second_v[...], up_block[...]) + bias[0:1, pl.ds(number * width, width)]
+                hidden_v[number % 2] = dot(second_v[...], up_block[...]) + bias[number : number + 1, :]
             if number > 0:
                 window = pl.ds((number - 1) * width, width)
                 activated, slope = gelu_parts(hidden_v[(number - 1) % 2])
@@ -519,11 +525,8 @@
             copy.wait()
 
 
-def forward_tick(active, entry, small, weights, kept, cell, cell_count):
-    length, width = entry.shape
-    deep = weights[2].shape[1]
-    ups = deep // width
-    shapes = [
+def kept_shapes(length, width, deep):
+    return [
         ((length, width), LOW),
         ((length, width), LOW),
         ((length, 3 * width), LOW),
@@ -533,6 +536,13 @@
         ((length, deep), LOW),
         ((length, deep), LOW),
     ]
+
+
+def forward_tick(active, entry, rows, weights, kept, cell, cell_count):
+    length, width = entry.shape
+    deep = weights[2].shape[1]
+    ups = deep // width
+    shapes = kept_shapes(length, width, deep)
     outs = [jax.ShapeDtypeStruct(*shapes[0])] + [
         jax.ShapeDtypeStruct((cell_count,) + shape, kind) for shape, kind in shapes
     ]
@@ -543,9 +553,9 @@
     sent, *kept = pl.pallas_call(
         functools.partial(forward_kernel, cell, held),
         out_shape=outs,
-        in_specs=[pl.BlockSpec(memory_space=pltpu.SMEM), hbm] + [vmem] * 3 + [hbm] * (4 + held),
+        in_specs=[pl.BlockSpec(memory_space=pltpu.SMEM), hbm, vmem] + [hbm] * (4 + held),
         out_specs=[hbm] * 9,
-        input_output_aliases={9 + number: 1 + number for number in range(held)},
+        input_output_aliases={7 + number: 1 + number for number in range(held)},
         scratch_shapes=[
             pltpu.VMEM((4, width, width), LOW),
             pltpu.SemaphoreType.DMA((4,)),
@@ -562,11 +572,11 @@
         cost_estimate=pl.CostEstimate(
             flops=flops, bytes_accessed=2 * width * (4 * width + 2 * deep), transcendentals=0
         ),
-    )(active, entry, *small, *weights, *kept)
+    )(active, entry, rows, *weights, *kept)
     return (sent, kept)
 
 
-def backward_kernel(cell, held, active, scale, grad_h, entry_h, gains, shifts, *refs):
+def backward_kernel(cell, held, active, scale, grad_h, entry_h, rows, *refs):
     packed, middle, slope = [ref.at[cell] for ref in refs[:3]]
     w_qkv, w_out, w_up, w_down = refs[3:7]
     refs = refs[7 + held :]
@@ -574,6 +584,7 @@
     rows_h, packed_h, branch_h, inner_h, low_h, sums_h = [ref.at[cell] for ref in refs[1:7]]
     (buffers, buffer_sems, load_sems, save_sems, rows_v, grad_packed_v, branch_v, inner_v, low_v, sums_v) = refs[7:17]
     (packed_v, middle_v, slope_v, mixed_v, grad_act_v, total_v, grad_middle_v, grad, entry) = refs[17:]
+    gains = rows.at[0:2]
     length, width = entry.shape
     ups = w_up.shape[1] // width
 
@@ -680,7 +691,7 @@
             copy.wait()
 
 
-def backward_tick(active, incoming, entry, small, saved, weights, kept, cell, cell_count):
+def backward_tick(active, incoming, entry, rows, saved, weights, kept, cell, cell_count):
     length, width = entry.shape
     deep = weights[2].shape[1]
     ups = deep // width
@@ -704,9 +715,9 @@
     sent, *kept = pl.pallas_call(
         functools.partial(backward_kernel, cell, held),
         out_shape=outs,
-        in_specs=[smem] * 2 + [hbm] * 2 + [vmem] * 2 + [hbm] * (7 + held),
+        in_specs=[smem] * 2 + [hbm] * 2 + [vmem] + [hbm] * (7 + held),
         out_specs=[hbm] * 7,
-        input_output_aliases={13 + number: 1 + number for number in range(held)},
+        input_output_aliases={12 + number: 1 + number for number in range(held)},
         scratch_shapes=[
             pltpu.VMEM((4, width, width), LOW),
             pltpu.SemaphoreType.DMA((4,)),
@@ -729,8 +740,446 @@
         cost_estimate=pl.CostEstimate(
             flops=flops, bytes_accessed=2 * width * (4 * width + 2 * deep), transcendentals=0
         ),
-    )(active, scale, grad, entry, *small[:2], *saved, *weights, *kept)
+    )(active, scale, grad, entry, rows, *saved, *weights, *kept)
     return (sent, kept)
+
+
+def small_rows(small, rows, width, ups):
+    devices, _, own = small.shape
+    lane = lax.broadcasted_iota(jnp.int32, (own, width), 1)
+    depth = lax.broadcasted_iota(jnp.int32, (own, width), 0)
+    row = lax.broadcasted_iota(jnp.int32, (16, width), 0)
+    across = lax.broadcasted_iota(jnp.int32, (16, width), 1)
+    top = jnp.zeros((16, width), F32)
+    for device in range(devices):
+        spot = jnp.where(lane == depth + device * own, 1.0, 0.0).astype(LOW)
+        top = top + dot(small[device], spot)
+    rows[0:8, :] = top[0:8]
+    share = devices // ups
+    for block in range(ups):
+        total = jnp.zeros((1, width), F32)
+        for index in range(share):
+            start = index * ups * own
+            spot = jnp.zeros((own, width), F32)
+            for up in range(ups):
+                spot = spot + jnp.where(lane == depth + (start + up * own), 1.0, 0.0)
+            low = start + (row - 8) * own
+            inside = (row >= 8) & (row < 8 + ups) & (across >= low) & (across < low + own)
+            placed = dot(small[block * share + index], spot.astype(LOW))
+            total = total + jnp.sum(jnp.where(inside, placed, 0.0), axis=0, keepdims=True)
+        rows[8 + block : 9 + block, :] = total
+
+
+def gather_forward_kernel(chips, items, groups, cells, *refs):
+    shards, inputs_h = (refs[:5], refs[5])
+    outs, rows_h, arrived_h, later_h = (refs[6:11], refs[11], refs[12], refs[13])
+    out_h, lowered_h, packed_h, mixed_h, middle_h, second_h, active_h, slope_h = refs[14:22]
+    (ring_send, ring_recv, pair_send, pair_recv, own_sem, hop_send, hop_recv) = refs[22:29]
+    (load_sem, save_sem, wide_sem, deep_sem) = refs[29:33]
+    (small_v, rows_v, entry_v, out_v, lowered_v, packed_v, mixed_v, middle_v, second_v, active_v, slope_v) = refs[33:44]
+    (total_v, hidden_v, wide_v, deep_v) = refs[44:]
+    length, width = entry_v.shape[1:]
+    ups = active_v.shape[2] // width
+    half = chips // 2
+    me, core, position, right, left, sibling = ring_place(chips)
+    stage = lax.axis_index("pipe")
+    first = stage == 0
+    barrier = pltpu.get_barrier_semaphore()
+    for device in (left, right, sibling):
+        pl.semaphore_signal(barrier, inc=1, device_id={"dp": device}, device_id_type=MESH)
+    pl.semaphore_signal(barrier, inc=1, device_id={"pipe": 1 - stage}, device_id_type=MESH)
+    pl.semaphore_wait(barrier, 4)
+
+    def shard(item):
+        array, start, rows, _ = items[item]
+        return shards[array].at[pl.ds(start, rows)]
+
+    def out(item, block):
+        array, start, rows, _ = items[item]
+        return outs[array].at[block, pl.ds(start, rows)]
+
+    def owner(step, way):
+        return ring_chip(position - step if way == 0 else position + step, chips) * 2 + core
+
+    def travels(item, way, step):
+        return step < half or (step == half and items[item][3] == way)
+
+    def ring_copy(item, way, step):
+        block = owner(step - 1, way)
+        return pltpu.make_async_remote_copy(
+            src_ref=shard(item) if step == 1 else out(item, block),
+            dst_ref=out(item, block),
+            send_sem=ring_send.at[item, way, step - 1],
+            recv_sem=ring_recv.at[item, way, step - 1],
+            device_id={"dp": right if way == 0 else left},
+            device_id_type=MESH,
+        )
+
+    def pair_copy(item, offset, block, source):
+        return pltpu.make_async_remote_copy(
+            src_ref=source,
+            dst_ref=out(item, block),
+            send_sem=pair_send.at[item, offset],
+            recv_sem=pair_recv.at[item, offset],
+            device_id={"dp": sibling},
+            device_id_type=MESH,
+        )
+
+    def own_copy(item):
+        return pltpu.make_async_copy(shard(item), out(item, me), own_sem.at[item])
+
+    sent, paired = ([], [])
+
+    def open_group(group):
+        for item in group:
+            for way in (0, 1):
+                if travels(item, way, 1):
+                    sent.append(ring_copy(item, way, 1))
+                    sent[-1].start()
+        for item in group:
+            paired.append(pair_copy(item, 0, me, shard(item)))
+            paired[-1].start()
+            own_copy(item).start()
+
+    def ring_step(item, way, step):
+        ring_copy(item, way, step).wait_recv()
+        if travels(item, way, step + 1):
+            sent.append(ring_copy(item, way, step + 1))
+            sent[-1].start()
+        block = owner(step, way)
+        offset = step if way == 0 else chips - step
+        paired.append(pair_copy(item, offset, block, out(item, block)))
+        paired[-1].start()
+
+    def pair_arrived(item, offset):
+        block = ring_chip(position - offset, chips) * 2 + core
+        pair_copy(item, offset, block, out(item, block)).wait_recv()
+
+    saves = []
+
+    def save(source, target):
+        number = len(saves)
+        saves.append(lambda: pltpu.make_async_copy(source(), target(), save_sem.at[number]))
+        saves[-1]().start()
+
+    def entry_load(cell):
+        return pltpu.make_async_copy(inputs_h.at[cell], entry_v.at[cell], load_sem.at[cell])
+
+    def wide_load(array, column, slot):
+        source = outs[array].at[:, :, pl.ds(column * width, width)]
+        return pltpu.make_async_copy(source, wide_v.at[slot], wide_sem.at[slot])
+
+    def wide(slot):
+        return wide_v[slot].reshape(width, width)
+
+    def gains(number):
+        return rows_v[number : number + 1, :]
+
+    def shifts(number):
+        return rows_v[2 + number : 3 + number, :]
+
+    def begin(cell):
+        def step():
+            entry_load(cell).wait()
+            normed, _ = row_norm(entry_v[cell].astype(F32))
+            lowered_v[cell] = (normed * gains(0) + shifts(0)).astype(LOW)
+            save(lambda: lowered_v.at[cell], lambda: lowered_h.at[cell])
+
+        return step
+
+    def project(cell, number):
+        def step():
+            if cell == 0:
+                wide_load(1, number, number).wait()
+            part = dot(lowered_v[cell], wide(number))
+            if number != 1:
+                part = part + shifts(1 + number // 2)
+            packed_v[cell, :, pl.ds(number * width, width)] = part.astype(LOW)
+            if number == 2:
+                save(lambda: packed_v.at[cell], lambda: packed_h.at[cell])
+
+        return step
+
+    def mix(cell, low, high, last):
+        def step():
+            attend(packed_v.at[cell], mixed_v.at[cell], width, low, high)
+            if last:
+                save(lambda: mixed_v.at[cell], lambda: mixed_h.at[cell])
+
+        return step
+
+    def join(cell):
+        def step():
+            if cell == 0:
+                wide_load(2, 0, 3).wait()
+            middle_v[cell] = entry_v[cell].astype(F32) + dot(mixed_v[cell], wide(3)) + shifts(3)
+            save(lambda: middle_v.at[cell], lambda: middle_h.at[cell])
+
+        return step
+
+    def renorm(cell):
+        def step():
+            middle = middle_v[cell]
+            normed, _ = row_norm(middle)
+            second_v[cell] = (normed * gains(1) + shifts(4)).astype(LOW)
+            total_v[cell] = middle + shifts(5)
+            save(lambda: second_v.at[cell], lambda: second_h.at[cell])
+
+        return step
+
+    def rise(cell, number):
+        def step():
+            if cell == 0:
+                wide_load(3, number, number).wait()
+            hidden_v[...] = dot(second_v[cell], wide(number)) + rows_v[8 + number : 9 + number, :]
+
+        return step
+
+    def bend(cell, number):
+        def step():
+            window = pl.ds(number * width, width)
+            activated, slope = gelu_parts(hidden_v[...])
+            active_v[cell, :, window] = activated.astype(LOW)
+            slope_v[cell, :, window] = slope.astype(LOW)
+            if number == ups - 1:
+                save(lambda: active_v.at[cell], lambda: active_h.at[cell])
+                save(lambda: slope_v.at[cell], lambda: slope_h.at[cell])
+
+        return step
+
+    deep_rows = deep_v.shape[1] * deep_v.shape[2]
+
+    def deep_load(offset, slot):
+        chip = ring_chip(position - offset, chips)
+        return pltpu.make_async_copy(outs[4].at[pl.ds(chip * 2, 2)], deep_v.at[slot], deep_sem.at[slot])
+
+    def fall(cell, offset, slot):
+        def step():
+            if cell == 0:
+                deep_load(offset, slot).wait()
+            chip = ring_chip(position - offset, chips)
+            window = pl.ds(pl.multiple_of(chip * deep_rows, 128), deep_rows)
+            total_v[cell] += dot(active_v[cell, :, window], deep_v[slot].reshape(deep_rows, width))
+
+        return step
+
+    def hop():
+        return pltpu.make_async_remote_copy(
+            src_ref=out_v.at[0],
+            dst_ref=arrived_h,
+            send_sem=hop_send,
+            recv_sem=hop_recv,
+            device_id={"pipe": 1 - stage},
+            device_id_type=MESH,
+        )
+
+    def finish(cell):
+        def step():
+            out_v[cell] = total_v[cell].astype(LOW)
+            if cell == 0:
+                hop().start()
+            else:
+                save(lambda: out_v.at[cell], lambda: later_h)
+            save(lambda: out_v.at[cell], lambda: out_h.at[cell])
+
+        return step
+
+    def on_first(step):
+        pl.when(first)(step)
+
+    queue = []
+
+    def ready(group, steps, loads):
+        for item in group:
+            own_copy(item).wait()
+            for offset in range(chips):
+                pair_arrived(item, offset)
+
+        @pl.when(first)
+        def _():
+            for load in loads:
+                load().start()
+
+        queue.extend(steps)
+
+    pairs = width // 128
+    heads = []
+    for cell in range(cells):
+        heads.append(begin(cell))
+        heads += [project(cell, number) for number in range(3)]
+        heads += [mix(cell, low, low + 2, low + 2 >= pairs) for low in range(0, pairs, 2)]
+    joins = [make(cell) for cell in range(cells) for make in (join, renorm)]
+    def load_ups():
+        for number in range(ups):
+            wide_load(3, number, number).start()
+
+    climbs = [load_ups]
+    climbs += [make(cell, number) for number in range(ups) for cell in range(cells) for make in (rise, bend)]
+
+    @pl.when(first)
+    def _():
+        for cell in range(cells):
+            entry_load(cell).start()
+
+    def lay_rows():
+        copy = pltpu.make_async_copy(outs[0], small_v, load_sem.at[cells])
+        copy.start()
+        copy.wait()
+        small_rows(small_v, rows_v, width, ups)
+        pltpu.make_async_copy(rows_v, rows_h, load_sem.at[cells + 1]).start()
+
+    def ready_small():
+        for item in groups[0]:
+            if items[item][0] == 0:
+                own_copy(item).wait()
+                for offset in range(chips):
+                    pair_arrived(item, offset)
+        lay_rows()
+
+    plan = []
+    for number, group in enumerate(groups):
+        for step in range(1, half + 1):
+            if step == half and number + 1 < len(groups):
+                plan.append(("open", number + 1))
+            for item in group:
+                for way in (0, 1):
+                    if travels(item, way, step):
+                        plan.append(("ring", item, way, step))
+            if number == len(groups) - 1:
+                plan.append(("deep", step))
+        plan.append(("done", number))
+    open_group(groups[0])
+    late = []
+    slots = [0]
+
+    def deep_ready(offsets):
+        for offset in offsets:
+            for item in groups[-1]:
+                if offset == 0:
+                    own_copy(item).wait()
+                pair_arrived(item, offset)
+            slot = slots[0] % deep_v.shape[0]
+            slots[0] += 1
+
+            def opening(offset=offset, slot=slot):
+                deep_load(offset, slot).start()
+
+            queue.append(opening)
+            queue.extend(fall(cell, offset, slot) for cell in range(cells))
+
+    def serve(limit):
+        for _ in range(limit):
+            if queue:
+                on_first(queue.pop(0))
+
+    for entry in plan:
+        if entry[0] == "open":
+            open_group(groups[entry[1]])
+        elif entry[0] == "ring":
+            ring_step(*entry[1:])
+            for wait in list(late):
+                wait[0] -= 1
+                if wait[0] == 0:
+                    wait[1]()
+                    late.remove(wait)
+            serve(3 if entry[1] in groups[-1] else 2)
+        elif entry[0] == "done":
+            if entry[1] == 0:
+                rest = [item for item in groups[0] if items[item][0] != 0]
+                late.append([1, ready_small])
+                late.append(
+                    [
+                        2,
+                        lambda: ready(
+                            rest,
+                            heads + joins,
+                            [functools.partial(wide_load, 1, number, number) for number in range(3)]
+                            + [functools.partial(wide_load, 2, 0, 3)],
+                        ),
+                    ]
+                )
+            elif entry[1] == 1:
+                late.append([2, lambda: ready(groups[1], climbs, [])])
+        elif entry[0] == "deep":
+            step = entry[1]
+            if step == 1:
+                late.append([3, lambda: deep_ready([0])])
+            if step < half:
+                late.append([2, lambda step=step: deep_ready([step, chips - step])])
+            else:
+                for wait in late:
+                    wait[1]()
+                serve(len(queue))
+                deep_ready([half])
+    serve(len(queue))
+    for cell in range(cells):
+        on_first(finish(cell))
+    for copy in sent:
+        copy.wait_send()
+    for copy in paired:
+        copy.wait_send()
+    pltpu.make_async_copy(rows_v, rows_h, load_sem.at[cells + 1]).wait()
+
+    @pl.when(first)
+    def _():
+        for copy in saves:
+            copy().wait()
+        hop().wait_send()
+
+    @pl.when(jnp.logical_not(first))
+    def _():
+        hop().wait_recv()
+
+
+def gather_forward(shards, inputs, items, groups, count):
+    chips = count // 2
+    cells, length, width = inputs.shape
+    deep = shards[3].shape[1]
+    ups = deep // width
+    pieces = len(items)
+    shapes = kept_shapes(length, width, deep)
+    hbm = pl.BlockSpec(memory_space=pl.ANY)
+    flops = 2 * cells * length * width * (4 * width + 2 * deep)
+    outs = pl.pallas_call(
+        functools.partial(gather_forward_kernel, chips, items, groups, cells),
+        out_shape=[jax.ShapeDtypeStruct((count,) + shard.shape, shard.dtype) for shard in shards]
+        + [
+            jax.ShapeDtypeStruct((16, width), F32),
+            jax.ShapeDtypeStruct((length, width), LOW),
+            jax.ShapeDtypeStruct((length, width), LOW),
+        ]
+        + [jax.ShapeDtypeStruct((cells,) + shape, kind) for shape, kind in shapes],
+        in_specs=[hbm] * 6,
+        out_specs=[hbm] * 16,
+        scratch_shapes=[
+            pltpu.SemaphoreType.DMA((pieces, 2, chips // 2)),
+            pltpu.SemaphoreType.DMA((pieces, 2, chips // 2)),
+            pltpu.SemaphoreType.DMA((pieces, chips)),
+            pltpu.SemaphoreType.DMA((pieces, chips)),
+            pltpu.SemaphoreType.DMA((pieces,)),
+            pltpu.SemaphoreType.DMA,
+            pltpu.SemaphoreType.DMA,
+            pltpu.SemaphoreType.DMA((cells + 2,)),
+            pltpu.SemaphoreType.DMA((9 * cells,)),
+            pltpu.SemaphoreType.DMA((4,)),
+            pltpu.SemaphoreType.DMA((2,)),
+            pltpu.VMEM((count,) + shards[0].shape, LOW),
+            pltpu.VMEM((16, width), F32),
+            pltpu.VMEM((cells, length, width), LOW),
+        ]
+        + [pltpu.VMEM((cells,) + shape, kind) for shape, kind in shapes]
+        + [
+            pltpu.VMEM((cells, length, width), F32),
+            pltpu.VMEM((length, width), F32),
+            pltpu.VMEM((4, count, width // count, width), LOW),
+            pltpu.VMEM((2, 2, shards[4].shape[0], width), LOW),
+        ],
+        compiler_params=pltpu.CompilerParams(
+            collective_id=3, has_side_effects=True, vmem_limit_bytes=62 * 2**20
+        ),
+        cost_estimate=pl.CostEstimate(flops=flops, bytes_accessed=8 * width * (4 * width + 2 * deep), transcendentals=0),
+    )(*shards, inputs)
+    return (outs[:5], outs[5], outs[6], outs[7], list(outs[8:]))
 
 
 def grads_kernel(chips, width, items, *refs):
@@ -1117,9 +1566,27 @@
     shards = [small_pack(gains[0], shifts[0], b_up[0], 1)[0]] + [
         array[0].reshape(shape) for array, shape in zip((w_qkv, w_out, w_up, w_down), shapes)
     ]
-    packs = gather(shards, items, count)
-    gain_rows, shift_rows, bias = small_split(packs[0].astype(F32), ups)
-    small = (gain_rows, shift_rows, bias[None])
+    fused = stages == 2 and cell_count == 2 and own % 16 == 0 and width % 256 == 0 and 4 * deep_own == width
+    if fused:
+        piece = own // 2 // 16 * 16
+        arrivals = (
+            (0, 0, 16, 0),
+            (1, 0, own - piece, 0),
+            (1, own - piece, piece, 1),
+            (2, 0, own, 1),
+            (3, 0, own - piece, 0),
+            (3, own - piece, piece, 1),
+            (4, 0, cut, 0),
+            (4, cut, deep_own - cut, 1),
+        )
+        packs, rows, arrived, later, kept = gather_forward(
+            shards, inputs, arrivals, ((0, 1, 2, 3), (4, 5), (6, 7)), count
+        )
+    else:
+        packs = gather(shards, items, count)
+        gain_rows, shift_rows, bias = small_split(packs[0].astype(F32), ups)
+        blank = jnp.zeros((8 - ups, width), F32)
+        rows = jnp.concatenate([gain_rows, shift_rows, bias.reshape(ups, width), blank])
     weights = (
         packs[1].reshape(width, 3 * width),
         packs[2].reshape(width, width),
@@ -1132,12 +1599,16 @@
         pairs = [(source, source + steps) for source in range(stages) if 0 <= source + steps < stages]
         return lax.ppermute(value, "pipe", pairs)
 
-    entries, kept = ([[inputs[cell] for cell in range(cell_count)]], None)
-    for turn in range(stages):
+    entries = [[inputs[cell] for cell in range(cell_count)]]
+    if fused:
+        entries.append([arrived] + [along(later, 1)])
+    else:
+        kept = None
+    for turn in range(1 if fused else 0, stages):
         active = (stage == turn).astype(jnp.int32)[None]
         arrived = []
         for cell in range(cell_count):
-            sent, kept = forward_tick(active, entries[turn][cell], small, weights, kept, cell, cell_count)
+            sent, kept = forward_tick(active, entries[turn][cell], rows, weights, kept, cell, cell_count)
             if turn + 1 < stages:
                 arrived.append(along(sent, 1))
         entries.append(arrived)
@@ -1149,7 +1620,7 @@
         arrived = []
         for cell in range(cell_count):
             sent, back = backward_tick(
-                active, incoming[cell], entries[turn][cell], small, (packed, middle, slope), weights, back, cell, cell_count
+                active, incoming[cell], entries[turn][cell], rows, (packed, middle, slope), weights, back, cell, cell_count
             )
             if turn > 0:
                 arrived.append((along(sent, -1), jnp.ones((1,), F32)))
@@ -1162,7 +1633,7 @@
         array.reshape(cell_count * length, -1)
         for array in (lowered, grad_packed, mixed, grad_branch, second, grad_inner, activated, grad_ff)
     ]
-    if own % 16 == 0 and width % 256 == 0 and 4 * deep_own == width:
+    if fused:
         shares = weight_grads(small_part, sides, items, shapes, count)
     else:
         products = [dot_left(sides[at], sides[at + 1]).astype(LOW) for at in (0, 2, 4, 6)]

time: 711 us -> 685 us (0.963)
  Pallas kernels: 598 us -> 558 us
  waiting for transfers between devices: 74.9 us -> 88 us
    pallas_call x4 -> x2, Pallas kernels: 79.9 us -> 10.9 us  [forward_tick(): pl.pallas_call(functools.partial(forward_kernel, cell, held), out_shape=o...]
    pallas_call x1, Pallas kernels: 194 us -> 224 us  [gather_forward(): pl.pallas_call(functools.partial(gather_forward_kernel, chips, items, gro...]
    ppermute x4 -> x3, waiting for transfers between devices: 74.9 us -> 88 us  [along(): return lax.ppermute(value, 'pipe', pairs)]
  transfers between devices with their start and end apart: 4 -> 3, of which waited for: 3 -> 3; matrix products, arithmetic and copies ran while one was open for 0% -> 1% of each run, Pallas kernels for 13% -> 8%
where the time goes in v5:
time: 685 us; the launch traced here: 676 us
  Pallas kernels  558 us (81%)
  waiting for transfers between devices  88 us (13%)
  local copies, waits for them, and re-layouts  17.9 us (3%)
  starting transfers between devices  7.14 us (1%)
    pallas_call x1, Pallas kernels, gather_forward(): pl.pallas_call(functools.partial(gather_forward_kernel, chips, items, gro...  224 us
    pallas_call x1, Pallas kernels, weight_grads(): pl.pallas_call(functools.partial(grads_kernel, chips, width, items), out_...  212 us
    pallas_call x4, Pallas kernels, backward_tick(): pl.pallas_call(functools.partial(backward_kernel, cell, held), out_shape=...  112 us
    ppermute x3, waiting for transfers between devices, along(): return lax.ppermute(value, 'pipe', pairs)  88 us
  transfers between devices with their start and end apart: 3, of which 3 were waited for; matrix products, arithmetic and copies ran while one was open for 1% of the time, Pallas kernels for 8%

profile of v5, /device:TPU:0, one launch (start us, length us, event | category | flops | bytes accessed | tf_op | source)
XLA Modules:
  0.0 675.9 jit_solution(14369278424798065961)
XLA Ops:
  0.6 0.7 reduce
  1.5 1.4 maximum_bitcast_fusion.refs_0_
  2.9 223.6 %shard_map.169 = (bf16[16,16,80]{2,1,0:T(8,128)(2,1)}, bf16[16,80,3840]{2,1,0:T(8,128)(2,1)}, bf16[16,80,1280]{2,1,0:T(8,128)(2,1)}, bf16[16,80,5120]{2,1,0:T(8,...) custom-call(bf16[16,80]{1,0:T(8,128)(2,1)} %maximum_bitcast_fusion.r, ...), custom_call_target="tpu_custom_call" | custom-call | flops 30198988800 | bytes 157286400 | tf_op jit(solution)/shard_map/pallas_call | solution.py:1143
  226.4 4.6 collective-permute-start
  231.7 1.6 shard_map.170
  233.3 1.4 slice_bitcast_fusion
  234.7 0.9 copy-done.2
  235.6 1.5 slice_bitcast_fusion.2
  237.1 11.9 %collective-permute-done.entry_h = bf16[384,1280]{1,0:T(8,128)(2,1)S(1)} collective-permute-done((bf16[384,1280]{1,0:T(8,128)(2,1)}, bf16[384,1280]{1,0:T(8,128)(2,1)S(1)}, u32[]{:S(2)}, u32[]{:S(2)}) %collective-permute-start) | collective-permute-done | bytes 983072 | tf_op jit(solution)/shard_map/ppermute | solution.py:1600
  249.0 0.9 copy-done.6
  249.9 9.4 %shard_map.171 = (bf16[384,1280]{1,0:T(8,128)(2,1)}, bf16[2,384,1280]{2,1,0:T(8,128)(2,1)}, bf16[2,384,1280]{2,1,0:T(8,128)(2,1)}, bf16[2,384,3840]{2,1,0:T(8,12...) custom-call(s32[1]{0:T(128)} %bitcast.active, ...), custom_call_target="tpu_custom_call", output_to_operand_aliasing={{1}: (7, {}), {2}: (8, {}), {3}: (9, {}), {4}: (10, {}), {5... | custom-call | flops 18119393280 | bytes 39321600 | tf_op jit(solution)/shard_map/pallas_call | solution.py:553
  259.3 13.7 %shard_map.172 = (bf16[384,1280]{1,0:T(8,128)(2,1)}, bf16[2,384,1280]{2,1,0:T(8,128)(2,1)}, bf16[2,384,3840]{2,1,0:T(8,128)(2,1)}, bf16[2,384,1280]{2,1,0:T(8,12...) custom-call(s32[1]{0:T(128)} %bitcast.active, ...), custom_call_target="tpu_custom_call" | custom-call | flops 22649241600 | bytes 39321600 | tf_op jit(solution)/shard_map/pallas_call | solution.py:715
  273.0 1.3 collective-permute-start.2
  274.3 12.5 %shard_map.173 = (bf16[384,1280]{1,0:T(8,128)(2,1)}, bf16[2,384,1280]{2,1,0:T(8,128)(2,1)}, bf16[2,384,3840]{2,1,0:T(8,128)(2,1)}, bf16[2,384,1280]{2,1,0:T(8,12...) custom-call(s32[1]{0:T(128)} %bitcast.active, ...), custom_call_target="tpu_custom_call", output_to_operand_aliasing={{1}: (12, {}), {2}: (13, {}), {3}: (14, {}), {4}: (15, {}),... | custom-call | flops 22649241600 | bytes 39321600 | tf_op jit(solution)/shard_map/pallas_call | solution.py:715
  286.8 1.3 collective-permute-start.1
  288.1 74.8 %collective-permute-done.2.grad_h = bf16[384,1280]{1,0:T(8,128)(2,1)S(1)} collective-permute-done((bf16[384,1280]{1,0:T(8,128)(2,1)}, bf16[384,1280]{1,0:T(8,128)(2,1)S(1)}, u32[]{:S(2)}, u32[]{:S(2)}) %collective-permute-start.2) | collective-permute-done | bytes 983072 | tf_op jit(solution)/shard_map/ppermute | solution.py:1600
  362.9 0.9 copy-done.9
  363.8 42.8 %shard_map.174 = (bf16[384,1280]{1,0:T(8,128)(2,1)}, bf16[2,384,1280]{2,1,0:T(8,128)(2,1)}, bf16[2,384,3840]{2,1,0:T(8,128)(2,1)}, bf16[2,384,1280]{2,1,0:T(8,12...) custom-call(s32[1]{0:T(128)} %bitcast.11.active, ...), custom_call_target="tpu_custom_call", output_to_operand_aliasing={{1}: (12, {}), {2}: (13, {}), {3}: (14, {}), {4}: (15, {}),... | custom-call | flops 22649241600 | bytes 39321600 | tf_op jit(solution)/shard_map/pallas_call | solution.py:715
  406.6 1.3 collective-permute-done.1.grad_h
  407.9 0.9 copy-done.8
  408.9 43.0 %shard_map.175 = (bf16[384,1280]{1,0:T(8,128)(2,1)}, bf16[2,384,1280]{2,1,0:T(8,128)(2,1)}, bf16[2,384,3840]{2,1,0:T(8,128)(2,1)}, bf16[2,384,1280]{2,1,0:T(8,12...) custom-call(s32[1]{0:T(128)} %bitcast.11.active, ...), custom_call_target="tpu_custom_call", output_to_operand_aliasing={{1}: (12, {}), {2}: (13, {}), {3}: (14, {}), {4}: (15, {}),... | custom-call | flops 22649241600 | bytes 39321600 | tf_op jit(solution)/shard_map/pallas_call | solution.py:715
  451.9 0.9 reduce_sum.9
  453.1 0.7 maximum_maximum_fusion.refs_0_
  453.9 211.6 %shard_map.176 = (f32[16,80]{1,0:T(8,128)}, f32[80,3840]{1,0:T(8,128)}, f32[80,1280]{1,0:T(8,128)}, f32[80,5120]{1,0:T(8,128)}, f32[320,1280]{1,0:T(8,128)}, /*i...) custom-call(f32[16,16,80]{2,1,0:T(8,128)} %maximum_maximum_fusion.re, ...), custom_call_target="tpu_custom_call" | custom-call | flops 30198988800 | bytes 157286400 | tf_op jit(solution)/shard_map/pallas_call | solution.py:1509
  665.5 1.2 slice.51
  666.8 0.7 slice.52
  669.4 1.3 copy.100
  670.6 0.7 copy-done.5
  671.4 1.0 copy.101
  672.6 0.8 copy.102
  673.4 1.2 copy.103
  674.5 1.2 copy.104
  (35 shorter events, 3.3 us)
Async XLA Ops:
  2.9 228.1 %copy-start.10 = (s32[2]{0:T(128)S(1)}, s32[2]{0:T(128)}, u32[]{:S(2)}) copy-start(s32[2]{0:T(128)} %param.12) | copy-start | bytes 28
  226.4 22.5 %collective-permute-start = (bf16[384,1280]{1,0:T(8,128)(2,1)}, bf16[384,1280]{1,0:T(8,128)(2,1)S(1)}, u32[]{:S(2)}, u32[]{:S(2)}) collective-permute-start(bf16[384,1280]{1,0:T(8,128)(2,1)} %get-tuple-element.71), channel_id=1, source_target_pairs={{0,16},{1,17},{2,18},{3,19},{4,20},{5,21},{6,22},{7,23},{8,24},{9,... | collective-permute-start | bytes 2949128 | tf_op jit(solution)/shard_map/ppermute | solution.py:1600
  231.7 1.6 copy-start.1
  233.3 2.3 copy-start.2
  249.0 0.9 copy-start.6
  273.0 89.9 %collective-permute-start.2 = (bf16[384,1280]{1,0:T(8,128)(2,1)}, bf16[384,1280]{1,0:T(8,128)(2,1)S(1)}, u32[]{:S(2)}, u32[]{:S(2)}) collective-permute-start(bf16[384,1280]{1,0:T(8,128)(2,1)} %get-tuple-element.105), channel_id=1, source_target_pairs={{16,0},{17,1},{18,2},{19,3},{20,4},{21,5},{22,6},{23,7},{24,8},{25... | collective-permute-start | bytes 2949128 | tf_op jit(solution)/shard_map/ppermute | solution.py:1600
  286.8 121.1 %collective-permute-start.1 = (bf16[384,1280]{1,0:T(8,128)(2,1)}, bf16[384,1280]{1,0:T(8,128)(2,1)S(1)}, u32[]{:S(2)}, u32[]{:S(2)}) collective-permute-start(bf16[384,1280]{1,0:T(8,128)(2,1)} %get-tuple-element.104), channel_id=1, source_target_pairs={{16,0},{17,1},{18,2},{19,3},{20,4},{21,5},{22,6},{23,7},{24,8},{25... | collective-permute-start | bytes 2949128 | tf_op jit(solution)/shard_map/ppermute | solution.py:1600
  362.9 0.9 copy-start.9
  407.9 0.9 copy-start.8
  453.9 215.5 %copy-start = (bf16[2,384,1280]{2,1,0:T(8,128)(2,1)S(1)}, bf16[2,384,1280]{2,1,0:T(8,128)(2,1)}, u32[]{:S(2)}) copy-start(bf16[2,384,1280]{2,1,0:T(8,128)(2,1)} %get-tuple-element.94) | copy-start | bytes 5898244
  669.4 2.0 copy-start.5
  671.3 1.3 copy-start.7
  671.4 2.0 copy-start.4
  672.6 1.9 copy-start.3

commit v6 on v5

--- a/solution.py
+++ b/solution.py
@@ -403,13 +403,13 @@
         pair_of(index * 2 + 1)
 
 
-def attend_back(packed, grad_mixed, grad_packed, width):
+def attend_back(packed, grad_mixed, grad_packed, width, low=0, high=None):
     length = packed.shape[0]
     side = head_masks(length)
     scale = 1.0 / math.sqrt(HEAD_DIM)
 
     def pair_of(pair):
-        start = pl.multiple_of(pair * 128, 128)
+        start = pair * 128 if isinstance(pair, int) else pl.multiple_of(pair * 128, 128)
         queries = packed[:, pl.ds(start, 128)]
         keys = packed[:, pl.ds(start + width, 128)] * jnp.asarray(scale, LOW)
         grads = grad_mixed[:, pl.ds(start, 128)]
@@ -431,6 +431,11 @@
         grad_packed[:, pl.ds(start, 128)] = dot_left(jnp.concatenate(grad_scores, axis=0), keys_two).astype(LOW)
         grad_packed[:, pl.ds(start + width, 128)] = (dot(beside, queries_two) * scale).astype(LOW)
         grad_packed[:, pl.ds(start + 2 * width, 128)] = dot(jnp.concatenate(probs, axis=1), grads_two).astype(LOW)
+
+    if high is not None:
+        for pair in range(low, high):
+            pair_of(pair)
+        return
 
     @pl.loop(0, width // 256)
     def _(index):
@@ -1182,134 +1187,123 @@
     return (outs[:5], outs[5], outs[6], outs[7], list(outs[8:]))
 
 
-def grads_kernel(chips, width, items, *refs):
-    count = len(items)
-    small_part, sides = (refs[0], refs[1:9])
-    outs, parts = (refs[9:14], [small_part] + list(refs[14:18]))
-    refs = refs[18:]
-    landed, paired, mine = (refs[:count], refs[count : 2 * count], refs[2 * count : 3 * count])
-    (big, cuts, stage, stage_down, final) = refs[3 * count : 3 * count + 5]
-    (ring_send, ring_recv, pair_send, pair_recv, mine_sem, big_sem, cut_sem, stage_sem, final_sem) = refs[3 * count + 5 :]
-    lowered, grad_packed, mixed, grad_branch, second, grad_inner, activated, grad_ff = sides
-    splits = [way for _, _, _, way in items]
-    half = chips // 2
-    devices = 2 * chips
-    own = width // devices
-    deep_own = activated.shape[1] // devices
-    cut = cuts.shape[2]
-    me, core, position, right, left, sibling = ring_place(chips)
-
-    def load_big(source, slot):
-        return pltpu.make_async_copy(source, big.at[slot], big_sem.at[slot])
-
-    def load_cut(source, index, slot):
-        window = pl.ds(pl.multiple_of(index * cut, cut), cut)
-        return pltpu.make_async_copy(source.at[:, window], cuts.at[slot], cut_sem.at[slot])
-
-    load_big(grad_ff, 0).start()
-    greet((left, right, sibling))
-
-    def part(item, block):
-        array, start, rows, _ = items[item]
-        return parts[array].at[block, pl.ds(start, rows)]
-
-    def first(item, way):
-        return 1 if splits[item] == way else 2
-
-    def slot_of(item, way, step):
-        return step - 1 if splits[item] == way else half + step - 2
-
-    def offset_of(step, way):
-        return half - step + 1 if way == 0 else chips - (half - step + 1)
-
-    def pair_copy(item, offset):
-        block = ring_chip(position + offset, chips) * 2 + 1 - core
+class RingSum:
+    def __init__(self, chips, items, parts, outs, landed, paired, mine, final, sems):
+        self.chips, self.items, self.parts, self.outs = (chips, items, parts, outs)
+        self.landed, self.paired, self.mine, self.final = (landed, paired, mine, final)
+        self.ring_send, self.ring_recv, self.pair_send, self.pair_recv, self.mine_sem, self.final_sem = sems
+        self.half = chips // 2
+        self.me, self.core, self.position, self.right, self.left, self.sibling = ring_place(chips)
+        self.sent, self.final_copies, self.exchanged = ([], [], [])
+        self.uses = [0] * len(items)
+        self.fetched = None
+
+    def part(self, item, block):
+        array, start, rows, _ = self.items[item]
+        return self.parts[array].at[block, pl.ds(start, rows)]
+
+    def first(self, item, way):
+        return 1 if self.items[item][3] == way else 2
+
+    def slot_of(self, item, way, step):
+        return step - 1 if self.items[item][3] == way else self.half + step - 2
+
+    def offset_of(self, step, way):
+        return self.half - step + 1 if way == 0 else self.chips - (self.half - step + 1)
+
+    def pair_copy(self, item, offset):
+        block = ring_chip(self.position + offset, self.chips) * 2 + 1 - self.core
         return pltpu.make_async_remote_copy(
-            src_ref=part(item, block),
-            dst_ref=paired[item].at[offset],
-            send_sem=pair_send.at[item, offset],
-            recv_sem=pair_recv.at[item, offset],
-            device_id={"dp": sibling},
+            src_ref=self.part(item, block),
+            dst_ref=self.paired[item].at[offset],
+            send_sem=self.pair_send.at[item, offset],
+            recv_sem=self.pair_recv.at[item, offset],
+            device_id={"dp": self.sibling},
             device_id_type=MESH,
         )
 
-    def ring_copy(item, way, step):
-        if step == first(item, way):
-            source = paired[item].at[offset_of(step, way)]
+    def ring_copy(self, item, way, step):
+        if step == self.first(item, way):
+            source = self.paired[item].at[self.offset_of(step, way)]
         else:
-            source = landed[item].at[slot_of(item, way, step - 1)]
-        here = slot_of(item, way, step)
+            source = self.landed[item].at[self.slot_of(item, way, step - 1)]
+        here = self.slot_of(item, way, step)
         return pltpu.make_async_remote_copy(
             src_ref=source,
-            dst_ref=landed[item].at[here],
-            send_sem=ring_send.at[item, here],
-            recv_sem=ring_recv.at[item, here],
-            device_id={"dp": right if way == 0 else left},
+            dst_ref=self.landed[item].at[here],
+            send_sem=self.ring_send.at[item, here],
+            recv_sem=self.ring_recv.at[item, here],
+            device_id={"dp": self.right if way == 0 else self.left},
             device_id_type=MESH,
         )
 
-    def load(item, offset, buffer):
-        block = ring_chip(position + offset, chips) * 2 + core
-        return pltpu.make_async_copy(part(item, block), mine[item].at[buffer], mine_sem.at[item, buffer])
-
-    def starts(wanted):
+    def load(self, item, offset, buffer):
+        block = ring_chip(self.position + offset, self.chips) * 2 + self.core
+        return pltpu.make_async_copy(self.part(item, block), self.mine[item].at[buffer], self.mine_sem.at[item, buffer])
+
+    def exchange(self, wanted, offsets):
+        for offset in offsets:
+            for item in wanted:
+                self.pair_copy(item, offset).start()
+                self.exchanged.append((item, offset))
+
+    def starts(self, wanted):
         return [
-            (step, item, way, offset_of(step, way))
+            (step, item, way, self.offset_of(step, way))
             for step in (1, 2)
             for item in wanted
             for way in (0, 1)
-            if step == first(item, way)
+            if step == self.first(item, way)
         ]
 
-    downs = [item for item in range(count) if items[item][0] == 4]
-    ups = [item for item in range(count) if items[item][0] == 3]
-    others = [item for item in range(count) if items[item][0] < 3]
-    every = downs + ups + others
-    rest = [
-        (step, item, way, offset_of(step, way))
-        for step in range(2, half + 1)
-        for item in every
-        for way in (0, 1)
-        if step > first(item, way)
-    ] + [(half + 1, item, None, 0) for item in every]
-    uses = [0] * count
-
-    def numbered(plan):
-        result = []
+    def rest(self, wanted):
+        return [
+            (step, item, way, self.offset_of(step, way))
+            for step in range(2, self.half + 1)
+            for item in wanted
+            for way in (0, 1)
+            if step > self.first(item, way)
+        ] + [(self.half + 1, item, None, 0) for item in wanted]
+
+    def run(self, plan, between=None):
+        numbered = []
         for entry in plan:
-            result.append(entry + (uses[entry[1]] % 2,))
-            uses[entry[1]] += 1
-        return result
-
-    finals = [0]
-
-    def fetch(entry):
-        load(entry[1], entry[3], entry[4]).start()
-
-    def work(entry):
+            numbered.append(entry + (self.uses[entry[1]] % 2,))
+            self.uses[entry[1]] += 1
+        for number, entry in enumerate(numbered):
+            if number == 0:
+                self.load(entry[1], entry[3], entry[4]).start()
+            if number + 1 < len(numbered):
+                later = numbered[number + 1]
+                self.load(later[1], later[3], later[4]).start()
+            self.work(entry)
+            if between is not None:
+                between()
+
+    def work(self, entry):
         step, item, way, offset, buffer = entry
-        array, start, rows, _ = items[item]
-        load(item, offset, buffer).wait()
-        pair_copy(item, offset).wait_recv()
-        kind = parts[array].dtype
-        columns = parts[array].shape[2]
+        array, start, rows, _ = self.items[item]
+        half, final = (self.half, self.final)
+        self.load(item, offset, buffer).wait()
+        self.pair_copy(item, offset).wait_recv()
+        kind = self.parts[array].dtype
+        columns = self.parts[array].shape[2]
         chunk = 16
-        from_pair, from_mine, from_ring = (paired[item], mine[item], landed[item])
+        from_pair, from_mine, from_ring = (self.paired[item], self.mine[item], self.landed[item])
         if way is None:
-            ring_copy(item, 0, half).wait_recv()
-            ring_copy(item, 1, half).wait_recv()
-            slot_a, slot_b = (slot_of(item, 0, half), slot_of(item, 1, half))
-            if array == 0:
-                outs[0][...] = (from_ring[slot_a] + from_ring[slot_b]) + (from_mine[buffer] + from_pair[offset])
+            self.ring_copy(item, 0, half).wait_recv()
+            self.ring_copy(item, 1, half).wait_recv()
+            slot_a, slot_b = (self.slot_of(item, 0, half), self.slot_of(item, 1, half))
+            if kind == F32:
+                self.outs[array][...] = (from_ring[slot_a] + from_ring[slot_b]) + (from_mine[buffer] + from_pair[offset])
                 return
             high, wide = (min(rows, final.shape[1]), min(columns, final.shape[2]))
             for top in range(0, rows, high):
                 for across in range(0, columns, wide):
-                    number = finals[0]
-                    finals[0] += 1
+                    number = len(self.final_copies)
                     turn = number % final.shape[0]
                     if number >= final.shape[0]:
-                        final_copies[number - final.shape[0]].wait()
+                        self.final_copies[number - final.shape[0]].wait()
                     span = pl.ds(across, wide)
 
                     @pl.loop(0, high // chunk)
@@ -1319,16 +1313,16 @@
                             from_ring[slot_a, here, span].astype(F32) + from_ring[slot_b, here, span].astype(F32)
                         ) + (from_mine[buffer, here, span].astype(F32) + from_pair[offset, here, span].astype(F32))
 
-                    final_copies.append(
+                    self.final_copies.append(
                         pltpu.make_async_copy(
                             final.at[turn, pl.ds(0, high), pl.ds(0, wide)],
-                            outs[array].at[pl.ds(start + top, high), span],
-                            final_sem.at[turn],
+                            self.outs[array].at[pl.ds(start + top, high), span],
+                            self.final_sem.at[turn],
                         )
                     )
-                    final_copies[-1].start()
+                    self.final_copies[-1].start()
             return
-        if step == first(item, way):
+        if step == self.first(item, way):
 
             @pl.loop(0, rows // chunk)
             def _(index):
@@ -1338,8 +1332,8 @@
                 ).astype(kind)
 
         else:
-            ring_copy(item, way, step - 1).wait_recv()
-            arrived = slot_of(item, way, step - 1)
+            self.ring_copy(item, way, step - 1).wait_recv()
+            arrived = self.slot_of(item, way, step - 1)
 
             @pl.loop(0, rows // chunk)
             def _(index):
@@ -1349,194 +1343,494 @@
                     + (from_mine[buffer, here, :].astype(F32) + from_pair[offset, here, :].astype(F32))
                 ).astype(kind)
 
-        sent.append(ring_copy(item, way, step))
-        sent[-1].start()
-
-    def run(plan):
-        plan = numbered(plan)
-        if plan:
-            fetch(plan[0])
-        for number, entry in enumerate(plan):
-            if number + 1 < len(plan):
-                fetch(plan[number + 1])
-            work(entry)
-
-    sent, final_copies = ([], [])
-    def farthest_first(index):
-        step = index // 2
-        return ring_chip(position + jnp.where(lax.rem(index, 2) == 0, half - step, half + step + 1), chips)
-
-    def keep_down(index):
-        return pltpu.make_async_copy(
-            stage_down.at[lax.rem(index, 2)],
-            parts[4].at[pl.ds(farthest_first(index) * 2, 2)],
-            stage_sem.at[lax.rem(index, 2)],
-        )
-
-    def cut_down(index):
-        return load_cut(activated, farthest_first(index), lax.rem(index, 2))
-
-    def down_products(low, high):
-        @pl.loop(low, high)
-        def _(index):
-            slot = lax.rem(index, 2)
-
-            @pl.when(index + 1 < chips)
-            def _():
-                cut_down(index + 1).start()
-
-            cut_down(index).wait()
-
-            @pl.when(index >= low + 2)
-            def _():
-                keep_down(index - 2).wait()
-
-            product = dot_left(cuts[slot], big[0]).astype(LOW)
-            for side in (0, 1):
-                stage_down[slot, side] = product[side * deep_own : (side + 1) * deep_own]
-            keep_down(index).start()
-
-        for index in range(max(low, high - 2), high):
-            keep_down(index).wait()
-
-    def block(source, index, slot):
-        window = pl.ds(pl.multiple_of(index * width, width), width)
-        return pltpu.make_async_copy(source.at[:, window], big.at[slot], big_sem.at[slot])
-
-    def keep(array, index):
-        window = pl.ds(pl.multiple_of(index // 2 * width, width), width)
-        return pltpu.make_async_copy(
-            stage.at[lax.rem(index, 2)],
-            parts[array].at[pl.ds(lax.rem(index, 2) * chips, chips), :, window],
-            stage_sem.at[2 + lax.rem(index, 2)],
-        )
-
-    def open_products(left_side, right_side, slot):
-        for index in (0, 1):
-            load_cut(left_side, index, index).start()
-        block(right_side, 0, slot).start()
-
-    def products(array, left_side, right_side, shift, low, high):
-        number = 2 * (right_side.shape[1] // width)
-        if low == 0:
-            for index in (0, 1):
-                load_cut(left_side, index, index).wait()
-
-        @pl.loop(low, high)
-        def _(index):
-            slot = lax.rem(index, 2)
-            here = lax.rem(index // 2 + shift, 2)
-
-            @pl.when(slot == 0)
-            def _():
-                block(right_side, index // 2, here).wait()
-
-                @pl.when(index + 2 < number)
-                def _():
-                    block(right_side, index // 2 + 1, 1 - here).start()
-
-            @pl.when(index >= low + 2)
-            def _():
-                keep(array, index - 2).wait()
-
-            product = dot_left(cuts[slot], big[here]).astype(LOW)
-            for device in range(chips):
-                stage[slot, device] = product[device * own : (device + 1) * own]
-            keep(array, index).start()
-
-        for index in range(max(low, high - 2), high):
-            keep(array, index).wait()
-
-    def exchange(wanted, offsets):
-        for offset in offsets:
-            for item in wanted:
-                pair_copy(item, offset).start()
-
-    far = [half, half - 1, half + 1]
-    near = [offset for offset in range(chips) if offset not in far]
-    order = far + near
-
-    def advance(wanted, steps):
-        return [entry for entry in rest if entry[1] in wanted and entry[0] in steps]
-
-    deep_blocks = grad_inner.shape[1] // width
-    head_blocks = grad_packed.shape[1] // width
-    cut_down(0).start()
-    load_big(grad_ff, 0).wait()
-    down_products(0, 3)
-    exchange(downs, far)
-    down_products(3, 5)
-    run(starts(downs))
-    down_products(5, chips)
-    exchange(downs, near)
-    open_products(second, grad_inner, 1)
-    products(3, second, grad_inner, 1, 0, deep_blocks)
-    run(advance(downs, (2,)))
-    products(3, second, grad_inner, 1, deep_blocks, 2 * deep_blocks)
-    exchange(ups, order)
-    open_products(mixed, grad_branch, 1)
-    run(advance(downs, (3,)))
-    products(2, mixed, grad_branch, 1, 0, 2)
-    open_products(lowered, grad_packed, 0)
-    run(starts(ups))
-    products(1, lowered, grad_packed, 0, 0, head_blocks)
-    run(advance(ups, (2,)))
-    products(1, lowered, grad_packed, 0, head_blocks, 2 * head_blocks)
-    exchange(others, order)
-    run(advance(ups, (3,)))
-    run(starts(others))
-    done = advance(downs, (2, 3)) + advance(ups, (2, 3))
-    run([entry for entry in rest if entry not in done])
-    for copy in sent:
-        copy.wait_send()
-    for item in every:
-        for offset in range(chips):
-            pair_copy(item, offset).wait_send()
-    for copy in final_copies[-final.shape[0] :]:
-        copy.wait()
-
-
-def weight_grads(small_part, sides, items, shapes, count):
-    chips = count // 2
-    rows_in, width = sides[0].shape
+        self.sent.append(self.ring_copy(item, way, step))
+        self.sent[-1].start()
+
+    def close(self):
+        for copy in self.sent:
+            copy.wait_send()
+        for item, offset in self.exchanged:
+            self.pair_copy(item, offset).wait_send()
+        for copy in self.final_copies[-self.final.shape[0] :]:
+            copy.wait()
+
+
+def ring_scratch(chips, items, shapes, kinds, pieces_rows):
+    held = [(rows,) + tuple(shapes[array][1:]) for array, _, rows, _ in items]
+    kinds = [kinds[array] for array, _, _, _ in items]
     pieces = len(items)
-    wholes = [small_part.shape[1:]] + list(shapes)
-    held = [(rows,) + wholes[array][1:] for array, _, rows, _ in items]
-    kinds = [F32 if array == 0 else LOW for array, _, _, _ in items]
-    hbm = pl.BlockSpec(memory_space=pl.ANY)
-    cut = width // 2
-    flops = 2 * rows_in * sum(shape[0] * shape[1] for shape in shapes) * count
-    outs = pl.pallas_call(
-        functools.partial(grads_kernel, chips, width, items),
-        out_shape=[jax.ShapeDtypeStruct(shape, F32) for shape in wholes]
-        + [jax.ShapeDtypeStruct((count,) + tuple(shape), LOW) for shape in shapes],
-        in_specs=[hbm] * 9,
-        out_specs=[pl.BlockSpec(memory_space=pltpu.VMEM)] + [hbm] * 8,
-        scratch_shapes=[pltpu.VMEM((chips - 1,) + shape, kind) for shape, kind in zip(held, kinds)]
+    return (
+        [pltpu.VMEM((chips - 1,) + shape, kind) for shape, kind in zip(held, kinds)]
         + [pltpu.VMEM((chips,) + shape, kind) for shape, kind in zip(held, kinds)]
         + [pltpu.VMEM((2,) + shape, kind) for shape, kind in zip(held, kinds)]
+        + [pltpu.VMEM(pieces_rows, F32)]
         + [
-            pltpu.VMEM((2, rows_in, width), LOW),
-            pltpu.VMEM((2, rows_in, cut), LOW),
-            pltpu.VMEM((2, chips, width // count, width), LOW),
-            pltpu.VMEM((2, 2, shapes[3][0], width), LOW),
-            pltpu.VMEM((4, shapes[0][0], width), F32),
             pltpu.SemaphoreType.DMA((pieces, chips - 1)),
             pltpu.SemaphoreType.DMA((pieces, chips - 1)),
             pltpu.SemaphoreType.DMA((pieces, chips)),
             pltpu.SemaphoreType.DMA((pieces, chips)),
             pltpu.SemaphoreType.DMA((pieces, 2)),
+            pltpu.SemaphoreType.DMA((pieces_rows[0],)),
+        ]
+    )
+
+
+class Products:
+    def __init__(self, chips, width, own, cuts, big, stage, cut_sem, big_sem, stage_sem):
+        self.chips, self.width, self.own = (chips, width, own)
+        self.cuts, self.big, self.stage = (cuts, big, stage)
+        self.cut_sem, self.big_sem, self.stage_sem = (cut_sem, big_sem, stage_sem)
+
+    def load_cut(self, source, index, slot):
+        cut = self.cuts.shape[2]
+        window = pl.ds(pl.multiple_of(index * cut, cut), cut)
+        return pltpu.make_async_copy(source.at[:, window], self.cuts.at[slot], self.cut_sem.at[slot])
+
+    def block(self, source, index, slot):
+        window = pl.ds(pl.multiple_of(index * self.width, self.width), self.width)
+        return pltpu.make_async_copy(source.at[:, window], self.big.at[slot], self.big_sem.at[slot])
+
+    def keep(self, target, index):
+        window = pl.ds(pl.multiple_of(index // 2 * self.width, self.width), self.width)
+        return pltpu.make_async_copy(
+            self.stage.at[lax.rem(index, 2)],
+            target.at[pl.ds(lax.rem(index, 2) * self.chips, self.chips), :, window],
+            self.stage_sem.at[lax.rem(index, 2)],
+        )
+
+    def open(self, left, right, slot):
+        for index in (0, 1):
+            self.load_cut(left, index, index).start()
+        self.block(right, 0, slot).start()
+
+    def run(self, target, left, right, shift, low, high):
+        number = 2 * (right.shape[1] // self.width)
+        if low == 0:
+            for index in (0, 1):
+                self.load_cut(left, index, index).wait()
+
+        @pl.loop(low, high)
+        def _(index):
+            slot = lax.rem(index, 2)
+            here = lax.rem(index // 2 + shift, 2)
+
+            @pl.when(slot == 0)
+            def _():
+                self.block(right, index // 2, here).wait()
+
+                @pl.when(index + 2 < number)
+                def _():
+                    self.block(right, index // 2 + 1, 1 - here).start()
+
+            @pl.when(index >= low + 2)
+            def _():
+                self.keep(target, index - 2).wait()
+
+            product = dot_left(self.cuts[slot], self.big[here]).astype(LOW)
+            for device in range(self.chips):
+                self.stage[slot, device] = product[device * self.own : (device + 1) * self.own]
+            self.keep(target, index).start()
+
+        for index in range(max(low, high - 2), high):
+            self.keep(target, index).wait()
+
+
+def other_grads_kernel(chips, width, items, *refs):
+    count = len(items)
+    small_part, up_part, lowered, grad_packed, mixed, grad_branch = refs[:6]
+    outs = refs[6:10]
+    parts = [small_part, refs[10], refs[11], up_part]
+    refs = refs[12:]
+    landed, paired, mine, final = (refs[:count], refs[count : 2 * count], refs[2 * count : 3 * count], refs[3 * count])
+    sems = refs[3 * count + 1 : 3 * count + 7]
+    big, cuts, stage, big_sem, cut_sem, stage_sem = refs[3 * count + 7 :]
+    ring = RingSum(chips, items, parts, outs, landed, paired, mine, final, sems)
+    products = Products(chips, width, width // (2 * chips), cuts, big, stage, cut_sem, big_sem, stage_sem)
+    products.open(mixed, grad_branch, 1)
+    greet((ring.left, ring.right, ring.sibling))
+    half = ring.half
+    far = [half, half - 1, half + 1]
+    order = far + [offset for offset in range(chips) if offset not in far]
+    ups = [item for item in range(count) if items[item][0] == 3]
+    others = [item for item in range(count) if items[item][0] < 3]
+    smalls = [item for item in others if items[item][0] == 0]
+    heads = [item for item in others if items[item][0] > 0]
+    head_blocks = grad_packed.shape[1] // width
+    ring.exchange(ups, order)
+    ring.exchange(smalls, order)
+    products.run(parts[2], mixed, grad_branch, 1, 0, 2)
+    products.open(lowered, grad_packed, 0)
+    ring.run(ring.starts(ups))
+    ring.run(ring.starts(smalls))
+    products.run(parts[1], lowered, grad_packed, 0, 0, head_blocks)
+    rest = ring.rest(ups + heads + smalls)
+    early = [entry for entry in rest if entry[1] in ups and entry[0] == 2]
+    ring.run(early)
+    products.run(parts[1], lowered, grad_packed, 0, head_blocks, 2 * head_blocks)
+    ring.exchange(heads, order)
+    soon = [entry for entry in rest if entry[1] in ups and entry[0] == 3]
+    ring.run(soon)
+    ring.run(ring.starts(heads))
+    ring.run([entry for entry in rest if entry not in early + soon])
+    ring.close()
+
+
+def other_grads(small_part, up_part, sides, items, shapes, count):
+    chips = count // 2
+    rows_in, width = sides[0].shape
+    wholes = [small_part.shape[1:]] + [tuple(shape) for shape in shapes[:3]]
+    hbm = pl.BlockSpec(memory_space=pl.ANY)
+    cut = width // 2
+    flops = 2 * rows_in * 4 * width * width
+    outs = pl.pallas_call(
+        functools.partial(other_grads_kernel, chips, width, items),
+        out_shape=[jax.ShapeDtypeStruct(shape, F32) for shape in wholes]
+        + [jax.ShapeDtypeStruct((count,) + shape, LOW) for shape in wholes[1:3]],
+        in_specs=[hbm] * 6,
+        out_specs=[pl.BlockSpec(memory_space=pltpu.VMEM)] + [hbm] * 5,
+        scratch_shapes=ring_scratch(chips, items, wholes, [F32, LOW, LOW, LOW], (4, shapes[0][0], width))
+        + [
+            pltpu.VMEM((2, rows_in, width), LOW),
+            pltpu.VMEM((2, rows_in, cut), LOW),
+            pltpu.VMEM((2, chips, width // count, width), LOW),
             pltpu.SemaphoreType.DMA((2,)),
             pltpu.SemaphoreType.DMA((2,)),
-            pltpu.SemaphoreType.DMA((4,)),
-            pltpu.SemaphoreType.DMA((4,)),
+            pltpu.SemaphoreType.DMA((2,)),
         ],
         compiler_params=pltpu.CompilerParams(
             collective_id=2, has_side_effects=True, vmem_limit_bytes=62 * 2**20
         ),
-        cost_estimate=pl.CostEstimate(flops=flops, bytes_accessed=8 * width * width * 12, transcendentals=0),
-    )(small_part, *sides)
-    return outs[:5]
+        cost_estimate=pl.CostEstimate(flops=flops, bytes_accessed=80 * width * width, transcendentals=0),
+    )(small_part, up_part, *sides)
+    return outs[:4]
+
+
+def last_backward_kernel(chips, items, cell, *refs):
+    count = len(items)
+    (grad_h, entry_h, rows, packed_h, middle_h, slope_h, w_qkv, w_out, w_up, w_down) = refs[:10]
+    (activated_h, grad_ff_h, second_h) = refs[10:13]
+    refs = refs[13 + 5 :]
+    rows_o, packed_o, branch_o, inner_o, sums_o = refs[:5]
+    share_o, down_part, up_part = refs[5:8]
+    refs = refs[8:]
+    landed, paired, mine, final = (refs[:count], refs[count : 2 * count], refs[2 * count : 3 * count], refs[3 * count])
+    sems = refs[3 * count + 1 : 3 * count + 7]
+    (big, cuts, stage, stage_down, big_sem, cut_sem, stage_sem) = refs[3 * count + 7 : 3 * count + 14]
+    (buffers, buffer_sems, load_sems, save_sems, slope_sems, inner_sems) = refs[3 * count + 14 : 3 * count + 20]
+    (grad, entry, packed_v, middle_v, slope_v, inner_v, grad_packed_v, mixed_v, branch_v, grad_act_v, total_v, sums_v) = refs[
+        3 * count + 20 :
+    ]
+    length, width = grad.shape
+    devices = 2 * chips
+    deep_own = down_part.shape[1]
+    ups = w_up.shape[1] // width
+    first = lax.axis_index("pipe") == 0
+    ring = RingSum(chips, items, [down_part], [share_o], landed, paired, mine, final, sems)
+    half, position = (ring.half, ring.position)
+    products = Products(chips, width, width // devices, cuts, big, stage, cut_sem, big_sem, stage_sem)
+    gains = rows.at[0:2]
+
+    def farthest_first(index):
+        step = index // 2
+        return ring_chip(position + jnp.where(lax.rem(index, 2) == 0, half - step, half + step + 1), chips)
+
+    def keep_down(index):
+        return pltpu.make_async_copy(
+            stage_down.at[lax.rem(index, 2)],
+            down_part.at[pl.ds(farthest_first(index) * 2, 2)],
+            stage_sem.at[2 + lax.rem(index, 2)],
+        )
+
+    def cut_down(index):
+        return products.load_cut(activated_h, farthest_first(index), lax.rem(index, 2))
+
+    def down_products(low, high):
+        @pl.loop(low, high)
+        def _(index):
+            slot = lax.rem(index, 2)
+
+            @pl.when(index + 1 < chips)
+            def _():
+                cut_down(index + 1).start()
+
+            cut_down(index).wait()
+
+            @pl.when(index >= low + 2)
+            def _():
+                keep_down(index - 2).wait()
+
+            product = dot_left(cuts[slot], big[0]).astype(LOW)
+            for side in (0, 1):
+                stage_down[slot, side] = product[side * deep_own : (side + 1) * deep_own]
+            keep_down(index).start()
+
+        for index in range(max(low, high - 2), high):
+            keep_down(index).wait()
+
+    def here(ref, at):
+        return ref.at[pl.ds(at * length, length)]
+
+    def ff_load(at):
+        return pltpu.make_async_copy(here(grad_ff_h, at), here(big.at[0], at), load_sems.at[at])
+
+    def ff_arrived():
+        return pltpu.make_async_copy(grad_h, here(big.at[0], cell), load_sems.at[cell])
+
+    for at in range(cell):
+        ff_load(at).start()
+    pl.when(first)(lambda: ff_arrived().start())
+    pl.when(jnp.logical_not(first))(lambda: ff_load(cell).start())
+    cut_down(0).start()
+
+    def own_load(number):
+        source, target = (
+            (grad_h, grad),
+            (entry_h, entry),
+            (middle_h.at[cell], middle_v),
+            (packed_h.at[cell], packed_v),
+        )[number]
+        return pltpu.make_async_copy(source, target, load_sems.at[cell + 1 + number])
+
+    def slope_load(number):
+        window = pl.ds(number * width, width)
+        return pltpu.make_async_copy(
+            slope_h.at[cell].at[:, window], slope_v.at[number % 2], slope_sems.at[number % 2]
+        )
+
+    order, place_up, place_down = ([], {}, {})
+    for number in range(ups + 1):
+        if number < ups:
+            place_down[number] = len(order)
+            order.append((w_down, 0, number))
+        if number > 0:
+            place_up[number - 1] = len(order)
+            order.append((w_up, 1, number - 1))
+    place_out = len(order)
+    order = order + [(w_out, 0, 0)] + [(w_qkv, 1, number) for number in range(3)]
+    depth = buffers.shape[0]
+
+    def weight_load(number):
+        ref, axis, at = order[number]
+        window = pl.ds(at * width, width)
+        source = ref.at[:, window] if axis else ref.at[window, :]
+        return pltpu.make_async_copy(source, buffers.at[number % depth], buffer_sems.at[number % depth])
+
+    def take(number):
+        weight_load(number).wait()
+        return buffers.at[number % depth]
+
+    def release(number):
+        if number + depth < len(order):
+            weight_load(number + depth).start()
+
+    def save(number, wait=False):
+        source, target = (
+            (branch_v, branch_o.at[cell]),
+            (grad_packed_v, packed_o.at[cell]),
+            (sums_v, sums_o.at[cell]),
+            (mixed_v, rows_o.at[cell]),
+        )[number]
+        copy = pltpu.make_async_copy(source, target, save_sems.at[number])
+        copy.wait() if wait else copy.start()
+
+    def inner_save(number):
+        window = pl.ds(number * width, width)
+        return pltpu.make_async_copy(
+            inner_v.at[number % 2], inner_o.at[pl.ds(cell * length, length), window], inner_sems.at[number % 2]
+        )
+
+    def column_sum(array):
+        return jnp.sum(array.astype(F32), axis=0, keepdims=True)
+
+    def begin():
+        own_load(0).start()
+        slope_load(0).start()
+        for number in range(depth):
+            weight_load(number).start()
+        for number in (1, 2, 3):
+            own_load(number).start()
+        own_load(0).wait()
+        sums_v[7:8, :] = column_sum(grad[...])
+
+    def climb(number):
+        def step():
+            if number < ups:
+                down_block = take(place_down[number])
+                grad_act_v[number % 2] = dot_right(grad[...], down_block[...])
+                release(place_down[number])
+            if number > 0:
+                at = number - 1
+                slope_load(at).wait()
+                if at + 1 < ups:
+                    slope_load(at + 1).start()
+                up_block = take(place_up[at])
+                if at >= 2:
+                    inner_save(at - 2).wait()
+                inner = (grad_act_v[at % 2] * slope_v[at % 2].astype(F32)).astype(LOW)
+                inner_v[at % 2] = inner
+                sums_v[8 + at : 9 + at, :] = column_sum(inner)
+                part = dot_right(inner, up_block[...])
+                if at == 0:
+                    total_v[...] = part
+                else:
+                    total_v[...] += part
+                inner_save(at).start()
+                release(place_up[at])
+
+        return step
+
+    def turn():
+        own_load(2).wait()
+        normed, inverse = row_norm(middle_v[...])
+        grad_second = total_v[...]
+        sums_v[1:2, :] = column_sum(grad_second * normed)
+        sums_v[6:7, :] = column_sum(grad_second)
+        grad_middle = grad[...].astype(F32) + norm_back(grad_second * gains[1:2, :], normed, inverse)
+        middle_v[...] = grad_middle
+        branch_v[...] = grad_middle.astype(LOW)
+        sums_v[5:6, :] = column_sum(branch_v[...])
+        save(0)
+        for at in range(max(0, ups - 2), ups):
+            inner_save(at).wait()
+
+    def outer():
+        block = take(place_out)
+        mixed_v[...] = dot_right(branch_v[...], block[...]).astype(LOW)
+        release(place_out)
+        own_load(3).wait()
+
+    def heads(low, high):
+        def step():
+            attend_back(packed_v, mixed_v, grad_packed_v, width, low, high)
+
+        return step
+
+    def sums():
+        save(1)
+        sums_v[3:4, :] = column_sum(grad_packed_v[:, pl.ds(0, width)])
+        sums_v[4:5, :] = column_sum(grad_packed_v[:, pl.ds(2 * width, width)])
+
+    def lower(number):
+        def step():
+            block = take(place_out + 1 + number)
+            part = dot_right(grad_packed_v[:, pl.ds(number * width, width)], block[...])
+            if number == 0:
+                total_v[...] = part
+            else:
+                total_v[...] += part
+            release(place_out + 1 + number)
+
+        return step
+
+    def finish():
+        own_load(1).wait()
+        normed, inverse = row_norm(entry[...].astype(F32))
+        grad_lowered = total_v[...]
+        sums_v[0:1, :] = column_sum(grad_lowered * normed)
+        sums_v[2:3, :] = column_sum(grad_lowered)
+        mixed_v[...] = (middle_v[...] + norm_back(grad_lowered * gains[0:1, :], normed, inverse)).astype(LOW)
+        save(2)
+        save(3)
+
+    queue = [(True, climb(number)) for number in range(ups + 1)] + [(True, turn)]
+    queue.append((False, lambda: products.open(second_h, inner_o, 1)))
+    for low in range(0, 2 * ups, 2):
+        queue.append((False, lambda low=low: products.run(up_part, second_h, inner_o, 1, low, low + 2)))
+    queue.append((True, outer))
+    pairs = width // 128
+    queue += [(True, heads(low, low + 2)) for low in range(0, pairs, 2)]
+    queue.append((True, sums))
+    queue += [(True, lower(number)) for number in range(3)] + [(True, finish)]
+
+    def serve():
+        if queue:
+            own, step = queue.pop(0)
+            if own:
+                pl.when(first)(step)
+            else:
+                step()
+
+    greet((ring.left, ring.right, ring.sibling))
+    far = [half, half - 1, half + 1]
+    near = [offset for offset in range(chips) if offset not in far]
+    every = list(range(count))
+    for at in range(cell + 1):
+        ff_load(at).wait()
+    down_products(0, 3)
+    ring.exchange(every, far)
+    down_products(3, 5)
+    pl.when(first)(begin)
+    ring.run(ring.starts(every))
+    down_products(5, chips)
+    ring.exchange(every, near)
+    for _ in range(3):
+        serve()
+    ring.run(ring.rest(every), lambda: (serve(), serve()))
+    while queue:
+        serve()
+    ring.close()
+
+    @pl.when(first)
+    def _():
+        for number in range(4):
+            save(number, wait=True)
+
+
+def last_backward(arrived, entry, rows, saved, weights, kept, sides, items, down_shape, own, count):
+    chips = count // 2
+    length, width = entry.shape
+    deep = weights[2].shape[1]
+    ups = deep // width
+    cells = kept[0].shape[0]
+    rows_in = cells * length
+    hbm = pl.BlockSpec(memory_space=pl.ANY)
+    cut = width // 2
+    flops = 2 * length * width * (4 * width + 2 * deep) + 4 * rows_in * width * deep
+    outs = pl.pallas_call(
+        functools.partial(last_backward_kernel, chips, items, cells - 1),
+        out_shape=[jax.ShapeDtypeStruct(array.shape, array.dtype) for array in kept]
+        + [
+            jax.ShapeDtypeStruct(down_shape, F32),
+            jax.ShapeDtypeStruct((count,) + tuple(down_shape), LOW),
+            jax.ShapeDtypeStruct((count, own, deep), LOW),
+        ],
+        in_specs=[hbm] * 2 + [pl.BlockSpec(memory_space=pltpu.VMEM)] + [hbm] * 15,
+        out_specs=[hbm] * 8,
+        input_output_aliases={13 + number: number for number in range(5)},
+        scratch_shapes=ring_scratch(chips, items, [down_shape], [LOW], (4, 80, width))
+        + [
+            pltpu.VMEM((2, rows_in, width), LOW),
+            pltpu.VMEM((2, rows_in, cut), LOW),
+            pltpu.VMEM((2, chips, own, width), LOW),
+            pltpu.VMEM((2, 2, down_shape[0], width), LOW),
+            pltpu.SemaphoreType.DMA((2,)),
+            pltpu.SemaphoreType.DMA((2,)),
+            pltpu.SemaphoreType.DMA((4,)),
+            pltpu.VMEM((2, width, width), LOW),
+            pltpu.SemaphoreType.DMA((2,)),
+            pltpu.SemaphoreType.DMA((cells + 4,)),
+            pltpu.SemaphoreType.DMA((4,)),
+            pltpu.SemaphoreType.DMA((2,)),
+            pltpu.SemaphoreType.DMA((2,)),
+            pltpu.VMEM((length, width), LOW),
+            pltpu.VMEM((length, width), LOW),
+            pltpu.VMEM((length, 3 * width), LOW),
+            pltpu.VMEM((length, width), F32),
+            pltpu.VMEM((2, length, width), LOW),
+            pltpu.VMEM((2, length, width), LOW),
+            pltpu.VMEM((length, 3 * width), LOW),
+            pltpu.VMEM((length, width), LOW),
+            pltpu.VMEM((length, width), LOW),
+            pltpu.VMEM((2, length, width), F32),
+            pltpu.VMEM((length, width), F32),
+            pltpu.VMEM((16, width), F32),
+        ],
+        compiler_params=pltpu.CompilerParams(
+            collective_id=4, has_side_effects=True, vmem_limit_bytes=62 * 2**20
+        ),
+        cost_estimate=pl.CostEstimate(flops=flops, bytes_accessed=80 * width * width, transcendentals=0),
+    )(arrived, entry, rows, *saved, *weights, *sides, *kept)
+    return (list(outs[:5]), outs[5], outs[7])
 
 
 def on_device(inputs, out_grad, query_counts, gains, shifts, w_qkv, w_out, w_up, b_up, w_down):
@@ -1619,23 +1913,42 @@
         active = (stage == turn).astype(jnp.int32)[None]
         arrived = []
         for cell in range(cell_count):
+            if fused and turn == 0 and cell == cell_count - 1:
+                continue
             sent, back = backward_tick(
                 active, incoming[cell], entries[turn][cell], rows, (packed, middle, slope), weights, back, cell, cell_count
             )
             if turn > 0:
                 arrived.append((along(sent, -1), jnp.ones((1,), F32)))
-        incoming = arrived
+        incoming = arrived if turn > 0 else incoming
+
+    def flat(array):
+        return array.reshape(cell_count * length, -1)
+
     input_grads, grad_packed, grad_branch, grad_inner, grad_ff, sums = back
+    if fused:
+        (input_grads, grad_packed, grad_branch, grad_inner, sums), down_share, up_part = last_backward(
+            incoming[-1][0],
+            entries[0][-1],
+            rows,
+            (packed, middle, slope),
+            weights,
+            (input_grads, grad_packed, grad_branch, flat(grad_inner), sums),
+            (flat(activated), flat(grad_ff), flat(second)),
+            ((0, 0, cut, 0), (0, cut, deep_own - cut, 1)),
+            shapes[3],
+            own,
+            count,
+        )
     sums = jnp.sum(sums, axis=0)
-
     small_part = small_pack(sums[0:2], sums[2:8], sums[8 : 8 + ups].reshape(deep), count)
-    sides = [
-        array.reshape(cell_count * length, -1)
-        for array in (lowered, grad_packed, mixed, grad_branch, second, grad_inner, activated, grad_ff)
-    ]
     if fused:
-        shares = weight_grads(small_part, sides, items, shapes, count)
+        shares = other_grads(
+            small_part, up_part, [flat(array) for array in (lowered, grad_packed, mixed, grad_branch)], items[:4], shapes, count
+        )
+        shares = list(shares) + [down_share]
     else:
+        sides = [flat(array) for array in (lowered, grad_packed, mixed, grad_branch, second, grad_inner, activated, grad_ff)]
         products = [dot_left(sides[at], sides[at + 1]).astype(LOW) for at in (0, 2, 4, 6)]
         parts = [small_part] + [whole.reshape((count,) + shape) for whole, shape in zip(products, shapes)]
         shares = scatter(parts, items, count)

time: 685 us -> 673 us (0.982)
  Pallas kernels: 558 us -> 544 us
    pallas_call x4 -> x3, Pallas kernels: 112 us -> 69 us  [backward_tick(): pl.pallas_call(functools.partial(backward_kernel, cell, held), out_shape=...]
    pallas_call x1 -> x2, Pallas kernels: 212 us -> 240 us  [the longest x1 141 us: other_grads(): pl.pallas_call(functools.partial(other_grads_kernel, chips, width, items)...]
  transfers between devices with their start and end apart: 3 -> 3, of which waited for: 3 -> 3; matrix products, arithmetic and copies ran while one was open for 1% -> 1% of each run, Pallas kernels for 8% -> 9%
where the time goes in v6:
time: 673 us; the launch traced here: 664 us
  Pallas kernels  544 us (81%)
  waiting for transfers between devices  87.9 us (13%)
  local copies, waits for them, and re-layouts  20.6 us (3%)
  starting transfers between devices  7.14 us (1%)
    pallas_call x1, Pallas kernels, gather_forward(): pl.pallas_call(functools.partial(gather_forward_kernel, chips, items, gro...  224 us
    pallas_call x1, Pallas kernels, other_grads(): pl.pallas_call(functools.partial(other_grads_kernel, chips, width, items)...  141 us
    pallas_call x1, Pallas kernels, last_backward(): pl.pallas_call(functools.partial(last_backward_kernel, chips, items, cell...  98.7 us
    ppermute x3, waiting for transfers between devices, along(): return lax.ppermute(value, 'pipe', pairs)  87.9 us
    pallas_call x3, Pallas kernels, backward_tick(): pl.pallas_call(functools.partial(backward_kernel, cell, held), out_shape=...  69 us
  transfers between devices with their start and end apart: 3, of which 3 were waited for; matrix products, arithmetic and copies ran while one was open for 1% of the time, Pallas kernels for 9%

profile of v6, /device:TPU:0, one launch (start us, length us, event | category | flops | bytes accessed | tf_op | source)
XLA Modules:
  0.0 664.0 jit_solution(2732350572749519741)
XLA Ops:
  1.5 1.4 maximum_bitcast_fusion.refs_0_
  2.9 223.6 %shard_map.169 = (bf16[16,16,80]{2,1,0:T(8,128)(2,1)}, bf16[16,80,3840]{2,1,0:T(8,128)(2,1)}, bf16[16,80,1280]{2,1,0:T(8,128)(2,1)}, bf16[16,80,5120]{2,1,0:T(8,...) custom-call(bf16[16,80]{1,0:T(8,128)(2,1)} %maximum_bitcast_fusion.r, ...), custom_call_target="tpu_custom_call" | custom-call | flops 30198988800 | bytes 157286400 | tf_op jit(solution)/shard_map/pallas_call | solution.py:1148
  226.4 4.6 collective-permute-start
  232.2 1.6 shard_map.170
  233.8 1.4 slice_bitcast_fusion
  235.2 0.9 copy-done.2
  236.1 1.4 slice_bitcast_fusion.2
  237.5 11.5 %collective-permute-done.entry_h = bf16[384,1280]{1,0:T(8,128)(2,1)S(1)} collective-permute-done((bf16[384,1280]{1,0:T(8,128)(2,1)}, bf16[384,1280]{1,0:T(8,128)(2,1)S(1)}, u32[]{:S(2)}, u32[]{:S(2)}) %collective-permute-start) | collective-permute-done | bytes 983072 | tf_op jit(solution)/shard_map/ppermute | solution.py:1894
  249.0 0.9 copy-done.7
  249.9 9.4 %shard_map.171 = (bf16[384,1280]{1,0:T(8,128)(2,1)}, bf16[2,384,1280]{2,1,0:T(8,128)(2,1)}, bf16[2,384,1280]{2,1,0:T(8,128)(2,1)}, bf16[2,384,3840]{2,1,0:T(8,12...) custom-call(s32[1]{0:T(128)} %bitcast.active, ...), custom_call_target="tpu_custom_call", output_to_operand_aliasing={{1}: (7, {}), {2}: (8, {}), {3}: (9, {}), {4}: (10, {}), {5... | custom-call | flops 18119393280 | bytes 39321600 | tf_op jit(solution)/shard_map/pallas_call | solution.py:558
  259.3 13.7 %shard_map.172 = (bf16[384,1280]{1,0:T(8,128)(2,1)}, bf16[2,384,1280]{2,1,0:T(8,128)(2,1)}, bf16[2,384,3840]{2,1,0:T(8,128)(2,1)}, bf16[2,384,1280]{2,1,0:T(8,12...) custom-call(s32[1]{0:T(128)} %bitcast.active, ...), custom_call_target="tpu_custom_call" | custom-call | flops 22649241600 | bytes 39321600 | tf_op jit(solution)/shard_map/pallas_call | solution.py:720
  273.0 1.3 collective-permute-start.2
  274.3 12.5 %shard_map.173 = (bf16[384,1280]{1,0:T(8,128)(2,1)}, bf16[2,384,1280]{2,1,0:T(8,128)(2,1)}, bf16[2,384,3840]{2,1,0:T(8,128)(2,1)}, bf16[2,384,1280]{2,1,0:T(8,12...) custom-call(s32[1]{0:T(128)} %bitcast.active, ...), custom_call_target="tpu_custom_call", output_to_operand_aliasing={{1}: (12, {}), {2}: (13, {}), {3}: (14, {}), {4}: (15, {}),... | custom-call | flops 22649241600 | bytes 39321600 | tf_op jit(solution)/shard_map/pallas_call | solution.py:720
  286.8 1.3 collective-permute-start.1
  288.1 75.1 %collective-permute-done.2.grad_h = bf16[384,1280]{1,0:T(8,128)(2,1)S(1)} collective-permute-done((bf16[384,1280]{1,0:T(8,128)(2,1)}, bf16[384,1280]{1,0:T(8,128)(2,1)S(1)}, u32[]{:S(2)}, u32[]{:S(2)}) %collective-permute-start.2) | collective-permute-done | bytes 983072 | tf_op jit(solution)/shard_map/ppermute | solution.py:1894
  363.2 0.9 copy-done.11
  364.2 42.8 %shard_map.174 = (bf16[384,1280]{1,0:T(8,128)(2,1)}, bf16[2,384,1280]{2,1,0:T(8,128)(2,1)}, bf16[2,384,3840]{2,1,0:T(8,128)(2,1)}, bf16[2,384,1280]{2,1,0:T(8,12...) custom-call(s32[1]{0:T(128)} %bitcast.15.active, ...), custom_call_target="tpu_custom_call", output_to_operand_aliasing={{1}: (12, {}), {2}: (13, {}), {3}: (14, {}), {4}: (15, {}),... | custom-call | flops 22649241600 | bytes 39321600 | tf_op jit(solution)/shard_map/pallas_call | solution.py:720
  407.0 1.3 collective-permute-done.1.refs_0_
  408.3 0.9 copy-done.10
  409.2 98.7 %shard_map.175 = (bf16[2,384,1280]{2,1,0:T(8,128)(2,1)}, bf16[2,384,3840]{2,1,0:T(8,128)(2,1)}, bf16[2,384,1280]{2,1,0:T(8,128)(2,1)}, bf16[768,5120]{1,0:T(8,12...) custom-call(bf16[384,1280]{1,0:T(8,128)(2,1)} %copy-done.10, ...), custom_call_target="tpu_custom_call", output_to_operand_aliasing={{0}: (13, {}), {1}: (14, {}), {2}: (15, {}), {3}: (16, {}),... | custom-call | flops 35232153600 | bytes 131072000 | tf_op jit(solution)/shard_map/pallas_call | solution.py:1789
  507.9 0.9 reduce_sum.9
  509.2 0.7 maximum_maximum_fusion.refs_0_
  510.0 141.3 %shard_map.176 = (f32[16,80]{1,0:T(8,128)}, f32[80,3840]{1,0:T(8,128)}, f32[80,1280]{1,0:T(8,128)}, f32[80,5120]{1,0:T(8,128)}, bf16[16,80,3840]{2,1,0:T(8,128)(2,1)}, /*index=5*/bf16[16,80,1280]{2,1,0:T(8,128)(2,1)}) custom-call(f32[16,16,80]{2,1,0:T(8,128)} %maximum_maximum_fusion.refs_0_, bf16[16,80,5120]{2,1,0:T(8,128)(2,1)} %get-tuple-element.121.refs_1_, ...), custom_call_target="tpu_custom_call" | custom-call | flops 10066329600 | bytes 131072000 | tf_op jit(solution)/shard_map/pallas_call | solution.py:1485
  652.7 1.2 slice.51
  655.1 1.3 copy.99
  656.4 1.0 copy-done.3
  657.4 1.3 copy.100
  658.7 0.7 copy-done.6
  659.4 1.0 copy.101
  660.7 0.8 copy.102
  661.4 1.2 copy.103
  662.6 1.2 copy.104
  (40 shorter events, 5.2 us)
Async XLA Ops:
  2.9 228.1 %copy-start.12 = (s32[2]{0:T(128)S(1)}, s32[2]{0:T(128)}, u32[]{:S(2)}) copy-start(s32[2]{0:T(128)} %param.12) | copy-start | bytes 28
  226.4 22.5 %collective-permute-start = (bf16[384,1280]{1,0:T(8,128)(2,1)}, bf16[384,1280]{1,0:T(8,128)(2,1)S(1)}, u32[]{:S(2)}, u32[]{:S(2)}) collective-permute-start(bf16[384,1280]{1,0:T(8,128)(2,1)} %get-tuple-element.70), channel_id=1, source_target_pairs={{0,16},{1,17},{2,18},{3,19},{4,20},{5,21},{6,22},{7,23},{8,24},{9,... | collective-permute-start | bytes 2949128 | tf_op jit(solution)/shard_map/ppermute | solution.py:1894
  232.2 1.6 copy-start.1
  233.8 2.3 copy-start.2
  249.0 0.9 copy-start.7
  273.0 90.2 %collective-permute-start.2 = (bf16[384,1280]{1,0:T(8,128)(2,1)}, bf16[384,1280]{1,0:T(8,128)(2,1)S(1)}, u32[]{:S(2)}, u32[]{:S(2)}) collective-permute-start(bf16[384,1280]{1,0:T(8,128)(2,1)} %get-tuple-element.105), channel_id=1, source_target_pairs={{16,0},{17,1},{18,2},{19,3},{20,4},{21,5},{22,6},{23,7},{24,8},{25... | collective-permute-start | bytes 2949128 | tf_op jit(solution)/shard_map/ppermute | solution.py:1894
  286.8 121.5 %collective-permute-start.1 = (bf16[384,1280]{1,0:T(8,128)(2,1)}, bf16[384,1280]{1,0:T(8,128)(2,1)S(1)}, u32[]{:S(2)}, u32[]{:S(2)}) collective-permute-start(bf16[384,1280]{1,0:T(8,128)(2,1)} %get-tuple-element.103), channel_id=1, source_target_pairs={{16,0},{17,1},{18,2},{19,3},{20,4},{21,5},{22,6},{23,7},{24,8},{25... | collective-permute-start | bytes 2949128 | tf_op jit(solution)/shard_map/ppermute | solution.py:1894
  363.2 0.9 copy-start.11
  408.3 0.9 copy-start.10
  409.2 100.0 %copy-start.9 = (f32[16]{0:T(128)S(1)}, f32[16]{0:T(128)}, u32[]{:S(2)}) copy-start(f32[16]{0:T(128)} %pad.3.clone) | copy-start | bytes 196
  510.0 145.2 %copy-start = (bf16[2,384,1280]{2,1,0:T(8,128)(2,1)S(1)}, bf16[2,384,1280]{2,1,0:T(8,128)(2,1)}, u32[]{:S(2)}) copy-start(bf16[2,384,1280]{2,1,0:T(8,128)(2,1)} %get-tuple-element.93) | copy-start | bytes 5898244
  655.1 2.3 copy-start.3
  657.4 2.0 copy-start.6
  659.4 1.3 copy-start.8
  659.4 2.0 copy-start.5
  660.7 1.9 copy-start.4

commit v7 on v6

--- a/solution.py
+++ b/solution.py
@@ -1188,15 +1188,15 @@
 
 
 class RingSum:
-    def __init__(self, chips, items, parts, outs, landed, paired, mine, final, sems):
+    def __init__(self, chips, items, parts, outs, landed, paired, buffers, final, sems):
         self.chips, self.items, self.parts, self.outs = (chips, items, parts, outs)
-        self.landed, self.paired, self.mine, self.final = (landed, paired, mine, final)
-        self.ring_send, self.ring_recv, self.pair_send, self.pair_recv, self.mine_sem, self.final_sem = sems
+        self.landed, self.paired, self.final = (landed, paired, final)
+        self.mine, self.pairs, self.rings = buffers
+        self.ring_send, self.ring_recv, self.pair_send, self.pair_recv, self.load_sem, self.final_sem = sems
         self.half = chips // 2
         self.me, self.core, self.position, self.right, self.left, self.sibling = ring_place(chips)
-        self.sent, self.final_copies, self.exchanged = ([], [], [])
+        self.sent, self.final_copies, self.exchanged = ({}, [], [])
         self.uses = [0] * len(items)
-        self.fetched = None
 
     def part(self, item, block):
         array, start, rows, _ = self.items[item]
@@ -1222,14 +1222,10 @@
             device_id_type=MESH,
         )
 
-    def ring_copy(self, item, way, step):
-        if step == self.first(item, way):
-            source = self.paired[item].at[self.offset_of(step, way)]
-        else:
-            source = self.landed[item].at[self.slot_of(item, way, step - 1)]
+    def ring_copy(self, item, way, step, buffer=0):
         here = self.slot_of(item, way, step)
         return pltpu.make_async_remote_copy(
-            src_ref=source,
+            src_ref=self.mine[item].at[buffer],
             dst_ref=self.landed[item].at[here],
             send_sem=self.ring_send.at[item, here],
             recv_sem=self.ring_recv.at[item, here],
@@ -1237,9 +1233,19 @@
             device_id_type=MESH,
         )
 
-    def load(self, item, offset, buffer):
+    def load_mine(self, item, offset, buffer):
         block = ring_chip(self.position + offset, self.chips) * 2 + self.core
-        return pltpu.make_async_copy(self.part(item, block), self.mine[item].at[buffer], self.mine_sem.at[item, buffer])
+        return pltpu.make_async_copy(self.part(item, block), self.mine[item].at[buffer], self.load_sem.at[item, buffer])
+
+    def load_pair(self, item, offset, buffer):
+        return pltpu.make_async_copy(
+            self.paired[item].at[offset], self.pairs[item].at[buffer], self.load_sem.at[item, 2 + buffer]
+        )
+
+    def load_ring(self, item, way, step, buffer):
+        return pltpu.make_async_copy(
+            self.landed[item].at[self.slot_of(item, way, step)], self.rings[item].at[buffer], self.load_sem.at[item, 4 + buffer]
+        )
 
     def exchange(self, wanted, offsets):
         for offset in offsets:
@@ -1256,14 +1262,23 @@
             if step == self.first(item, way)
         ]
 
-    def rest(self, wanted):
+    def rest(self, wanted, steps):
         return [
             (step, item, way, self.offset_of(step, way))
-            for step in range(2, self.half + 1)
+            for step in steps
+            if step <= self.half
             for item in wanted
             for way in (0, 1)
             if step > self.first(item, way)
-        ] + [(self.half + 1, item, None, 0) for item in wanted]
+        ] + [(step, item, None, 0) for step in steps if step > self.half for item in wanted]
+
+    def fetch(self, entry):
+        step, item, way, offset, buffer = entry
+        if (item, buffer) in self.sent:
+            self.sent.pop((item, buffer)).wait_send()
+        self.load_mine(item, offset, buffer).start()
+        self.pair_copy(item, offset).wait_recv()
+        self.load_pair(item, offset, buffer).start()
 
     def run(self, plan, between=None):
         numbered = []
@@ -1272,10 +1287,9 @@
             self.uses[entry[1]] += 1
         for number, entry in enumerate(numbered):
             if number == 0:
-                self.load(entry[1], entry[3], entry[4]).start()
+                self.fetch(entry)
             if number + 1 < len(numbered):
-                later = numbered[number + 1]
-                self.load(later[1], later[3], later[4]).start()
+                self.fetch(numbered[number + 1])
             self.work(entry)
             if between is not None:
                 between()
@@ -1284,18 +1298,20 @@
         step, item, way, offset, buffer = entry
         array, start, rows, _ = self.items[item]
         half, final = (self.half, self.final)
-        self.load(item, offset, buffer).wait()
-        self.pair_copy(item, offset).wait_recv()
         kind = self.parts[array].dtype
         columns = self.parts[array].shape[2]
         chunk = 16
-        from_pair, from_mine, from_ring = (self.paired[item], self.mine[item], self.landed[item])
+        mine, pairs, rings = (self.mine[item], self.pairs[item], self.rings[item])
         if way is None:
-            self.ring_copy(item, 0, half).wait_recv()
-            self.ring_copy(item, 1, half).wait_recv()
-            slot_a, slot_b = (self.slot_of(item, 0, half), self.slot_of(item, 1, half))
+            for side in (0, 1):
+                self.ring_copy(item, side, half).wait_recv()
+                self.load_ring(item, side, half, side).start()
+            self.load_mine(item, offset, buffer).wait()
+            self.load_pair(item, offset, buffer).wait()
+            for side in (0, 1):
+                self.load_ring(item, side, half, side).wait()
             if kind == F32:
-                self.outs[array][...] = (from_ring[slot_a] + from_ring[slot_b]) + (from_mine[buffer] + from_pair[offset])
+                self.outs[array][...] = (rings[0] + rings[1]) + (mine[buffer] + pairs[buffer])
                 return
             high, wide = (min(rows, final.shape[1]), min(columns, final.shape[2]))
             for top in range(0, rows, high):
@@ -1310,8 +1326,8 @@
                     def _(index):
                         here = pl.ds(pl.multiple_of(top + index * chunk, chunk), chunk)
                         final[turn, pl.ds(pl.multiple_of(index * chunk, chunk), chunk), pl.ds(0, wide)] = (
-                            from_ring[slot_a, here, span].astype(F32) + from_ring[slot_b, here, span].astype(F32)
-                        ) + (from_mine[buffer, here, span].astype(F32) + from_pair[offset, here, span].astype(F32))
+                            rings[0, here, span].astype(F32) + rings[1, here, span].astype(F32)
+                        ) + (mine[buffer, here, span].astype(F32) + pairs[buffer, here, span].astype(F32))
 
                     self.final_copies.append(
                         pltpu.make_async_copy(
@@ -1322,57 +1338,34 @@
                     )
                     self.final_copies[-1].start()
             return
-        if step == self.first(item, way):
-
-            @pl.loop(0, rows // chunk)
-            def _(index):
-                here = pl.ds(pl.multiple_of(index * chunk, chunk), chunk)
-                from_pair[offset, here, :] = (
-                    from_mine[buffer, here, :].astype(F32) + from_pair[offset, here, :].astype(F32)
-                ).astype(kind)
-
-        else:
+        carried = step > self.first(item, way)
+        if carried:
             self.ring_copy(item, way, step - 1).wait_recv()
-            arrived = self.slot_of(item, way, step - 1)
-
-            @pl.loop(0, rows // chunk)
-            def _(index):
-                here = pl.ds(pl.multiple_of(index * chunk, chunk), chunk)
-                from_ring[arrived, here, :] = (
-                    from_ring[arrived, here, :].astype(F32)
-                    + (from_mine[buffer, here, :].astype(F32) + from_pair[offset, here, :].astype(F32))
-                ).astype(kind)
-
-        self.sent.append(self.ring_copy(item, way, step))
-        self.sent[-1].start()
+            self.load_ring(item, way, step - 1, buffer).start()
+        self.load_mine(item, offset, buffer).wait()
+        self.load_pair(item, offset, buffer).wait()
+        if carried:
+            self.load_ring(item, way, step - 1, buffer).wait()
+
+        @pl.loop(0, rows // chunk)
+        def _(index):
+            here = pl.ds(pl.multiple_of(index * chunk, chunk), chunk)
+            total = mine[buffer, here, :].astype(F32) + pairs[buffer, here, :].astype(F32)
+            if carried:
+                total = rings[buffer, here, :].astype(F32) + total
+            mine[buffer, here, :] = total.astype(kind)
+
+        copy = self.ring_copy(item, way, step, buffer)
+        copy.start()
+        self.sent[(item, buffer)] = copy
 
     def close(self):
-        for copy in self.sent:
+        for copy in self.sent.values():
             copy.wait_send()
         for item, offset in self.exchanged:
             self.pair_copy(item, offset).wait_send()
         for copy in self.final_copies[-self.final.shape[0] :]:
             copy.wait()
-
-
-def ring_scratch(chips, items, shapes, kinds, pieces_rows):
-    held = [(rows,) + tuple(shapes[array][1:]) for array, _, rows, _ in items]
-    kinds = [kinds[array] for array, _, _, _ in items]
-    pieces = len(items)
-    return (
-        [pltpu.VMEM((chips - 1,) + shape, kind) for shape, kind in zip(held, kinds)]
-        + [pltpu.VMEM((chips,) + shape, kind) for shape, kind in zip(held, kinds)]
-        + [pltpu.VMEM((2,) + shape, kind) for shape, kind in zip(held, kinds)]
-        + [pltpu.VMEM(pieces_rows, F32)]
-        + [
-            pltpu.SemaphoreType.DMA((pieces, chips - 1)),
-            pltpu.SemaphoreType.DMA((pieces, chips - 1)),
-            pltpu.SemaphoreType.DMA((pieces, chips)),
-            pltpu.SemaphoreType.DMA((pieces, chips)),
-            pltpu.SemaphoreType.DMA((pieces, 2)),
-            pltpu.SemaphoreType.DMA((pieces_rows[0],)),
-        ]
-    )
 
 
 class Products:
@@ -1435,97 +1428,30 @@
             self.keep(target, index).wait()
 
 
-def other_grads_kernel(chips, width, items, *refs):
-    count = len(items)
-    small_part, up_part, lowered, grad_packed, mixed, grad_branch = refs[:6]
-    outs = refs[6:10]
-    parts = [small_part, refs[10], refs[11], up_part]
-    refs = refs[12:]
-    landed, paired, mine, final = (refs[:count], refs[count : 2 * count], refs[2 * count : 3 * count], refs[3 * count])
-    sems = refs[3 * count + 1 : 3 * count + 7]
-    big, cuts, stage, big_sem, cut_sem, stage_sem = refs[3 * count + 7 :]
-    ring = RingSum(chips, items, parts, outs, landed, paired, mine, final, sems)
-    products = Products(chips, width, width // (2 * chips), cuts, big, stage, cut_sem, big_sem, stage_sem)
-    products.open(mixed, grad_branch, 1)
-    greet((ring.left, ring.right, ring.sibling))
-    half = ring.half
-    far = [half, half - 1, half + 1]
-    order = far + [offset for offset in range(chips) if offset not in far]
-    ups = [item for item in range(count) if items[item][0] == 3]
-    others = [item for item in range(count) if items[item][0] < 3]
-    smalls = [item for item in others if items[item][0] == 0]
-    heads = [item for item in others if items[item][0] > 0]
-    head_blocks = grad_packed.shape[1] // width
-    ring.exchange(ups, order)
-    ring.exchange(smalls, order)
-    products.run(parts[2], mixed, grad_branch, 1, 0, 2)
-    products.open(lowered, grad_packed, 0)
-    ring.run(ring.starts(ups))
-    ring.run(ring.starts(smalls))
-    products.run(parts[1], lowered, grad_packed, 0, 0, head_blocks)
-    rest = ring.rest(ups + heads + smalls)
-    early = [entry for entry in rest if entry[1] in ups and entry[0] == 2]
-    ring.run(early)
-    products.run(parts[1], lowered, grad_packed, 0, head_blocks, 2 * head_blocks)
-    ring.exchange(heads, order)
-    soon = [entry for entry in rest if entry[1] in ups and entry[0] == 3]
-    ring.run(soon)
-    ring.run(ring.starts(heads))
-    ring.run([entry for entry in rest if entry not in early + soon])
-    ring.close()
-
-
-def other_grads(small_part, up_part, sides, items, shapes, count):
-    chips = count // 2
-    rows_in, width = sides[0].shape
-    wholes = [small_part.shape[1:]] + [tuple(shape) for shape in shapes[:3]]
-    hbm = pl.BlockSpec(memory_space=pl.ANY)
-    cut = width // 2
-    flops = 2 * rows_in * 4 * width * width
-    outs = pl.pallas_call(
-        functools.partial(other_grads_kernel, chips, width, items),
-        out_shape=[jax.ShapeDtypeStruct(shape, F32) for shape in wholes]
-        + [jax.ShapeDtypeStruct((count,) + shape, LOW) for shape in wholes[1:3]],
-        in_specs=[hbm] * 6,
-        out_specs=[pl.BlockSpec(memory_space=pltpu.VMEM)] + [hbm] * 5,
-        scratch_shapes=ring_scratch(chips, items, wholes, [F32, LOW, LOW, LOW], (4, shapes[0][0], width))
-        + [
-            pltpu.VMEM((2, rows_in, width), LOW),
-            pltpu.VMEM((2, rows_in, cut), LOW),
-            pltpu.VMEM((2, chips, width // count, width), LOW),
-            pltpu.SemaphoreType.DMA((2,)),
-            pltpu.SemaphoreType.DMA((2,)),
-            pltpu.SemaphoreType.DMA((2,)),
-        ],
-        compiler_params=pltpu.CompilerParams(
-            collective_id=2, has_side_effects=True, vmem_limit_bytes=62 * 2**20
-        ),
-        cost_estimate=pl.CostEstimate(flops=flops, bytes_accessed=80 * width * width, transcendentals=0),
-    )(small_part, up_part, *sides)
-    return outs[:4]
-
-
 def last_backward_kernel(chips, items, cell, *refs):
     count = len(items)
     (grad_h, entry_h, rows, packed_h, middle_h, slope_h, w_qkv, w_out, w_up, w_down) = refs[:10]
-    (activated_h, grad_ff_h, second_h) = refs[10:13]
-    refs = refs[13 + 5 :]
+    (activated_h, grad_ff_h, second_h, mixed_h, lowered_h) = refs[10:15]
+    refs = refs[15 + 5 :]
     rows_o, packed_o, branch_o, inner_o, sums_o = refs[:5]
-    share_o, down_part, up_part = refs[5:8]
-    refs = refs[8:]
-    landed, paired, mine, final = (refs[:count], refs[count : 2 * count], refs[2 * count : 3 * count], refs[3 * count])
-    sems = refs[3 * count + 1 : 3 * count + 7]
-    (big, cuts, stage, stage_down, big_sem, cut_sem, stage_sem) = refs[3 * count + 7 : 3 * count + 14]
-    (buffers, buffer_sems, load_sems, save_sems, slope_sems, inner_sems) = refs[3 * count + 14 : 3 * count + 20]
-    (grad, entry, packed_v, middle_v, slope_v, inner_v, grad_packed_v, mixed_v, branch_v, grad_act_v, total_v, sums_v) = refs[
-        3 * count + 20 :
-    ]
+    outs, parts = (refs[5:10], refs[10:14])
+    landed, paired = (refs[14 : 14 + count], refs[14 + count : 14 + 2 * count])
+    refs = refs[14 + 2 * count :]
+    ring_buffers = (refs[:count], refs[count : 2 * count], refs[2 * count : 3 * count])
+    final, small_v, both_v = refs[3 * count : 3 * count + 3]
+    sems = refs[3 * count + 3 : 3 * count + 9]
+    refs = refs[3 * count + 9 :]
+    (big, cuts, stage, stage_down, big_sem, cut_sem, stage_sem) = refs[:7]
+    (buffers, buffer_sems, load_sems, save_sems, slope_sems, inner_sems) = refs[7:13]
+    (grad, entry, packed_v, middle_v, slope_v, inner_v, grad_packed_v, mixed_v, branch_v, grad_act_v, total_v, sums_v) = refs[13:]
+    parts = [small_v] + list(parts)
+    down_part, up_part = (parts[4], parts[3])
     length, width = grad.shape
     devices = 2 * chips
     deep_own = down_part.shape[1]
     ups = w_up.shape[1] // width
     first = lax.axis_index("pipe") == 0
-    ring = RingSum(chips, items, [down_part], [share_o], landed, paired, mine, final, sems)
+    ring = RingSum(chips, items, parts, outs, landed, paired, ring_buffers, final, sems)
     half, position = (ring.half, ring.position)
     products = Products(chips, width, width // devices, cuts, big, stage, cut_sem, big_sem, stage_sem)
     gains = rows.at[0:2]
@@ -1625,8 +1551,8 @@
 
     def save(number, wait=False):
         source, target = (
-            (branch_v, branch_o.at[cell]),
-            (grad_packed_v, packed_o.at[cell]),
+            (branch_v, branch_o.at[pl.ds(cell * length, length)]),
+            (grad_packed_v, packed_o.at[pl.ds(cell * length, length)]),
             (sums_v, sums_o.at[cell]),
             (mixed_v, rows_o.at[cell]),
         )[number]
@@ -1690,6 +1616,7 @@
         branch_v[...] = grad_middle.astype(LOW)
         sums_v[5:6, :] = column_sum(branch_v[...])
         save(0)
+        save(0, wait=True)
         for at in range(max(0, ups - 2), ups):
             inner_save(at).wait()
 
@@ -1709,6 +1636,7 @@
         save(1)
         sums_v[3:4, :] = column_sum(grad_packed_v[:, pl.ds(0, width)])
         sums_v[4:5, :] = column_sum(grad_packed_v[:, pl.ds(2 * width, width)])
+        save(1, wait=True)
 
     def lower(number):
         def step():
@@ -1732,77 +1660,151 @@
         save(2)
         save(3)
 
-    queue = [(True, climb(number)) for number in range(ups + 1)] + [(True, turn)]
-    queue.append((False, lambda: products.open(second_h, inner_o, 1)))
-    for low in range(0, 2 * ups, 2):
-        queue.append((False, lambda low=low: products.run(up_part, second_h, inner_o, 1, low, low + 2)))
-    queue.append((True, outer))
+    def lay_small():
+        @pl.when(first)
+        def _():
+            save(2, wait=True)
+
+        copy = pltpu.make_async_copy(sums_o, both_v, load_sems.at[0])
+        copy.start()
+        copy.wait()
+        sums = both_v[0]
+        for at in range(1, cell + 1):
+            sums = sums + both_v[at]
+        own = width // devices
+        windows = [pltpu.roll(sums, (width - at * own) % width, 1)[:, :own] for at in range(devices)]
+        share = devices // ups
+        for device in range(devices):
+            small_v[device, 0:8, :] = windows[device][0:8]
+            for up in range(ups):
+                row = 8 + device // share
+                small_v[device, 8 + up : 9 + up, :] = windows[device % share * ups + up][row : row + 1]
+            small_v[device, 8 + ups : 16, :] = jnp.zeros((8 - ups, own), F32)
+
     pairs = width // 128
-    queue += [(True, heads(low, low + 2)) for low in range(0, pairs, 2)]
-    queue.append((True, sums))
-    queue += [(True, lower(number)) for number in range(3)] + [(True, finish)]
-
-    def serve():
-        if queue:
-            own, step = queue.pop(0)
-            if own:
-                pl.when(first)(step)
-            else:
-                step()
-
-    greet((ring.left, ring.right, ring.sibling))
+    head_blocks = packed_o.shape[1] // width
+    downs = [item for item in range(count) if items[item][0] == 4]
+    up_items = [item for item in range(count) if items[item][0] == 3]
+    outers = [item for item in range(count) if items[item][0] == 2]
+    head_items = [item for item in range(count) if items[item][0] == 1]
+    smalls = [item for item in range(count) if items[item][0] == 0]
     far = [half, half - 1, half + 1]
     near = [offset for offset in range(chips) if offset not in far]
-    every = list(range(count))
+    everywhere = far + near
+
+    def work(*steps):
+        for step in steps:
+            pl.when(first)(step)
+
+    def up_products(low, high):
+        products.run(up_part, second_h, inner_o, 1, low, high)
+
+    def head_products(low, high):
+        products.run(parts[1], lowered_h, packed_o, 0, low, high)
+
+    greet((ring.left, ring.right, ring.sibling))
     for at in range(cell + 1):
         ff_load(at).wait()
     down_products(0, 3)
-    ring.exchange(every, far)
+    ring.exchange(downs, far)
     down_products(3, 5)
-    pl.when(first)(begin)
-    ring.run(ring.starts(every))
+    work(begin)
+    ring.run(ring.starts(downs))
     down_products(5, chips)
-    ring.exchange(every, near)
-    for _ in range(3):
-        serve()
-    ring.run(ring.rest(every), lambda: (serve(), serve()))
-    while queue:
-        serve()
+    ring.exchange(downs, near)
+    later = [climb(number) for number in range(ups + 1)] + [turn]
+
+    def between():
+        if later:
+            work(later.pop(0))
+
+    work(later.pop(0), later.pop(0))
+    ring.run(ring.rest(downs, (2,)), between)
+    ring.run(ring.rest(downs, (3,)), between)
+    while later:
+        between()
+    products.open(second_h, inner_o, 1)
+    up_products(0, ups)
+    ring.run(ring.rest(downs, (4,))[:2])
+    up_products(ups, 2 * ups)
+    ring.exchange(up_items, everywhere)
+    products.open(mixed_h, branch_o, 1)
+    ring.run(ring.rest(downs, (4,))[2:])
+    products.run(parts[2], mixed_h, branch_o, 1, 0, 2)
+    ring.exchange(outers, everywhere)
+    ring.run(ring.starts(up_items))
+    later = [outer] + [heads(low, low + 2) for low in range(0, pairs, 2)] + [sums]
+    work(later.pop(0), later.pop(0))
+    ring.run(ring.starts(outers), between)
+    ring.run(ring.rest(up_items + outers, (2,)), between)
+    while later:
+        between()
+    products.open(lowered_h, packed_o, 0)
+    head_products(0, head_blocks)
+    ring.run(ring.rest(up_items + outers, (3,))[:2])
+    head_products(head_blocks, 2 * head_blocks)
+    ring.exchange(head_items, everywhere)
+    ring.run(ring.rest(up_items + outers, (3,))[2:])
+    ring.run(ring.starts(head_items))
+    later = [lower(number) for number in range(3)] + [finish]
+    ring.run(ring.rest(head_items, (2,)), between)
+    while later:
+        between()
+    lay_small()
+    ring.exchange(smalls, everywhere)
+    ring.run(ring.rest(up_items + outers, (4,)))
+    ring.run(ring.starts(smalls))
+    ring.run(ring.rest(head_items, (3,)))
+    ring.run(ring.rest(smalls, (2, 3)))
+    ring.run(ring.rest(downs + up_items, (half + 1,)))
+    ring.run(ring.rest(smalls + head_items, (4,)))
+    ring.run(ring.rest(outers + smalls + head_items, (half + 1,)))
     ring.close()
 
     @pl.when(first)
     def _():
-        for number in range(4):
-            save(number, wait=True)
-
-
-def last_backward(arrived, entry, rows, saved, weights, kept, sides, items, down_shape, own, count):
+        save(3, wait=True)
+
+
+def last_backward(arrived, entry, rows, saved, weights, kept, sides, items, shapes, count):
     chips = count // 2
-    length, width = entry.shape
+    length, width = arrived.shape
     deep = weights[2].shape[1]
-    ups = deep // width
     cells = kept[0].shape[0]
     rows_in = cells * length
+    own = width // count
     hbm = pl.BlockSpec(memory_space=pl.ANY)
     cut = width // 2
-    flops = 2 * length * width * (4 * width + 2 * deep) + 4 * rows_in * width * deep
+    wholes = [(16, own)] + [tuple(shape) for shape in shapes]
+    held = [(many,) + wholes[array][1:] for array, _, many, _ in items]
+    kinds = [F32 if array == 0 else LOW for array, _, _, _ in items]
+    pieces = len(items)
+    flops = 2 * length * width * (4 * width + 2 * deep) + 2 * rows_in * width * (4 * width + 2 * deep)
     outs = pl.pallas_call(
         functools.partial(last_backward_kernel, chips, items, cells - 1),
         out_shape=[jax.ShapeDtypeStruct(array.shape, array.dtype) for array in kept]
+        + [jax.ShapeDtypeStruct(shape, F32) for shape in wholes]
+        + [jax.ShapeDtypeStruct((count,) + shape, LOW) for shape in wholes[1:]]
+        + [jax.ShapeDtypeStruct((chips - 1,) + shape, kind) for shape, kind in zip(held, kinds)]
+        + [jax.ShapeDtypeStruct((chips,) + shape, kind) for shape, kind in zip(held, kinds)],
+        in_specs=[hbm] * 2 + [pl.BlockSpec(memory_space=pltpu.VMEM)] + [hbm] * 17,
+        out_specs=[hbm] * 5 + [pl.BlockSpec(memory_space=pltpu.VMEM)] + [hbm] * (8 + 2 * pieces),
+        input_output_aliases={15 + number: number for number in range(5)},
+        scratch_shapes=[pltpu.VMEM((2,) + shape, kind) for shape, kind in zip(held, kinds)] * 3
         + [
-            jax.ShapeDtypeStruct(down_shape, F32),
-            jax.ShapeDtypeStruct((count,) + tuple(down_shape), LOW),
-            jax.ShapeDtypeStruct((count, own, deep), LOW),
-        ],
-        in_specs=[hbm] * 2 + [pl.BlockSpec(memory_space=pltpu.VMEM)] + [hbm] * 15,
-        out_specs=[hbm] * 8,
-        input_output_aliases={13 + number: number for number in range(5)},
-        scratch_shapes=ring_scratch(chips, items, [down_shape], [LOW], (4, 80, width))
-        + [
+            pltpu.VMEM((4, 80, width), F32),
+            pltpu.VMEM((count, 16, own), F32),
+            pltpu.VMEM((cells, 16, width), F32),
+            pltpu.SemaphoreType.DMA((pieces, chips - 1)),
+            pltpu.SemaphoreType.DMA((pieces, chips - 1)),
+            pltpu.SemaphoreType.DMA((pieces, chips)),
+            pltpu.SemaphoreType.DMA((pieces, chips)),
+            pltpu.SemaphoreType.DMA((pieces, 6)),
+            pltpu.SemaphoreType.DMA((4,)),
             pltpu.VMEM((2, rows_in, width), LOW),
             pltpu.VMEM((2, rows_in, cut), LOW),
             pltpu.VMEM((2, chips, own, width), LOW),
-            pltpu.VMEM((2, 2, down_shape[0], width), LOW),
+            pltpu.VMEM((2, 2, shapes[3][0], width), LOW),
             pltpu.SemaphoreType.DMA((2,)),
             pltpu.SemaphoreType.DMA((2,)),
             pltpu.SemaphoreType.DMA((4,)),
@@ -1826,11 +1828,11 @@
             pltpu.VMEM((16, width), F32),
         ],
         compiler_params=pltpu.CompilerParams(
-            collective_id=4, has_side_effects=True, vmem_limit_bytes=62 * 2**20
+            collective_id=2, has_side_effects=True, vmem_limit_bytes=62 * 2**20
         ),
-        cost_estimate=pl.CostEstimate(flops=flops, bytes_accessed=80 * width * width, transcendentals=0),
+        cost_estimate=pl.CostEstimate(flops=flops, bytes_accessed=160 * width * width, transcendentals=0),
     )(arrived, entry, rows, *saved, *weights, *sides, *kept)
-    return (list(outs[:5]), outs[5], outs[7])
+    return (list(outs[:5]), outs[5:10])
 
 
 def on_device(inputs, out_grad, query_counts, gains, shifts, w_qkv, w_out, w_up, b_up, w_down):
@@ -1927,27 +1929,21 @@
 
     input_grads, grad_packed, grad_branch, grad_inner, grad_ff, sums = back
     if fused:
-        (input_grads, grad_packed, grad_branch, grad_inner, sums), down_share, up_part = last_backward(
+        (input_grads, grad_packed, grad_branch, grad_inner, sums), shares = last_backward(
             incoming[-1][0],
             entries[0][-1],
             rows,
             (packed, middle, slope),
             weights,
-            (input_grads, grad_packed, grad_branch, flat(grad_inner), sums),
-            (flat(activated), flat(grad_ff), flat(second)),
-            ((0, 0, cut, 0), (0, cut, deep_own - cut, 1)),
-            shapes[3],
-            own,
+            (input_grads, flat(grad_packed), flat(grad_branch), flat(grad_inner), sums),
+            [flat(array) for array in (activated, grad_ff, second, mixed, lowered)],
+            items,
+            shapes,
             count,
         )
-    sums = jnp.sum(sums, axis=0)
-    small_part = small_pack(sums[0:2], sums[2:8], sums[8 : 8 + ups].reshape(deep), count)
-    if fused:
-        shares = other_grads(
-            small_part, up_part, [flat(array) for array in (lowered, grad_packed, mixed, grad_branch)], items[:4], shapes, count
-        )
-        shares = list(shares) + [down_share]
     else:
+        sums = jnp.sum(sums, axis=0)
+        small_part = small_pack(sums[0:2], sums[2:8], sums[8 : 8 + ups].reshape(deep), count)
         sides = [flat(array) for array in (lowered, grad_packed, mixed, grad_branch, second, grad_inner, activated, grad_ff)]
         products = [dot_left(sides[at], sides[at + 1]).astype(LOW) for at in (0, 2, 4, 6)]
         parts = [small_part] + [whole.reshape((count,) + shape) for whole, shape in zip(products, shapes)]

time: 673 us -> 676 us (level)
    pallas_call x1, Pallas kernels: 98.7 us -> 245 us  [last_backward(): pl.pallas_call(functools.partial(last_backward_kernel, chips, items, cell...]
    pallas_call x1 -> x0, Pallas kernels: 141 us -> none  [other_grads(): pl.pallas_call(functools.partial(other_grads_kernel, chips, width, items)...]
where the time goes in v7:
time: 676 us; the launch traced here: 666 us
  Pallas kernels  548 us (81%)
  waiting for transfers between devices  88 us (13%)
  local copies, waits for them, and re-layouts  19.7 us (3%)
  starting transfers between devices  7.14 us (1%)
    pallas_call x1, Pallas kernels, last_backward(): pl.pallas_call(functools.partial(last_backward_kernel, chips, items, cell...  245 us
    pallas_call x1, Pallas kernels, gather_forward(): pl.pallas_call(functools.partial(gather_forward_kernel, chips, items, gro...  224 us
    ppermute x3, waiting for transfers between devices, along(): return lax.ppermute(value, 'pipe', pairs)  88 us
    pallas_call x3, Pallas kernels, backward_tick(): pl.pallas_call(functools.partial(backward_kernel, cell, held), out_shape=...  69.1 us
  transfers between devices with their start and end apart: 3, of which 3 were waited for; matrix products, arithmetic and copies ran while one was open for 1% of the time, Pallas kernels for 9%

profile of v7, /device:TPU:0, one launch (start us, length us, event | category | flops | bytes accessed | tf_op | source)
XLA Modules:
  0.0 666.3 jit_solution(5711263011330938621)
XLA Ops:
  0.6 0.7 reduce
  1.5 1.4 maximum_bitcast_fusion.refs_0_
  2.9 223.6 %shard_map.169 = (bf16[16,16,80]{2,1,0:T(8,128)(2,1)}, bf16[16,80,3840]{2,1,0:T(8,128)(2,1)}, bf16[16,80,1280]{2,1,0:T(8,128)(2,1)}, bf16[16,80,5120]{2,1,0:T(8,...) custom-call(bf16[16,80]{1,0:T(8,128)(2,1)} %maximum_bitcast_fusion.r, ...), custom_call_target="tpu_custom_call" | custom-call | flops 30198988800 | bytes 157286400 | tf_op jit(solution)/shard_map/pallas_call | solution.py:1148
  226.4 4.6 collective-permute-start
  231.6 1.6 shard_map.170
  233.2 1.5 slice_bitcast_fusion
  234.7 0.8 copy-done.2
  235.5 1.4 slice_bitcast_fusion.2
  236.9 12.1 %collective-permute-done.entry_h = bf16[384,1280]{1,0:T(8,128)(2,1)S(1)} collective-permute-done((bf16[384,1280]{1,0:T(8,128)(2,1)}, bf16[384,1280]{1,0:T(8,128)(2,1)S(1)}, u32[]{:S(2)}, u32[]{:S(2)}) %collective-permute-start) | collective-permute-done | bytes 983072 | tf_op jit(solution)/shard_map/ppermute | solution.py:1896
  249.0 0.9 copy-done.7
  249.9 9.4 %shard_map.171 = (bf16[384,1280]{1,0:T(8,128)(2,1)}, bf16[2,384,1280]{2,1,0:T(8,128)(2,1)}, bf16[2,384,1280]{2,1,0:T(8,128)(2,1)}, bf16[2,384,3840]{2,1,0:T(8,12...) custom-call(s32[1]{0:T(128)} %bitcast.active, ...), custom_call_target="tpu_custom_call", output_to_operand_aliasing={{1}: (7, {}), {2}: (8, {}), {3}: (9, {}), {4}: (10, {}), {5... | custom-call | flops 18119393280 | bytes 39321600 | tf_op jit(solution)/shard_map/pallas_call | solution.py:558
  259.3 13.7 %shard_map.172 = (bf16[384,1280]{1,0:T(8,128)(2,1)}, bf16[2,384,1280]{2,1,0:T(8,128)(2,1)}, bf16[2,384,3840]{2,1,0:T(8,128)(2,1)}, bf16[2,384,1280]{2,1,0:T(8,12...) custom-call(s32[1]{0:T(128)} %bitcast.active, ...), custom_call_target="tpu_custom_call" | custom-call | flops 22649241600 | bytes 39321600 | tf_op jit(solution)/shard_map/pallas_call | solution.py:720
  273.0 1.3 collective-permute-start.2
  274.3 12.5 %shard_map.173 = (bf16[384,1280]{1,0:T(8,128)(2,1)}, bf16[2,384,1280]{2,1,0:T(8,128)(2,1)}, bf16[2,384,3840]{2,1,0:T(8,128)(2,1)}, bf16[2,384,1280]{2,1,0:T(8,12...) custom-call(s32[1]{0:T(128)} %bitcast.active, ...), custom_call_target="tpu_custom_call", output_to_operand_aliasing={{1}: (12, {}), {2}: (13, {}), {3}: (14, {}), {4}: (15, {}),... | custom-call | flops 22649241600 | bytes 39321600 | tf_op jit(solution)/shard_map/pallas_call | solution.py:720
  286.8 1.3 collective-permute-start.1
  288.1 74.6 %collective-permute-done.2.grad_h = bf16[384,1280]{1,0:T(8,128)(2,1)S(1)} collective-permute-done((bf16[384,1280]{1,0:T(8,128)(2,1)}, bf16[384,1280]{1,0:T(8,128)(2,1)S(1)}, u32[]{:S(2)}, u32[]{:S(2)}) %collective-permute-start.2) | collective-permute-done | bytes 983072 | tf_op jit(solution)/shard_map/ppermute | solution.py:1896
  362.7 0.9 copy-done.10
  363.7 42.8 %shard_map.174 = (bf16[384,1280]{1,0:T(8,128)(2,1)}, bf16[2,384,1280]{2,1,0:T(8,128)(2,1)}, bf16[2,384,3840]{2,1,0:T(8,128)(2,1)}, bf16[2,384,1280]{2,1,0:T(8,12...) custom-call(s32[1]{0:T(128)} %bitcast.15.active, ...), custom_call_target="tpu_custom_call", output_to_operand_aliasing={{1}: (12, {}), {2}: (13, {}), {3}: (14, {}), {4}: (15, {}),... | custom-call | flops 22649241600 | bytes 39321600 | tf_op jit(solution)/shard_map/pallas_call | solution.py:720
  406.5 1.3 collective-permute-done.1.refs_0_
  407.8 0.9 copy-done.9
  408.8 244.9 %shard_map.175 = (bf16[2,384,1280]{2,1,0:T(8,128)(2,1)}, bf16[768,3840]{1,0:T(8,128)(2,1)}, bf16[768,1280]{1,0:T(8,128)(2,1)}, bf16[768,5120]{1,0:T(8,128)(2,1)}...) custom-call(bf16[384,1280]{1,0:T(8,128)(2,1)} %copy-done.9, ...), custom_call_target="tpu_custom_call", output_to_operand_aliasing={{0}: (15, {}), {1}: (16, {}), {2}: (17, {}), {3}: (18, {}),... | custom-call | flops 45298483200 | bytes 262144000 | tf_op jit(solution)/shard_map/pallas_call | solution.py:1783
  653.6 1.2 slice.36
  654.9 0.7 slice.38
  655.6 0.7 slice.37
  657.5 1.3 copy.92
  658.7 1.0 copy-done.3
  659.7 1.3 copy.93
  661.0 0.7 copy-done.6
  661.7 1.0 copy.94
  663.0 0.8 copy.95
  663.7 1.2 copy.96
  664.9 1.2 copy.97
  (25 shorter events, 2.2 us)
Async XLA Ops:
  2.9 228.1 %copy-start.11 = (s32[2]{0:T(128)S(1)}, s32[2]{0:T(128)}, u32[]{:S(2)}) copy-start(s32[2]{0:T(128)} %param.12) | copy-start | bytes 28
  226.4 22.5 %collective-permute-start = (bf16[384,1280]{1,0:T(8,128)(2,1)}, bf16[384,1280]{1,0:T(8,128)(2,1)S(1)}, u32[]{:S(2)}, u32[]{:S(2)}) collective-permute-start(bf16[384,1280]{1,0:T(8,128)(2,1)} %get-tuple-element.66), channel_id=1, source_target_pairs={{0,16},{1,17},{2,18},{3,19},{4,20},{5,21},{6,22},{7,23},{8,24},{9,... | collective-permute-start | bytes 2949128 | tf_op jit(solution)/shard_map/ppermute | solution.py:1896
  231.6 1.6 copy-start.1
  233.2 2.3 copy-start.2
  249.0 0.9 copy-start.7
  273.0 89.7 %collective-permute-start.2 = (bf16[384,1280]{1,0:T(8,128)(2,1)}, bf16[384,1280]{1,0:T(8,128)(2,1)S(1)}, u32[]{:S(2)}, u32[]{:S(2)}) collective-permute-start(bf16[384,1280]{1,0:T(8,128)(2,1)} %get-tuple-element.101), channel_id=1, source_target_pairs={{16,0},{17,1},{18,2},{19,3},{20,4},{21,5},{22,6},{23,7},{24,8},{25... | collective-permute-start | bytes 2949128 | tf_op jit(solution)/shard_map/ppermute | solution.py:1896
  286.8 121.0 %collective-permute-start.1 = (bf16[384,1280]{1,0:T(8,128)(2,1)}, bf16[384,1280]{1,0:T(8,128)(2,1)S(1)}, u32[]{:S(2)}, u32[]{:S(2)}) collective-permute-start(bf16[384,1280]{1,0:T(8,128)(2,1)} %get-tuple-element.99), channel_id=1, source_target_pairs={{16,0},{17,1},{18,2},{19,3},{20,4},{21,5},{22,6},{23,7},{24,8},{25... | collective-permute-start | bytes 2949128 | tf_op jit(solution)/shard_map/ppermute | solution.py:1896
  362.7 0.9 copy-start.10
  407.8 0.9 copy-start.9
  408.7 248.7 %copy-start = (bf16[2,384,1280]{2,1,0:T(8,128)(2,1)S(1)}, bf16[2,384,1280]{2,1,0:T(8,128)(2,1)}, u32[]{:S(2)}) copy-start(bf16[2,384,1280]{2,1,0:T(8,128)(2,1)} %get-tuple-element.89) | copy-start | bytes 5898244
  657.5 2.3 copy-start.3
  659.7 2.0 copy-start.6
  661.7 1.3 copy-start.8
  661.7 2.0 copy-start.5
  663.0 1.9 copy-start.4

commit v8 on v7

--- a/solution.py
+++ b/solution.py
@@ -1247,12 +1247,6 @@
             self.landed[item].at[self.slot_of(item, way, step)], self.rings[item].at[buffer], self.load_sem.at[item, 4 + buffer]
         )
 
-    def exchange(self, wanted, offsets):
-        for offset in offsets:
-            for item in wanted:
-                self.pair_copy(item, offset).start()
-                self.exchanged.append((item, offset))
-
     def starts(self, wanted):
         return [
             (step, item, way, self.offset_of(step, way))
@@ -1280,19 +1274,79 @@
         self.pair_copy(item, offset).wait_recv()
         self.load_pair(item, offset, buffer).start()
 
-    def run(self, plan, between=None):
-        numbered = []
-        for entry in plan:
-            numbered.append(entry + (self.uses[entry[1]] % 2,))
-            self.uses[entry[1]] += 1
-        for number, entry in enumerate(numbered):
-            if number == 0:
-                self.fetch(entry)
-            if number + 1 < len(numbered):
-                self.fetch(numbered[number + 1])
-            self.work(entry)
-            if between is not None:
-                between()
+    def bytes_of(self, item):
+        array, _, rows, _ = self.items[item]
+        return rows * self.parts[array].shape[2] * self.parts[array].dtype.itemsize
+
+    def arrange(self, steps, ends):
+        waiting = self.starts(range(len(self.items)))
+        waiting += self.rest(range(len(self.items)), range(2, self.half + 2))
+        opened, arrival, sends, used = ({}, {}, {}, [0] * len(self.items))
+        clock, link, order, steps = (0.0, [0.0, 0.0], [], list(steps))
+
+        def ready_at(entry):
+            step, item, way, offset = entry
+            if (item, offset) not in opened:
+                return None
+            when = opened[(item, offset)]
+            sides = (0, 1) if way is None else ((way,) if step > self.first(item, way) else ())
+            for side in sides:
+                if (item, side, step - 1) not in arrival:
+                    return None
+                when = max(when, arrival[(item, side, step - 1)])
+            return max(when, sends.get((item, used[item] - 2), 0.0))
+
+        while waiting or steps:
+            best = None
+            for entry in waiting:
+                when = ready_at(entry)
+                if when is None or (entry[2] is None and (steps or any(other[2] is not None for other in waiting if ready_at(other) is not None and ready_at(other) <= clock))):
+                    continue
+                backlog = 0.0 if entry[2] is None else max(0.0, link[entry[2]] - max(clock, when))
+                rank = (max(when, clock) + 0.5 * backlog, entry[0])
+                if best is None or rank < best[0]:
+                    best = (rank, entry, when)
+            far_off = best is None or best[2] > clock + 0.3
+            idle = best is not None and best[1][2] is not None and link[best[1][2]] > clock + ends
+            if steps and (far_off or idle):
+                spent, step, opens = steps.pop(0)
+                clock += spent
+                for item, offset in opens:
+                    opened[(item, offset)] = clock + 2.0 + self.bytes_of(item) / 2e5
+                order.append((step, opens))
+                continue
+            _, entry, when = best
+            waiting.remove(entry)
+            step, item, way, offset = entry
+            clock = max(clock, when) + 0.8 + self.bytes_of(item) * 1.6e-6
+            if way is not None:
+                link[way] = max(clock, link[way]) + 2 * self.bytes_of(item) / 9.4e4
+                arrival[(item, way, step)] = link[way] + 1.5
+                sends[(item, used[item])] = link[way]
+            order.append(entry + (used[item] % 2,))
+            used[item] += 1
+        return order, clock
+
+    def follow(self, order):
+        entries = [number for number, action in enumerate(order) if len(action) == 5]
+        fetched = set()
+        for number, action in enumerate(order):
+            if len(action) == 2:
+                step, opens = action
+                step()
+                for item, offset in opens:
+                    self.pair_copy(item, offset).start()
+                    self.exchanged.append((item, offset))
+                continue
+            if number not in fetched:
+                self.fetch(action)
+                fetched.add(number)
+            if number + 1 in entries:
+                following = order[number + 1]
+                if following[1] != action[1]:
+                    self.fetch(following)
+                    fetched.add(number + 1)
+            self.work(action)
 
     def work(self, entry):
         step, item, way, offset, buffer = entry
@@ -1384,11 +1438,11 @@
         return pltpu.make_async_copy(source.at[:, window], self.big.at[slot], self.big_sem.at[slot])
 
     def keep(self, target, index):
-        window = pl.ds(pl.multiple_of(index // 2 * self.width, self.width), self.width)
+        window = pl.ds(index // 2 * self.width, self.width)
         return pltpu.make_async_copy(
-            self.stage.at[lax.rem(index, 2)],
-            target.at[pl.ds(lax.rem(index, 2) * self.chips, self.chips), :, window],
-            self.stage_sem.at[lax.rem(index, 2)],
+            self.stage.at[index % 2],
+            target.at[pl.ds(index % 2 * self.chips, self.chips), :, window],
+            self.stage_sem.at[index % 2],
         )
 
     def open(self, left, right, slot):
@@ -1396,35 +1450,26 @@
             self.load_cut(left, index, index).start()
         self.block(right, 0, slot).start()
 
-    def run(self, target, left, right, shift, low, high):
+    def run(self, target, left, right, shift, index):
         number = 2 * (right.shape[1] // self.width)
-        if low == 0:
-            for index in (0, 1):
-                self.load_cut(left, index, index).wait()
-
-        @pl.loop(low, high)
-        def _(index):
-            slot = lax.rem(index, 2)
-            here = lax.rem(index // 2 + shift, 2)
-
-            @pl.when(slot == 0)
-            def _():
-                self.block(right, index // 2, here).wait()
-
-                @pl.when(index + 2 < number)
-                def _():
-                    self.block(right, index // 2 + 1, 1 - here).start()
-
-            @pl.when(index >= low + 2)
-            def _():
-                self.keep(target, index - 2).wait()
-
-            product = dot_left(self.cuts[slot], self.big[here]).astype(LOW)
-            for device in range(self.chips):
-                self.stage[slot, device] = product[device * self.own : (device + 1) * self.own]
-            self.keep(target, index).start()
-
-        for index in range(max(low, high - 2), high):
+        slot, here = (index % 2, (index // 2 + shift) % 2)
+        if index == 0:
+            for side in (0, 1):
+                self.load_cut(left, side, side).wait()
+        if slot == 0:
+            self.block(right, index // 2, here).wait()
+            if index + 2 < number:
+                self.block(right, index // 2 + 1, 1 - here).start()
+        if index >= 2:
+            self.keep(target, index - 2).wait()
+        product = dot_left(self.cuts[slot], self.big[here]).astype(LOW)
+        for device in range(self.chips):
+            self.stage[slot, device] = product[device * self.own : (device + 1) * self.own]
+        self.keep(target, index).start()
+
+    def close(self, target, right):
+        number = 2 * (right.shape[1] // self.width)
+        for index in (number - 2, number - 1):
             self.keep(target, index).wait()
 
 
@@ -1458,40 +1503,41 @@
 
     def farthest_first(index):
         step = index // 2
-        return ring_chip(position + jnp.where(lax.rem(index, 2) == 0, half - step, half + step + 1), chips)
+        return ring_chip(position + (half - step if index % 2 == 0 else half + step + 1), chips)
 
     def keep_down(index):
         return pltpu.make_async_copy(
-            stage_down.at[lax.rem(index, 2)],
+            stage_down.at[index % 2],
             down_part.at[pl.ds(farthest_first(index) * 2, 2)],
-            stage_sem.at[2 + lax.rem(index, 2)],
+            stage_sem.at[2 + index % 2],
         )
 
     def cut_down(index):
-        return products.load_cut(activated_h, farthest_first(index), lax.rem(index, 2))
-
-    def down_products(low, high):
-        @pl.loop(low, high)
-        def _(index):
-            slot = lax.rem(index, 2)
-
-            @pl.when(index + 1 < chips)
-            def _():
+        return products.load_cut(activated_h, farthest_first(index), index % 2)
+
+    def down_product(index):
+        def step():
+            slot = index % 2
+            if index == 0:
+                for at in range(cell + 1):
+                    ff_load(at).wait()
+            if index + 1 < chips:
                 cut_down(index + 1).start()
-
             cut_down(index).wait()
-
-            @pl.when(index >= low + 2)
-            def _():
+            if index == 2 or index >= 5:
                 keep_down(index - 2).wait()
-
             product = dot_left(cuts[slot], big[0]).astype(LOW)
             for side in (0, 1):
                 stage_down[slot, side] = product[side * deep_own : (side + 1) * deep_own]
             keep_down(index).start()
-
-        for index in range(max(low, high - 2), high):
-            keep_down(index).wait()
+            if index == 2:
+                for at in (1, 2):
+                    keep_down(at).wait()
+            if index == chips - 1:
+                for at in (chips - 2, chips - 1):
+                    keep_down(at).wait()
+
+        return step
 
     def here(ref, at):
         return ref.at[pl.ds(at * length, length)]
@@ -1682,7 +1728,6 @@
             small_v[device, 8 + ups : 16, :] = jnp.zeros((8 - ups, own), F32)
 
     pairs = width // 128
-    head_blocks = packed_o.shape[1] // width
     downs = [item for item in range(count) if items[item][0] == 4]
     up_items = [item for item in range(count) if items[item][0] == 3]
     outers = [item for item in range(count) if items[item][0] == 2]
@@ -1692,73 +1737,49 @@
     near = [offset for offset in range(chips) if offset not in far]
     everywhere = far + near
 
-    def work(*steps):
-        for step in steps:
-            pl.when(first)(step)
-
-    def up_products(low, high):
-        products.run(up_part, second_h, inner_o, 1, low, high)
-
-    def head_products(low, high):
-        products.run(parts[1], lowered_h, packed_o, 0, low, high)
-
+    def only_first(step):
+        return lambda: pl.when(first)(step)
+
+    def product(target, left, right, shift, index):
+        def step():
+            products.run(target, left, right, shift, index)
+            if index + 1 == 2 * (right.shape[1] // width):
+                products.close(target, right)
+
+        return step
+
+    def all_of(wanted, offsets):
+        return [(item, offset) for offset in offsets for item in wanted]
+
+    def opening(left, right, shift):
+        return lambda: products.open(left, right, shift)
+
+    def blocks(target, left, right, shift, wanted):
+        number = 2 * (right.shape[1] // width)
+        made = [(0.3, opening(left, right, shift), [])]
+        for index in range(number):
+            opens = all_of(wanted, everywhere) if index + 1 == number else []
+            made.append((1.8, product(target, left, right, shift, index), opens))
+        return made
+
+    steps = [(1.8, down_product(index), all_of(downs, far) if index == 2 else []) for index in range(3)]
+    steps.append((0.3, only_first(begin), []))
+    for index in range(3, chips):
+        steps.append((1.8, down_product(index), all_of(downs, near) if index == chips - 1 else []))
+    steps += [(1.7 if number in (0, ups) else 3.0, only_first(climb(number)), []) for number in range(ups + 1)]
+    steps.append((2.5, only_first(turn), []))
+    steps += blocks(up_part, second_h, inner_o, 1, up_items)
+    steps += blocks(parts[2], mixed_h, branch_o, 1, outers)
+    steps.append((1.7, only_first(outer), []))
+    steps += [(1.25, only_first(heads(low, low + 1)), []) for low in range(pairs)]
+    steps.append((0.8, only_first(sums), []))
+    steps += blocks(parts[1], lowered_h, packed_o, 0, head_items)
+    steps += [(1.5, only_first(lower(number)), []) for number in range(3)]
+    steps.append((2.5, only_first(finish), []))
+    steps.append((2.0, lay_small, all_of(smalls, everywhere)))
     greet((ring.left, ring.right, ring.sibling))
-    for at in range(cell + 1):
-        ff_load(at).wait()
-    down_products(0, 3)
-    ring.exchange(downs, far)
-    down_products(3, 5)
-    work(begin)
-    ring.run(ring.starts(downs))
-    down_products(5, chips)
-    ring.exchange(downs, near)
-    later = [climb(number) for number in range(ups + 1)] + [turn]
-
-    def between():
-        if later:
-            work(later.pop(0))
-
-    work(later.pop(0), later.pop(0))
-    ring.run(ring.rest(downs, (2,)), between)
-    ring.run(ring.rest(downs, (3,)), between)
-    while later:
-        between()
-    products.open(second_h, inner_o, 1)
-    up_products(0, ups)
-    ring.run(ring.rest(downs, (4,))[:2])
-    up_products(ups, 2 * ups)
-    ring.exchange(up_items, everywhere)
-    products.open(mixed_h, branch_o, 1)
-    ring.run(ring.rest(downs, (4,))[2:])
-    products.run(parts[2], mixed_h, branch_o, 1, 0, 2)
-    ring.exchange(outers, everywhere)
-    ring.run(ring.starts(up_items))
-    later = [outer] + [heads(low, low + 2) for low in range(0, pairs, 2)] + [sums]
-    work(later.pop(0), later.pop(0))
-    ring.run(ring.starts(outers), between)
-    ring.run(ring.rest(up_items + outers, (2,)), between)
-    while later:
-        between()
-    products.open(lowered_h, packed_o, 0)
-    head_products(0, head_blocks)
-    ring.run(ring.rest(up_items + outers, (3,))[:2])
-    head_products(head_blocks, 2 * head_blocks)
-    ring.exchange(head_items, everywhere)
-    ring.run(ring.rest(up_items + outers, (3,))[2:])
-    ring.run(ring.starts(head_items))
-    later = [lower(number) for number in range(3)] + [finish]
-    ring.run(ring.rest(head_items, (2,)), between)
-    while later:
-        between()
-    lay_small()
-    ring.exchange(smalls, everywhere)
-    ring.run(ring.rest(up_items + outers, (4,)))
-    ring.run(ring.starts(smalls))
-    ring.run(ring.rest(head_items, (3,)))
-    ring.run(ring.rest(smalls, (2, 3)))
-    ring.run(ring.rest(downs + up_items, (half + 1,)))
-    ring.run(ring.rest(smalls + head_items, (4,)))
-    ring.run(ring.rest(outers + smalls + head_items, (half + 1,)))
+    schedule, _ = ring.arrange(steps, 8.0)
+    ring.follow(schedule)
     ring.close()
 
     @pl.when(first)
@@ -1937,7 +1958,7 @@
             weights,
             (input_grads, flat(grad_packed), flat(grad_branch), flat(grad_inner), sums),
             [flat(array) for array in (activated, grad_ff, second, mixed, lowered)],
-            items,
+            arrivals,
             shapes,
             count,
         )

time: 676 us -> 652 us (0.964)
  Pallas kernels: 548 us -> 524 us
    pallas_call x1, Pallas kernels: 245 us -> 221 us  [last_backward(): pl.pallas_call(functools.partial(last_backward_kernel, chips, items, cell...]
where the time goes in v8:
time: 652 us; the launch traced here: 642 us
  Pallas kernels  524 us (80%)
  waiting for transfers between devices  87.4 us (13%)
  local copies, waits for them, and re-layouts  19.9 us (3%)
  starting transfers between devices  7.14 us (1%)
    pallas_call x1, Pallas kernels, gather_forward(): pl.pallas_call(functools.partial(gather_forward_kernel, chips, items, gro...  224 us
    pallas_call x1, Pallas kernels, last_backward(): pl.pallas_call(functools.partial(last_backward_kernel, chips, items, cell...  221 us
    ppermute x3, waiting for transfers between devices, along(): return lax.ppermute(value, 'pipe', pairs)  87.4 us
    pallas_call x3, Pallas kernels, backward_tick(): pl.pallas_call(functools.partial(backward_kernel, cell, held), out_shape=...  69.2 us
  transfers between devices with their start and end apart: 3, of which 3 were waited for; matrix products, arithmetic and copies ran while one was open for 1% of the time, Pallas kernels for 9%

profile of v8, /device:TPU:0, one launch (start us, length us, event | category | flops | bytes accessed | tf_op | source)
XLA Modules:
  0.0 641.7 jit_solution(15280143013665841070)
XLA Ops:
  0.6 0.7 reduce
  1.5 1.4 maximum_bitcast_fusion.refs_0_
  2.9 223.6 %shard_map.169 = (bf16[16,16,80]{2,1,0:T(8,128)(2,1)}, bf16[16,80,3840]{2,1,0:T(8,128)(2,1)}, bf16[16,80,1280]{2,1,0:T(8,128)(2,1)}, bf16[16,80,5120]{2,1,0:T(8,...) custom-call(bf16[16,80]{1,0:T(8,128)(2,1)} %maximum_bitcast_fusion.r, ...), custom_call_target="tpu_custom_call" | custom-call | flops 30198988800 | bytes 157286400 | tf_op jit(solution)/shard_map/pallas_call | solution.py:1148
  226.5 4.6 collective-permute-start
  231.6 1.4 shard_map.170
  233.2 1.4 slice_bitcast_fusion
  234.7 0.8 copy-done.2
  235.5 1.4 slice_bitcast_fusion.2
  236.9 12.1 %collective-permute-done.entry_h = bf16[384,1280]{1,0:T(8,128)(2,1)S(1)} collective-permute-done((bf16[384,1280]{1,0:T(8,128)(2,1)}, bf16[384,1280]{1,0:T(8,128)(2,1)S(1)}, u32[]{:S(2)}, u32[]{:S(2)}) %collective-permute-start) | collective-permute-done | bytes 983072 | tf_op jit(solution)/shard_map/ppermute | solution.py:1917
  249.0 0.9 copy-done.7
  249.9 9.6 %shard_map.171 = (bf16[384,1280]{1,0:T(8,128)(2,1)}, bf16[2,384,1280]{2,1,0:T(8,128)(2,1)}, bf16[2,384,1280]{2,1,0:T(8,128)(2,1)}, bf16[2,384,3840]{2,1,0:T(8,12...) custom-call(s32[1]{0:T(128)} %bitcast.active, ...), custom_call_target="tpu_custom_call", output_to_operand_aliasing={{1}: (7, {}), {2}: (8, {}), {3}: (9, {}), {4}: (10, {}), {5... | custom-call | flops 18119393280 | bytes 39321600 | tf_op jit(solution)/shard_map/pallas_call | solution.py:558
  259.5 13.8 %shard_map.172 = (bf16[384,1280]{1,0:T(8,128)(2,1)}, bf16[2,384,1280]{2,1,0:T(8,128)(2,1)}, bf16[2,384,3840]{2,1,0:T(8,128)(2,1)}, bf16[2,384,1280]{2,1,0:T(8,12...) custom-call(s32[1]{0:T(128)} %bitcast.active, ...), custom_call_target="tpu_custom_call" | custom-call | flops 22649241600 | bytes 39321600 | tf_op jit(solution)/shard_map/pallas_call | solution.py:720
  273.2 1.3 collective-permute-start.2
  274.5 12.3 %shard_map.173 = (bf16[384,1280]{1,0:T(8,128)(2,1)}, bf16[2,384,1280]{2,1,0:T(8,128)(2,1)}, bf16[2,384,3840]{2,1,0:T(8,128)(2,1)}, bf16[2,384,1280]{2,1,0:T(8,12...) custom-call(s32[1]{0:T(128)} %bitcast.active, ...), custom_call_target="tpu_custom_call", output_to_operand_aliasing={{1}: (12, {}), {2}: (13, {}), {3}: (14, {}), {4}: (15, {}),... | custom-call | flops 22649241600 | bytes 39321600 | tf_op jit(solution)/shard_map/pallas_call | solution.py:720
  286.8 1.3 collective-permute-start.1
  288.1 74.5 %collective-permute-done.2.grad_h = bf16[384,1280]{1,0:T(8,128)(2,1)S(1)} collective-permute-done((bf16[384,1280]{1,0:T(8,128)(2,1)}, bf16[384,1280]{1,0:T(8,128)(2,1)S(1)}, u32[]{:S(2)}, u32[]{:S(2)}) %collective-permute-start.2) | collective-permute-done | bytes 983072 | tf_op jit(solution)/shard_map/ppermute | solution.py:1917
  362.6 0.9 copy-done.10
  363.6 43.1 %shard_map.174 = (bf16[384,1280]{1,0:T(8,128)(2,1)}, bf16[2,384,1280]{2,1,0:T(8,128)(2,1)}, bf16[2,384,3840]{2,1,0:T(8,128)(2,1)}, bf16[2,384,1280]{2,1,0:T(8,12...) custom-call(s32[1]{0:T(128)} %bitcast.15.active, ...), custom_call_target="tpu_custom_call", output_to_operand_aliasing={{1}: (12, {}), {2}: (13, {}), {3}: (14, {}), {4}: (15, {}),... | custom-call | flops 22649241600 | bytes 39321600 | tf_op jit(solution)/shard_map/pallas_call | solution.py:720
  406.7 0.8 collective-permute-done.1.refs_0_
  407.5 0.9 copy-done.9
  408.4 220.6 %shard_map.175 = (bf16[2,384,1280]{2,1,0:T(8,128)(2,1)}, bf16[768,3840]{1,0:T(8,128)(2,1)}, bf16[768,1280]{1,0:T(8,128)(2,1)}, bf16[768,5120]{1,0:T(8,128)(2,1)}...) custom-call(bf16[384,1280]{1,0:T(8,128)(2,1)} %copy-done.9, ...), custom_call_target="tpu_custom_call", output_to_operand_aliasing={{0}: (15, {}), {1}: (16, {}), {2}: (17, {}), {3}: (18, {}),... | custom-call | flops 45298483200 | bytes 262144000 | tf_op jit(solution)/shard_map/pallas_call | solution.py:1804
  629.0 1.2 slice.36
  630.3 0.7 slice.38
  631.0 0.7 slice.37
  632.9 1.3 copy.92
  634.2 1.0 copy-done.3
  635.1 1.3 copy.93
  636.4 0.7 copy-done.6
  637.1 1.0 copy.94
  638.4 0.8 copy.95
  639.1 1.2 copy.96
  640.3 1.2 copy.97
  (25 shorter events, 2.4 us)
Async XLA Ops:
  2.9 228.2 %copy-start.11 = (s32[2]{0:T(128)S(1)}, s32[2]{0:T(128)}, u32[]{:S(2)}) copy-start(s32[2]{0:T(128)} %param.12) | copy-start | bytes 28
  226.5 22.5 %collective-permute-start = (bf16[384,1280]{1,0:T(8,128)(2,1)}, bf16[384,1280]{1,0:T(8,128)(2,1)S(1)}, u32[]{:S(2)}, u32[]{:S(2)}) collective-permute-start(bf16[384,1280]{1,0:T(8,128)(2,1)} %get-tuple-element.66), channel_id=1, source_target_pairs={{0,16},{1,17},{2,18},{3,19},{4,20},{5,21},{6,22},{7,23},{8,24},{9,... | collective-permute-start | bytes 2949128 | tf_op jit(solution)/shard_map/ppermute | solution.py:1917
  231.6 1.6 copy-start.1
  233.2 2.3 copy-start.2
  249.0 0.9 copy-start.7
  273.2 89.4 %collective-permute-start.2 = (bf16[384,1280]{1,0:T(8,128)(2,1)}, bf16[384,1280]{1,0:T(8,128)(2,1)S(1)}, u32[]{:S(2)}, u32[]{:S(2)}) collective-permute-start(bf16[384,1280]{1,0:T(8,128)(2,1)} %get-tuple-element.101), channel_id=1, source_target_pairs={{16,0},{17,1},{18,2},{19,3},{20,4},{21,5},{22,6},{23,7},{24,8},{25... | collective-permute-start | bytes 2949128 | tf_op jit(solution)/shard_map/ppermute | solution.py:1917
  286.8 120.7 %collective-permute-start.1 = (bf16[384,1280]{1,0:T(8,128)(2,1)}, bf16[384,1280]{1,0:T(8,128)(2,1)S(1)}, u32[]{:S(2)}, u32[]{:S(2)}) collective-permute-start(bf16[384,1280]{1,0:T(8,128)(2,1)} %get-tuple-element.99), channel_id=1, source_target_pairs={{16,0},{17,1},{18,2},{19,3},{20,4},{21,5},{22,6},{23,7},{24,8},{25... | collective-permute-start | bytes 2949128 | tf_op jit(solution)/shard_map/ppermute | solution.py:1917
  362.6 0.9 copy-start.10
  407.5 0.9 copy-start.9
  408.4 224.4 %copy-start = (bf16[2,384,1280]{2,1,0:T(8,128)(2,1)S(1)}, bf16[2,384,1280]{2,1,0:T(8,128)(2,1)}, u32[]{:S(2)}) copy-start(bf16[2,384,1280]{2,1,0:T(8,128)(2,1)} %get-tuple-element.89) | copy-start | bytes 5898244
  632.9 2.3 copy-start.3
  635.1 2.0 copy-start.6
  637.1 1.3 copy-start.8
  637.1 2.0 copy-start.5
  638.4 1.9 copy-start.4

commit v9 on v8

--- a/solution.py
+++ b/solution.py
@@ -443,13 +443,14 @@
         pair_of(index * 2 + 1)
 
 
-def forward_kernel(cell, held, active, entry_h, rows, w_qkv, w_out, w_up, w_down, *refs):
+def forward_kernel(cell, held, at, active, entry_h, rows, w_qkv, w_out, w_up, w_down, *refs):
     sent_h = refs[held]
     out_h, lowered_h, packed_h, mixed_h, middle_h, second_h, active_h, slope_h = [
         ref.at[cell] for ref in refs[held + 1 : held + 9]
     ]
     (buffers, buffer_sems, save_sems, out_v, lowered_v, packed_v, mixed_v, middle_v) = refs[held + 9 : held + 17]
     (second_v, active_v, slope_v, hidden_v, total_v, entry, entry_sem) = refs[held + 17 :]
+    entry = entry_h if at is None else entry
     width = entry.shape[1]
     gains, shifts, bias = (rows.at[0:2], rows.at[2:8], rows.at[8:16])
     ups = w_up.shape[1] // width
@@ -466,15 +467,17 @@
             if number > 0:
                 place_down[number - 1] = len(order)
                 order.append(down[number - 1])
-        fetched = pltpu.make_async_copy(entry_h, entry, entry_sem)
-        fetched.start()
+        if at is not None:
+            fetched = pltpu.make_async_copy(entry_h.at[at], entry, entry_sem)
+            fetched.start()
         saves = []
 
         def save(source, target):
             saves.append(pltpu.make_async_copy(source, target, save_sems.at[len(saves)]))
             saves[-1].start()
 
-        fetched.wait()
+        if at is not None:
+            fetched.wait()
         stream = Stream(order, buffers, buffer_sems)
         rows_in = entry[...].astype(F32)
         normed, _ = row_norm(rows_in)
@@ -544,7 +547,8 @@
 
 
 def forward_tick(active, entry, rows, weights, kept, cell, cell_count):
-    length, width = entry.shape
+    entry, at = entry
+    length, width = entry.shape[-2:]
     deep = weights[2].shape[1]
     ups = deep // width
     shapes = kept_shapes(length, width, deep)
@@ -556,9 +560,9 @@
     kept = () if kept is None else tuple(kept)
     held = len(kept)
     sent, *kept = pl.pallas_call(
-        functools.partial(forward_kernel, cell, held),
+        functools.partial(forward_kernel, cell, held, at),
         out_shape=outs,
-        in_specs=[pl.BlockSpec(memory_space=pltpu.SMEM), hbm, vmem] + [hbm] * (4 + held),
+        in_specs=[pl.BlockSpec(memory_space=pltpu.SMEM), vmem if at is None else hbm, vmem] + [hbm] * (4 + held),
         out_specs=[hbm] * 9,
         input_output_aliases={7 + number: 1 + number for number in range(held)},
         scratch_shapes=[
@@ -581,7 +585,7 @@
     return (sent, kept)
 
 
-def backward_kernel(cell, held, active, scale, grad_h, entry_h, rows, *refs):
+def backward_kernel(cell, held, grad_at, entry_at, active, scale, grad_h, entry_h, rows, *refs):
     packed, middle, slope = [ref.at[cell] for ref in refs[:3]]
     w_qkv, w_out, w_up, w_down = refs[3:7]
     refs = refs[7 + held :]
@@ -590,6 +594,8 @@
     (buffers, buffer_sems, load_sems, save_sems, rows_v, grad_packed_v, branch_v, inner_v, low_v, sums_v) = refs[7:17]
     (packed_v, middle_v, slope_v, mixed_v, grad_act_v, total_v, grad_middle_v, grad, entry) = refs[17:]
     gains = rows.at[0:2]
+    grad = grad_h if grad_at is None else grad
+    entry_h = entry_h if entry_at is None else entry_h.at[entry_at]
     length, width = entry.shape
     ups = w_up.shape[1] // width
 
@@ -600,10 +606,11 @@
             pltpu.make_async_copy(slope, slope_v, load_sems.at[0]),
             pltpu.make_async_copy(middle, middle_v, load_sems.at[1]),
             pltpu.make_async_copy(packed, packed_v, load_sems.at[2]),
-            pltpu.make_async_copy(grad_h, grad, load_sems.at[3]),
-            pltpu.make_async_copy(entry_h, entry, load_sems.at[4]),
+            pltpu.make_async_copy(entry_h, entry, load_sems.at[3]),
         ]
-        loads[3].start()
+        if grad_at is not None:
+            loads.append(pltpu.make_async_copy(grad_h.at[grad_at], grad, load_sems.at[4]))
+            loads[4].start()
         order, place_up, place_down = ([], {}, {})
         for number in range(ups + 1):
             if number < ups:
@@ -623,7 +630,8 @@
         def column_sum(array):
             return jnp.sum(array.astype(F32), axis=0, keepdims=True)
 
-        loads[3].wait()
+        if grad_at is not None:
+            loads[4].wait()
         stream = Stream(order, buffers, buffer_sems)
         loads[0].start()
         low_v[...] = (grad[...].astype(F32) * scale[0]).astype(LOW)
@@ -635,7 +643,7 @@
                 loads[1].start()
             if number == 2:
                 loads[2].start()
-                loads[4].start()
+                loads[3].start()
             if number < ups:
                 down_block = stream.take(place_down[number])
             if number > 0:
@@ -683,7 +691,7 @@
             else:
                 total_v[...] += part
             stream.release()
-        loads[4].wait()
+        loads[3].wait()
         normed, inverse = row_norm(entry[...].astype(F32))
         grad_lowered = total_v[...]
         sums_v[0:1, :] = column_sum(grad_lowered * normed)
@@ -697,7 +705,9 @@
 
 
 def backward_tick(active, incoming, entry, rows, saved, weights, kept, cell, cell_count):
-    length, width = entry.shape
+    entry, entry_at = entry
+    (grad, grad_at), scale = incoming
+    length, width = entry.shape[-2:]
     deep = weights[2].shape[1]
     ups = deep // width
     shapes = [
@@ -716,11 +726,10 @@
     flops = 2 * length * width * (4 * width + 2 * deep) + 40 * length * length * width
     kept = () if kept is None else tuple(kept)
     held = len(kept)
-    grad, scale = incoming
     sent, *kept = pl.pallas_call(
-        functools.partial(backward_kernel, cell, held),
+        functools.partial(backward_kernel, cell, held, grad_at, entry_at),
         out_shape=outs,
-        in_specs=[smem] * 2 + [hbm] * 2 + [vmem] + [hbm] * (7 + held),
+        in_specs=[smem] * 2 + [vmem if grad_at is None else hbm, hbm, vmem] + [hbm] * (7 + held),
         out_specs=[hbm] * 7,
         input_output_aliases={12 + number: 1 + number for number in range(held)},
         scratch_shapes=[
@@ -1365,7 +1374,11 @@
             for side in (0, 1):
                 self.load_ring(item, side, half, side).wait()
             if kind == F32:
-                self.outs[array][...] = (rings[0] + rings[1]) + (mine[buffer] + pairs[buffer])
+                total = (rings[0] + rings[1]) + (mine[buffer] + pairs[buffer])
+                top = 0
+                for out in self.outs[array]:
+                    out[...] = total[top : top + out.shape[0]]
+                    top += out.shape[0]
                 return
             high, wide = (min(rows, final.shape[1]), min(columns, final.shape[2]))
             for top in range(0, rows, high):
@@ -1475,20 +1488,20 @@
 
 def last_backward_kernel(chips, items, cell, *refs):
     count = len(items)
-    (grad_h, entry_h, rows, packed_h, middle_h, slope_h, w_qkv, w_out, w_up, w_down) = refs[:10]
+    (grad, entry_h, rows, packed_h, middle_h, slope_h, w_qkv, w_out, w_up, w_down) = refs[:10]
     (activated_h, grad_ff_h, second_h, mixed_h, lowered_h) = refs[10:15]
     refs = refs[15 + 5 :]
     rows_o, packed_o, branch_o, inner_o, sums_o = refs[:5]
-    outs, parts = (refs[5:10], refs[10:14])
-    landed, paired = (refs[14 : 14 + count], refs[14 + count : 14 + 2 * count])
-    refs = refs[14 + 2 * count :]
+    outs, parts = ([refs[5:8]] + list(refs[8:12]), refs[12:16])
+    landed, paired = (refs[16 : 16 + count], refs[16 + count : 16 + 2 * count])
+    refs = refs[16 + 2 * count :]
     ring_buffers = (refs[:count], refs[count : 2 * count], refs[2 * count : 3 * count])
     final, small_v, both_v = refs[3 * count : 3 * count + 3]
     sems = refs[3 * count + 3 : 3 * count + 9]
     refs = refs[3 * count + 9 :]
     (big, cuts, stage, stage_down, big_sem, cut_sem, stage_sem) = refs[:7]
     (buffers, buffer_sems, load_sems, save_sems, slope_sems, inner_sems) = refs[7:13]
-    (grad, entry, packed_v, middle_v, slope_v, inner_v, grad_packed_v, mixed_v, branch_v, grad_act_v, total_v, sums_v) = refs[13:]
+    (entry, packed_v, middle_v, slope_v, inner_v, grad_packed_v, mixed_v, branch_v, grad_act_v, total_v, sums_v) = refs[13:]
     parts = [small_v] + list(parts)
     down_part, up_part = (parts[4], parts[3])
     length, width = grad.shape
@@ -1546,7 +1559,7 @@
         return pltpu.make_async_copy(here(grad_ff_h, at), here(big.at[0], at), load_sems.at[at])
 
     def ff_arrived():
-        return pltpu.make_async_copy(grad_h, here(big.at[0], cell), load_sems.at[cell])
+        return pltpu.make_async_copy(grad, here(big.at[0], cell), load_sems.at[cell])
 
     for at in range(cell):
         ff_load(at).start()
@@ -1555,13 +1568,8 @@
     cut_down(0).start()
 
     def own_load(number):
-        source, target = (
-            (grad_h, grad),
-            (entry_h, entry),
-            (middle_h.at[cell], middle_v),
-            (packed_h.at[cell], packed_v),
-        )[number]
-        return pltpu.make_async_copy(source, target, load_sems.at[cell + 1 + number])
+        source, target = ((entry_h, entry), (middle_h, middle_v), (packed_h, packed_v))[number - 1]
+        return pltpu.make_async_copy(source.at[cell], target, load_sems.at[cell + 1 + number])
 
     def slope_load(number):
         window = pl.ds(number * width, width)
@@ -1615,13 +1623,11 @@
         return jnp.sum(array.astype(F32), axis=0, keepdims=True)
 
     def begin():
-        own_load(0).start()
         slope_load(0).start()
         for number in range(depth):
             weight_load(number).start()
         for number in (1, 2, 3):
             own_load(number).start()
-        own_load(0).wait()
         sums_v[7:8, :] = column_sum(grad[...])
 
     def climb(number):
@@ -1794,7 +1800,7 @@
     cells = kept[0].shape[0]
     rows_in = cells * length
     own = width // count
-    hbm = pl.BlockSpec(memory_space=pl.ANY)
+    vmem, hbm = (pl.BlockSpec(memory_space=pltpu.VMEM), pl.BlockSpec(memory_space=pl.ANY))
     cut = width // 2
     wholes = [(16, own)] + [tuple(shape) for shape in shapes]
     held = [(many,) + wholes[array][1:] for array, _, many, _ in items]
@@ -1804,12 +1810,13 @@
     outs = pl.pallas_call(
         functools.partial(last_backward_kernel, chips, items, cells - 1),
         out_shape=[jax.ShapeDtypeStruct(array.shape, array.dtype) for array in kept]
-        + [jax.ShapeDtypeStruct(shape, F32) for shape in wholes]
+        + [jax.ShapeDtypeStruct((many, own), F32) for many in (2, 6, deep // width)]
+        + [jax.ShapeDtypeStruct(shape, F32) for shape in wholes[1:]]
         + [jax.ShapeDtypeStruct((count,) + shape, LOW) for shape in wholes[1:]]
         + [jax.ShapeDtypeStruct((chips - 1,) + shape, kind) for shape, kind in zip(held, kinds)]
         + [jax.ShapeDtypeStruct((chips,) + shape, kind) for shape, kind in zip(held, kinds)],
-        in_specs=[hbm] * 2 + [pl.BlockSpec(memory_space=pltpu.VMEM)] + [hbm] * 17,
-        out_specs=[hbm] * 5 + [pl.BlockSpec(memory_space=pltpu.VMEM)] + [hbm] * (8 + 2 * pieces),
+        in_specs=[vmem, hbm, vmem] + [hbm] * 17,
+        out_specs=[hbm] * 5 + [vmem] * 3 + [hbm] * (8 + 2 * pieces),
         input_output_aliases={15 + number: number for number in range(5)},
         scratch_shapes=[pltpu.VMEM((2,) + shape, kind) for shape, kind in zip(held, kinds)] * 3
         + [
@@ -1836,7 +1843,6 @@
             pltpu.SemaphoreType.DMA((2,)),
             pltpu.SemaphoreType.DMA((2,)),
             pltpu.VMEM((length, width), LOW),
-            pltpu.VMEM((length, width), LOW),
             pltpu.VMEM((length, 3 * width), LOW),
             pltpu.VMEM((length, width), F32),
             pltpu.VMEM((2, length, width), LOW),
@@ -1853,7 +1859,7 @@
         ),
         cost_estimate=pl.CostEstimate(flops=flops, bytes_accessed=160 * width * width, transcendentals=0),
     )(arrived, entry, rows, *saved, *weights, *sides, *kept)
-    return (list(outs[:5]), outs[5:10])
+    return (list(outs[:5]), outs[5:8], outs[8:12])
 
 
 def on_device(inputs, out_grad, query_counts, gains, shifts, w_qkv, w_out, w_up, b_up, w_down):
@@ -1916,9 +1922,9 @@
         pairs = [(source, source + steps) for source in range(stages) if 0 <= source + steps < stages]
         return lax.ppermute(value, "pipe", pairs)
 
-    entries = [[inputs[cell] for cell in range(cell_count)]]
+    entries = [[(inputs, cell) for cell in range(cell_count)]]
     if fused:
-        entries.append([arrived] + [along(later, 1)])
+        entries.append([(arrived, None), (along(later, 1), None)])
     else:
         kept = None
     for turn in range(1 if fused else 0, stages):
@@ -1927,10 +1933,10 @@
         for cell in range(cell_count):
             sent, kept = forward_tick(active, entries[turn][cell], rows, weights, kept, cell, cell_count)
             if turn + 1 < stages:
-                arrived.append(along(sent, 1))
+                arrived.append((along(sent, 1), None))
         entries.append(arrived)
     section_out, lowered, packed, mixed, middle, second, activated, slope = kept
-    incoming = [(out_grad[cell], scales[cell][None]) for cell in range(cell_count)]
+    incoming = [((out_grad, cell), scales[cell][None]) for cell in range(cell_count)]
     back = None
     for turn in range(stages - 1, -1, -1):
         active = (stage == turn).astype(jnp.int32)[None]
@@ -1942,7 +1948,7 @@
                 active, incoming[cell], entries[turn][cell], rows, (packed, middle, slope), weights, back, cell, cell_count
             )
             if turn > 0:
-                arrived.append((along(sent, -1), jnp.ones((1,), F32)))
+                arrived.append(((along(sent, -1), None), jnp.ones((1,), F32)))
         incoming = arrived if turn > 0 else incoming
 
     def flat(array):
@@ -1950,9 +1956,9 @@
 
     input_grads, grad_packed, grad_branch, grad_inner, grad_ff, sums = back
     if fused:
-        (input_grads, grad_packed, grad_branch, grad_inner, sums), shares = last_backward(
-            incoming[-1][0],
-            entries[0][-1],
+        (input_grads, _, _, _, _), (grad_gains, grad_shifts, grad_bias), shares = last_backward(
+            incoming[-1][0][0],
+            inputs,
             rows,
             (packed, middle, slope),
             weights,
@@ -1968,18 +1974,18 @@
         sides = [flat(array) for array in (lowered, grad_packed, mixed, grad_branch, second, grad_inner, activated, grad_ff)]
         products = [dot_left(sides[at], sides[at + 1]).astype(LOW) for at in (0, 2, 4, 6)]
         parts = [small_part] + [whole.reshape((count,) + shape) for whole, shape in zip(products, shapes)]
-        shares = scatter(parts, items, count)
-    grad_gains, grad_shifts, grad_bias = small_split(shares[0][None], ups)
+        small_share, *shares = scatter(parts, items, count)
+        grad_gains, grad_shifts, grad_bias = small_split(small_share[None], ups)
     return (
         section_out[None],
         input_grads[None],
         grad_gains[None],
         grad_shifts[None],
-        shares[1].reshape(1, own, 3 * width),
-        shares[2].reshape(1, own, width),
-        shares[3].reshape(1, own, deep),
-        grad_bias[None],
-        shares[4].reshape(1, deep_own, width),
+        shares[0].reshape(1, own, 3 * width),
+        shares[1].reshape(1, own, width),
+        shares[2].reshape(1, own, deep),
+        grad_bias.reshape(1, ups * own),
+        shares[3].reshape(1, deep_own, width),
     )
 
 

time: 652 us -> 644 us (0.988)
  transfers between devices with their start and end apart: 3 -> 3, of which waited for: 3 -> 3; matrix products, arithmetic and copies ran while one was open for 1% -> 0% of each run, Pallas kernels for 9% -> 9%
where the time goes in v9:
time: 644 us; the launch traced here: 634 us
  Pallas kernels  524 us (81%)
  waiting for transfers between devices  86 us (13%)
  local copies, waits for them, and re-layouts  13.6 us (2%)
  starting transfers between devices  7.14 us (1%)
    pallas_call x1, Pallas kernels, gather_forward(): pl.pallas_call(functools.partial(gather_forward_kernel, chips, items, gro...  224 us
    pallas_call x1, Pallas kernels, last_backward(): pl.pallas_call(functools.partial(last_backward_kernel, chips, items, cell...  221 us
    ppermute x3, waiting for transfers between devices, along(): return lax.ppermute(value, 'pipe', pairs)  86 us
    pallas_call x3, Pallas kernels, backward_tick(): pl.pallas_call(functools.partial(backward_kernel, cell, held, grad_at, en...  68.3 us
  transfers between devices with their start and end apart: 3, of which 3 were waited for; matrix products, arithmetic and copies ran while one was open for 0% of the time, Pallas kernels for 9%

profile of v9, /device:TPU:0, one launch (start us, length us, event | category | flops | bytes accessed | tf_op | source)
XLA Modules:
  0.0 633.8 jit_solution(10399360599229238869)
XLA Ops:
  0.6 0.7 reduce
  1.3 0.1 reshape_squeeze.3
  1.4 0.1 pad.3.clone
  1.5 1.4 maximum_bitcast_fusion.refs_0_
  2.9 223.6 %shard_map.169 = (bf16[16,16,80]{2,1,0:T(8,128)(2,1)}, bf16[16,80,3840]{2,1,0:T(8,128)(2,1)}, bf16[16,80,1280]{2,1,0:T(8,128)(2,1)}, bf16[16,80,5120]{2,1,0:T(8,...) custom-call(bf16[16,80]{1,0:T(8,128)(2,1)} %maximum_bitcast_fusion.r, ...), custom_call_target="tpu_custom_call" | custom-call | flops 30198988800 | bytes 157286400 | tf_op jit(solution)/shard_map/pallas_call | solution.py:1157
  226.5 4.6 collective-permute-start
  231.0 0.6 fusion
  231.6 1.6 shard_map.170
  233.2 15.8 %collective-permute-done.entry_h = bf16[384,1280]{1,0:T(8,128)(2,1)S(1)} collective-permute-done((bf16[384,1280]{1,0:T(8,128)(2,1)}, bf16[384,1280]{1,0:T(8,128)(2,1)S(1)}, u32[]{:S(2)}, u32[]{:S(2)}) %collective-permute-start) | collective-permute-done | bytes 983072 | tf_op jit(solution)/shard_map/ppermute | solution.py:1923
  249.0 0.9 copy-done.5
  249.9 9.9 %shard_map.171 = (bf16[384,1280]{1,0:T(8,128)(2,1)}, bf16[2,384,1280]{2,1,0:T(8,128)(2,1)}, bf16[2,384,1280]{2,1,0:T(8,128)(2,1)}, bf16[2,384,3840]{2,1,0:T(8,12...) custom-call(s32[1]{0:T(128)} %bitcast.active, ...), custom_call_target="tpu_custom_call", output_to_operand_aliasing={{1}: (7, {}), {2}: (8, {}), {3}: (9, {}), {4}: (10, {}), {5... | custom-call | flops 18119393280 | bytes 39321600 | tf_op jit(solution)/shard_map/pallas_call | solution.py:562
  259.8 13.8 %shard_map.172 = (bf16[384,1280]{1,0:T(8,128)(2,1)}, bf16[2,384,1280]{2,1,0:T(8,128)(2,1)}, bf16[2,384,3840]{2,1,0:T(8,128)(2,1)}, bf16[2,384,1280]{2,1,0:T(8,12...) custom-call(s32[1]{0:T(128)} %bitcast.active, ...), custom_call_target="tpu_custom_call" | custom-call | flops 22649241600 | bytes 39321600 | tf_op jit(solution)/shard_map/pallas_call | solution.py:729
  273.6 1.3 collective-permute-start.2
  274.9 12.3 %shard_map.173 = (bf16[384,1280]{1,0:T(8,128)(2,1)}, bf16[2,384,1280]{2,1,0:T(8,128)(2,1)}, bf16[2,384,3840]{2,1,0:T(8,128)(2,1)}, bf16[2,384,1280]{2,1,0:T(8,12...) custom-call(s32[1]{0:T(128)} %bitcast.active, ...), custom_call_target="tpu_custom_call", output_to_operand_aliasing={{1}: (12, {}), {2}: (13, {}), {3}: (14, {}), {4}: (15, {}),... | custom-call | flops 22649241600 | bytes 39321600 | tf_op jit(solution)/shard_map/pallas_call | solution.py:729
  287.1 1.3 collective-permute-start.1
  288.4 68.6 %collective-permute-done.2.grad_h = bf16[384,1280]{1,0:T(8,128)(2,1)S(1)} collective-permute-done((bf16[384,1280]{1,0:T(8,128)(2,1)}, bf16[384,1280]{1,0:T(8,128)(2,1)S(1)}, u32[]{:S(2)}, u32[]{:S(2)}) %collective-permute-start.2) | collective-permute-done | bytes 983072 | tf_op jit(solution)/shard_map/ppermute | solution.py:1923
  357.1 0.9 copy-done.9
  358.0 42.2 %shard_map.174 = (bf16[384,1280]{1,0:T(8,128)(2,1)}, bf16[2,384,1280]{2,1,0:T(8,128)(2,1)}, bf16[2,384,3840]{2,1,0:T(8,128)(2,1)}, bf16[2,384,1280]{2,1,0:T(8,12...) custom-call(s32[1]{0:T(128)} %bitcast.12.active, ...), custom_call_target="tpu_custom_call", output_to_operand_aliasing={{1}: (12, {}), {2}: (13, {}), {3}: (14, {}), {4}: (15, {}),... | custom-call | flops 22649241600 | bytes 39321600 | tf_op jit(solution)/shard_map/pallas_call | solution.py:729
  400.3 1.7 collective-permute-done.1.refs_0_
  401.9 0.9 copy-done.8
  402.9 220.7 %shard_map.175 = (bf16[2,384,1280]{2,1,0:T(8,128)(2,1)}, bf16[768,3840]{1,0:T(8,128)(2,1)}, bf16[768,1280]{1,0:T(8,128)(2,1)}, bf16[768,5120]{1,0:T(8,128)(2,1)}...) custom-call(bf16[384,1280]{1,0:T(8,128)(2,1)} %copy-done.8, ...), custom_call_target="tpu_custom_call", output_to_operand_aliasing={{0}: (15, {}), {1}: (16, {}), {2}: (17, {}), {3}: (18, {}),... | custom-call | flops 45298483200 | bytes 262144000 | tf_op jit(solution)/shard_map/pallas_call | solution.py:1810
  623.5 1.3 reshape.84
  624.8 1.4 copy.52
  626.2 1.3 copy.93
  627.5 0.0 copy-done.1
  627.5 1.3 copy.94
  628.8 0.6 copy.95
  629.3 0.1 copy-done.4
  629.5 1.0 copy.96
  630.5 0.8 copy.97
  631.3 1.2 copy.98
  632.4 1.2 copy.99
  (19 shorter events, 0.0 us)
Async XLA Ops:
  2.9 228.2 %copy-start.10 = (s32[2]{0:T(128)S(1)}, s32[2]{0:T(128)}, u32[]{:S(2)}) copy-start(s32[2]{0:T(128)} %param.12) | copy-start | bytes 28
  226.5 22.5 %collective-permute-start = (bf16[384,1280]{1,0:T(8,128)(2,1)}, bf16[384,1280]{1,0:T(8,128)(2,1)S(1)}, u32[]{:S(2)}, u32[]{:S(2)}) collective-permute-start(bf16[384,1280]{1,0:T(8,128)(2,1)} %get-tuple-element.68), channel_id=1, source_target_pairs={{0,16},{1,17},{2,18},{3,19},{4,20},{5,21},{6,22},{7,23},{8,24},{9,... | collective-permute-start | bytes 2949128 | tf_op jit(solution)/shard_map/ppermute | solution.py:1923
  249.0 0.9 copy-start.5
  273.6 83.5 %collective-permute-start.2 = (bf16[384,1280]{1,0:T(8,128)(2,1)}, bf16[384,1280]{1,0:T(8,128)(2,1)S(1)}, u32[]{:S(2)}, u32[]{:S(2)}) collective-permute-start(bf16[384,1280]{1,0:T(8,128)(2,1)} %get-tuple-element.103), channel_id=1, source_target_pairs={{16,0},{17,1},{18,2},{19,3},{20,4},{21,5},{22,6},{23,7},{24,8},{25... | collective-permute-start | bytes 2949128 | tf_op jit(solution)/shard_map/ppermute | solution.py:1923
  287.1 114.8 %collective-permute-start.1 = (bf16[384,1280]{1,0:T(8,128)(2,1)}, bf16[384,1280]{1,0:T(8,128)(2,1)S(1)}, u32[]{:S(2)}, u32[]{:S(2)}) collective-permute-start(bf16[384,1280]{1,0:T(8,128)(2,1)} %get-tuple-element.101), channel_id=1, source_target_pairs={{16,0},{17,1},{18,2},{19,3},{20,4},{21,5},{22,6},{23,7},{24,8},{25... | collective-permute-start | bytes 2949128 | tf_op jit(solution)/shard_map/ppermute | solution.py:1923
  357.1 0.9 copy-start.9
  401.9 0.9 copy-start.8
  402.9 223.4 %copy-start = (bf16[2,384,1280]{2,1,0:T(8,128)(2,1)S(1)}, bf16[2,384,1280]{2,1,0:T(8,128)(2,1)}, u32[]{:S(2)}) copy-start(bf16[2,384,1280]{2,1,0:T(8,128)(2,1)} %get-tuple-element.91) | copy-start | bytes 5898244
  624.8 2.7 copy-start.1
  627.5 1.3 copy-start.7
  627.5 2.0 copy-start.4
  627.5 3.0 copy-start.6
  628.8 2.5 copy-start.3
  630.5 1.9 copy-start.2

commit v10 on v9

--- a/solution.py
+++ b/solution.py
@@ -786,12 +786,12 @@
 
 def gather_forward_kernel(chips, items, groups, cells, *refs):
     shards, inputs_h = (refs[:5], refs[5])
-    outs, rows_h, arrived_h, later_h = (refs[6:11], refs[11], refs[12], refs[13])
-    out_h, lowered_h, packed_h, mixed_h, middle_h, second_h, active_h, slope_h = refs[14:22]
-    (ring_send, ring_recv, pair_send, pair_recv, own_sem, hop_send, hop_recv) = refs[22:29]
-    (load_sem, save_sem, wide_sem, deep_sem) = refs[29:33]
-    (small_v, rows_v, entry_v, out_v, lowered_v, packed_v, mixed_v, middle_v, second_v, active_v, slope_v) = refs[33:44]
-    (total_v, hidden_v, wide_v, deep_v) = refs[44:]
+    outs, rows_h, arrived_h = (refs[6:11], refs[11], refs[12])
+    out_h, lowered_h, packed_h, mixed_h, middle_h, second_h, active_h, slope_h = refs[13:21]
+    (ring_send, ring_recv, pair_send, pair_recv, own_sem, hop_send, hop_recv) = refs[21:28]
+    (load_sem, save_sem, wide_sem, deep_sem) = refs[28:32]
+    (small_v, rows_v, entry_v, out_v, lowered_v, packed_v, mixed_v, middle_v, second_v, active_v, slope_v) = refs[32:43]
+    (total_v, hidden_v, wide_v, deep_v) = refs[43:]
     length, width = entry_v.shape[1:]
     ups = active_v.shape[2] // width
     half = chips // 2
@@ -869,12 +869,13 @@
         block = ring_chip(position - offset, chips) * 2 + core
         pair_copy(item, offset, block, out(item, block)).wait_recv()
 
-    saves = []
+    saves = [[], []]
+    runner = [0]
 
     def save(source, target):
-        number = len(saves)
-        saves.append(lambda: pltpu.make_async_copy(source(), target(), save_sem.at[number]))
-        saves[-1]().start()
+        number = len(saves[0]) + len(saves[1])
+        saves[runner[0]].append(lambda: pltpu.make_async_copy(source(), target(), save_sem.at[number]))
+        saves[runner[0]][-1]().start()
 
     def entry_load(cell):
         return pltpu.make_async_copy(inputs_h.at[cell], entry_v.at[cell], load_sem.at[cell])
@@ -894,7 +895,8 @@
 
     def begin(cell):
         def step():
-            entry_load(cell).wait()
+            if runner[0] == 0:
+                entry_load(cell).wait()
             normed, _ = row_norm(entry_v[cell].astype(F32))
             lowered_v[cell] = (normed * gains(0) + shifts(0)).astype(LOW)
             save(lambda: lowered_v.at[cell], lambda: lowered_h.at[cell])
@@ -977,12 +979,12 @@
 
         return step
 
-    def hop():
+    def hop(cell):
         return pltpu.make_async_remote_copy(
-            src_ref=out_v.at[0],
-            dst_ref=arrived_h,
-            send_sem=hop_send,
-            recv_sem=hop_recv,
+            src_ref=out_v.at[cell],
+            dst_ref=entry_v.at[cell],
+            send_sem=hop_send.at[cell],
+            recv_sem=hop_recv.at[cell],
             device_id={"pipe": 1 - stage},
             device_id_type=MESH,
         )
@@ -990,10 +992,8 @@
     def finish(cell):
         def step():
             out_v[cell] = total_v[cell].astype(LOW)
-            if cell == 0:
-                hop().start()
-            else:
-                save(lambda: out_v.at[cell], lambda: later_h)
+            if runner[0] == 0 and cell == 0:
+                hop(0).start()
             save(lambda: out_v.at[cell], lambda: out_h.at[cell])
 
         return step
@@ -1009,10 +1009,8 @@
             for offset in range(chips):
                 pair_arrived(item, offset)
 
-        @pl.when(first)
-        def _():
-            for load in loads:
-                load().start()
+        for load in loads:
+            load().start()
 
         queue.extend(steps)
 
@@ -1136,13 +1134,47 @@
 
     @pl.when(first)
     def _():
-        for copy in saves:
+        for cell in range(cells):
+            if cell > 0:
+                hop(cell).start()
+            hop(cell).wait_send()
+        for copy in saves[0]:
             copy().wait()
-        hop().wait_send()
 
     @pl.when(jnp.logical_not(first))
     def _():
-        hop().wait_recv()
+        runner[0] = 1
+
+        def arrive(cell):
+            hop(cell).wait_recv()
+            save(lambda: entry_v.at[cell], lambda: arrived_h.at[cell])
+
+        arrive(0)
+        begin(0)()
+        for number in range(3):
+            project(0, number)()
+            if number < ups:
+                wide_load(3, number, number).start()
+        attend(packed_v.at[0], mixed_v.at[0], width)
+        mix(0, 0, 0, True)()
+        join(0)()
+        for number in range(3, ups):
+            wide_load(3, number, number).start()
+        for offset in (0, 1):
+            deep_load(offset, offset).start()
+        renorm(0)()
+        for number in range(ups):
+            rise(0, number)()
+            bend(0, number)()
+        for offset in range(chips):
+            fall(0, offset, offset % 2)()
+            if offset + 2 < chips:
+                deep_load(offset + 2, offset % 2).start()
+        finish(0)()
+        for cell in range(1, cells):
+            arrive(cell)
+        for copy in saves[1]:
+            copy().wait()
 
 
 def gather_forward(shards, inputs, items, groups, count):
@@ -1159,22 +1191,21 @@
         out_shape=[jax.ShapeDtypeStruct((count,) + shard.shape, shard.dtype) for shard in shards]
         + [
             jax.ShapeDtypeStruct((16, width), F32),
-            jax.ShapeDtypeStruct((length, width), LOW),
-            jax.ShapeDtypeStruct((length, width), LOW),
+            jax.ShapeDtypeStruct((cells, length, width), LOW),
         ]
         + [jax.ShapeDtypeStruct((cells,) + shape, kind) for shape, kind in shapes],
         in_specs=[hbm] * 6,
-        out_specs=[hbm] * 16,
+        out_specs=[hbm] * 15,
         scratch_shapes=[
             pltpu.SemaphoreType.DMA((pieces, 2, chips // 2)),
             pltpu.SemaphoreType.DMA((pieces, 2, chips // 2)),
             pltpu.SemaphoreType.DMA((pieces, chips)),
             pltpu.SemaphoreType.DMA((pieces, chips)),
             pltpu.SemaphoreType.DMA((pieces,)),
-            pltpu.SemaphoreType.DMA,
-            pltpu.SemaphoreType.DMA,
+            pltpu.SemaphoreType.DMA((cells,)),
+            pltpu.SemaphoreType.DMA((cells,)),
             pltpu.SemaphoreType.DMA((cells + 2,)),
-            pltpu.SemaphoreType.DMA((9 * cells,)),
+            pltpu.SemaphoreType.DMA((9 * cells + 9 + cells,)),
             pltpu.SemaphoreType.DMA((4,)),
             pltpu.SemaphoreType.DMA((2,)),
             pltpu.VMEM((count,) + shards[0].shape, LOW),
@@ -1193,7 +1224,7 @@
         ),
         cost_estimate=pl.CostEstimate(flops=flops, bytes_accessed=8 * width * (4 * width + 2 * deep), transcendentals=0),
     )(*shards, inputs)
-    return (outs[:5], outs[5], outs[6], outs[7], list(outs[8:]))
+    return (outs[:5], outs[5], outs[6], list(outs[7:]))
 
 
 class RingSum:
@@ -1329,7 +1360,7 @@
             step, item, way, offset = entry
             clock = max(clock, when) + 0.8 + self.bytes_of(item) * 1.6e-6
             if way is not None:
-                link[way] = max(clock, link[way]) + 2 * self.bytes_of(item) / 9.4e4
+                link[way] = max(clock, link[way]) + 2 * self.bytes_of(item) / 9.1e4
                 arrival[(item, way, step)] = link[way] + 1.5
                 sends[(item, used[item])] = link[way]
             order.append(entry + (used[item] % 2,))
@@ -1537,20 +1568,20 @@
             if index + 1 < chips:
                 cut_down(index + 1).start()
             cut_down(index).wait()
-            if index == 2 or index >= 5:
-                keep_down(index - 2).wait()
             product = dot_left(cuts[slot], big[0]).astype(LOW)
             for side in (0, 1):
                 stage_down[slot, side] = product[side * deep_own : (side + 1) * deep_own]
             keep_down(index).start()
-            if index == 2:
-                for at in (1, 2):
-                    keep_down(at).wait()
-            if index == chips - 1:
-                for at in (chips - 2, chips - 1):
-                    keep_down(at).wait()
+            if index > 0:
+                keep_down(index - 1).wait()
 
         return step
+
+    def last_down():
+        keep_down(chips - 1).wait()
+
+    def far_offset(index):
+        return (half - index // 2 if index % 2 == 0 else half + index // 2 + 1) % chips
 
     def here(ref, at):
         return ref.at[pl.ds(at * length, length)]
@@ -1739,9 +1770,7 @@
     outers = [item for item in range(count) if items[item][0] == 2]
     head_items = [item for item in range(count) if items[item][0] == 1]
     smalls = [item for item in range(count) if items[item][0] == 0]
-    far = [half, half - 1, half + 1]
-    near = [offset for offset in range(chips) if offset not in far]
-    everywhere = far + near
+    everywhere = [far_offset(index) for index in range(chips)]
 
     def only_first(step):
         return lambda: pl.when(first)(step)
@@ -1765,23 +1794,25 @@
         made = [(0.3, opening(left, right, shift), [])]
         for index in range(number):
             opens = all_of(wanted, everywhere) if index + 1 == number else []
-            made.append((1.8, product(target, left, right, shift, index), opens))
+            made.append((1.9, product(target, left, right, shift, index), opens))
         return made
 
-    steps = [(1.8, down_product(index), all_of(downs, far) if index == 2 else []) for index in range(3)]
-    steps.append((0.3, only_first(begin), []))
-    for index in range(3, chips):
-        steps.append((1.8, down_product(index), all_of(downs, near) if index == chips - 1 else []))
-    steps += [(1.7 if number in (0, ups) else 3.0, only_first(climb(number)), []) for number in range(ups + 1)]
-    steps.append((2.5, only_first(turn), []))
+    steps = []
+    for index in range(chips):
+        steps.append((1.9, down_product(index), all_of(downs, [far_offset(index - 1)] if index else [])))
+        if index == 3:
+            steps.append((0.3, only_first(begin), []))
+    steps.append((0.7, last_down, all_of(downs, [far_offset(chips - 1)])))
+    steps += [(2.0 if number in (0, ups) else 3.5, only_first(climb(number)), []) for number in range(ups + 1)]
+    steps.append((3.0, only_first(turn), []))
     steps += blocks(up_part, second_h, inner_o, 1, up_items)
     steps += blocks(parts[2], mixed_h, branch_o, 1, outers)
     steps.append((1.7, only_first(outer), []))
-    steps += [(1.25, only_first(heads(low, low + 1)), []) for low in range(pairs)]
+    steps += [(2.5, only_first(heads(low, low + 2)), []) for low in range(0, pairs, 2)]
     steps.append((0.8, only_first(sums), []))
     steps += blocks(parts[1], lowered_h, packed_o, 0, head_items)
-    steps += [(1.5, only_first(lower(number)), []) for number in range(3)]
-    steps.append((2.5, only_first(finish), []))
+    steps += [(1.8, only_first(lower(number)), []) for number in range(3)]
+    steps.append((3.0, only_first(finish), []))
     steps.append((2.0, lay_small, all_of(smalls, everywhere)))
     greet((ring.left, ring.right, ring.sibling))
     schedule, _ = ring.arrange(steps, 8.0)
@@ -1902,7 +1933,7 @@
             (4, 0, cut, 0),
             (4, cut, deep_own - cut, 1),
         )
-        packs, rows, arrived, later, kept = gather_forward(
+        packs, rows, arrived, kept = gather_forward(
             shards, inputs, arrivals, ((0, 1, 2, 3), (4, 5), (6, 7)), count
         )
     else:
@@ -1924,13 +1955,13 @@
 
     entries = [[(inputs, cell) for cell in range(cell_count)]]
     if fused:
-        entries.append([(arrived, None), (along(later, 1), None)])
+        entries.append([(arrived, cell) for cell in range(cell_count)])
     else:
         kept = None
     for turn in range(1 if fused else 0, stages):
         active = (stage == turn).astype(jnp.int32)[None]
         arrived = []
-        for cell in range(cell_count):
+        for cell in range(1 if fused else 0, cell_count):
             sent, kept = forward_tick(active, entries[turn][cell], rows, weights, kept, cell, cell_count)
             if turn + 1 < stages:
                 arrived.append((along(sent, 1), None))

time: 644 us -> 641 us (level)
  Pallas kernels: 524 us -> 546 us
  waiting for transfers between devices: 86 us -> 65.6 us
    pallas_call x1, Pallas kernels: 224 us -> 250 us  [gather_forward(): pl.pallas_call(functools.partial(gather_forward_kernel, chips, items, gro...]
    ppermute x3 -> x2, waiting for transfers between devices: 86 us -> 65.6 us  [along(): return lax.ppermute(value, 'pipe', pairs)]
    pallas_call x2 -> x1, Pallas kernels: 11.4 us -> 13.8 us  [forward_tick(): pl.pallas_call(functools.partial(forward_kernel, cell, held, at), out_sha...]
  transfers between devices with their start and end apart: 3 -> 2, of which waited for: 3 -> 2; matrix products, arithmetic and copies ran while one was open for 0% -> 0% of each run, Pallas kernels for 9% -> 9%
where the time goes in v10:
time: 641 us; the launch traced here: 631 us
  Pallas kernels  546 us (85%)
  waiting for transfers between devices  65.6 us (10%)
  local copies, waits for them, and re-layouts  12.8 us (2%)
    pallas_call x1, Pallas kernels, gather_forward(): pl.pallas_call(functools.partial(gather_forward_kernel, chips, items, gro...  250 us
    pallas_call x1, Pallas kernels, last_backward(): pl.pallas_call(functools.partial(last_backward_kernel, chips, items, cell...  215 us
    pallas_call x3, Pallas kernels, backward_tick(): pl.pallas_call(functools.partial(backward_kernel, cell, held, grad_at, en...  68.2 us
    ppermute x2, waiting for transfers between devices, along(): return lax.ppermute(value, 'pipe', pairs)  65.6 us
    pallas_call x1, Pallas kernels, forward_tick(): pl.pallas_call(functools.partial(forward_kernel, cell, held, at), out_sha...  13.8 us
  transfers between devices with their start and end apart: 2, of which 2 were waited for; matrix products, arithmetic and copies ran while one was open for 0% of the time, Pallas kernels for 9%

profile of v10, /device:TPU:0, one launch (start us, length us, event | category | flops | bytes accessed | tf_op | source)
XLA Modules:
  0.0 631.0 jit_solution(17049286245225581441)
XLA Ops:
  0.6 0.7 multiply_sqrt_fusion
  1.3 0.6 fusion
  1.9 0.7 reduce
  2.6 0.1 reshape_squeeze.3
  2.7 0.1 pad.3.clone
  2.8 1.4 maximum_bitcast_fusion.refs_0_
  4.1 249.5 %shard_map.169 = (bf16[16,16,80]{2,1,0:T(8,128)(2,1)}, bf16[16,80,3840]{2,1,0:T(8,128)(2,1)}, bf16[16,80,1280]{2,1,0:T(8,128)(2,1)}, bf16[16,80,5120]{2,1,0:T(8,...) custom-call(bf16[16,80]{1,0:T(8,128)(2,1)} %maximum_bitcast_fusion.r, ...), custom_call_target="tpu_custom_call" | custom-call | flops 30198988800 | bytes 157286400 | tf_op jit(solution)/shard_map/pallas_call | solution.py:1189
  253.7 13.8 %shard_map.170 = (bf16[384,1280]{1,0:T(8,128)(2,1)}, bf16[2,384,1280]{2,1,0:T(8,128)(2,1)}, bf16[2,384,1280]{2,1,0:T(8,128)(2,1)}, bf16[2,384,3840]{2,1,0:T(8,12...) custom-call(s32[1]{0:T(128)} %bitcast.active, ...), custom_call_target="tpu_custom_call", output_to_operand_aliasing={{1}: (7, {}), {2}: (8, {}), {3}: (9, {}), {4}: (10, {}), {5... | custom-call | flops 18119393280 | bytes 39321600 | tf_op jit(solution)/shard_map/pallas_call | solution.py:562
  267.4 13.7 %shard_map.171 = (bf16[384,1280]{1,0:T(8,128)(2,1)}, bf16[2,384,1280]{2,1,0:T(8,128)(2,1)}, bf16[2,384,3840]{2,1,0:T(8,128)(2,1)}, bf16[2,384,1280]{2,1,0:T(8,12...) custom-call(s32[1]{0:T(128)} %bitcast.active, ...), custom_call_target="tpu_custom_call" | custom-call | flops 22649241600 | bytes 39321600 | tf_op jit(solution)/shard_map/pallas_call | solution.py:729
  281.2 1.3 collective-permute-start.1
  282.5 12.5 %shard_map.172 = (bf16[384,1280]{1,0:T(8,128)(2,1)}, bf16[2,384,1280]{2,1,0:T(8,128)(2,1)}, bf16[2,384,3840]{2,1,0:T(8,128)(2,1)}, bf16[2,384,1280]{2,1,0:T(8,12...) custom-call(s32[1]{0:T(128)} %bitcast.active, ...), custom_call_target="tpu_custom_call", output_to_operand_aliasing={{1}: (12, {}), {2}: (13, {}), {3}: (14, {}), {4}: (15, {}),... | custom-call | flops 22649241600 | bytes 39321600 | tf_op jit(solution)/shard_map/pallas_call | solution.py:729
  295.0 1.3 collective-permute-start
  296.3 63.4 %collective-permute-done.1.grad_h = bf16[384,1280]{1,0:T(8,128)(2,1)S(1)} collective-permute-done((bf16[384,1280]{1,0:T(8,128)(2,1)}, bf16[384,1280]{1,0:T(8,128)(2,1)S(1)}, u32[]{:S(2)}, u32[]{:S(2)}) %collective-permute-start.1) | collective-permute-done | bytes 983072 | tf_op jit(solution)/shard_map/ppermute | solution.py:1954
  359.7 0.9 copy-done.8
  360.6 41.9 %shard_map.173 = (bf16[384,1280]{1,0:T(8,128)(2,1)}, bf16[2,384,1280]{2,1,0:T(8,128)(2,1)}, bf16[2,384,3840]{2,1,0:T(8,128)(2,1)}, bf16[2,384,1280]{2,1,0:T(8,12...) custom-call(s32[1]{0:T(128)} %bitcast.12.active, ...), custom_call_target="tpu_custom_call", output_to_operand_aliasing={{1}: (12, {}), {2}: (13, {}), {3}: (14, {}), {4}: (15, {}),... | custom-call | flops 22649241600 | bytes 39321600 | tf_op jit(solution)/shard_map/pallas_call | solution.py:729
  402.6 2.2 collective-permute-done.refs_0_
  404.8 0.9 copy-done.7
  405.7 215.0 %shard_map.174 = (bf16[2,384,1280]{2,1,0:T(8,128)(2,1)}, bf16[768,3840]{1,0:T(8,128)(2,1)}, bf16[768,1280]{1,0:T(8,128)(2,1)}, bf16[768,5120]{1,0:T(8,128)(2,1)}...) custom-call(bf16[384,1280]{1,0:T(8,128)(2,1)} %copy-done.7, ...), custom_call_target="tpu_custom_call", output_to_operand_aliasing={{0}: (15, {}), {1}: (16, {}), {2}: (17, {}), {3}: (18, {}),... | custom-call | flops 45298483200 | bytes 262144000 | tf_op jit(solution)/shard_map/pallas_call | solution.py:1841
  620.7 1.3 reshape.84
  622.0 1.4 copy.44
  623.4 0.0 copy-done
  623.4 1.3 copy.77
  624.7 0.0 copy-done.1
  624.7 1.3 copy.78
  626.0 0.6 copy.79
  626.6 0.1 copy-done.4
  626.7 1.0 copy.80
  627.8 0.0 copy-done.5
  627.8 0.8 copy.81
  628.5 0.0 copy-done.3
  628.5 1.2 copy.82
  629.7 1.2 copy.83
  (12 shorter events, 0.0 us)
Async XLA Ops:
  281.2 78.5 %collective-permute-start.1 = (bf16[384,1280]{1,0:T(8,128)(2,1)}, bf16[384,1280]{1,0:T(8,128)(2,1)S(1)}, u32[]{:S(2)}, u32[]{:S(2)}) collective-permute-start(bf16[384,1280]{1,0:T(8,128)(2,1)} %get-tuple-element.85), channel_id=1, source_target_pairs={{16,0},{17,1},{18,2},{19,3},{20,4},{21,5},{22,6},{23,7},{24,8},{25... | collective-permute-start | bytes 2949128 | tf_op jit(solution)/shard_map/ppermute | solution.py:1954
  295.0 109.8 %collective-permute-start = (bf16[384,1280]{1,0:T(8,128)(2,1)}, bf16[384,1280]{1,0:T(8,128)(2,1)S(1)}, u32[]{:S(2)}, u32[]{:S(2)}) collective-permute-start(bf16[384,1280]{1,0:T(8,128)(2,1)} %get-tuple-element.83), channel_id=1, source_target_pairs={{16,0},{17,1},{18,2},{19,3},{20,4},{21,5},{22,6},{23,7},{24,8},{25... | collective-permute-start | bytes 2949128 | tf_op jit(solution)/shard_map/ppermute | solution.py:1954
  359.7 0.9 copy-start.8
  404.8 0.9 copy-start.7
  405.7 217.7 %copy-start = (bf16[2,384,1280]{2,1,0:T(8,128)(2,1)S(1)}, bf16[2,384,1280]{2,1,0:T(8,128)(2,1)}, u32[]{:S(2)}) copy-start(bf16[2,384,1280]{2,1,0:T(8,128)(2,1)} %get-tuple-element.73) | copy-start | bytes 5898244
  622.0 2.7 copy-start.1
  624.7 1.3 copy-start.6
  624.7 2.0 copy-start.4
  624.7 3.0 copy-start.5
  626.0 2.5 copy-start.3
  627.8 1.9 copy-start.2

commit v11 on v9

--- a/solution.py
+++ b/solution.py
@@ -1329,7 +1329,7 @@
             step, item, way, offset = entry
             clock = max(clock, when) + 0.8 + self.bytes_of(item) * 1.6e-6
             if way is not None:
-                link[way] = max(clock, link[way]) + 2 * self.bytes_of(item) / 9.4e4
+                link[way] = max(clock, link[way]) + 2 * self.bytes_of(item) / 9.1e4
                 arrival[(item, way, step)] = link[way] + 1.5
                 sends[(item, used[item])] = link[way]
             order.append(entry + (used[item] % 2,))
@@ -1375,10 +1375,12 @@
                 self.load_ring(item, side, half, side).wait()
             if kind == F32:
                 total = (rings[0] + rings[1]) + (mine[buffer] + pairs[buffer])
-                top = 0
-                for out in self.outs[array]:
-                    out[...] = total[top : top + out.shape[0]]
-                    top += out.shape[0]
+                gains, shifts, bias = self.outs[array]
+                gains[...] = total[0:2]
+                for row in range(6):
+                    shifts[row] = total[2 + row : 3 + row]
+                ups = bias.shape[1] // total.shape[1]
+                bias[...] = jnp.concatenate([total[8 + up : 9 + up] for up in range(ups)], axis=1)
                 return
             high, wide = (min(rows, final.shape[1]), min(columns, final.shape[2]))
             for top in range(0, rows, high):
@@ -1537,20 +1539,20 @@
             if index + 1 < chips:
                 cut_down(index + 1).start()
             cut_down(index).wait()
-            if index == 2 or index >= 5:
-                keep_down(index - 2).wait()
             product = dot_left(cuts[slot], big[0]).astype(LOW)
             for side in (0, 1):
                 stage_down[slot, side] = product[side * deep_own : (side + 1) * deep_own]
             keep_down(index).start()
-            if index == 2:
-                for at in (1, 2):
-                    keep_down(at).wait()
-            if index == chips - 1:
-                for at in (chips - 2, chips - 1):
-                    keep_down(at).wait()
+            if index > 0:
+                keep_down(index - 1).wait()
 
         return step
+
+    def last_down():
+        keep_down(chips - 1).wait()
+
+    def far_offset(index):
+        return (half - index // 2 if index % 2 == 0 else half + index // 2 + 1) % chips
 
     def here(ref, at):
         return ref.at[pl.ds(at * length, length)]
@@ -1739,9 +1741,7 @@
     outers = [item for item in range(count) if items[item][0] == 2]
     head_items = [item for item in range(count) if items[item][0] == 1]
     smalls = [item for item in range(count) if items[item][0] == 0]
-    far = [half, half - 1, half + 1]
-    near = [offset for offset in range(chips) if offset not in far]
-    everywhere = far + near
+    everywhere = [far_offset(index) for index in range(chips)]
 
     def only_first(step):
         return lambda: pl.when(first)(step)
@@ -1765,23 +1765,25 @@
         made = [(0.3, opening(left, right, shift), [])]
         for index in range(number):
             opens = all_of(wanted, everywhere) if index + 1 == number else []
-            made.append((1.8, product(target, left, right, shift, index), opens))
+            made.append((1.9, product(target, left, right, shift, index), opens))
         return made
 
-    steps = [(1.8, down_product(index), all_of(downs, far) if index == 2 else []) for index in range(3)]
-    steps.append((0.3, only_first(begin), []))
-    for index in range(3, chips):
-        steps.append((1.8, down_product(index), all_of(downs, near) if index == chips - 1 else []))
-    steps += [(1.7 if number in (0, ups) else 3.0, only_first(climb(number)), []) for number in range(ups + 1)]
-    steps.append((2.5, only_first(turn), []))
+    steps = []
+    for index in range(chips):
+        steps.append((1.9, down_product(index), all_of(downs, [far_offset(index - 1)] if index else [])))
+        if index == 3:
+            steps.append((0.3, only_first(begin), []))
+    steps.append((0.7, last_down, all_of(downs, [far_offset(chips - 1)])))
+    steps += [(2.0 if number in (0, ups) else 3.5, only_first(climb(number)), []) for number in range(ups + 1)]
+    steps.append((3.0, only_first(turn), []))
     steps += blocks(up_part, second_h, inner_o, 1, up_items)
     steps += blocks(parts[2], mixed_h, branch_o, 1, outers)
     steps.append((1.7, only_first(outer), []))
-    steps += [(1.25, only_first(heads(low, low + 1)), []) for low in range(pairs)]
+    steps += [(2.5, only_first(heads(low, low + 2)), []) for low in range(0, pairs, 2)]
     steps.append((0.8, only_first(sums), []))
     steps += blocks(parts[1], lowered_h, packed_o, 0, head_items)
-    steps += [(1.5, only_first(lower(number)), []) for number in range(3)]
-    steps.append((2.5, only_first(finish), []))
+    steps += [(1.8, only_first(lower(number)), []) for number in range(3)]
+    steps.append((3.0, only_first(finish), []))
     steps.append((2.0, lay_small, all_of(smalls, everywhere)))
     greet((ring.left, ring.right, ring.sibling))
     schedule, _ = ring.arrange(steps, 8.0)
@@ -1810,7 +1812,7 @@
     outs = pl.pallas_call(
         functools.partial(last_backward_kernel, chips, items, cells - 1),
         out_shape=[jax.ShapeDtypeStruct(array.shape, array.dtype) for array in kept]
-        + [jax.ShapeDtypeStruct((many, own), F32) for many in (2, 6, deep // width)]
+        + [jax.ShapeDtypeStruct(shape, F32) for shape in ((2, own), (6, 1, own), (1, deep // count))]
         + [jax.ShapeDtypeStruct(shape, F32) for shape in wholes[1:]]
         + [jax.ShapeDtypeStruct((count,) + shape, LOW) for shape in wholes[1:]]
         + [jax.ShapeDtypeStruct((chips - 1,) + shape, kind) for shape, kind in zip(held, kinds)]
@@ -1976,11 +1978,12 @@
         parts = [small_part] + [whole.reshape((count,) + shape) for whole, shape in zip(products, shapes)]
         small_share, *shares = scatter(parts, items, count)
         grad_gains, grad_shifts, grad_bias = small_split(small_share[None], ups)
+        grad_shifts = grad_shifts[:, None]
     return (
         section_out[None],
         input_grads[None],
         grad_gains[None],
-        grad_shifts[None],
+        grad_shifts.swapaxes(0, 1),
         shares[0].reshape(1, own, 3 * width),
         shares[1].reshape(1, own, width),
         shares[2].reshape(1, own, deep),

time: 644 us -> 638 us (level)
  no operation moved by 1% of the time
where the time goes in v11:
time: 638 us; the launch traced here: 628 us
  Pallas kernels  518 us (81%)
  waiting for transfers between devices  86.4 us (14%)
  local copies, waits for them, and re-layouts  12.9 us (2%)
  starting transfers between devices  7.14 us (1%)
    pallas_call x1, Pallas kernels, gather_forward(): pl.pallas_call(functools.partial(gather_forward_kernel, chips, items, gro...  224 us
    pallas_call x1, Pallas kernels, last_backward(): pl.pallas_call(functools.partial(last_backward_kernel, chips, items, cell...  215 us
    ppermute x3, waiting for transfers between devices, along(): return lax.ppermute(value, 'pipe', pairs)  86.4 us
    pallas_call x3, Pallas kernels, backward_tick(): pl.pallas_call(functools.partial(backward_kernel, cell, held, grad_at, en...  68.1 us
  transfers between devices with their start and end apart: 3, of which 3 were waited for; matrix products, arithmetic and copies ran while one was open for 0% of the time, Pallas kernels for 9%

profile of v11, /device:TPU:0, one launch (start us, length us, event | category | flops | bytes accessed | tf_op | source)
XLA Modules:
  0.0 627.7 jit_solution(8925965934509226877)
XLA Ops:
  0.6 0.7 reduce
  1.3 0.1 reshape_squeeze.3
  1.4 0.1 pad.3.clone
  1.5 1.4 maximum_bitcast_fusion.refs_0_
  2.9 223.6 %shard_map.169 = (bf16[16,16,80]{2,1,0:T(8,128)(2,1)}, bf16[16,80,3840]{2,1,0:T(8,128)(2,1)}, bf16[16,80,1280]{2,1,0:T(8,128)(2,1)}, bf16[16,80,5120]{2,1,0:T(8,...) custom-call(bf16[16,80]{1,0:T(8,128)(2,1)} %maximum_bitcast_fusion.r, ...), custom_call_target="tpu_custom_call" | custom-call | flops 30198988800 | bytes 157286400 | tf_op jit(solution)/shard_map/pallas_call | solution.py:1157
  226.5 4.6 collective-permute-start
  231.0 0.6 fusion
  231.6 1.8 shard_map.170
  233.4 15.6 %collective-permute-done.entry_h = bf16[384,1280]{1,0:T(8,128)(2,1)S(1)} collective-permute-done((bf16[384,1280]{1,0:T(8,128)(2,1)}, bf16[384,1280]{1,0:T(8,128)(2,1)S(1)}, u32[]{:S(2)}, u32[]{:S(2)}) %collective-permute-start) | collective-permute-done | bytes 983072 | tf_op jit(solution)/shard_map/ppermute | solution.py:1925
  249.0 0.9 copy-done.5
  249.9 9.7 %shard_map.171 = (bf16[384,1280]{1,0:T(8,128)(2,1)}, bf16[2,384,1280]{2,1,0:T(8,128)(2,1)}, bf16[2,384,1280]{2,1,0:T(8,128)(2,1)}, bf16[2,384,3840]{2,1,0:T(8,12...) custom-call(s32[1]{0:T(128)} %bitcast.active, ...), custom_call_target="tpu_custom_call", output_to_operand_aliasing={{1}: (7, {}), {2}: (8, {}), {3}: (9, {}), {4}: (10, {}), {5... | custom-call | flops 18119393280 | bytes 39321600 | tf_op jit(solution)/shard_map/pallas_call | solution.py:562
  259.6 13.7 %shard_map.172 = (bf16[384,1280]{1,0:T(8,128)(2,1)}, bf16[2,384,1280]{2,1,0:T(8,128)(2,1)}, bf16[2,384,3840]{2,1,0:T(8,128)(2,1)}, bf16[2,384,1280]{2,1,0:T(8,12...) custom-call(s32[1]{0:T(128)} %bitcast.active, ...), custom_call_target="tpu_custom_call" | custom-call | flops 22649241600 | bytes 39321600 | tf_op jit(solution)/shard_map/pallas_call | solution.py:729
  273.3 1.3 collective-permute-start.2
  274.6 12.5 %shard_map.173 = (bf16[384,1280]{1,0:T(8,128)(2,1)}, bf16[2,384,1280]{2,1,0:T(8,128)(2,1)}, bf16[2,384,3840]{2,1,0:T(8,128)(2,1)}, bf16[2,384,1280]{2,1,0:T(8,12...) custom-call(s32[1]{0:T(128)} %bitcast.active, ...), custom_call_target="tpu_custom_call", output_to_operand_aliasing={{1}: (12, {}), {2}: (13, {}), {3}: (14, {}), {4}: (15, {}),... | custom-call | flops 22649241600 | bytes 39321600 | tf_op jit(solution)/shard_map/pallas_call | solution.py:729
  287.1 1.3 collective-permute-start.1
  288.4 68.6 %collective-permute-done.2.grad_h = bf16[384,1280]{1,0:T(8,128)(2,1)S(1)} collective-permute-done((bf16[384,1280]{1,0:T(8,128)(2,1)}, bf16[384,1280]{1,0:T(8,128)(2,1)S(1)}, u32[]{:S(2)}, u32[]{:S(2)}) %collective-permute-start.2) | collective-permute-done | bytes 983072 | tf_op jit(solution)/shard_map/ppermute | solution.py:1925
  357.0 0.9 copy-done.11
  357.9 41.9 %shard_map.174 = (bf16[384,1280]{1,0:T(8,128)(2,1)}, bf16[2,384,1280]{2,1,0:T(8,128)(2,1)}, bf16[2,384,3840]{2,1,0:T(8,128)(2,1)}, bf16[2,384,1280]{2,1,0:T(8,12...) custom-call(s32[1]{0:T(128)} %bitcast.12.active, ...), custom_call_target="tpu_custom_call", output_to_operand_aliasing={{1}: (12, {}), {2}: (13, {}), {3}: (14, {}), {4}: (15, {}),... | custom-call | flops 22649241600 | bytes 39321600 | tf_op jit(solution)/shard_map/pallas_call | solution.py:729
  399.8 2.2 collective-permute-done.1.refs_0_
  402.1 0.9 copy-done.10
  403.0 215.0 %shard_map.175 = (bf16[2,384,1280]{2,1,0:T(8,128)(2,1)}, bf16[768,3840]{1,0:T(8,128)(2,1)}, bf16[768,1280]{1,0:T(8,128)(2,1)}, bf16[768,5120]{1,0:T(8,128)(2,1)}...) custom-call(bf16[384,1280]{1,0:T(8,128)(2,1)} %copy-done.10, ...), custom_call_target="tpu_custom_call", output_to_operand_aliasing={{0}: (15, {}), {1}: (16, {}), {2}: (17, {}), {3}: (18, {}),... | custom-call | flops 45298483200 | bytes 262144000 | tf_op jit(solution)/shard_map/pallas_call | solution.py:1812
  618.1 1.3 copy.94
  619.4 1.0 copy-done.1
  620.4 1.3 copy.95
  621.6 0.6 copy.96
  622.2 0.0 copy-done.7
  622.2 0.6 copy.97
  622.8 1.0 copy.98
  623.8 0.8 copy.99
  624.6 1.2 copy.100
  625.7 0.6 copy.101
  626.3 1.2 copy.102
  (23 shorter events, 0.0 us)
Async XLA Ops:
  2.9 228.2 %copy-start.12 = (s32[2]{0:T(128)S(1)}, s32[2]{0:T(128)}, u32[]{:S(2)}) copy-start(s32[2]{0:T(128)} %param.12) | copy-start | bytes 28
  226.5 22.5 %collective-permute-start = (bf16[384,1280]{1,0:T(8,128)(2,1)}, bf16[384,1280]{1,0:T(8,128)(2,1)S(1)}, u32[]{:S(2)}, u32[]{:S(2)}) collective-permute-start(bf16[384,1280]{1,0:T(8,128)(2,1)} %get-tuple-element.68), channel_id=1, source_target_pairs={{0,16},{1,17},{2,18},{3,19},{4,20},{5,21},{6,22},{7,23},{8,24},{9,... | collective-permute-start | bytes 2949128 | tf_op jit(solution)/shard_map/ppermute | solution.py:1925
  249.0 0.9 copy-start.5
  273.3 83.6 %collective-permute-start.2 = (bf16[384,1280]{1,0:T(8,128)(2,1)}, bf16[384,1280]{1,0:T(8,128)(2,1)S(1)}, u32[]{:S(2)}, u32[]{:S(2)}) collective-permute-start(bf16[384,1280]{1,0:T(8,128)(2,1)} %get-tuple-element.103), channel_id=1, source_target_pairs={{16,0},{17,1},{18,2},{19,3},{20,4},{21,5},{22,6},{23,7},{24,8},{25... | collective-permute-start | bytes 2949128 | tf_op jit(solution)/shard_map/ppermute | solution.py:1925
  287.1 115.0 %collective-permute-start.1 = (bf16[384,1280]{1,0:T(8,128)(2,1)}, bf16[384,1280]{1,0:T(8,128)(2,1)S(1)}, u32[]{:S(2)}, u32[]{:S(2)}) collective-permute-start(bf16[384,1280]{1,0:T(8,128)(2,1)} %get-tuple-element.101), channel_id=1, source_target_pairs={{16,0},{17,1},{18,2},{19,3},{20,4},{21,5},{22,6},{23,7},{24,8},{25... | collective-permute-start | bytes 2949128 | tf_op jit(solution)/shard_map/ppermute | solution.py:1925
  357.0 0.9 copy-start.11
  402.1 0.9 copy-start.10
  403.0 215.1 %copy-start = (bf16[2,384,1280]{2,1,0:T(8,128)(2,1)S(1)}, bf16[2,384,1280]{2,1,0:T(8,128)(2,1)}, u32[]{:S(2)}) copy-start(bf16[2,384,1280]{2,1,0:T(8,128)(2,1)} %get-tuple-element.91) | copy-start | bytes 5898244
  618.1 2.3 copy-start.1
  620.3 1.3 copy-start.9
  620.3 1.9 copy-start.7
  620.3 2.4 copy-start.4
  620.3 3.5 copy-start.6
  621.6 2.9 copy-start.3
  623.8 1.9 copy-start.8
  623.8 2.5 copy-start.2

commit v12 on v11

--- a/solution.py
+++ b/solution.py
@@ -397,10 +397,10 @@
             pair_of(pair)
         return
 
-    @pl.loop(0, width // 256)
+    @pl.loop(0, width // 640)
     def _(index):
-        pair_of(index * 2)
-        pair_of(index * 2 + 1)
+        for at in range(5):
+            pair_of(index * 5 + at)
 
 
 def attend_back(packed, grad_mixed, grad_packed, width, low=0, high=None):
@@ -437,10 +437,10 @@
             pair_of(pair)
         return
 
-    @pl.loop(0, width // 256)
+    @pl.loop(0, width // 640)
     def _(index):
-        pair_of(index * 2)
-        pair_of(index * 2 + 1)
+        for at in range(5):
+            pair_of(index * 5 + at)
 
 
 def forward_kernel(cell, held, at, active, entry_h, rows, w_qkv, w_out, w_up, w_down, *refs):
@@ -1028,7 +1028,7 @@
             wide_load(3, number, number).start()
 
     climbs = [load_ups]
-    climbs += [make(cell, number) for number in range(ups) for cell in range(cells) for make in (rise, bend)]
+    climbs += [make(0, number) for number in range(ups) for make in (rise, bend)]
 
     @pl.when(first)
     def _():
@@ -1079,7 +1079,7 @@
                 deep_load(offset, slot).start()
 
             queue.append(opening)
-            queue.extend(fall(cell, offset, slot) for cell in range(cells))
+            queue.append(fall(0, offset, slot))
 
     def serve(limit):
         for _ in range(limit):
@@ -1096,7 +1096,7 @@
                 if wait[0] == 0:
                     wait[1]()
                     late.remove(wait)
-            serve(3 if entry[1] in groups[-1] else 2)
+            serve(2)
         elif entry[0] == "done":
             if entry[1] == 0:
                 rest = [item for item in groups[0] if items[item][0] != 0]
@@ -1126,8 +1126,23 @@
                 serve(len(queue))
                 deep_ready([half])
     serve(len(queue))
-    for cell in range(cells):
-        on_first(finish(cell))
+
+    @pl.when(first)
+    def _():
+        finish(0)()
+        for cell in range(1, cells):
+            for offset in (0, 1):
+                deep_load(offset, offset).start()
+            for number in range(ups):
+                rise(cell, number)()
+                bend(cell, number)()
+            for offset in range(chips):
+                deep_load(offset, offset % 2).wait()
+                fall(cell, offset, offset % 2)()
+                if offset + 2 < chips:
+                    deep_load(offset + 2, offset % 2).start()
+            finish(cell)()
+
     for copy in sent:
         copy.wait_send()
     for copy in paired:

time: 638 us -> 633 us (level)
  waiting for transfers between devices: 86.4 us -> 79.5 us
    ppermute x3, waiting for transfers between devices: 86.4 us -> 79.5 us  [along(): return lax.ppermute(value, 'pipe', pairs)]
where the time goes in v12:
time: 633 us; the launch traced here: 623 us
  Pallas kernels  520 us (82%)
  waiting for transfers between devices  79.5 us (13%)
  local copies, waits for them, and re-layouts  12.9 us (2%)
  starting transfers between devices  7.14 us (1%)
    pallas_call x1, Pallas kernels, gather_forward(): pl.pallas_call(functools.partial(gather_forward_kernel, chips, items, gro...  223 us
    pallas_call x1, Pallas kernels, last_backward(): pl.pallas_call(functools.partial(last_backward_kernel, chips, items, cell...  215 us
    ppermute x3, waiting for transfers between devices, along(): return lax.ppermute(value, 'pipe', pairs)  79.5 us
    pallas_call x3, Pallas kernels, backward_tick(): pl.pallas_call(functools.partial(backward_kernel, cell, held, grad_at, en...  70.6 us
  transfers between devices with their start and end apart: 3, of which 3 were waited for; matrix products, arithmetic and copies ran while one was open for 0% of the time, Pallas kernels for 9%

profile of v12, /device:TPU:0, one launch (start us, length us, event | category | flops | bytes accessed | tf_op | source)
XLA Modules:
  0.0 623.1 jit_solution(10300818102546340061)
XLA Ops:
  0.6 0.7 reduce
  1.3 0.1 reshape_squeeze.3
  1.4 0.1 pad.3.clone
  1.5 1.4 maximum_bitcast_fusion.refs_0_
  2.9 223.4 %shard_map.169 = (bf16[16,16,80]{2,1,0:T(8,128)(2,1)}, bf16[16,80,3840]{2,1,0:T(8,128)(2,1)}, bf16[16,80,1280]{2,1,0:T(8,128)(2,1)}, bf16[16,80,5120]{2,1,0:T(8,...) custom-call(bf16[16,80]{1,0:T(8,128)(2,1)} %maximum_bitcast_fusion.r, ...), custom_call_target="tpu_custom_call" | custom-call | flops 30198988800 | bytes 157286400 | tf_op jit(solution)/shard_map/pallas_call | solution.py:1172
  226.3 4.6 collective-permute-start
  230.9 0.6 fusion
  231.5 1.8 shard_map.170
  233.3 15.9 %collective-permute-done.entry_h = bf16[384,1280]{1,0:T(8,128)(2,1)S(1)} collective-permute-done((bf16[384,1280]{1,0:T(8,128)(2,1)}, bf16[384,1280]{1,0:T(8,128)(2,1)S(1)}, u32[]{:S(2)}, u32[]{:S(2)}) %collective-permute-start) | collective-permute-done | bytes 983072 | tf_op jit(solution)/shard_map/ppermute | solution.py:1940
  249.2 0.9 copy-done.5
  250.1 9.7 %shard_map.171 = (bf16[384,1280]{1,0:T(8,128)(2,1)}, bf16[2,384,1280]{2,1,0:T(8,128)(2,1)}, bf16[2,384,1280]{2,1,0:T(8,128)(2,1)}, bf16[2,384,3840]{2,1,0:T(8,12...) custom-call(s32[1]{0:T(128)} %bitcast.active, ...), custom_call_target="tpu_custom_call", output_to_operand_aliasing={{1}: (7, {}), {2}: (8, {}), {3}: (9, {}), {4}: (10, {}), {5... | custom-call | flops 18119393280 | bytes 39321600 | tf_op jit(solution)/shard_map/pallas_call | solution.py:562
  259.8 15.6 %shard_map.172 = (bf16[384,1280]{1,0:T(8,128)(2,1)}, bf16[2,384,1280]{2,1,0:T(8,128)(2,1)}, bf16[2,384,3840]{2,1,0:T(8,128)(2,1)}, bf16[2,384,1280]{2,1,0:T(8,12...) custom-call(s32[1]{0:T(128)} %bitcast.active, ...), custom_call_target="tpu_custom_call" | custom-call | flops 22649241600 | bytes 39321600 | tf_op jit(solution)/shard_map/pallas_call | solution.py:729
  275.4 1.3 collective-permute-start.2
  276.7 14.3 %shard_map.173 = (bf16[384,1280]{1,0:T(8,128)(2,1)}, bf16[2,384,1280]{2,1,0:T(8,128)(2,1)}, bf16[2,384,3840]{2,1,0:T(8,128)(2,1)}, bf16[2,384,1280]{2,1,0:T(8,12...) custom-call(s32[1]{0:T(128)} %bitcast.active, ...), custom_call_target="tpu_custom_call", output_to_operand_aliasing={{1}: (12, {}), {2}: (13, {}), {3}: (14, {}), {4}: (15, {}),... | custom-call | flops 22649241600 | bytes 39321600 | tf_op jit(solution)/shard_map/pallas_call | solution.py:729
  291.1 1.3 collective-permute-start.1
  292.4 61.3 %collective-permute-done.2.grad_h = bf16[384,1280]{1,0:T(8,128)(2,1)S(1)} collective-permute-done((bf16[384,1280]{1,0:T(8,128)(2,1)}, bf16[384,1280]{1,0:T(8,128)(2,1)S(1)}, u32[]{:S(2)}, u32[]{:S(2)}) %collective-permute-start.2) | collective-permute-done | bytes 983072 | tf_op jit(solution)/shard_map/ppermute | solution.py:1940
  353.6 0.9 copy-done.11
  354.6 40.6 %shard_map.174 = (bf16[384,1280]{1,0:T(8,128)(2,1)}, bf16[2,384,1280]{2,1,0:T(8,128)(2,1)}, bf16[2,384,3840]{2,1,0:T(8,128)(2,1)}, bf16[2,384,1280]{2,1,0:T(8,12...) custom-call(s32[1]{0:T(128)} %bitcast.12.active, ...), custom_call_target="tpu_custom_call", output_to_operand_aliasing={{1}: (12, {}), {2}: (13, {}), {3}: (14, {}), {4}: (15, {}),... | custom-call | flops 22649241600 | bytes 39321600 | tf_op jit(solution)/shard_map/pallas_call | solution.py:729
  395.2 2.3 collective-permute-done.1.refs_0_
  397.5 0.9 copy-done.10
  398.5 215.0 %shard_map.175 = (bf16[2,384,1280]{2,1,0:T(8,128)(2,1)}, bf16[768,3840]{1,0:T(8,128)(2,1)}, bf16[768,1280]{1,0:T(8,128)(2,1)}, bf16[768,5120]{1,0:T(8,128)(2,1)}...) custom-call(bf16[384,1280]{1,0:T(8,128)(2,1)} %copy-done.10, ...), custom_call_target="tpu_custom_call", output_to_operand_aliasing={{0}: (15, {}), {1}: (16, {}), {2}: (17, {}), {3}: (18, {}),... | custom-call | flops 45298483200 | bytes 262144000 | tf_op jit(solution)/shard_map/pallas_call | solution.py:1827
  613.5 1.3 copy.94
  614.8 1.0 copy-done.1
  615.8 1.3 copy.95
  617.0 0.0 copy-done.9
  617.0 0.6 copy.96
  617.6 0.6 copy.97
  618.2 1.0 copy.98
  619.2 0.8 copy.99
  620.0 1.2 copy.100
  621.1 0.6 copy.101
  621.7 1.2 copy.102
  (23 shorter events, 0.0 us)
Async XLA Ops:
  2.9 228.0 %copy-start.12 = (s32[2]{0:T(128)S(1)}, s32[2]{0:T(128)}, u32[]{:S(2)}) copy-start(s32[2]{0:T(128)} %param.12) | copy-start | bytes 28
  226.3 22.9 %collective-permute-start = (bf16[384,1280]{1,0:T(8,128)(2,1)}, bf16[384,1280]{1,0:T(8,128)(2,1)S(1)}, u32[]{:S(2)}, u32[]{:S(2)}) collective-permute-start(bf16[384,1280]{1,0:T(8,128)(2,1)} %get-tuple-element.68), channel_id=1, source_target_pairs={{0,16},{1,17},{2,18},{3,19},{4,20},{5,21},{6,22},{7,23},{8,24},{9,... | collective-permute-start | bytes 2949128 | tf_op jit(solution)/shard_map/ppermute | solution.py:1940
  249.2 0.9 copy-start.5
  275.4 78.2 %collective-permute-start.2 = (bf16[384,1280]{1,0:T(8,128)(2,1)}, bf16[384,1280]{1,0:T(8,128)(2,1)S(1)}, u32[]{:S(2)}, u32[]{:S(2)}) collective-permute-start(bf16[384,1280]{1,0:T(8,128)(2,1)} %get-tuple-element.103), channel_id=1, source_target_pairs={{16,0},{17,1},{18,2},{19,3},{20,4},{21,5},{22,6},{23,7},{24,8},{25... | collective-permute-start | bytes 2949128 | tf_op jit(solution)/shard_map/ppermute | solution.py:1940
  291.1 106.5 %collective-permute-start.1 = (bf16[384,1280]{1,0:T(8,128)(2,1)}, bf16[384,1280]{1,0:T(8,128)(2,1)S(1)}, u32[]{:S(2)}, u32[]{:S(2)}) collective-permute-start(bf16[384,1280]{1,0:T(8,128)(2,1)} %get-tuple-element.101), channel_id=1, source_target_pairs={{16,0},{17,1},{18,2},{19,3},{20,4},{21,5},{22,6},{23,7},{24,8},{25... | collective-permute-start | bytes 2949128 | tf_op jit(solution)/shard_map/ppermute | solution.py:1940
  353.6 0.9 copy-start.11
  397.5 0.9 copy-start.10
  398.5 215.0 %copy-start = (bf16[2,384,1280]{2,1,0:T(8,128)(2,1)S(1)}, bf16[2,384,1280]{2,1,0:T(8,128)(2,1)}, u32[]{:S(2)}) copy-start(bf16[2,384,1280]{2,1,0:T(8,128)(2,1)} %get-tuple-element.91) | copy-start | bytes 5898244
  613.5 2.3 copy-start.1
  615.8 1.3 copy-start.9
  615.8 1.9 copy-start.7
  615.8 2.4 copy-start.4
  615.8 3.5 copy-start.6
  617.0 2.9 copy-start.3
  619.2 1.9 copy-start.8
  619.2 2.5 copy-start.2

commit v13 on v12

--- a/solution.py
+++ b/solution.py
@@ -1053,7 +1053,7 @@
     plan = []
     for number, group in enumerate(groups):
         for step in range(1, half + 1):
-            if step == half and number + 1 < len(groups):
+            if step == max(1, half - 1) and number + 1 < len(groups):
                 plan.append(("open", number + 1))
             for item in group:
                 for way in (0, 1):

time: 633 us -> 637 us (level)
  no operation moved by 1% of the time
where the time goes in v13:
time: 637 us; the launch traced here: 627 us
  Pallas kernels  524 us (82%)
  waiting for transfers between devices  79.5 us (12%)
  local copies, waits for them, and re-layouts  12.9 us (2%)
  starting transfers between devices  7.14 us (1%)
    pallas_call x1, Pallas kernels, gather_forward(): pl.pallas_call(functools.partial(gather_forward_kernel, chips, items, gro...  227 us
    pallas_call x1, Pallas kernels, last_backward(): pl.pallas_call(functools.partial(last_backward_kernel, chips, items, cell...  215 us
    ppermute x3, waiting for transfers between devices, along(): return lax.ppermute(value, 'pipe', pairs)  79.5 us
    pallas_call x3, Pallas kernels, backward_tick(): pl.pallas_call(functools.partial(backward_kernel, cell, held, grad_at, en...  70.6 us
  transfers between devices with their start and end apart: 3, of which 3 were waited for; matrix products, arithmetic and copies ran while one was open for 0% of the time, Pallas kernels for 9%

profile of v13, /device:TPU:0, one launch (start us, length us, event | category | flops | bytes accessed | tf_op | source)
XLA Modules:
  0.0 626.6 jit_solution(4306201426837226639)
XLA Ops:
  0.6 0.7 reduce
  1.3 0.1 reshape_squeeze.3
  1.4 0.1 pad.3.clone
  1.5 1.4 maximum_bitcast_fusion.refs_0_
  2.9 227.0 %shard_map.169 = (bf16[16,16,80]{2,1,0:T(8,128)(2,1)}, bf16[16,80,3840]{2,1,0:T(8,128)(2,1)}, bf16[16,80,1280]{2,1,0:T(8,128)(2,1)}, bf16[16,80,5120]{2,1,0:T(8,...) custom-call(bf16[16,80]{1,0:T(8,128)(2,1)} %maximum_bitcast_fusion.r, ...), custom_call_target="tpu_custom_call" | custom-call | flops 30198988800 | bytes 157286400 | tf_op jit(solution)/shard_map/pallas_call | solution.py:1172
  229.8 4.6 collective-permute-start
  234.4 0.6 fusion
  235.0 1.8 shard_map.170
  236.8 15.9 %collective-permute-done.entry_h = bf16[384,1280]{1,0:T(8,128)(2,1)S(1)} collective-permute-done((bf16[384,1280]{1,0:T(8,128)(2,1)}, bf16[384,1280]{1,0:T(8,128)(2,1)S(1)}, u32[]{:S(2)}, u32[]{:S(2)}) %collective-permute-start) | collective-permute-done | bytes 983072 | tf_op jit(solution)/shard_map/ppermute | solution.py:1940
  252.7 0.9 copy-done.5
  253.6 9.7 %shard_map.171 = (bf16[384,1280]{1,0:T(8,128)(2,1)}, bf16[2,384,1280]{2,1,0:T(8,128)(2,1)}, bf16[2,384,1280]{2,1,0:T(8,128)(2,1)}, bf16[2,384,3840]{2,1,0:T(8,12...) custom-call(s32[1]{0:T(128)} %bitcast.active, ...), custom_call_target="tpu_custom_call", output_to_operand_aliasing={{1}: (7, {}), {2}: (8, {}), {3}: (9, {}), {4}: (10, {}), {5... | custom-call | flops 18119393280 | bytes 39321600 | tf_op jit(solution)/shard_map/pallas_call | solution.py:562
  263.3 15.6 %shard_map.172 = (bf16[384,1280]{1,0:T(8,128)(2,1)}, bf16[2,384,1280]{2,1,0:T(8,128)(2,1)}, bf16[2,384,3840]{2,1,0:T(8,128)(2,1)}, bf16[2,384,1280]{2,1,0:T(8,12...) custom-call(s32[1]{0:T(128)} %bitcast.active, ...), custom_call_target="tpu_custom_call" | custom-call | flops 22649241600 | bytes 39321600 | tf_op jit(solution)/shard_map/pallas_call | solution.py:729
  278.9 1.3 collective-permute-start.2
  280.2 14.3 %shard_map.173 = (bf16[384,1280]{1,0:T(8,128)(2,1)}, bf16[2,384,1280]{2,1,0:T(8,128)(2,1)}, bf16[2,384,3840]{2,1,0:T(8,128)(2,1)}, bf16[2,384,1280]{2,1,0:T(8,12...) custom-call(s32[1]{0:T(128)} %bitcast.active, ...), custom_call_target="tpu_custom_call", output_to_operand_aliasing={{1}: (12, {}), {2}: (13, {}), {3}: (14, {}), {4}: (15, {}),... | custom-call | flops 22649241600 | bytes 39321600 | tf_op jit(solution)/shard_map/pallas_call | solution.py:729
  294.6 1.3 collective-permute-start.1
  295.9 61.3 %collective-permute-done.2.grad_h = bf16[384,1280]{1,0:T(8,128)(2,1)S(1)} collective-permute-done((bf16[384,1280]{1,0:T(8,128)(2,1)}, bf16[384,1280]{1,0:T(8,128)(2,1)S(1)}, u32[]{:S(2)}, u32[]{:S(2)}) %collective-permute-start.2) | collective-permute-done | bytes 983072 | tf_op jit(solution)/shard_map/ppermute | solution.py:1940
  357.2 0.9 copy-done.11
  358.1 40.6 %shard_map.174 = (bf16[384,1280]{1,0:T(8,128)(2,1)}, bf16[2,384,1280]{2,1,0:T(8,128)(2,1)}, bf16[2,384,3840]{2,1,0:T(8,128)(2,1)}, bf16[2,384,1280]{2,1,0:T(8,12...) custom-call(s32[1]{0:T(128)} %bitcast.12.active, ...), custom_call_target="tpu_custom_call", output_to_operand_aliasing={{1}: (12, {}), {2}: (13, {}), {3}: (14, {}), {4}: (15, {}),... | custom-call | flops 22649241600 | bytes 39321600 | tf_op jit(solution)/shard_map/pallas_call | solution.py:729
  398.7 2.3 collective-permute-done.1.refs_0_
  401.0 0.9 copy-done.10
  402.0 215.0 %shard_map.175 = (bf16[2,384,1280]{2,1,0:T(8,128)(2,1)}, bf16[768,3840]{1,0:T(8,128)(2,1)}, bf16[768,1280]{1,0:T(8,128)(2,1)}, bf16[768,5120]{1,0:T(8,128)(2,1)}...) custom-call(bf16[384,1280]{1,0:T(8,128)(2,1)} %copy-done.10, ...), custom_call_target="tpu_custom_call", output_to_operand_aliasing={{0}: (15, {}), {1}: (16, {}), {2}: (17, {}), {3}: (18, {}),... | custom-call | flops 45298483200 | bytes 262144000 | tf_op jit(solution)/shard_map/pallas_call | solution.py:1827
  617.0 1.3 copy.94
  618.3 1.0 copy-done.1
  619.3 1.3 copy.95
  620.6 0.6 copy.96
  621.1 0.0 copy-done.7
  621.1 0.6 copy.97
  621.7 1.0 copy.98
  622.7 0.8 copy.99
  623.5 1.2 copy.100
  624.7 0.6 copy.101
  625.2 1.2 copy.102
  (23 shorter events, 0.0 us)
Async XLA Ops:
  2.9 231.5 %copy-start.12 = (s32[2]{0:T(128)S(1)}, s32[2]{0:T(128)}, u32[]{:S(2)}) copy-start(s32[2]{0:T(128)} %param.12) | copy-start | bytes 28
  229.8 22.9 %collective-permute-start = (bf16[384,1280]{1,0:T(8,128)(2,1)}, bf16[384,1280]{1,0:T(8,128)(2,1)S(1)}, u32[]{:S(2)}, u32[]{:S(2)}) collective-permute-start(bf16[384,1280]{1,0:T(8,128)(2,1)} %get-tuple-element.68), channel_id=1, source_target_pairs={{0,16},{1,17},{2,18},{3,19},{4,20},{5,21},{6,22},{7,23},{8,24},{9,... | collective-permute-start | bytes 2949128 | tf_op jit(solution)/shard_map/ppermute | solution.py:1940
  252.7 0.9 copy-start.5
  278.9 78.2 %collective-permute-start.2 = (bf16[384,1280]{1,0:T(8,128)(2,1)}, bf16[384,1280]{1,0:T(8,128)(2,1)S(1)}, u32[]{:S(2)}, u32[]{:S(2)}) collective-permute-start(bf16[384,1280]{1,0:T(8,128)(2,1)} %get-tuple-element.103), channel_id=1, source_target_pairs={{16,0},{17,1},{18,2},{19,3},{20,4},{21,5},{22,6},{23,7},{24,8},{25... | collective-permute-start | bytes 2949128 | tf_op jit(solution)/shard_map/ppermute | solution.py:1940
  294.6 106.5 %collective-permute-start.1 = (bf16[384,1280]{1,0:T(8,128)(2,1)}, bf16[384,1280]{1,0:T(8,128)(2,1)S(1)}, u32[]{:S(2)}, u32[]{:S(2)}) collective-permute-start(bf16[384,1280]{1,0:T(8,128)(2,1)} %get-tuple-element.101), channel_id=1, source_target_pairs={{16,0},{17,1},{18,2},{19,3},{20,4},{21,5},{22,6},{23,7},{24,8},{25... | collective-permute-start | bytes 2949128 | tf_op jit(solution)/shard_map/ppermute | solution.py:1940
  357.2 0.9 copy-start.11
  401.0 0.9 copy-start.10
  402.0 215.0 %copy-start = (bf16[2,384,1280]{2,1,0:T(8,128)(2,1)S(1)}, bf16[2,384,1280]{2,1,0:T(8,128)(2,1)}, u32[]{:S(2)}) copy-start(bf16[2,384,1280]{2,1,0:T(8,128)(2,1)} %get-tuple-element.91) | copy-start | bytes 5898244
  617.0 2.3 copy-start.1
  619.3 1.3 copy-start.9
  619.3 1.9 copy-start.7
  619.3 2.4 copy-start.4
  619.3 3.5 copy-start.6
  620.6 2.9 copy-start.3
  622.7 1.9 copy-start.8
  622.7 2.5 copy-start.2
